TPU v7x, 32 devices: a whole 2x2x4 slice. The times are simulated.
32 devices in a mesh: fsdp: 2 (over core), ctx: 4 (over y, x), tp: 4 (over z).
Axes of the slice: x: 2, y: 2, z: 4, core: 2. Of those that a mesh axis runs over, the one named last changes fastest.
Arguments:
- hidden_in: bfloat16 [2, 2048, 2304], P('fsdp', 'ctx'), may hold values from -6 to 6
- lengths: int32 [2], P('fsdp'), may hold values from 512 to 2048
- query_weight: bfloat16 [2304, 2048], P(('fsdp', 'ctx'), 'tp'), may hold values from -0.125 to 0.125
- key_weight: bfloat16 [2304, 1024], P(('fsdp', 'ctx'), 'tp'), may hold values from -0.125 to 0.125
- value_weight: bfloat16 [2304, 1024], P(('fsdp', 'ctx'), 'tp'), may hold values from -0.125 to 0.125
- w_out: bfloat16 [2048, 2304], P('tp', ('fsdp', 'ctx')), may hold values from -0.125 to 0.125
- w_gate: bfloat16 [2304, 9216], P(('fsdp', 'ctx'), 'tp'), may hold values from -0.125 to 0.125
- w_up: bfloat16 [2304, 9216], P(('fsdp', 'ctx'), 'tp'), may hold values from -0.125 to 0.125
- w_down: bfloat16 [9216, 2304], P('tp', ('fsdp', 'ctx')), may hold values from -0.0625 to 0.0625
- gain_attn_in: bfloat16 [2304], P(('fsdp', 'ctx')), may hold values from -0.5 to 0.5
- gain_attn_out: bfloat16 [2304], P(('fsdp', 'ctx')), may hold values from -0.5 to 0.5
- gain_ffn_in: bfloat16 [2304], P(('fsdp', 'ctx')), may hold values from -0.5 to 0.5
- gain_ffn_out: bfloat16 [2304], P(('fsdp', 'ctx')), may hold values from -0.5 to 0.5
- cotangent: bfloat16 [2, 2048, 2304], P('fsdp', 'ctx'), may hold values from -6 to 6
Outputs:
- output: bfloat16 [2, 2048, 2304], P('fsdp', 'ctx')
- grad_hidden_in: bfloat16 [2, 2048, 2304], P('fsdp', 'ctx')
- grad_w_query: float32 [2304, 2048], P(('fsdp', 'ctx'), 'tp')
- grad_w_key: float32 [2304, 1024], P(('fsdp', 'ctx'), 'tp')
- grad_w_value: float32 [2304, 1024], P(('fsdp', 'ctx'), 'tp')
- grad_w_out: float32 [2048, 2304], P('tp', ('fsdp', 'ctx'))
- grad_w_gate: float32 [2304, 9216], P(('fsdp', 'ctx'), 'tp')
- grad_w_up: float32 [2304, 9216], P(('fsdp', 'ctx'), 'tp')
- grad_w_down: float32 [9216, 2304], P('tp', ('fsdp', 'ctx'))
- grad_gain_attn_in: float32 [2304], P(('fsdp', 'ctx'))
- grad_gain_attn_out: float32 [2304], P(('fsdp', 'ctx'))
- grad_gain_ffn_in: float32 [2304], P(('fsdp', 'ctx'))
- grad_gain_ffn_out: float32 [2304], P(('fsdp', 'ctx'))
All inputs are finite; a program needn't handle non-finite values.
Results may differ from a plain program's by a relative error of at most 0.024.
Values may be sent and summed in bfloat16 or wider, within the bound.
No kernel may reach another device: no remote copies, remote signals or barrier semaphores. Data moves between devices by JAX's collectives and lax.ppermute only.
A program may use at most 192 MiB of HBM per device.

v0:
```python
import jax
import jax.numpy as jnp
from jax import lax
from jax.sharding import PartitionSpec as P

QUERY_HEADS = 8
KEY_VALUE_HEADS = 4
HEAD_SIZE = 256
SEQUENCE_SLOTS = 2048


EPS = 1e-06
CAP = 50.0
QSCALE = 0.0625
NEG = -1e30


def normalize(value_rows):
    factor = lax.rsqrt(jnp.mean(value_rows * value_rows, -1, keepdims=True) + EPS)
    return (value_rows * factor, factor)


def norm_back(grad_hat, normed, factor):
    return factor * (grad_hat - normed * jnp.mean(grad_hat * normed, -1, keepdims=True))


def plain_dot(first, second):
    return jnp.dot(first, second, preferred_element_type=jnp.float32)


def left_dot(first, second):
    return lax.dot_general(
        first, second, (((0,), (0,)), ((), ())), preferred_element_type=jnp.float32
    )


def right_dot(first, second):
    return lax.dot_general(
        first, second, (((1,), (1,)), ((), ())), preferred_element_type=jnp.float32
    )


def gelu_tanh(value_rows):
    return jax.nn.gelu(value_rows, approximate=True)


def body(
    hidden_in,
    lengths,
    query_weight,
    key_weight,
    value_weight,
    w_out,
    w_gate,
    w_up,
    w_down,
    gain_attn_in,
    gain_attn_out,
    gain_ffn_in,
    gain_ffn_out,
    cotangent,
):
    seqs_here, tok_here, width = hidden_in.shape
    row_count = seqs_here * tok_here
    head_groups = QUERY_HEADS // KEY_VALUE_HEADS
    gathered = (
        lax.all_gather(query_weight, ("fsdp", "ctx"), axis=0, tiled=True),
        lax.all_gather(key_weight, ("fsdp", "ctx"), axis=0, tiled=True),
        lax.all_gather(value_weight, ("fsdp", "ctx"), axis=0, tiled=True),
        lax.all_gather(w_out, ("fsdp", "ctx"), axis=1, tiled=True),
        lax.all_gather(w_gate, ("fsdp", "ctx"), axis=0, tiled=True),
        lax.all_gather(w_up, ("fsdp", "ctx"), axis=0, tiled=True),
        lax.all_gather(w_down, ("fsdp", "ctx"), axis=1, tiled=True),
        lax.all_gather(gain_attn_in, ("fsdp", "ctx"), axis=0, tiled=True),
        lax.all_gather(gain_attn_out, ("fsdp", "ctx"), axis=0, tiled=True),
        lax.all_gather(gain_ffn_in, ("fsdp", "ctx"), axis=0, tiled=True),
        lax.all_gather(gain_ffn_out, ("fsdp", "ctx"), axis=0, tiled=True),
    )
    query_full, key_full, value_full, out_full, gate_full, up_full, down_full = gathered[:7]
    scale_one = 1.0 + gathered[7].astype(jnp.float32)
    scale_two = 1.0 + gathered[8].astype(jnp.float32)
    scale_three = 1.0 + gathered[9].astype(jnp.float32)
    scale_four = 1.0 + gathered[10].astype(jnp.float32)
    kv_local = key_full.shape[1] // HEAD_SIZE
    own_start = lax.axis_index("ctx") * tok_here
    query_pos = own_start + jnp.arange(tok_here, dtype=jnp.int32)
    key_pos = jnp.arange(SEQUENCE_SLOTS, dtype=jnp.int32)
    valid = query_pos[None, :] < lengths[:, None]
    allowed = (
        (key_pos[None, None, :] <= query_pos[None, :, None])
        & (key_pos[None, None, :] < lengths[:, None, None])
    )[:, None, None]
    flat_in = hidden_in.astype(jnp.float32).reshape(row_count, width)
    normed_one, factor_one = normalize(flat_in)
    attention_input = (normed_one * scale_one).astype(jnp.bfloat16)
    query_b = plain_dot(attention_input, query_full).astype(jnp.bfloat16)
    key_b = (
        plain_dot(attention_input, key_full)
        .astype(jnp.bfloat16)
        .reshape(seqs_here, tok_here, kv_local * HEAD_SIZE)
    )
    value_b = (
        plain_dot(attention_input, value_full)
        .astype(jnp.bfloat16)
        .reshape(seqs_here, tok_here, kv_local * HEAD_SIZE)
    )
    key_all, value_all = (
        lax.all_gather(key_b, "ctx", axis=1, tiled=True),
        lax.all_gather(value_b, "ctx", axis=1, tiled=True),
    )
    query_five = query_b.reshape(seqs_here, tok_here, kv_local, head_groups, HEAD_SIZE)
    key_four = key_all.reshape(seqs_here, SEQUENCE_SLOTS, kv_local, HEAD_SIZE)
    value_four = value_all.reshape(seqs_here, SEQUENCE_SLOTS, kv_local, HEAD_SIZE)
    raw = (
        jnp.einsum("stkgd,sukd->skgtu", query_five, key_four, preferred_element_type=jnp.float32)
        * QSCALE
    )
    bent = jnp.tanh(raw / CAP)
    masked = jnp.where(allowed, CAP * bent, NEG)
    largest = jnp.max(masked, -1, keepdims=True)
    logsum = largest + jnp.log(jnp.sum(jnp.exp(masked - largest), -1, keepdims=True))
    probs = jnp.exp(masked - logsum)
    probs_b = probs.astype(jnp.bfloat16)
    attended = (
        jnp.einsum("skgtu,sukd->stkgd", probs_b, value_four, preferred_element_type=jnp.float32)
        .astype(jnp.bfloat16)
        .reshape(row_count, -1)
    )
    attn = lax.psum(plain_dot(attended, out_full).astype(jnp.bfloat16), "tp").astype(jnp.float32)
    normed_two, factor_two = normalize(attn)
    after_attn = flat_in + normed_two * scale_two
    normed_three, factor_three = normalize(after_attn)
    ffn_in = (normed_three * scale_three).astype(jnp.bfloat16)
    gate = plain_dot(ffn_in, gate_full)
    upward = plain_dot(ffn_in, up_full)
    activated, gelu_pull = jax.vjp(gelu_tanh, gate)
    hidden_b = (activated * upward).astype(jnp.bfloat16)
    ffn_out = lax.psum(plain_dot(hidden_b, down_full).astype(jnp.bfloat16), "tp").astype(
        jnp.float32
    )
    normed_four, factor_four = normalize(ffn_out)
    result = after_attn + normed_four * scale_four
    cot = cotangent.astype(jnp.float32).reshape(row_count, width) * valid.reshape(
        row_count, 1
    ).astype(jnp.float32)
    query_back, key_back, value_back, out_back, gate_back, up_back, down_back = (
        lax.all_gather(query_weight, ("fsdp", "ctx"), axis=0, tiled=True),
        lax.all_gather(key_weight, ("fsdp", "ctx"), axis=0, tiled=True),
        lax.all_gather(value_weight, ("fsdp", "ctx"), axis=0, tiled=True),
        lax.all_gather(w_out, ("fsdp", "ctx"), axis=1, tiled=True),
        lax.all_gather(w_gate, ("fsdp", "ctx"), axis=0, tiled=True),
        lax.all_gather(w_up, ("fsdp", "ctx"), axis=0, tiled=True),
        lax.all_gather(w_down, ("fsdp", "ctx"), axis=1, tiled=True),
    )
    grad_gain_four = jnp.sum(cot * normed_four, 0)
    dffn_b = norm_back(cot * scale_four, normed_four, factor_four).astype(jnp.bfloat16)
    grad_down = left_dot(hidden_b, dffn_b)
    dhidden = right_dot(dffn_b, down_back)
    dgate_b = gelu_pull(dhidden * upward)[0].astype(jnp.bfloat16)
    dup_b = (dhidden * activated).astype(jnp.bfloat16)
    grad_gate = left_dot(ffn_in, dgate_b)
    grad_up = left_dot(ffn_in, dup_b)
    dffn_in = lax.psum(
        (right_dot(dgate_b, gate_back) + right_dot(dup_b, up_back)).astype(jnp.bfloat16), "tp"
    ).astype(jnp.float32)
    grad_gain_three = jnp.sum(dffn_in * normed_three, 0)
    dafter = cot + norm_back(dffn_in * scale_three, normed_three, factor_three)
    grad_gain_two = jnp.sum(dafter * normed_two, 0)
    dattn_b = norm_back(dafter * scale_two, normed_two, factor_two).astype(jnp.bfloat16)
    grad_out = left_dot(attended, dattn_b)
    dattended = right_dot(dattn_b, out_back).astype(jnp.bfloat16).reshape(query_five.shape)
    dprobs = jnp.einsum(
        "stkgd,sukd->skgtu", dattended, value_four, preferred_element_type=jnp.float32
    )
    weighted = jnp.sum(probs * dprobs, -1, keepdims=True)
    draw_b = (probs * (dprobs - weighted) * (1.0 - bent * bent)).astype(jnp.bfloat16)
    dquery_b = (
        (
            jnp.einsum("skgtu,sukd->stkgd", draw_b, key_four, preferred_element_type=jnp.float32)
            * QSCALE
        )
        .astype(jnp.bfloat16)
        .reshape(row_count, -1)
    )
    dvalue_part = jnp.einsum(
        "skgtu,stkgd->sukd", probs_b, dattended, preferred_element_type=jnp.float32
    )
    dkey_part = (
        jnp.einsum("skgtu,stkgd->sukd", draw_b, query_five, preferred_element_type=jnp.float32)
        * QSCALE
    )
    dkey, dvalue = (
        lax.psum_scatter(
            dkey_part.astype(jnp.bfloat16), "ctx", scatter_dimension=1, tiled=True
        ).astype(jnp.float32),
        lax.psum_scatter(
            dvalue_part.astype(jnp.bfloat16), "ctx", scatter_dimension=1, tiled=True
        ).astype(jnp.float32),
    )
    dkey_b = dkey.astype(jnp.bfloat16).reshape(row_count, -1)
    dvalue_b = dvalue.astype(jnp.bfloat16).reshape(row_count, -1)
    grad_query = left_dot(attention_input, dquery_b)
    grad_key = left_dot(attention_input, dkey_b)
    grad_value = left_dot(attention_input, dvalue_b)
    dattn_in = lax.psum(
        (
            right_dot(dquery_b, query_back)
            + right_dot(dkey_b, key_back)
            + right_dot(dvalue_b, value_back)
        ).astype(jnp.bfloat16),
        "tp",
    ).astype(jnp.float32)
    grad_gain_one = jnp.sum(dattn_in * normed_one, 0)
    grad_input = dafter + norm_back(dattn_in * scale_one, normed_one, factor_one)
    summed = (
        lax.psum_scatter(
            grad_query.astype(jnp.bfloat16), ("fsdp", "ctx"), scatter_dimension=0, tiled=True
        ).astype(jnp.float32),
        lax.psum_scatter(
            grad_key.astype(jnp.bfloat16), ("fsdp", "ctx"), scatter_dimension=0, tiled=True
        ).astype(jnp.float32),
        lax.psum_scatter(
            grad_value.astype(jnp.bfloat16), ("fsdp", "ctx"), scatter_dimension=0, tiled=True
        ).astype(jnp.float32),
        lax.psum_scatter(
            grad_out.astype(jnp.bfloat16), ("fsdp", "ctx"), scatter_dimension=1, tiled=True
        ).astype(jnp.float32),
        lax.psum_scatter(
            grad_gate.astype(jnp.bfloat16), ("fsdp", "ctx"), scatter_dimension=0, tiled=True
        ).astype(jnp.float32),
        lax.psum_scatter(
            grad_up.astype(jnp.bfloat16), ("fsdp", "ctx"), scatter_dimension=0, tiled=True
        ).astype(jnp.float32),
        lax.psum_scatter(
            grad_down.astype(jnp.bfloat16), ("fsdp", "ctx"), scatter_dimension=1, tiled=True
        ).astype(jnp.float32),
        lax.psum_scatter(
            grad_gain_one.astype(jnp.bfloat16), ("fsdp", "ctx"), scatter_dimension=0, tiled=True
        ).astype(jnp.float32),
        lax.psum_scatter(
            grad_gain_two.astype(jnp.bfloat16), ("fsdp", "ctx"), scatter_dimension=0, tiled=True
        ).astype(jnp.float32),
        lax.psum_scatter(
            grad_gain_three.astype(jnp.bfloat16), ("fsdp", "ctx"), scatter_dimension=0, tiled=True
        ).astype(jnp.float32),
        lax.psum_scatter(
            grad_gain_four.astype(jnp.bfloat16), ("fsdp", "ctx"), scatter_dimension=0, tiled=True
        ).astype(jnp.float32),
    )
    return (
        result.astype(jnp.bfloat16).reshape(hidden_in.shape),
        grad_input.astype(jnp.bfloat16).reshape(hidden_in.shape),
        summed[0],
        summed[1],
        summed[2],
        summed[3],
        summed[4],
        summed[5],
        summed[6],
        summed[7],
        summed[8],
        summed[9],
        summed[10],
    )


def solution(mesh):
    return jax.shard_map(
        body,
        mesh=mesh,
        in_specs=(
            P("fsdp", "ctx", None),
            P("fsdp"),
            P(("fsdp", "ctx"), "tp"),
            P(("fsdp", "ctx"), "tp"),
            P(("fsdp", "ctx"), "tp"),
            P("tp", ("fsdp", "ctx")),
            P(("fsdp", "ctx"), "tp"),
            P(("fsdp", "ctx"), "tp"),
            P("tp", ("fsdp", "ctx")),
            P(("fsdp", "ctx")),
            P(("fsdp", "ctx")),
            P(("fsdp", "ctx")),
            P(("fsdp", "ctx")),
            P("fsdp", "ctx", None),
        ),
        out_specs=(
            P("fsdp", "ctx", None),
            P("fsdp", "ctx", None),
            P(("fsdp", "ctx"), "tp"),
            P(("fsdp", "ctx"), "tp"),
            P(("fsdp", "ctx"), "tp"),
            P("tp", ("fsdp", "ctx")),
            P(("fsdp", "ctx"), "tp"),
            P(("fsdp", "ctx"), "tp"),
            P("tp", ("fsdp", "ctx")),
            P(("fsdp", "ctx")),
            P(("fsdp", "ctx")),
            P(("fsdp", "ctx")),
            P(("fsdp", "ctx")),
        ),
        check_vma=False,
    )
```

profile of v0, /device:TPU:0, one launch (start us, length us, event | category | flops | bytes accessed | tf_op | source)
XLA Modules:
  0.0 1342.0 jit_solution(2437237849600074473)
XLA Ops:
  14.9 28.2 %all-reduce.9 = (bf16[2304]{0:T(1024)(128)(2,1)S(1)}, bf16[2304]{0:T(1024)(128)(2,1)S(1)}, bf16[2304]{0:T(1024)(128)(2,1)S(1)}, bf16[2304]{0:T(1024)(128)(2,1)S(1)}) all-reduce(bf16[2304]{0:T(1024)(128)(2,1)S(1)} %dynamic-update-slice.2, ...), channel_id=1, replica_groups=mesh['fsdp'=2,'ctx'=4,'tp'=4] {'fsdp','ctx'}, use_global_device_ids=true, to_apply=%add.2 | all-reduce | flops 9216 | bytes 36864
  49.3 13.6 %all-gather.12.cloned.1.call-done = bf16[2304,256]{1,0:T(8,128)(2,1)} async-done(((bf16[288,256]{1,0:T(8,128)(2,1)}), bf16[2304,256]{1,0:T(8,128)(2,1)}) %all-gather.12.cloned.1.call-update) | async-done | bytes 1179664 | tf_op jit(solution)/shard_map/all_gather | solution.py:69
  68.4 25.4 %all-gather.16.cloned.1.call-done = bf16[2304,512]{1,0:T(8,128)(2,1)} async-done(((bf16[288,512]{1,0:T(8,128)(2,1)}), bf16[2304,512]{1,0:T(8,128)(2,1)}) %all-gather.16.cloned.1.call-update) | async-done | bytes 2359312 | tf_op jit(solution)/shard_map/all_gather | solution.py:67
  97.8 25.0 %all-gather.28.cloned.1.call-done = bf16[2048,256]{1,0:T(8,128)(2,1)} async-done(((bf16[512,256]{1,0:T(8,128)(2,1)}), bf16[2048,256]{1,0:T(8,128)(2,1)}) %all-gather.28.cloned.1.call-update) | async-done | bytes 1048592 | tf_op jit(solution)/shard_map/all_gather | solution.py:108
  129.5 22.2 %all-gather.26.cloned.1.call-done = bf16[2048,256]{1,0:T(8,128)(2,1)} async-done(((bf16[512,256]{1,0:T(8,128)(2,1)}), bf16[2048,256]{1,0:T(8,128)(2,1)}) %all-gather.26.cloned.1.call-update) | async-done | bytes 1048592 | tf_op jit(solution)/shard_map/all_gather | solution.py:109
  151.7 7.8 convolution_convert_fusion.10
  159.5 23.0 %all-gather.18.cloned.1.call-done = bf16[512,2304]{0,1:T(8,128)(2,1)} async-done(((bf16[512,288]{0,1:T(8,128)(2,1)}), bf16[512,2304]{0,1:T(8,128)(2,1)}) %all-gather.18.cloned.1.call-update) | async-done | bytes 2359312 | tf_op jit(solution)/shard_map/all_gather | solution.py:70
  189.5 93.5 %all-reduce.15.cloned.1.call-done = bf16[512,2304]{1,0:T(8,128)(2,1)} async-done(((bf16[512,2304]{1,0:T(8,128)(2,1)}), bf16[512,2304]{1,0:T(8,128)(2,1)}) %all-reduce.15.cloned.1.call-update) | async-done | bytes 2359312 | tf_op jit(solution)/shard_map/psum | solution.py:129
  290.9 56.8 %all-gather.20.cloned.1.call-done = bf16[2304,2304]{1,0:T(8,128)(2,1)} async-done(((bf16[288,2304]{1,0:T(8,128)(2,1)}), bf16[2304,2304]{1,0:T(8,128)(2,1)}) %all-gather.20.cloned.1.call-update) | async-done | bytes 10616848 | tf_op jit(solution)/shard_map/all_gather | solution.py:71
  347.7 11.6 fusion.112
  359.3 54.1 %all-gather.22.cloned.1.call-done = bf16[2304,2304]{1,0:T(8,128)(2,1)} async-done(((bf16[288,2304]{1,0:T(8,128)(2,1)}), bf16[2304,2304]{1,0:T(8,128)(2,1)}) %all-gather.22.cloned.1.call-update) | async-done | bytes 10616848 | tf_op jit(solution)/shard_map/all_gather | solution.py:72
  413.4 12.8 multiply_convert_fusion.1
  426.3 52.7 %all-gather.24.cloned.1.call-done = bf16[2304,2304]{0,1:T(8,128)(2,1)} async-done(((bf16[2304,288]{0,1:T(8,128)(2,1)}), bf16[2304,2304]{0,1:T(8,128)(2,1)}) %all-gather.24.cloned.1.call-update) | async-done | bytes 10616848 | tf_op jit(solution)/shard_map/all_gather | solution.py:73
  479.0 11.3 convolution_convert_fusion.5
  490.6 95.5 %all-reduce.17.cloned.1.call-done = bf16[512,2304]{1,0:T(8,128)(2,1)} async-done(((bf16[512,2304]{1,0:T(8,128)(2,1)}), bf16[512,2304]{1,0:T(8,128)(2,1)}) %all-reduce.17.cloned.1.call-update) | async-done | bytes 2359312 | tf_op jit(solution)/shard_map/psum | solution.py:138
  593.3 16.0 %multiply_convert_fusion = (bf16[512,2304]{1,0:T(8,128)(2,1)}, bf16[512,2304]{1,0:T(8,128)(2,1)}) fusion(f32[512,2304]{1,0:T(8,128)} %fusion.112, f32[512,2304]{1,0:T(8,128)} %get-tuple-element.38, bf16[2304,2304]{0,1:T(8,128)(2,1)} %all-gather.24.cloned.1.call-done, bf16[512,2304]{1,0:T(8,128)(2,1)S(1)} %copy-done.5, ...), kind=kOutput, calls=%fused_computation.82 | convolution fusion | flops 5474746368 | bytes 29506560 | tf_op jit(solution)/shard_map/dot_general | solution.py:38
  609.3 8.6 fusion.113
  617.9 12.0 fusion.58
  630.4 94.4 %all-reduce.19.cloned.1.call-done = bf16[512,2304]{1,0:T(8,128)(2,1)} async-done(((bf16[512,2304]{1,0:T(8,128)(2,1)}), bf16[512,2304]{1,0:T(8,128)(2,1)}) %all-reduce.19.cloned.1.call-update) | async-done | bytes 2359312 | tf_op jit(solution)/shard_map/psum | solution.py:163
  748.4 7.3 fusion.1
  780.8 25.0 %reduce-scatter.10.cloned.1.call-done = bf16[1,512,1,256]{1,3,2,0:T(8,128)(2,1)} async-done(((bf16[1,2048,1,256]{1,3,2,0:T(8,128)(2,1)}), bf16[1,512,1,256]{1,3,2,0:T(8,128)(2,1)}) %reduce-scatter.10.cloned.1.call-update) | async-done | bytes 262160 | tf_op jit(solution)/shard_map/reduce_scatter | solution.py:193
  815.0 11.7 convolution_convert_fusion
  826.8 10.4 convolution_convert_fusion.1
  837.5 10.3 convolution_convert_fusion.2
  853.4 44.3 %reduce-scatter.14.cloned.1.call-done = bf16[288,512]{1,0:T(8,128)(2,1)} async-done(((bf16[2304,512]{1,0:T(8,128)(2,1)}), bf16[288,512]{1,0:T(8,128)(2,1)}) %reduce-scatter.14.cloned.1.call-update) | async-done | bytes 294928 | tf_op jit(solution)/shard_map/reduce_scatter | solution.py:216
  899.5 38.1 %reduce-scatter.18.cloned.1.call-done = bf16[288,256]{1,0:T(8,128)(2,1)} async-done(((bf16[2304,256]{1,0:T(8,128)(2,1)}), bf16[288,256]{1,0:T(8,128)(2,1)}) %reduce-scatter.18.cloned.1.call-update) | async-done | bytes 147472 | tf_op jit(solution)/shard_map/reduce_scatter | solution.py:222
  939.2 38.6 %reduce-scatter.16.cloned.1.call-done = bf16[288,256]{1,0:T(8,128)(2,1)} async-done(((bf16[2304,256]{1,0:T(8,128)(2,1)}), bf16[288,256]{1,0:T(8,128)(2,1)}) %reduce-scatter.16.cloned.1.call-update) | async-done | bytes 147472 | tf_op jit(solution)/shard_map/reduce_scatter | solution.py:219
  979.4 96.4 %all-reduce.21.cloned.1.call-done = bf16[512,2304]{1,0:T(8,128)(2,1)} async-done(((bf16[512,2304]{1,0:T(8,128)(2,1)}), bf16[512,2304]{1,0:T(8,128)(2,1)}) %all-reduce.21.cloned.1.call-update) | async-done | bytes 2359312 | tf_op jit(solution)/shard_map/psum | solution.py:205
  1078.9 26.5 %all-reduce.8 = (bf16[2304]{0:T(1024)(128)(2,1)S(1)}, bf16[2304]{0:T(1024)(128)(2,1)S(1)}, bf16[2304]{0:T(1024)(128)(2,1)S(1)}, bf16[2304]{0:T(1024)(128)(2,1)S(1)}) all-reduce(bf16[2304]{0:T(1024)(128)(2,1)S(1)} %get-tuple-element.19, ...), channel_id=13, replica_groups=mesh['fsdp'=2,'ctx'=4,'tp'=4] {'fsdp','ctx'}, use_global_device_ids=true, to_apply=%region_25.26.clone | all-reduce | flops 9216 | bytes 36864
  1114.0 46.4 %reduce-scatter.26.cloned.1.call-done = bf16[2304,288]{0,1:T(8,128)(2,1)} async-done(((bf16[2304,2304]{0,1:T(8,128)(2,1)}), bf16[2304,288]{0,1:T(8,128)(2,1)}) %reduce-scatter.26.cloned.1.call-update) | async-done | bytes 1327120 | tf_op jit(solution)/shard_map/reduce_scatter | solution.py:234
  1163.4 82.7 %reduce-scatter.24.cloned.1.call-done = bf16[288,2304]{1,0:T(8,128)(2,1)} async-done(((bf16[2304,2304]{1,0:T(8,128)(2,1)}), bf16[288,2304]{1,0:T(8,128)(2,1)}) %reduce-scatter.24.cloned.1.call-update) | async-done | bytes 1327120 | tf_op jit(solution)/shard_map/reduce_scatter | solution.py:231
  1249.1 82.7 %reduce-scatter.22.cloned.1.call-done = bf16[288,2304]{1,0:T(8,128)(2,1)} async-done(((bf16[2304,2304]{1,0:T(8,128)(2,1)}), bf16[288,2304]{1,0:T(8,128)(2,1)}) %reduce-scatter.22.cloned.1.call-update) | async-done | bytes 1327120 | tf_op jit(solution)/shard_map/reduce_scatter | solution.py:228
  (172 shorter events, 140.1 us)
Async XLA Ops:
  7.2 38.3 %all-gather.14.cloned.1.call-start = ((), (), s32[]{:S(2)}) async-start(), calls=%async_computation.10 | async-start | bytes 1327104 | tf_op jit(solution)/shard_map/all_gather | solution.py:68
  7.9 55.0 %all-gather.12.cloned.1.call-start = ((), (), s32[]{:S(2)}) async-start(), calls=%async_computation.9 | async-start | bytes 1327104 | tf_op jit(solution)/shard_map/all_gather | solution.py:69
  8.7 85.2 %all-gather.16.cloned.1.call-start = ((), (), s32[]{:S(2)}) async-start(), calls=%async_computation.11 | async-start | bytes 2654208 | tf_op jit(solution)/shard_map/all_gather | solution.py:67
  9.4 113.4 %all-gather.28.cloned.1.call-start = ((), (), s32[]{:S(2)}) async-start(), calls=%async_computation.30 | async-start | bytes 1310720 | tf_op jit(solution)/shard_map/all_gather | solution.py:108
  45.4 48.4 %copy-start.18 = (f32[512]{0:T(512)}, f32[512]{0:T(512)S(1)}, u32[]{:S(2)}) copy-start(f32[512]{0:T(512)S(1)} %add_rsqrt_fusion.3) | copy-start | bytes 6148
  45.4 48.4 %copy-start.15 = (f32[2304]{0:T(1024)}, f32[2304]{0:T(1024)S(1)}, u32[]{:S(2)}) copy-start(f32[2304]{0:T(1024)S(1)} %convert_add_fusion.3) | copy-start | bytes 27652
  45.4 17.5 %copy-start = (bf16[1,512,2304]{2,1,0:T(8,128)(2,1)S(1)}, bf16[1,512,2304]{2,1,0:T(8,128)(2,1)}, u32[]{:S(2)}) copy-start(bf16[1,512,2304]{2,1,0:T(8,128)(2,1)} %param.14) | copy-start | bytes 7077892
  49.2 102.5 %all-gather.26.cloned.1.call-start = ((), (), s32[]{:S(2)}) async-start(), calls=%async_computation.29 | async-start | bytes 1310720 | tf_op jit(solution)/shard_map/all_gather | solution.py:109
  65.7 116.7 %all-gather.18.cloned.1.call-start = ((), (), s32[]{:S(2)}) async-start(), calls=%async_computation.12 | async-start | bytes 2654208 | tf_op jit(solution)/shard_map/all_gather | solution.py:70
  66.3 216.6 %all-reduce.15.cloned.1.call-start = ((), (), s32[]{:S(2)}) async-start(), calls=%async_computation.13 | async-start | bytes 4718592 | tf_op jit(solution)/shard_map/psum | solution.py:129
  187.2 160.5 %all-gather.20.cloned.1.call-start = ((), (), s32[]{:S(2)}) async-start(), calls=%async_computation.14 | async-start | bytes 11943936 | tf_op jit(solution)/shard_map/all_gather | solution.py:71
  187.9 225.5 %all-gather.22.cloned.1.call-start = ((), (), s32[]{:S(2)}) async-start(), calls=%async_computation.15 | async-start | bytes 11943936 | tf_op jit(solution)/shard_map/all_gather | solution.py:72
  188.7 290.4 %all-gather.24.cloned.1.call-start = ((), (), s32[]{:S(2)}) async-start(), calls=%async_computation.16 | async-start | bytes 11943936 | tf_op jit(solution)/shard_map/all_gather | solution.py:73
  189.2 396.9 %all-reduce.17.cloned.1.call-start = ((), (), s32[]{:S(2)}) async-start(), calls=%async_computation.17 | async-start | bytes 4718592 | tf_op jit(solution)/shard_map/psum | solution.py:138
  490.3 234.5 %all-reduce.19.cloned.1.call-start = ((), (), s32[]{:S(2)}) async-start(), calls=%async_computation.18 | async-start | bytes 4718592 | tf_op jit(solution)/shard_map/psum | solution.py:163
  586.1 7.2 copy-start.5
  586.1 7.2 copy-start.8
  588.5 20.8 %slice-start.2 = ((s8[10616832]{0:T(1024)(128)(4,1)}), s8[4194304]{0:T(1024)(128)(4,1)S(1)}, s32[]{:S(2)}) async-start(s8[10616832]{0:T(1024)(128)(4,1)} %bitcast.223), calls=%async_computation.33 | async-start | bytes 8388608
  593.3 16.0 %slice-start.3 = ((s8[10616832]{0:T(1024)(128)(4,1)}), s8[4194304]{0:T(1024)(128)(4,1)S(1)}, s32[]{:S(2)}) async-start(s8[10616832]{0:T(1024)(128)(4,1)} %bitcast.223), calls=%async_computation.34 | async-start | bytes 8388608
  593.3 16.0 %slice-start.4 = ((s8[10616832]{0:T(1024)(128)(4,1)}), s8[2228224]{0:T(1024)(128)(4,1)S(1)}, s32[]{:S(2)}) async-start(s8[10616832]{0:T(1024)(128)(4,1)} %bitcast.223), calls=%async_computation.35 | async-start | bytes 4456448
  630.0 147.5 %reduce-scatter.12.cloned.1.call-start = ((), (), s32[]{:S(2)}) async-start(), calls=%async_computation.20 | async-start | bytes 1310720 | tf_op jit(solution)/shard_map/reduce_scatter | solution.py:196
  748.2 57.7 %reduce-scatter.10.cloned.1.call-start = ((), (), s32[]{:S(2)}) async-start(), calls=%async_computation.19 | async-start | bytes 1310720 | tf_op jit(solution)/shard_map/reduce_scatter | solution.py:193
  755.7 8.0 copy-start.21
  765.9 85.6 %reduce-scatter.20.cloned.1.call-start = ((), (), s32[]{:S(2)}) async-start(), calls=%async_computation.25 | async-start | bytes 2654208 | tf_op jit(solution)/shard_map/reduce_scatter | solution.py:225
  770.6 127.1 %reduce-scatter.14.cloned.1.call-start = ((), (), s32[]{:S(2)}) async-start(), calls=%async_computation.22 | async-start | bytes 2654208 | tf_op jit(solution)/shard_map/reduce_scatter | solution.py:216
  777.5 160.1 %reduce-scatter.18.cloned.1.call-start = ((), (), s32[]{:S(2)}) async-start(), calls=%async_computation.24 | async-start | bytes 1327104 | tf_op jit(solution)/shard_map/reduce_scatter | solution.py:222
  780.6 197.2 %reduce-scatter.16.cloned.1.call-start = ((), (), s32[]{:S(2)}) async-start(), calls=%async_computation.23 | async-start | bytes 1327104 | tf_op jit(solution)/shard_map/reduce_scatter | solution.py:219
  808.9 266.9 %all-reduce.21.cloned.1.call-start = ((), (), s32[]{:S(2)}) async-start(), calls=%async_computation.21 | async-start | bytes 4718592 | tf_op jit(solution)/shard_map/psum | solution.py:205
  815.0 345.4 %reduce-scatter.26.cloned.1.call-start = ((), (), s32[]{:S(2)}) async-start(), calls=%async_computation.28 | async-start | bytes 11943936 | tf_op jit(solution)/shard_map/reduce_scatter | solution.py:234
  826.7 419.4 %reduce-scatter.24.cloned.1.call-start = ((), (), s32[]{:S(2)}) async-start(), calls=%async_computation.27 | async-start | bytes 11943936 | tf_op jit(solution)/shard_map/reduce_scatter | solution.py:231
  837.2 494.7 %reduce-scatter.22.cloned.1.call-start = ((), (), s32[]{:S(2)}) async-start(), calls=%async_computation.26 | async-start | bytes 11943936 | tf_op jit(solution)/shard_map/reduce_scatter | solution.py:228
  847.8 231.1 %copy-start.17 = (bf16[2304]{0:T(1024)(128)(2,1)S(1)}, bf16[2304]{0:T(1024)(128)(2,1)}, u32[]{:S(2)}) copy-start(bf16[2304]{0:T(1024)(128)(2,1)} %get-tuple-element.17) | copy-start | bytes 13828
  (19 other events, 60.2 us)
Sparse Core Ops, SparseCore 0:
  9.9 26.9 all-gather.13
  38.7 24.1 all-gather.11
  64.8 28.9 all-gather.15
  96.1 26.6 all-gather.27
  125.0 26.6 all-gather.25
  153.4 28.9 all-gather.17
  187.3 95.6 all-reduce.14
  284.8 62.8 all-gather.19
  349.6 63.8 all-gather.21
  415.2 63.7 all-gather.23
  490.5 95.6 all-reduce.16
  630.1 94.6 all-reduce.18
  748.3 26.7 reduce-scatter.11
  778.1 27.7 reduce-scatter.9
  809.0 42.4 reduce-scatter.19
  855.1 42.4 reduce-scatter.13
  900.7 36.7 reduce-scatter.17
  941.0 36.7 reduce-scatter.15
  980.1 95.6 all-reduce.20
  1079.1 81.2 reduce-scatter.25
  1163.9 82.1 reduce-scatter.23
  1249.6 82.1 reduce-scatter.21
where the time goes:
time: 1350 us; the launch traced here: 1340 us
  waiting for transfers between devices  1020 us (76%)
  matrix products  170 us (13%)
  other arithmetic  67.6 us (5%)
  blocking collectives  54.7 us (4%)
  between operations  17 us (1%)
    psum x1, waiting for transfers between devices, body(): lax.psum((right_dot(dquery_b, query_back) + right_dot(dkey_b, key_back) +...  96.4 us
    psum x1, waiting for transfers between devices, body(): lax.psum(plain_dot(hidden_b, down_full).astype(jnp.bfloat16), 'tp')  95.5 us
    psum x1, waiting for transfers between devices, body(): lax.psum((right_dot(dgate_b, gate_back) + right_dot(dup_b, up_back)).asty...  94.4 us
    psum x1, waiting for transfers between devices, body(): lax.psum(plain_dot(attended, out_full).astype(jnp.bfloat16), 'tp')  93.5 us
    reduce_scatter x1, waiting for transfers between devices, body(): lax.psum_scatter(grad_up.astype(jnp.bfloat16), ('fsdp', 'ctx'), scatter_d...  82.7 us
    reduce_scatter x1, waiting for transfers between devices, body(): lax.psum_scatter(grad_gate.astype(jnp.bfloat16), ('fsdp', 'ctx'), scatter...  82.7 us
    all_gather x1, waiting for transfers between devices, body(): lax.all_gather(w_gate, ('fsdp', 'ctx'), axis=0, tiled=True)  56.8 us
    unnamed x2, blocking collectives  54.7 us
  transfers between devices with their start and end apart: 22, of which 20 were waited for; matrix products, arithmetic and copies ran while one was open for 12% of the time, Pallas kernels for 0%

commit v1 on v0

v1 whole, which is shorter than its diff:
```python
import jax
import jax.numpy as jnp
from jax import lax
from jax.sharding import PartitionSpec as P

QUERY_HEADS = 8
KEY_VALUE_HEADS = 4
HEAD_SIZE = 256
SEQUENCE_SLOTS = 2048


EPS = 1e-06
CAP = 50.0
QSCALE = 0.0625
NEG = -1e30
BF = jnp.bfloat16
F32 = jnp.float32

X_PAIRS = [(0, 1), (1, 0), (2, 3), (3, 2)]
Y_PAIRS = [(0, 2), (2, 0), (1, 3), (3, 1)]
D_PAIRS = [(0, 3), (3, 0), (1, 2), (2, 1)]


def normalize(value_rows):
    factor = lax.rsqrt(jnp.mean(value_rows * value_rows, -1, keepdims=True) + EPS)
    return (value_rows * factor, factor)


def norm_back(grad_hat, normed, factor):
    return factor * (grad_hat - normed * jnp.mean(grad_hat * normed, -1, keepdims=True))


def plain_dot(first, second):
    return jnp.dot(first, second, preferred_element_type=F32)


def left_dot(first, second):
    return lax.dot_general(first, second, (((0,), (0,)), ((), ())), preferred_element_type=F32)


def right_dot(first, second):
    return lax.dot_general(first, second, (((1,), (1,)), ((), ())), preferred_element_type=F32)


def gelu_tanh(value_rows):
    return jax.nn.gelu(value_rows, approximate=True)


def over_x(value):
    return lax.ppermute(value, "ctx", X_PAIRS)


def over_y(value):
    return lax.ppermute(value, "ctx", Y_PAIRS)


def over_diagonal(value):
    return lax.ppermute(value, "ctx", D_PAIRS)


def to_other_core(value):
    return lax.ppermute(value, "fsdp", [(0, 1), (1, 0)])


def square_plane():
    return lax.axis_size("ctx") == 4


def place(pieces, at):
    rows = pieces[0].shape[0]
    whole = jnp.zeros((rows * len(pieces),) + pieces[0].shape[1:], pieces[0].dtype)
    for piece, index in zip(pieces, at):
        whole = lax.dynamic_update_slice_in_dim(whole, piece, index * rows, 0)
    return whole


def gather_ctx(shard):
    if not square_plane():
        return lax.all_gather(shard, "ctx", axis=0, tiled=True)
    me = lax.axis_index("ctx")
    half = shard.shape[0] // 2
    from_x, from_y = over_x(shard), over_y(shard)
    diag = jnp.concatenate([over_y(from_x[:half]), over_x(from_y[half:])], 0)
    return place([shard, from_x, from_y, diag], [me, me ^ 1, me ^ 2, me ^ 3])


def gather_ctx_direct(shard):
    if not square_plane():
        return lax.all_gather(shard, "ctx", axis=0, tiled=True)
    me = lax.axis_index("ctx")
    return place(
        [shard, over_x(shard), over_y(shard), over_diagonal(shard)],
        [me, me ^ 1, me ^ 2, me ^ 3],
    )


def block_of(whole, index, count):
    rows = whole.shape[0] // count
    return lax.dynamic_slice_in_dim(whole, index * rows, rows, 0)


def scatter_ctx(whole):
    if not square_plane():
        return lax.psum_scatter(whole, "ctx", scatter_dimension=0, tiled=True).astype(F32)
    me = lax.axis_index("ctx")
    own, to_x, to_y, to_d = (block_of(whole, me ^ k, 4) for k in range(4))
    half = own.shape[0] // 2
    d_x, d_y = over_x(to_d[:half]), over_y(to_d[half:])
    x_top, y_low = over_x(to_x[:half]), over_y(to_y[half:])
    y_top = over_y((to_y[:half].astype(F32) + d_x.astype(F32)).astype(BF))
    x_low = over_x((to_x[half:].astype(F32) + d_y.astype(F32)).astype(BF))
    top = own[:half].astype(F32) + x_top.astype(F32) + y_top.astype(F32)
    low = own[half:].astype(F32) + x_low.astype(F32) + y_low.astype(F32)
    return jnp.concatenate([top, low], 0)


def scatter_ctx_direct(whole):
    if not square_plane():
        return lax.psum_scatter(whole, "ctx", scatter_dimension=0, tiled=True).astype(F32)
    me = lax.axis_index("ctx")
    own, to_x, to_y, to_d = (block_of(whole, me ^ k, 4) for k in range(4))
    return (
        own.astype(F32)
        + over_x(to_x).astype(F32)
        + over_y(to_y).astype(F32)
        + over_diagonal(to_d).astype(F32)
    )


def body(
    hidden_in,
    lengths,
    query_weight,
    key_weight,
    value_weight,
    w_out,
    w_gate,
    w_up,
    w_down,
    gain_attn_in,
    gain_attn_out,
    gain_ffn_in,
    gain_ffn_out,
    cotangent,
):
    seqs_here, tok_here, width = hidden_in.shape
    row_count = seqs_here * tok_here
    head_groups = QUERY_HEADS // KEY_VALUE_HEADS
    core = lax.axis_index("fsdp")
    half_width = width // 2
    q_cols, kv_cols = query_weight.shape[1], key_weight.shape[1]
    kv_local = kv_cols // HEAD_SIZE

    def near(value):
        return lax.dynamic_slice_in_dim(value, core * half_width, half_width, 1)

    def far(value):
        return lax.dynamic_slice_in_dim(value, (1 - core) * half_width, half_width, 1)

    def gather(shard):
        mine = gather_ctx(shard)
        return mine, to_other_core(mine)

    def times(value, weight):
        return plain_dot(near(value), weight[0]) + plain_dot(far(value), weight[1])

    def join(own, other):
        return jnp.where(
            core == 0, jnp.concatenate([own, other], 1), jnp.concatenate([other, own], 1)
        )

    gains = jnp.stack([gain_attn_in, gain_attn_out, gain_ffn_in, gain_ffn_out])[None]
    gains = gather_ctx_direct(gains)
    gains = place([gains, to_other_core(gains)], [core, 1 - core])
    gains = gains.transpose(1, 0, 2).reshape(4, width).astype(F32)
    scale_one, scale_two, scale_three, scale_four = (1.0 + gains[i][None] for i in range(4))
    qkv_w = gather(jnp.concatenate([query_weight, key_weight, value_weight], 1))
    out_w = gather(w_out.T)
    gate_w = gather(w_gate)
    up_w = gather(w_up)
    down_w = gather(w_down.T)

    own_start = lax.axis_index("ctx") * tok_here
    query_pos = own_start + jnp.arange(tok_here, dtype=jnp.int32)
    key_pos = jnp.arange(SEQUENCE_SLOTS, dtype=jnp.int32)
    valid = query_pos[None, :] < lengths[:, None]
    allowed = (
        (key_pos[None, None, :] <= query_pos[None, :, None])
        & (key_pos[None, None, :] < lengths[:, None, None])
    )[:, None, None]
    flat_in = hidden_in.astype(F32).reshape(row_count, width)
    normed_one, factor_one = normalize(flat_in)
    attention_input = (normed_one * scale_one).astype(BF)
    qkv = times(attention_input, qkv_w).astype(BF)
    query_b = qkv[:, :q_cols]
    kv = qkv[:, q_cols:].reshape(seqs_here, tok_here, 2 * kv_cols).transpose(1, 0, 2)
    kv_all = gather_ctx_direct(kv).transpose(1, 0, 2)
    query_five = query_b.reshape(seqs_here, tok_here, kv_local, head_groups, HEAD_SIZE)
    key_four = kv_all[:, :, :kv_cols].reshape(seqs_here, SEQUENCE_SLOTS, kv_local, HEAD_SIZE)
    value_four = kv_all[:, :, kv_cols:].reshape(seqs_here, SEQUENCE_SLOTS, kv_local, HEAD_SIZE)
    raw = jnp.einsum("stkgd,sukd->skgtu", query_five, key_four, preferred_element_type=F32) * QSCALE
    bent = jnp.tanh(raw / CAP)
    masked = jnp.where(allowed, CAP * bent, NEG)
    largest = jnp.max(masked, -1, keepdims=True)
    logsum = largest + jnp.log(jnp.sum(jnp.exp(masked - largest), -1, keepdims=True))
    probs = jnp.exp(masked - logsum)
    probs_b = probs.astype(BF)
    attended = (
        jnp.einsum("skgtu,sukd->stkgd", probs_b, value_four, preferred_element_type=F32)
        .astype(BF)
        .reshape(row_count, -1)
    )
    attn = join(right_dot(attended, out_w[0]).astype(BF), right_dot(attended, out_w[1]).astype(BF))
    attn = lax.psum(attn, "tp").astype(F32)
    normed_two, factor_two = normalize(attn)
    after_attn = flat_in + normed_two * scale_two
    normed_three, factor_three = normalize(after_attn)
    ffn_in = (normed_three * scale_three).astype(BF)
    gate = times(ffn_in, gate_w)
    upward = times(ffn_in, up_w)
    activated, gelu_pull = jax.vjp(gelu_tanh, gate)
    hidden_b = (activated * upward).astype(BF)
    ffn_out = join(right_dot(hidden_b, down_w[0]).astype(BF), right_dot(hidden_b, down_w[1]).astype(BF))
    ffn_out = lax.psum(ffn_out, "tp").astype(F32)
    normed_four, factor_four = normalize(ffn_out)
    result = after_attn + normed_four * scale_four
    cot = cotangent.astype(F32).reshape(row_count, width) * valid.reshape(row_count, 1).astype(F32)

    def weight_grad(rows_from, cols_from):
        lhs = jnp.concatenate([near(rows_from), to_other_core(far(rows_from))], 0)
        rhs = jnp.concatenate([cols_from, to_other_core(cols_from)], 0)
        return scatter_ctx(left_dot(lhs, rhs).astype(BF))

    grad_gain_four = jnp.sum(cot * normed_four, 0)
    dffn_b = norm_back(cot * scale_four, normed_four, factor_four).astype(BF)
    grad_down = weight_grad(dffn_b, hidden_b).T
    dhidden = plain_dot(near(dffn_b), down_w[0]) + plain_dot(far(dffn_b), down_w[1])
    dgate_b = gelu_pull(dhidden * upward)[0].astype(BF)
    dup_b = (dhidden * activated).astype(BF)
    grad_gate = weight_grad(ffn_in, dgate_b)
    grad_up = weight_grad(ffn_in, dup_b)
    dffn_in = join(
        *(
            (right_dot(dgate_b, gate_w[i]) + right_dot(dup_b, up_w[i])).astype(BF)
            for i in range(2)
        )
    )
    dffn_in = lax.psum(dffn_in, "tp").astype(F32)
    grad_gain_three = jnp.sum(dffn_in * normed_three, 0)
    dafter = cot + norm_back(dffn_in * scale_three, normed_three, factor_three)
    grad_gain_two = jnp.sum(dafter * normed_two, 0)
    dattn_b = norm_back(dafter * scale_two, normed_two, factor_two).astype(BF)
    grad_out = weight_grad(dattn_b, attended).T
    dattended = (
        plain_dot(near(dattn_b), out_w[0]) + plain_dot(far(dattn_b), out_w[1])
    ).astype(BF).reshape(query_five.shape)
    dprobs = jnp.einsum("stkgd,sukd->skgtu", dattended, value_four, preferred_element_type=F32)
    weighted = jnp.sum(probs * dprobs, -1, keepdims=True)
    draw_b = (probs * (dprobs - weighted) * (1.0 - bent * bent)).astype(BF)
    dquery_b = (
        (jnp.einsum("skgtu,sukd->stkgd", draw_b, key_four, preferred_element_type=F32) * QSCALE)
        .astype(BF)
        .reshape(row_count, -1)
    )
    dvalue_part = jnp.einsum("skgtu,stkgd->sukd", probs_b, dattended, preferred_element_type=F32)
    dkey_part = (
        jnp.einsum("skgtu,stkgd->sukd", draw_b, query_five, preferred_element_type=F32) * QSCALE
    )
    dkv_part = jnp.concatenate(
        [
            dkey_part.astype(BF).reshape(seqs_here, SEQUENCE_SLOTS, kv_cols),
            dvalue_part.astype(BF).reshape(seqs_here, SEQUENCE_SLOTS, kv_cols),
        ],
        2,
    ).transpose(1, 0, 2)
    dkv_b = scatter_ctx_direct(dkv_part).astype(BF).transpose(1, 0, 2).reshape(row_count, -1)
    dqkv_b = jnp.concatenate([dquery_b, dkv_b], 1)
    dattn_in = join(*(right_dot(dqkv_b, qkv_w[i]).astype(BF) for i in range(2)))
    dattn_in = lax.psum(dattn_in, "tp").astype(F32)
    grad_qkv = weight_grad(attention_input, dqkv_b)
    grad_gain_one = jnp.sum(dattn_in * normed_one, 0)
    grad_input = dafter + norm_back(dattn_in * scale_one, normed_one, factor_one)
    grad_gains = jnp.stack([grad_gain_one, grad_gain_two, grad_gain_three, grad_gain_four])
    grad_gains = grad_gains.reshape(4, 2, half_width).transpose(1, 0, 2)
    grad_gains = block_of(grad_gains, core, 2) + to_other_core(block_of(grad_gains, 1 - core, 2))
    grad_gains = grad_gains.reshape(4, lax.axis_size("ctx"), -1).transpose(1, 0, 2)
    grad_gains = scatter_ctx_direct(grad_gains).reshape(4, -1)
    return (
        result.astype(BF).reshape(hidden_in.shape),
        grad_input.astype(BF).reshape(hidden_in.shape),
        grad_qkv[:, :q_cols],
        grad_qkv[:, q_cols : q_cols + kv_cols],
        grad_qkv[:, q_cols + kv_cols :],
        grad_out,
        grad_gate,
        grad_up,
        grad_down,
        grad_gains[0],
        grad_gains[1],
        grad_gains[2],
        grad_gains[3],
    )


def solution(mesh):
    return jax.shard_map(
        body,
        mesh=mesh,
        in_specs=(
            P("fsdp", "ctx", None),
            P("fsdp"),
            P(("fsdp", "ctx"), "tp"),
            P(("fsdp", "ctx"), "tp"),
            P(("fsdp", "ctx"), "tp"),
            P("tp", ("fsdp", "ctx")),
            P(("fsdp", "ctx"), "tp"),
            P(("fsdp", "ctx"), "tp"),
            P("tp", ("fsdp", "ctx")),
            P(("fsdp", "ctx")),
            P(("fsdp", "ctx")),
            P(("fsdp", "ctx")),
            P(("fsdp", "ctx")),
            P("fsdp", "ctx", None),
        ),
        out_specs=(
            P("fsdp", "ctx", None),
            P("fsdp", "ctx", None),
            P(("fsdp", "ctx"), "tp"),
            P(("fsdp", "ctx"), "tp"),
            P(("fsdp", "ctx"), "tp"),
            P("tp", ("fsdp", "ctx")),
            P(("fsdp", "ctx"), "tp"),
            P(("fsdp", "ctx"), "tp"),
            P("tp", ("fsdp", "ctx")),
            P(("fsdp", "ctx")),
            P(("fsdp", "ctx")),
            P(("fsdp", "ctx")),
            P(("fsdp", "ctx")),
        ),
        check_vma=False,
    )
```

time: 1350 us -> 922 us (0.68)
  waiting for transfers between devices: 1020 us -> 510 us
  local copies, waits for them, and re-layouts: 11.7 us -> 85.8 us
  starting transfers between devices: 2.84 us -> 64.8 us
  blocking collectives: 54.7 us -> 0 us
  matrix products: 170 us -> 146 us
  other arithmetic: 67.6 us -> 87.1 us
    reduce_scatter x9 -> x0, waiting for transfers between devices: 361 us -> none  [the longest x1 82.7 us: body(): lax.psum_scatter(grad_up.astype(jnp.bfloat16), ('fsdp', 'ctx'), scatter_d...]
    ppermute x0 -> x78, waiting for transfers between devices: none -> 289 us  [the longest x29 160 us: over_y(): return lax.ppermute(value, 'ctx', Y_PAIRS)]
    all_gather x9 -> x0, waiting for transfers between devices: 273 us -> none  [the longest x1 56.8 us: body(): lax.all_gather(w_gate, ('fsdp', 'ctx'), axis=0, tiled=True)]
    psum x4, waiting for transfers between devices: 380 us -> 221 us  [the longest x1 94.6 us: body(): ffn_out = lax.psum(ffn_out, 'tp').astype(F32)]
    ppermute x0 -> x78, starting transfers between devices: none -> 64.6 us  [the longest x29 33.7 us: over_x(): return lax.ppermute(value, 'ctx', X_PAIRS)]
    unnamed x2 -> x0, blocking collectives: 54.7 us -> none
    dynamic_update_slice x0 -> x24, local copies, waits for them, and re-layouts: none -> 33.4 us  [place(): whole = lax.dynamic_update_slice_in_dim(whole, piece, index * rows, 0)]
    slice x0 -> x17, local copies, waits for them, and re-layouts: none -> 17.4 us  [the longest x10 10.7 us: gather_ctx(): diag = jnp.concatenate([over_y(from_x[:half]), over_x(from_y[half:])], 0)]
  transfers between devices with their start and end apart: 22 -> 82, of which waited for: 20 -> 30; matrix products, arithmetic and copies ran while one was open for 12% -> 32% of each run, Pallas kernels for 0% -> 0%
where the time goes in v1:
time: 922 us; the launch traced here: 911 us
  waiting for transfers between devices  510 us (55%)
  matrix products  146 us (16%)
  other arithmetic  87.1 us (9%)
  local copies, waits for them, and re-layouts  85.8 us (9%)
  starting transfers between devices  64.8 us (7%)
  between operations  16.3 us (2%)
    ppermute x29, waiting for transfers between devices, over_y(): return lax.ppermute(value, 'ctx', Y_PAIRS)  160 us
    ppermute x29, waiting for transfers between devices, over_x(): return lax.ppermute(value, 'ctx', X_PAIRS)  117 us
    psum x1, waiting for transfers between devices, body(): ffn_out = lax.psum(ffn_out, 'tp').astype(F32)  94.6 us
    psum x1, waiting for transfers between devices, body(): attn = lax.psum(attn, 'tp').astype(F32)  65.9 us
    psum x1, waiting for transfers between devices, body(): dffn_in = lax.psum(dffn_in, 'tp').astype(F32)  60.9 us
    dot_general x10, matrix products, plain_dot(): return jnp.dot(first, second, preferred_element_type=F32)  51.1 us
    dot_general x10, matrix products, right_dot(): lax.dot_general(first, second, (((1,), (1,)), ((), ())), preferred_elemen...  43.5 us
    ppermute x29, starting transfers between devices, over_x(): return lax.ppermute(value, 'ctx', X_PAIRS)  33.7 us
  transfers between devices with their start and end apart: 82, of which 30 were waited for; matrix products, arithmetic and copies ran while one was open for 32% of the time, Pallas kernels for 0%

profile of v1, /device:TPU:0, one launch (start us, length us, event | category | flops | bytes accessed | tf_op | source)
XLA Modules:
  0.0 911.0 jit_solution(11176178088174170071)
XLA Ops:
  57.5 26.5 %collective-permute-done.7 = bf16[144,1024]{1,0:T(8,128)(2,1)} collective-permute-done((bf16[144,1024]{1,0:T(8,128)(2,1)}, bf16[144,1024]{1,0:T(8,128)(2,1)}, u32[]{:S(2)}, u32[]{:S(2)}) %collective-permute-start.7) | collective-permute-done | bytes 294944 | tf_op jit(solution)/shard_map/ppermute | solution.py:50
  93.4 22.8 %collective-permute-done.18 = bf16[288,2304]{1,0:T(8,128)(2,1)S(1)} collective-permute-done((bf16[288,2304]{1,0:T(8,128)(2,1)}, bf16[288,2304]{1,0:T(8,128)(2,1)S(1)}, u32[]{:S(2)}, u32[]{:S(2)}) %collective-permute-start.18) | collective-permute-done | bytes 1327136 | tf_op jit(solution)/shard_map/ppermute | solution.py:54
  117.6 27.0 %collective-permute-done.23 = bf16[288,2304]{1,0:T(8,128)(2,1)S(1)} collective-permute-done((bf16[288,2304]{1,0:T(8,128)(2,1)S(1)}, bf16[288,2304]{1,0:T(8,128)(2,1)S(1)}, u32[]{:S(2)}, u32[]{:S(2)}) %collective-permute-start.23) | collective-permute-done | bytes 1327136 | tf_op jit(solution)/shard_map/ppermute | solution.py:54
  161.6 31.3 %collective-permute-done.19 = bf16[144,2304]{1,0:T(8,128)(2,1)S(1)} collective-permute-done((bf16[144,2304]{1,0:T(8,128)(2,1)S(1)}, bf16[144,2304]{1,0:T(8,128)(2,1)S(1)}, u32[]{:S(2)}, u32[]{:S(2)}) %collective-permute-start.19) | collective-permute-done | bytes 663584 | tf_op jit(solution)/shard_map/ppermute | solution.py:54
  244.4 9.6 %collective-permute-done.30 = bf16[144,2304]{1,0:T(8,128)(2,1)S(1)} collective-permute-done((bf16[144,2304]{1,0:T(8,128)(2,1)S(1)}, bf16[144,2304]{1,0:T(8,128)(2,1)S(1)}, u32[]{:S(2)}, u32[]{:S(2)}) %collective-permute-start.30) | collective-permute-done | bytes 663584 | tf_op jit(solution)/shard_map/ppermute | solution.py:50
  257.4 65.9 %all-reduce.5.cloned.1.call-done = bf16[512,2304]{1,0:T(8,128)(2,1)} async-done(((bf16[512,2304]{1,0:T(8,128)(2,1)}), bf16[512,2304]{1,0:T(8,128)(2,1)}) %all-reduce.5.cloned.1.call-update) | async-done | bytes 2359312 | tf_op jit(solution)/shard_map/psum | solution.py:214
  328.6 6.6 fusion.151
  341.0 5.8 convolution_add_fusion.2
  346.8 9.6 %multiply_convert_fusion.1 = (bf16[512,2304]{1,0:T(8,128)(2,1)S(1)}, f32[512,2304]{1,0:T(8,128)}) fusion(f32[512,2304]{1,0:T(8,128)S(1)} %convolution_add_fusion.2, f32[512,2304]{1,0:T(8,128)S(1)} %fusion.152, bf16[512,1152]{1,0:T(8,128)(2,1)S(1)} %get-tuple-element.63, bf16[1152,2304]{1,0:T(8,128)(2,1)} %maximum_dynamic-update-slice_fusion.1), kind=kOutput, calls=%fused_computation.88 | convolution fusion | flops 2730885120 | bytes 23003136 | tf_op jit(solution)/shard_map/dot_general | solution.py:34
  356.4 6.6 convolution_convert_fusion.8
  370.7 94.6 %all-reduce.7.cloned.1.call-done = bf16[512,2304]{1,0:T(8,128)(2,1)} async-done(((bf16[512,2304]{1,0:T(8,128)(2,1)}), bf16[512,2304]{1,0:T(8,128)(2,1)}) %all-reduce.7.cloned.1.call-update) | async-done | bytes 2359312 | tf_op jit(solution)/shard_map/psum | solution.py:224
  474.1 6.6 fusion.153
  480.7 7.8 fusion.46
  488.5 7.4 fusion.154
  515.1 9.4 %convolution_convert_fusion = bf16[1152,2304]{1,0:T(8,128)(2,1)S(1)} fusion(bf16[512,2304]{1,0:T(8,128)(2,1)} %collective-permute-done.67, bf16[512,2304]{1,0:T(8,128)(2,1)} %copy-done.61, bf16[512,1152]{1,0:T(8,128)(2,1)} %collective-permute-done.66, bf16[512,1152]{1,0:T(8,128)(2,1)} %copy-done.36), kind=kOutput, calls=%fused_computation | convolution fusion | flops 5452627968 | bytes 12386304 | tf_op jit(solution)/shard_map/dot_general | solution.py:38
  530.8 14.8 %collective-permute-done.69 = bf16[144,2304]{1,0:T(8,128)(2,1)} collective-permute-done((bf16[144,2304]{1,0:T(8,128)(2,1)}, bf16[144,2304]{1,0:T(8,128)(2,1)}, u32[]{:S(2)}, u32[]{:S(2)}) %collective-permute-start.69) | collective-permute-done | bytes 663584 | tf_op jit(solution)/shard_map/ppermute | solution.py:50
  549.4 60.9 %all-reduce.9.cloned.1.call-done = bf16[512,2304]{1,0:T(8,128)(2,1)} async-done(((bf16[512,2304]{1,0:T(8,128)(2,1)}), bf16[512,2304]{1,0:T(8,128)(2,1)}) %all-reduce.9.cloned.1.call-update) | async-done | bytes 2359312 | tf_op jit(solution)/shard_map/psum | solution.py:248
  615.0 7.3 fusion.29
  631.7 8.4 convolution_convert_fusion.2
  653.5 8.4 convolution_convert_fusion.1
  684.9 8.7 collective-permute-done.34
  693.7 9.1 collective-permute-done.33
  712.8 8.1 collective-permute-done.54
  722.9 25.4 %collective-permute-done.61 = bf16[144,2304]{1,0:T(8,128)(2,1)S(1)} collective-permute-done((bf16[144,2304]{1,0:T(8,128)(2,1)S(1)}, bf16[144,2304]{1,0:T(8,128)(2,1)S(1)}, u32[]{:S(2)}, u32[]{:S(2)}) %collective-permute-start.61) | collective-permute-done | bytes 663584 | tf_op jit(solution)/shard_map/ppermute | solution.py:50
  751.3 13.0 %collective-permute-done.72 = bf16[144,2304]{1,0:T(8,128)(2,1)S(1)} collective-permute-done((bf16[144,2304]{1,0:T(8,128)(2,1)S(1)}, bf16[144,2304]{1,0:T(8,128)(2,1)S(1)}, u32[]{:S(2)}, u32[]{:S(2)}) %collective-permute-start.72) | collective-permute-done | bytes 663584 | tf_op jit(solution)/shard_map/ppermute | solution.py:50
  774.9 7.2 collective-permute-done.55
  790.0 6.4 collective-permute-done.63
  797.2 13.5 %collective-permute-done.62 = bf16[144,2304]{1,0:T(8,128)(2,1)S(1)} collective-permute-done((bf16[144,2304]{1,0:T(8,128)(2,1)S(1)}, bf16[144,2304]{1,0:T(8,128)(2,1)S(1)}, u32[]{:S(2)}, u32[]{:S(2)}) %collective-permute-start.62) | collective-permute-done | bytes 663584 | tf_op jit(solution)/shard_map/ppermute | solution.py:54
  823.1 23.6 %collective-permute-done.50 = bf16[144,512]{1,0:T(8,128)(2,1)S(1)} collective-permute-done((bf16[144,512]{1,0:T(8,128)(2,1)S(1)}, bf16[144,512]{1,0:T(8,128)(2,1)S(1)}, u32[]{:S(2)}, u32[]{:S(2)}) %collective-permute-start.50) | collective-permute-done | bytes 147488 | tf_op jit(solution)/shard_map/ppermute | solution.py:54
  849.2 5.9 collective-permute-done.40
  870.8 9.4 %collective-permute-done.41 = bf16[144,1024]{1,0:T(8,128)(2,1)S(1)} collective-permute-done((bf16[144,1024]{1,0:T(8,128)(2,1)S(1)}, bf16[144,1024]{1,0:T(8,128)(2,1)S(1)}, u32[]{:S(2)}, u32[]{:S(2)}) %collective-permute-start.41) | collective-permute-done | bytes 294944 | tf_op jit(solution)/shard_map/ppermute | solution.py:50
  897.4 6.0 fusion.85
  (458 shorter events, 321.2 us)
Async XLA Ops:
  7.2 316.1 %all-reduce.5.cloned.1.call-start = ((), (), s32[]{:S(2)}) async-start(), calls=%async_computation | async-start | bytes 4718592 | tf_op jit(solution)/shard_map/psum | solution.py:214
  41.8 74.5 %collective-permute-start.17 = (bf16[288,2304]{1,0:T(8,128)(2,1)}, bf16[288,2304]{1,0:T(8,128)(2,1)}, u32[]{:S(2)}, u32[]{:S(2)}) collective-permute-start(bf16[288,2304]{1,0:T(8,128)(2,1)} %param.20), channel_id=1, source_target_pairs={{0,4},{4,0},{8,12},{12,8},{1,5},{5,1},{9,13},{13,9},{2,6},{6,2},{1... | collective-permute-start | bytes 3981320 | tf_op jit(solution)/shard_map/ppermute | solution.py:50
  45.5 38.4 %collective-permute-start.7 = (bf16[144,1024]{1,0:T(8,128)(2,1)}, bf16[144,1024]{1,0:T(8,128)(2,1)}, u32[]{:S(2)}, u32[]{:S(2)}) collective-permute-start(bf16[144,1024]{1,0:T(8,128)(2,1)} %slice.270), channel_id=1, source_target_pairs={{0,4},{4,0},{8,12},{12,8},{1,5},{5,1},{9,13},{13,9},{2,6},{6,2},{1... | collective-permute-start | bytes 884744 | tf_op jit(solution)/shard_map/ppermute | solution.py:50
  84.0 61.6 %collective-permute-start.22 = (bf16[288,2304]{1,0:T(8,128)(2,1)}, bf16[288,2304]{1,0:T(8,128)(2,1)S(1)}, u32[]{:S(2)}, u32[]{:S(2)}) collective-permute-start(bf16[288,2304]{1,0:T(8,128)(2,1)} %param.21), channel_id=1, source_target_pairs={{0,4},{4,0},{8,12},{12,8},{1,5},{5,1},{9,13},{13,9},{2,6},{6,2},{1... | collective-permute-start | bytes 3981320 | tf_op jit(solution)/shard_map/ppermute | solution.py:50
  86.3 58.3 %collective-permute-start.23 = (bf16[288,2304]{1,0:T(8,128)(2,1)S(1)}, bf16[288,2304]{1,0:T(8,128)(2,1)S(1)}, u32[]{:S(2)}, u32[]{:S(2)}) collective-permute-start(bf16[288,2304]{1,0:T(8,128)(2,1)S(1)} %copy-done.26), channel_id=1, source_target_pairs={{0,8},{8,0},{4,12},{12,4},{1,9},{9,1},{5,13},{13,5},{2,10},{10,2},... | collective-permute-start | bytes 3981320 | tf_op jit(solution)/shard_map/ppermute | solution.py:54
  88.0 64.6 %collective-permute-start.8 = (bf16[1152,1024]{1,0:T(8,128)(2,1)}, bf16[1152,1024]{1,0:T(8,128)(2,1)S(1)}, u32[]{:S(2)}, u32[]{:S(2)}) collective-permute-start(bf16[1152,1024]{1,0:T(8,128)(2,1)} %maximum_dynamic-update-slice_fusion.3), channel_id=1, source_target_pairs={{0,16},{16,0},{1,17},{17,1},{2,18},{18,2},{3,19},{19,3},{4,20},{20... | collective-permute-start | bytes 7077896 | tf_op jit(solution)/shard_map/ppermute | solution.py:62
  116.2 121.8 %collective-permute-start.27 = (bf16[288,2304]{1,0:T(8,128)(2,1)}, bf16[288,2304]{1,0:T(8,128)(2,1)}, u32[]{:S(2)}, u32[]{:S(2)}) collective-permute-start(bf16[288,2304]{1,0:T(8,128)(2,1)} %bitcast.23), channel_id=1, source_target_pairs={{0,4},{4,0},{8,12},{12,8},{1,5},{5,1},{9,13},{13,9},{2,6},{6,2},{1... | collective-permute-start | bytes 3981320 | tf_op jit(solution)/shard_map/ppermute | solution.py:50
  116.4 119.1 %collective-permute-start.28 = (bf16[288,2304]{1,0:T(8,128)(2,1)}, bf16[288,2304]{1,0:T(8,128)(2,1)}, u32[]{:S(2)}, u32[]{:S(2)}) collective-permute-start(bf16[288,2304]{1,0:T(8,128)(2,1)} %bitcast.23), channel_id=1, source_target_pairs={{0,8},{8,0},{4,12},{12,4},{1,9},{9,1},{5,13},{13,5},{2,10},{10,2},... | collective-permute-start | bytes 3981320 | tf_op jit(solution)/shard_map/ppermute | solution.py:54
  145.6 47.3 %collective-permute-start.19 = (bf16[144,2304]{1,0:T(8,128)(2,1)S(1)}, bf16[144,2304]{1,0:T(8,128)(2,1)S(1)}, u32[]{:S(2)}, u32[]{:S(2)}) collective-permute-start(bf16[144,2304]{1,0:T(8,128)(2,1)S(1)} %slice.279), channel_id=1, source_target_pairs={{0,8},{8,0},{4,12},{12,4},{1,9},{9,1},{5,13},{13,5},{2,10},{10,2},... | collective-permute-start | bytes 1990664 | tf_op jit(solution)/shard_map/ppermute | solution.py:54
  157.7 39.9 %collective-permute-start.9 = (bf16[512,1,512]{2,0,1:T(8,128)(2,1)}, bf16[512,1,512]{2,0,1:T(8,128)(2,1)}, u32[]{:S(2)}, u32[]{:S(2)}) collective-permute-start(bf16[512,1,512]{2,0,1:T(8,128)(2,1)} %get-tuple-element.79), channel_id=1, source_target_pairs={{0,4},{4,0},{8,12},{12,8},{1,5},{5,1},{9,13},{13,9},{2,6},{6,2},{1... | collective-permute-start | bytes 1572872 | tf_op jit(solution)/shard_map/ppermute | solution.py:50
  159.6 45.4 %collective-permute-start.10 = (bf16[512,1,512]{2,0,1:T(8,128)(2,1)}, bf16[512,1,512]{2,0,1:T(8,128)(2,1)}, u32[]{:S(2)}, u32[]{:S(2)}) collective-permute-start(bf16[512,1,512]{2,0,1:T(8,128)(2,1)} %get-tuple-element.79), channel_id=1, source_target_pairs={{0,8},{8,0},{4,12},{12,4},{1,9},{9,1},{5,13},{13,5},{2,10},{10,2},... | collective-permute-start | bytes 1572872 | tf_op jit(solution)/shard_map/ppermute | solution.py:54
  223.8 104.8 %collective-permute-start.21 = (bf16[1152,2304]{1,0:T(8,128)(2,1)}, bf16[1152,2304]{1,0:T(8,128)(2,1)}, u32[]{:S(2)}, u32[]{:S(2)}) collective-permute-start(bf16[1152,2304]{1,0:T(8,128)(2,1)} %maximum_dynamic-update-slice_fusion), channel_id=1, source_target_pairs={{0,16},{16,0},{1,17},{17,1},{2,18},{18,2},{3,19},{19,3},{4,20},{20... | collective-permute-start | bytes 15925256 | tf_op jit(solution)/shard_map/ppermute | solution.py:62
  227.4 237.9 %all-reduce.7.cloned.1.call-start = ((), (), s32[]{:S(2)}) async-start(), calls=%async_computation.1 | async-start | bytes 4718592 | tf_op jit(solution)/shard_map/psum | solution.py:224
  230.0 105.2 %collective-permute-start.26 = (bf16[1152,2304]{1,0:T(8,128)(2,1)}, bf16[1152,2304]{1,0:T(8,128)(2,1)}, u32[]{:S(2)}, u32[]{:S(2)}) collective-permute-start(bf16[1152,2304]{1,0:T(8,128)(2,1)} %maximum_dynamic-update-slice_fusion.1), channel_id=1, source_target_pairs={{0,16},{16,0},{1,17},{17,1},{2,18},{18,2},{3,19},{19,3},{4,20},{20... | collective-permute-start | bytes 15925256 | tf_op jit(solution)/shard_map/ppermute | solution.py:62
  257.4 105.6 %collective-permute-start.31 = (bf16[1152,2304]{1,0:T(8,128)(2,1)}, bf16[1152,2304]{1,0:T(8,128)(2,1)}, u32[]{:S(2)}, u32[]{:S(2)}) collective-permute-start(bf16[1152,2304]{1,0:T(8,128)(2,1)} %maximum_dynamic-update-slice_fusion.2), channel_id=1, source_target_pairs={{0,16},{16,0},{1,17},{17,1},{2,18},{18,2},{3,19},{19,3},{4,20},{20... | collective-permute-start | bytes 15925256 | tf_op jit(solution)/shard_map/ppermute | solution.py:62
  370.5 239.8 %all-reduce.9.cloned.1.call-start = ((), (), s32[]{:S(2)}) async-start(), calls=%async_computation.2 | async-start | bytes 4718592 | tf_op jit(solution)/shard_map/psum | solution.py:248
  370.6 144.4 %collective-permute-start.67 = (bf16[512,2304]{1,0:T(8,128)(2,1)}, bf16[512,2304]{1,0:T(8,128)(2,1)}, u32[]{:S(2)}, u32[]{:S(2)}) collective-permute-start(bf16[512,2304]{1,0:T(8,128)(2,1)} %copy-done.61), channel_id=1, source_target_pairs={{0,16},{16,0},{1,17},{17,1},{2,18},{18,2},{3,19},{19,3},{4,20},{20... | collective-permute-start | bytes 7077896 | tf_op jit(solution)/shard_map/ppermute | solution.py:62
  474.0 41.1 %collective-permute-start.66 = (bf16[512,1152]{1,0:T(8,128)(2,1)}, bf16[512,1152]{1,0:T(8,128)(2,1)}, u32[]{:S(2)}, u32[]{:S(2)}) collective-permute-start(bf16[512,1152]{1,0:T(8,128)(2,1)} %get-tuple-element.62), channel_id=1, source_target_pairs={{0,16},{16,0},{1,17},{17,1},{2,18},{18,2},{3,19},{19,3},{4,20},{20... | collective-permute-start | bytes 3538952 | tf_op jit(solution)/shard_map/ppermute | solution.py:62
  515.0 374.1 %all-reduce.11.cloned.1.call-start = ((), (), s32[]{:S(2)}) async-start(), calls=%async_computation.3 | async-start | bytes 4718592 | tf_op jit(solution)/shard_map/psum | solution.py:279
  529.2 238.4 %collective-permute-start.44 = (bf16[512,512]{0,1:T(8,128)(2,1)}, bf16[512,512]{0,1:T(8,128)(2,1)}, u32[]{:S(2)}, u32[]{:S(2)}) collective-permute-start(bf16[512,512]{0,1:T(8,128)(2,1)} %bitcast.257), channel_id=1, source_target_pairs={{0,16},{16,0},{1,17},{17,1},{2,18},{18,2},{3,19},{19,3},{4,20},{20... | collective-permute-start | bytes 1572872 | tf_op jit(solution)/shard_map/ppermute | solution.py:62
  529.7 99.0 %collective-permute-start.51 = (bf16[512,1152]{1,0:T(8,128)(2,1)}, bf16[512,1152]{1,0:T(8,128)(2,1)}, u32[]{:S(2)}, u32[]{:S(2)}) collective-permute-start(bf16[512,1152]{1,0:T(8,128)(2,1)} %copy-done.35), channel_id=1, source_target_pairs={{0,16},{16,0},{1,17},{17,1},{2,18},{18,2},{3,19},{19,3},{4,20},{20... | collective-permute-start | bytes 3538952 | tf_op jit(solution)/shard_map/ppermute | solution.py:62
  529.7 100.6 %collective-permute-start.52 = (bf16[512,2304]{1,0:T(8,128)(2,1)}, bf16[512,2304]{1,0:T(8,128)(2,1)}, u32[]{:S(2)}, u32[]{:S(2)}) collective-permute-start(bf16[512,2304]{1,0:T(8,128)(2,1)} %copy-done.59), channel_id=1, source_target_pairs={{0,16},{16,0},{1,17},{17,1},{2,18},{18,2},{3,19},{19,3},{4,20},{20... | collective-permute-start | bytes 7077896 | tf_op jit(solution)/shard_map/ppermute | solution.py:62
  530.2 122.3 %collective-permute-start.59 = (bf16[512,2304]{1,0:T(8,128)(2,1)}, bf16[512,2304]{1,0:T(8,128)(2,1)}, u32[]{:S(2)}, u32[]{:S(2)}) collective-permute-start(bf16[512,2304]{1,0:T(8,128)(2,1)} %copy-done.57), channel_id=1, source_target_pairs={{0,16},{16,0},{1,17},{17,1},{2,18},{18,2},{3,19},{19,3},{4,20},{20... | collective-permute-start | bytes 7077896 | tf_op jit(solution)/shard_map/ppermute | solution.py:62
  545.6 204.4 %collective-permute-start.73 = (bf16[144,2304]{1,0:T(8,128)(2,1)}, bf16[144,2304]{1,0:T(8,128)(2,1)}, u32[]{:S(2)}, u32[]{:S(2)}) collective-permute-start(bf16[144,2304]{1,0:T(8,128)(2,1)} %get-tuple-element.39), channel_id=1, source_target_pairs={{0,8},{8,0},{4,12},{12,4},{1,9},{9,1},{5,13},{13,5},{2,10},{10,2},... | collective-permute-start | bytes 1990664 | tf_op jit(solution)/shard_map/ppermute | solution.py:54
  628.7 49.1 %collective-permute-start.68 = (bf16[144,2304]{1,0:T(8,128)(2,1)}, bf16[144,2304]{1,0:T(8,128)(2,1)}, u32[]{:S(2)}, u32[]{:S(2)}) collective-permute-start(bf16[144,2304]{1,0:T(8,128)(2,1)} %get-tuple-element.36), channel_id=1, source_target_pairs={{0,4},{4,0},{8,12},{12,8},{1,5},{5,1},{9,13},{13,9},{2,6},{6,2},{1... | collective-permute-start | bytes 1990664 | tf_op jit(solution)/shard_map/ppermute | solution.py:50
  630.3 48.8 %collective-permute-start.71 = (bf16[144,2304]{1,0:T(8,128)(2,1)}, bf16[144,2304]{1,0:T(8,128)(2,1)}, u32[]{:S(2)}, u32[]{:S(2)}) collective-permute-start(bf16[144,2304]{1,0:T(8,128)(2,1)} %get-tuple-element.38), channel_id=1, source_target_pairs={{0,8},{8,0},{4,12},{12,4},{1,9},{9,1},{5,13},{13,5},{2,10},{10,2},... | collective-permute-start | bytes 1990664 | tf_op jit(solution)/shard_map/ppermute | solution.py:54
  693.7 73.9 %collective-permute-start.43 = (bf16[512,1152]{1,0:T(8,128)(2,1)}, bf16[512,1152]{1,0:T(8,128)(2,1)}, u32[]{:S(2)}, u32[]{:S(2)}) collective-permute-start(bf16[512,1152]{1,0:T(8,128)(2,1)} %get-tuple-element.60), channel_id=1, source_target_pairs={{0,16},{16,0},{1,17},{17,1},{2,18},{18,2},{3,19},{19,3},{4,20},{20... | collective-permute-start | bytes 3538952 | tf_op jit(solution)/shard_map/ppermute | solution.py:62
  703.3 69.5 %collective-permute-start.53 = (bf16[144,2304]{1,0:T(8,128)(2,1)}, bf16[144,2304]{1,0:T(8,128)(2,1)}, u32[]{:S(2)}, u32[]{:S(2)}) collective-permute-start(bf16[144,2304]{1,0:T(8,128)(2,1)} %get-tuple-element.48), channel_id=1, source_target_pairs={{0,4},{4,0},{8,12},{12,8},{1,5},{5,1},{9,13},{13,9},{2,6},{6,2},{1... | collective-permute-start | bytes 1990664 | tf_op jit(solution)/shard_map/ppermute | solution.py:50
  767.6 50.6 %collective-permute-start.35 = (bf16[512,1152]{1,0:T(8,128)(2,1)S(1)}, bf16[512,1152]{1,0:T(8,128)(2,1)S(1)}, u32[]{:S(2)}, u32[]{:S(2)}) collective-permute-start(bf16[512,1152]{1,0:T(8,128)(2,1)S(1)} %copy-done.30), channel_id=1, source_target_pairs={{0,16},{16,0},{1,17},{17,1},{2,18},{18,2},{3,19},{19,3},{4,20},{20... | collective-permute-start | bytes 3538952 | tf_op jit(solution)/shard_map/ppermute | solution.py:62
  813.1 42.4 %collective-permute-start.58 = (bf16[144,2304]{1,0:T(8,128)(2,1)S(1)}, bf16[144,2304]{1,0:T(8,128)(2,1)S(1)}, u32[]{:S(2)}, u32[]{:S(2)}) collective-permute-start(bf16[144,2304]{1,0:T(8,128)(2,1)S(1)} %copy-done.37), channel_id=1, source_target_pairs={{0,8},{8,0},{4,12},{12,4},{1,9},{9,1},{5,13},{13,5},{2,10},{10,2},... | collective-permute-start | bytes 1990664 | tf_op jit(solution)/shard_map/ppermute | solution.py:54
  814.5 44.5 %collective-permute-start.65 = (bf16[144,2304]{1,0:T(8,128)(2,1)S(1)}, bf16[144,2304]{1,0:T(8,128)(2,1)S(1)}, u32[]{:S(2)}, u32[]{:S(2)}) collective-permute-start(bf16[144,2304]{1,0:T(8,128)(2,1)S(1)} %copy-done.38), channel_id=1, source_target_pairs={{0,8},{8,0},{4,12},{12,4},{1,9},{9,1},{5,13},{13,5},{2,10},{10,2},... | collective-permute-start | bytes 1990664 | tf_op jit(solution)/shard_map/ppermute | solution.py:54
  818.2 38.9 %collective-permute-start.57 = (bf16[144,2304]{1,0:T(8,128)(2,1)S(1)}, bf16[144,2304]{1,0:T(8,128)(2,1)S(1)}, u32[]{:S(2)}, u32[]{:S(2)}) collective-permute-start(bf16[144,2304]{1,0:T(8,128)(2,1)S(1)} %get-tuple-element.47), channel_id=1, source_target_pairs={{0,4},{4,0},{8,12},{12,8},{1,5},{5,1},{9,13},{13,9},{2,6},{6,2},{1... | collective-permute-start | bytes 1990664 | tf_op jit(solution)/shard_map/ppermute | solution.py:50
  (123 other events, 1866.6 us)
Sparse Core Ops, SparseCore 0:
  227.6 95.7 all-reduce.4
  370.6 94.6 all-reduce.6
  515.1 95.1 all-reduce.8
  710.7 93.6 all-reduce.10

commit v2 on v0

--- a/solution.py
+++ b/solution.py
@@ -44,7 +44,345 @@
     return jax.nn.gelu(value_rows, approximate=True)
 
 
-def body(
+BF = jnp.bfloat16
+F32 = jnp.float32
+
+LINKS = {
+    "x": ("ctx", [(0, 1), (1, 0), (2, 3), (3, 2)]),
+    "y": ("ctx", [(0, 2), (2, 0), (1, 3), (3, 1)]),
+    "diagonal": ("ctx", [(0, 3), (3, 0), (1, 2), (2, 1)]),
+    "core": ("fsdp", [(0, 1), (1, 0)]),
+}
+ORDER = [(0, 0), (0, 1), (1, 1), (2, 0), (1, 0), (3, 0), (3, 1), (2, 1)]
+
+
+def tied(*values):
+    return lax.optimization_barrier(values)
+
+
+def send(link, value):
+    return lax.ppermute(value, *LINKS[link])
+
+
+def around(value, by=1):
+    size = lax.axis_size("tp")
+    return lax.ppermute(value, "tp", [(i, (i + by) % size) for i in range(size)])
+
+
+def halves(block):
+    half = block.shape[0] // 2
+    return block[:half], block[half:]
+
+
+class Scatter:
+    def __init__(self, partial):
+        block = partial.shape[0] // 4
+        self.half = block // 2
+        self.kept = partial[: 2 * block]
+        self.first = (send("x", partial[2 * block : 3 * block]), send("y", partial[3 * block :]))
+
+    def second(self):
+        half, (from_x, from_y) = self.half, self.first
+        x_low, y_top = self.kept[2 * half : 3 * half], self.kept[3 * half :]
+        self.last = (
+            send("y", (y_top.astype(F32) + from_x[half:].astype(F32)).astype(BF)),
+            send("x", (x_low.astype(F32) + from_y[:half].astype(F32)).astype(BF)),
+        )
+
+    def result(self):
+        half, (from_x, from_y), (y_top, x_low) = self.half, self.first, self.last
+        kept = self.kept
+        top = kept[:half].astype(F32) + from_x[:half].astype(F32) + y_top.astype(F32)
+        low = kept[half : 2 * half].astype(F32) + from_y[half:].astype(F32) + x_low.astype(F32)
+        return jnp.concatenate([top, low], 0)
+
+
+class Ring:
+    def __init__(self, value):
+        self.value, self.step = value, 0
+        self.size, self.me = lax.axis_size("tp"), lax.axis_index("tp")
+        self.rows = value.shape[0] // self.size
+        self.whole = jnp.zeros_like(value)
+        self.going = around(self.block(self.me - 1))
+
+    def block(self, index):
+        start = (index + self.size) % self.size * self.rows
+        return lax.dynamic_slice_in_dim(self.value, start, self.rows, 0)
+
+    def put(self):
+        index = (self.me - (self.step - self.size + 1) + self.size) % self.size
+        self.whole = lax.dynamic_update_slice_in_dim(self.whole, self.going, index * self.rows, 0)
+
+    def go(self):
+        if self.step < self.size - 1:
+            own = self.block(self.me - 2 - self.step)
+            self.going = (self.going.astype(F32) + own.astype(F32)).astype(BF)
+        self.step += 1
+        if self.step >= self.size - 1:
+            self.put()
+        if self.step < 2 * self.size - 2:
+            self.going = around(self.going)
+
+    def finish(self):
+        while self.step < 2 * self.size - 2:
+            self.go()
+        return self.whole
+
+
+def column_order(width):
+    core, me = lax.axis_index("fsdp"), lax.axis_index("ctx")
+    half_width, half = width // 2, width // 16
+    run = jnp.arange(half, dtype=jnp.int32)
+    place = jnp.concatenate([(me ^ k) * (2 * half) + low * half + run for k, low in ORDER])
+    place = jnp.concatenate([core * half_width + place, (1 - core) * half_width + place])
+    return (jnp.arange(width, dtype=jnp.int32)[:, None] == place[None, :]).astype(BF)
+
+
+def plane_body(
+    hidden_in,
+    lengths,
+    query_weight,
+    key_weight,
+    value_weight,
+    w_out,
+    w_gate,
+    w_up,
+    w_down,
+    gain_attn_in,
+    gain_attn_out,
+    gain_ffn_in,
+    gain_ffn_out,
+    cotangent,
+):
+    seqs_here, tok_here, width = hidden_in.shape
+    row_count = seqs_here * tok_here
+    head_groups = QUERY_HEADS // KEY_VALUE_HEADS
+    half_width = width // 2
+    q_cols, kv_cols = query_weight.shape[1], key_weight.shape[1]
+    kv_local = kv_cols // HEAD_SIZE
+    planes, me = lax.axis_size("ctx"), lax.axis_index("ctx")
+
+    def both_cores(mine):
+        return jnp.concatenate([mine, send("core", mine)], 0)
+
+    def gather(shard, axis):
+        return lax.all_gather(shard, ("fsdp", "ctx"), axis=axis, tiled=True)
+
+    attention_shards = jnp.concatenate([query_weight, key_weight, value_weight, w_out.T], 1)
+    attention_w = gather(attention_shards, 0)
+    gains = jnp.stack([gain_attn_in, gain_attn_out, gain_ffn_in, gain_ffn_out])[None]
+    gains = jnp.broadcast_to(gains, (2 * planes,) + gains.shape[1:])
+    gains = lax.all_to_all(gains, ("fsdp", "ctx"), 0, 0, tiled=True)
+    gains = gains.transpose(1, 0, 2).reshape(4, width).astype(F32)
+    scale_one, scale_two, scale_three, scale_four = (1.0 + gains[i][None] for i in range(4))
+    flat_in = hidden_in.astype(F32).reshape(row_count, width)
+    normed_one, factor_one = normalize(flat_in)
+    attention_input = (normed_one * scale_one).astype(BF)
+    to_blocks = column_order(width)
+
+    attention_w, attention_input, gate_t = tied(attention_w, attention_input, w_gate)
+    gate_w = gather(gate_t, 0)
+    qkv_cols = q_cols + 2 * kv_cols
+    qkv_w, out_w = attention_w[:, :qkv_cols], attention_w[:, qkv_cols:]
+    run = jnp.arange(tok_here, dtype=jnp.int32)
+    query_pos = me * tok_here + run
+    key_pos = jnp.arange(planes * tok_here, dtype=jnp.int32)
+    valid = query_pos[None, :] < lengths[:, None]
+    allowed = (
+        (key_pos[None, None, :] <= query_pos[None, :, None])
+        & (key_pos[None, None, :] < lengths[:, None, None])
+    )[:, None, None]
+    qkv = plain_dot(attention_input, qkv_w).astype(BF)
+    query_b = qkv[:, :q_cols]
+    kv = qkv[:, q_cols:].reshape(1, seqs_here, tok_here, 2 * kv_cols)
+    kv = lax.all_to_all(jnp.broadcast_to(kv, (planes,) + kv.shape[1:]), "ctx", 0, 0, tiled=True)
+
+    kv_all = kv.transpose(1, 0, 2, 3).reshape(seqs_here, SEQUENCE_SLOTS, 2 * kv_cols)
+    query_five = query_b.reshape(seqs_here, tok_here, kv_local, head_groups, HEAD_SIZE)
+    key_four = kv_all[:, :, :kv_cols].reshape(seqs_here, SEQUENCE_SLOTS, kv_local, HEAD_SIZE)
+    value_four = kv_all[:, :, kv_cols:].reshape(seqs_here, SEQUENCE_SLOTS, kv_local, HEAD_SIZE)
+    raw = jnp.einsum("stkgd,sukd->skgtu", query_five, key_four, preferred_element_type=F32) * QSCALE
+    bent = jnp.tanh(raw / CAP)
+    masked = jnp.where(allowed, CAP * bent, NEG)
+    largest = jnp.max(masked, -1, keepdims=True)
+    logsum = largest + jnp.log(jnp.sum(jnp.exp(masked - largest), -1, keepdims=True))
+    probs = jnp.exp(masked - logsum)
+    probs_b = probs.astype(BF)
+    attended = (
+        jnp.einsum("skgtu,sukd->stkgd", probs_b, value_four, preferred_element_type=F32)
+        .astype(BF)
+        .reshape(row_count, -1)
+    )
+    attn = right_dot(attended, out_w).astype(BF)
+    ring = Ring(attn)
+
+    ring.going, gate_w, up_t = tied(ring.going, gate_w, w_up)
+    up_w = gather(up_t, 0)
+    ring.go()
+    ring.go()
+    ring.go()
+    ring.go()
+    ring.going, up_w, down_t = tied(ring.going, up_w, w_down)
+    down_w = gather(down_t, 1)
+    attn = ring.finish().astype(F32)
+    normed_two, factor_two = normalize(attn)
+    after_attn = flat_in + normed_two * scale_two
+    normed_three, factor_three = normalize(after_attn)
+    ffn_in = (normed_three * scale_three).astype(BF)
+    gate = plain_dot(ffn_in, gate_w)
+    upward = plain_dot(ffn_in, up_w)
+    activated, gelu_pull = jax.vjp(gelu_tanh, gate)
+    hidden_b = (activated * upward).astype(BF)
+    hidden_b, down_w = tied(hidden_b, down_w)
+    ffn_out = lax.psum(plain_dot(hidden_b, down_w).astype(BF), "tp")
+    cot = cotangent.astype(F32).reshape(row_count, width) * valid.reshape(row_count, 1).astype(F32)
+
+    def near_far(rows_from):
+        blocks = plain_dot(rows_from, to_blocks).astype(BF)
+        return jnp.concatenate([blocks[:, :half_width], send("core", blocks[:, half_width:])], 0)
+
+    def weight_grad(rows_both, cols_both):
+        return left_dot(rows_both, cols_both).astype(BF)
+
+    hidden_both, attended_both = both_cores(hidden_b), both_cores(attended)
+    ffn_in_both, attention_input_both = near_far(ffn_in), near_far(attention_input)
+    ffn_out, hidden_both, attended_both, ffn_in_both, attention_input_both = tied(
+        ffn_out, hidden_both, attended_both, ffn_in_both, attention_input_both
+    )
+    ffn_out = ffn_out.astype(F32)
+    normed_four, factor_four = normalize(ffn_out)
+    result = after_attn + normed_four * scale_four
+    grad_gain_four = jnp.sum(cot * normed_four, 0)
+    dffn_b = norm_back(cot * scale_four, normed_four, factor_four).astype(BF)
+    dhidden = right_dot(dffn_b, down_w)
+    dgate_b = gelu_pull(dhidden * upward)[0].astype(BF)
+    dup_b = (dhidden * activated).astype(BF)
+    dffn_in = (right_dot(dgate_b, gate_w) + right_dot(dup_b, up_w)).astype(BF)
+    dffn_in, dgate_b, dup_b, dffn_b = tied(dffn_in, dgate_b, dup_b, dffn_b)
+
+    ring = Ring(dffn_in)
+    down_part = weight_grad(near_far(dffn_b), hidden_both)
+    ring.going, down_part, dgate_b = tied(ring.going, down_part, dgate_b)
+    ring.go()
+    down_s = Scatter(down_part)
+    gate_part = weight_grad(ffn_in_both, both_cores(dgate_b))
+    ring.going, gate_part = tied(ring.going, gate_part)
+    ring.go()
+    dup_both = both_cores(dup_b)
+    ring.going, down_s.first, dup_both = tied(ring.going, down_s.first, dup_both)
+    ring.go()
+    down_s.second()
+    gate_s = Scatter(gate_part)
+    output = result.astype(BF)
+    ring.going, output = tied(ring.going, output)
+    ring.go()
+    ring.going, down_s.last = tied(ring.going, down_s.last)
+    ring.go()
+    grad_down = down_s.result().T
+    ring.going, gate_s.first, grad_down = tied(ring.going, gate_s.first, grad_down)
+    gate_s.second()
+    dffn_in = ring.finish()
+    dffn_in = dffn_in.astype(F32)
+    grad_gain_three = jnp.sum(dffn_in * normed_three, 0)
+    dafter = cot + norm_back(dffn_in * scale_three, normed_three, factor_three)
+    grad_gain_two = jnp.sum(dafter * normed_two, 0)
+    dattn_b = norm_back(dafter * scale_two, normed_two, factor_two).astype(BF)
+    dattended = plain_dot(dattn_b, out_w).astype(BF).reshape(query_five.shape)
+    dprobs = jnp.einsum("stkgd,sukd->skgtu", dattended, value_four, preferred_element_type=F32)
+    weighted = jnp.sum(probs * dprobs, -1, keepdims=True)
+    draw_b = (probs * (dprobs - weighted) * (1.0 - bent * bent)).astype(BF)
+    dvalue_part = jnp.einsum("skgtu,stkgd->sukd", probs_b, dattended, preferred_element_type=F32)
+    dkey_part = (
+        jnp.einsum("skgtu,stkgd->sukd", draw_b, query_five, preferred_element_type=F32) * QSCALE
+    )
+    dkv = jnp.concatenate(
+        [
+            part.astype(BF).reshape(seqs_here, planes, tok_here, kv_cols)
+            for part in (dkey_part, dvalue_part)
+        ],
+        3,
+    ).transpose(1, 0, 2, 3)
+    dkv, dattn_b, dup_both, gate_s.last = tied(dkv, dattn_b, dup_both, gate_s.last)
+    dkv = lax.all_to_all(dkv, "ctx", 0, 0, tiled=True)
+    up_part = weight_grad(ffn_in_both, dup_both)
+    out_part = weight_grad(near_far(dattn_b), attended_both)
+    dquery_b = (
+        (jnp.einsum("skgtu,sukd->stkgd", draw_b, key_four, preferred_element_type=F32) * QSCALE)
+        .astype(BF)
+        .reshape(row_count, -1)
+    )
+    grad_gate = gate_s.result()
+    dkv, dquery_b, up_part, out_part, grad_gate = tied(dkv, dquery_b, up_part, out_part, grad_gate)
+    up_s = Scatter(up_part)
+    dkv_b = jnp.sum(dkv.astype(F32), 0).astype(BF).reshape(row_count, -1)
+    dqkv_b = jnp.concatenate([dquery_b, dkv_b], 1)
+    dattn_in = right_dot(dqkv_b, qkv_w)
+    dattn_in, dqkv_b, dafter = tied(dattn_in.astype(BF), dqkv_b, dafter)
+
+    ring = Ring(dattn_in)
+    grad_gain_one = jnp.sum(dattn_in.astype(F32) * normed_one, 0)[None]
+    qkv_part = weight_grad(attention_input_both, both_cores(dqkv_b))
+    ring.going, up_s.first, qkv_part, grad_gain_one = tied(
+        ring.going, up_s.first, qkv_part, grad_gain_one
+    )
+    ring.go()
+    up_s.second()
+    qkv_s = Scatter(qkv_part)
+    grad_gain_one = grad_gain_one + sum(
+        around(grad_gain_one, by) for by in range(1, lax.axis_size("tp"))
+    )
+    ring.going, grad_gain_one = tied(ring.going, grad_gain_one)
+    ring.go()
+    ring.going, up_s.last, qkv_s.first = tied(ring.going, up_s.last, qkv_s.first)
+    ring.go()
+    qkv_s.second()
+    out_s = Scatter(out_part)
+    grad_up = up_s.result()
+    ring.going, qkv_s.last, out_s.first, grad_up = tied(
+        ring.going, qkv_s.last, out_s.first, grad_up
+    )
+    ring.go()
+    out_s.second()
+    grad_qkv = qkv_s.result()
+    grad_gains = jnp.concatenate(
+        [grad_gain_one, grad_gain_two[None], grad_gain_three[None], grad_gain_four[None]], 0
+    )
+    grad_gains = jnp.sum(
+        lax.all_to_all(
+            grad_gains.reshape(4, 2 * planes, -1).transpose(1, 0, 2),
+            ("fsdp", "ctx"),
+            0,
+            0,
+            tiled=True,
+        ),
+        0,
+    )
+    ring.going, out_s.last, grad_qkv = tied(ring.going, out_s.last, grad_qkv)
+    ring.go()
+    grad_out = out_s.result().T
+    ring.going, grad_out, grad_gains = tied(ring.going, grad_out, grad_gains)
+    dattn_in = ring.finish()
+    dattn_in = dattn_in.astype(F32)
+    grad_input = dafter + norm_back(dattn_in * scale_one, normed_one, factor_one)
+    grad_input = grad_input.astype(BF)
+    return (
+        output.reshape(hidden_in.shape),
+        grad_input.reshape(hidden_in.shape),
+        grad_qkv[:, :q_cols],
+        grad_qkv[:, q_cols : q_cols + kv_cols],
+        grad_qkv[:, q_cols + kv_cols :],
+        grad_out,
+        grad_gate,
+        grad_up,
+        grad_down,
+        grad_gains[0],
+        grad_gains[1],
+        grad_gains[2],
+        grad_gains[3],
+    )
+
+
+def general_body(
     hidden_in,
     lengths,
     query_weight,
@@ -265,8 +603,9 @@
 
 
 def solution(mesh):
+    square = mesh.shape["ctx"] == 4 and mesh.shape["fsdp"] == 2
     return jax.shard_map(
-        body,
+        plane_body if square else general_body,
         mesh=mesh,
         in_specs=(
             P("fsdp", "ctx", None),

time: 1350 us -> 799 us (0.59)
  waiting for transfers between devices: 1020 us -> 398 us
  blocking collectives: 54.7 us -> 0 us
  starting transfers between devices: 2.84 us -> 51.1 us
  other arithmetic: 67.6 us -> 107 us
  local copies, waits for them, and re-layouts: 11.7 us -> 43.6 us
    reduce_scatter x9 -> x0, waiting for transfers between devices: 361 us -> none  [the longest x1 82.7 us: body(): lax.psum_scatter(grad_up.astype(jnp.bfloat16), ('fsdp', 'ctx'), scatter_d...]
    psum x4 -> x1, waiting for transfers between devices: 380 us -> 75.1 us  [plane_body(): ffn_out = lax.psum(plain_dot(hidden_b, down_w).astype(BF), 'tp')]
    all_gather x9 -> x4, waiting for transfers between devices: 273 us -> 42.9 us  [gather(): return lax.all_gather(shard, ('fsdp', 'ctx'), axis=axis, tiled=True)]
    ppermute x0 -> x50, waiting for transfers between devices: none -> 229 us  [the longest x21 176 us: around(): lax.ppermute(value, 'tp', [(i, (i + by) % size) for i in range(size)])]
    unnamed x2 -> x0, blocking collectives: 54.7 us -> none
    all_to_all x0 -> x4, waiting for transfers between devices: none -> 50.6 us  [the longest x1 33.2 us: plane_body(): lax.all_to_all(jnp.broadcast_to(kv, (planes,) + kv.shape[1:]), 'ctx', 0,...]
    ppermute x0 -> x50, starting transfers between devices: none -> 32.1 us  [the longest x29 21.7 us: send(): return lax.ppermute(value, *LINKS[link])]
    dot_general x7 -> x9, matrix products: 51 us -> 77.3 us  [plain_dot(): return jnp.dot(first, second, preferred_element_type=jnp.float32)]
  transfers between devices with their start and end apart: 22 -> 59, of which waited for: 20 -> 33; matrix products, arithmetic and copies ran while one was open for 12% -> 25% of each run, Pallas kernels for 0% -> 0%
where the time goes in v2:
time: 799 us; the launch traced here: 789 us
  waiting for transfers between devices  398 us (50%)
  matrix products  174 us (22%)
  other arithmetic  107 us (13%)
  starting transfers between devices  51.1 us (6%)
  local copies, waits for them, and re-layouts  43.6 us (5%)
  between operations  16.1 us (2%)
    ppermute x21, waiting for transfers between devices, around(): lax.ppermute(value, 'tp', [(i, (i + by) % size) for i in range(size)])  176 us
    dot_general x9, matrix products, plain_dot(): return jnp.dot(first, second, preferred_element_type=jnp.float32)  77.3 us
    psum x1, waiting for transfers between devices, plane_body(): ffn_out = lax.psum(plain_dot(hidden_b, down_w).astype(BF), 'tp')  75.1 us
    ppermute x29, waiting for transfers between devices, send(): return lax.ppermute(value, *LINKS[link])  52.7 us
    dot_general x5, matrix products, right_dot(): lax.dot_general(first, second, (((1,), (1,)), ((), ())), preferred_elemen...  47.2 us
    all_gather x4, waiting for transfers between devices, gather(): return lax.all_gather(shard, ('fsdp', 'ctx'), axis=axis, tiled=True)  42.9 us
    all_to_all x1, waiting for transfers between devices, plane_body(): lax.all_to_all(jnp.broadcast_to(kv, (planes,) + kv.shape[1:]), 'ctx', 0,...  33.2 us
    dot_general x5, matrix products, left_dot(): lax.dot_general(first, second, (((0,), (0,)), ((), ())), preferred_elemen...  26.6 us
  transfers between devices with their start and end apart: 59, of which 33 were waited for; matrix products, arithmetic and copies ran while one was open for 25% of the time, Pallas kernels for 0%

profile of v2, /device:TPU:0, one launch (start us, length us, event | category | flops | bytes accessed | tf_op | source)
XLA Modules:
  0.0 789.3 jit_solution(441093673359267312)
XLA Ops:
  23.1 39.0 %all-gather.5.cloned.1.call-done = bf16[2304,1536]{1,0:T(8,128)(2,1)} async-done(((bf16[288,1536]{1,0:T(8,128)(2,1)}), bf16[2304,1536]{1,0:T(8,128)(2,1)}) %all-gather.5.cloned.1.call-update) | async-done | bytes 7077904 | tf_op jit(solution)/shard_map/all_gather | solution.py:169
  78.7 33.2 %all-to-all-done.1 = bf16[4,1,512,512]{3,2,1,0:T(8,128)(2,1)} async-done(((bf16[4,1,512,512]{3,2,1,0:T(8,128)(2,1)}), bf16[4,1,512,512]{3,2,1,0:T(8,128)(2,1)}, u32[]{:S(2)}, u32[]{:S(2)}) %all-to-all-start.1) | async-done | bytes 2097184 | tf_op jit(solution)/shard_map/all_to_all | solution.py:198
  131.7 14.7 %collective-permute-done = bf16[128,2304]{1,0:T(8,128)(2,1)S(1)} collective-permute-done((bf16[128,2304]{1,0:T(8,128)(2,1)S(1)}, bf16[128,2304]{1,0:T(8,128)(2,1)S(1)}, u32[]{:S(2)}, u32[]{:S(2)}) %collective-permute-start) | collective-permute-done | bytes 589856 | tf_op jit(solution)/shard_map/ppermute | solution.py:69
  153.1 15.8 %collective-permute-done.1 = bf16[128,2304]{1,0:T(8,128)(2,1)S(1)} collective-permute-done((bf16[128,2304]{1,0:T(8,128)(2,1)S(1)}, bf16[128,2304]{1,0:T(8,128)(2,1)S(1)}, u32[]{:S(2)}, u32[]{:S(2)}) %collective-permute-start.1) | collective-permute-done | bytes 589856 | tf_op jit(solution)/shard_map/ppermute | solution.py:69
  170.2 16.4 %collective-permute-done.2 = bf16[128,2304]{1,0:T(8,128)(2,1)S(1)} collective-permute-done((bf16[128,2304]{1,0:T(8,128)(2,1)S(1)}, bf16[128,2304]{1,0:T(8,128)(2,1)S(1)}, u32[]{:S(2)}, u32[]{:S(2)}) %collective-permute-start.2) | collective-permute-done | bytes 589856 | tf_op jit(solution)/shard_map/ppermute | solution.py:69
  190.3 15.6 %collective-permute-done.3 = bf16[128,2304]{1,0:T(8,128)(2,1)S(1)} collective-permute-done((bf16[128,2304]{1,0:T(8,128)(2,1)S(1)}, bf16[128,2304]{1,0:T(8,128)(2,1)S(1)}, u32[]{:S(2)}, u32[]{:S(2)}) %collective-permute-start.3) | collective-permute-done | bytes 589856 | tf_op jit(solution)/shard_map/ppermute | solution.py:69
  206.6 14.7 %collective-permute-done.4 = bf16[128,2304]{1,0:T(8,128)(2,1)} collective-permute-done((bf16[128,2304]{1,0:T(8,128)(2,1)S(1)}, bf16[128,2304]{1,0:T(8,128)(2,1)}, u32[]{:S(2)}, u32[]{:S(2)}) %collective-permute-start.4) | collective-permute-done | bytes 589856 | tf_op jit(solution)/shard_map/ppermute | solution.py:69
  222.4 10.2 %fusion.65 = bf16[512,2304]{1,0:T(8,128)(2,1)S(1)} fusion(bf16[512,2304]{1,0:T(8,128)(2,1)} %fusion.51, s32[2304]{0:T(1024)S(1)} %pad_add_fusion), kind=kOutput, calls=%fused_computation.96 | convolution fusion | flops 5442306048 | bytes 4727808 | tf_op jit(solution)/shard_map/dot_general | solution.py:28
  236.6 15.0 %collective-permute-done.5 = bf16[128,2304]{1,0:T(8,128)(2,1)S(1)} collective-permute-done((bf16[128,2304]{1,0:T(8,128)(2,1)}, bf16[128,2304]{1,0:T(8,128)(2,1)S(1)}, u32[]{:S(2)}, u32[]{:S(2)}) %collective-permute-start.5) | collective-permute-done | bytes 589856 | tf_op jit(solution)/shard_map/ppermute | solution.py:69
  261.2 10.1 %fusion.64 = bf16[512,2304]{1,0:T(8,128)(2,1)} fusion(bf16[512,2304]{1,0:T(8,128)(2,1)S(1)} %multiply_convert_fusion.2, s32[2304]{0:T(1024)S(1)} %copy-done.50), kind=kOutput, calls=%fused_computation.95 | convolution fusion | flops 5442306048 | bytes 4727808 | tf_op jit(solution)/shard_map/dot_general | solution.py:28
  278.7 9.5 %multiply_convert_fusion.1 = (bf16[512,2304]{1,0:T(8,128)(2,1)}, f32[512,2304]{1,0:T(8,128)}) fusion(f32[512,2304]{1,0:T(8,128)} %fusion.141, bf16[512,2304]{1,0:T(8,128)(2,1)S(1)} %multiply_convert_fusion.2, bf16[2304,2304]{1,0:T(8,128)(2,1)S(1)} %bitcast.210), kind=kOutput, calls=%fused_computation.91 | convolution fusion | flops 5447614464 | bytes 24772608 | tf_op jit(solution)/shard_map/dot_general | solution.py:28
  288.2 11.5 %convolution_convert_fusion.4 = bf16[512,2304]{1,0:T(8,128)(2,1)} fusion(bf16[512,2304]{1,0:T(8,128)(2,1)} %get-tuple-element.98, bf16[2304,2304]{0,1:T(8,128)(2,1)} %all-gather.11.cloned.1.call-done), kind=kOutput, calls=%fused_computation.100 | convolution fusion | flops 5436997632 | bytes 15335424 | tf_op jit(solution)/shard_map/dot_general | solution.py:28
  317.9 75.1 %all-reduce.2.cloned.1.call-done = bf16[512,2304]{1,0:T(8,128)(2,1)} async-done(((bf16[512,2304]{1,0:T(8,128)(2,1)}), bf16[512,2304]{1,0:T(8,128)(2,1)}) %all-reduce.2.cloned.1.call-update) | async-done | bytes 2359312 | tf_op jit(solution)/shard_map/psum | solution.py:237
  395.3 7.5 fusion.41
  404.3 14.7 %multiply_convert_fusion = (bf16[512,2304]{1,0:T(8,128)(2,1)}, bf16[512,2304]{1,0:T(8,128)(2,1)S(1)}) fusion(f32[512,2304]{1,0:T(8,128)S(1)} %bitcast.214, f32[512,2304]{1,0:T(8,128)} %get-tuple-element.236, bf16[512,2304]{1,0:T(8,128)(2,1)S(1)} %fusion.38, bf16[2304,2304]{0,1:T(8,128)(2,1)} %all-gather.11.cloned.1.call-done), kind=kOutput, calls=%fused_computation.90 | convolution fusion | flops 5464129536 | bytes 27131904 | tf_op jit(solution)/shard_map/dot_general | solution.py:38
  419.0 12.2 %fusion.142 = f32[512,2304]{1,0:T(8,128)} fusion(bf16[512,2304]{1,0:T(8,128)(2,1)S(1)} %get-tuple-element.107, bf16[2304,2304]{1,0:T(8,128)(2,1)} %all-gather.7.cloned.1.call-done), kind=kOutput, calls=%fused_computation.255 | convolution fusion | flops 5435817984 | bytes 17694720 | tf_op jit(solution)/shard_map/dot_general | solution.py:38
  431.2 11.5 %fusion.68 = bf16[512,2304]{1,0:T(8,128)(2,1)S(1)} fusion(f32[512,2304]{1,0:T(8,128)} %fusion.142, bf16[512,2304]{1,0:T(8,128)(2,1)} %get-tuple-element.110, bf16[2304,2304]{1,0:T(8,128)(2,1)} %all-gather.9.cloned.1.call-done), kind=kOutput, calls=%fused_computation.102 | convolution fusion | flops 5438177280 | bytes 20054016 | tf_op jit(solution)/shard_map/dot_general | solution.py:38
  442.7 10.2 %fusion.66 = bf16[512,2304]{1,0:T(8,128)(2,1)S(1)} fusion(bf16[512,2304]{1,0:T(8,128)(2,1)} %copy-done.21, s32[2304]{0:T(1024)S(1)} %copy-done.51), kind=kOutput, calls=%fused_computation.97 | convolution fusion | flops 5442306048 | bytes 4727808 | tf_op jit(solution)/shard_map/dot_general | solution.py:28
  462.2 8.6 %collective-permute-done.10 = bf16[128,2304]{1,0:T(8,128)(2,1)S(1)} collective-permute-done((bf16[128,2304]{1,0:T(8,128)(2,1)S(1)}, bf16[128,2304]{1,0:T(8,128)(2,1)S(1)}, u32[]{:S(2)}, u32[]{:S(2)}) %collective-permute-start.10) | collective-permute-done | bytes 589856 | tf_op jit(solution)/shard_map/ppermute | solution.py:69
  493.1 11.5 %collective-permute-done.15 = bf16[288,2304]{1,0:T(8,128)(2,1)} collective-permute-done((bf16[288,2304]{1,0:T(8,128)(2,1)}, bf16[288,2304]{1,0:T(8,128)(2,1)}, u32[]{:S(2)}, u32[]{:S(2)}) %collective-permute-start.15) | collective-permute-done | bytes 1327136 | tf_op jit(solution)/shard_map/ppermute | solution.py:64
  510.3 11.8 %collective-permute-done.18 = bf16[128,2304]{1,0:T(8,128)(2,1)S(1)} collective-permute-done((bf16[128,2304]{1,0:T(8,128)(2,1)S(1)}, bf16[128,2304]{1,0:T(8,128)(2,1)S(1)}, u32[]{:S(2)}, u32[]{:S(2)}) %collective-permute-start.18) | collective-permute-done | bytes 589856 | tf_op jit(solution)/shard_map/ppermute | solution.py:69
  526.6 10.5 %collective-permute-done.19 = bf16[128,2304]{1,0:T(8,128)(2,1)S(1)} collective-permute-done((bf16[128,2304]{1,0:T(8,128)(2,1)S(1)}, bf16[128,2304]{1,0:T(8,128)(2,1)S(1)}, u32[]{:S(2)}, u32[]{:S(2)}) %collective-permute-start.19) | collective-permute-done | bytes 589856 | tf_op jit(solution)/shard_map/ppermute | solution.py:69
  540.6 12.6 %collective-permute-done.23 = bf16[288,2304]{1,0:T(8,128)(2,1)S(1)} collective-permute-done((bf16[288,2304]{1,0:T(8,128)(2,1)S(1)}, bf16[288,2304]{1,0:T(8,128)(2,1)S(1)}, u32[]{:S(2)}, u32[]{:S(2)}) %collective-permute-start.23) | collective-permute-done | bytes 1327136 | tf_op jit(solution)/shard_map/ppermute | solution.py:64
  603.2 9.0 %fusion.67 = bf16[512,2304]{1,0:T(8,128)(2,1)S(1)} fusion(bf16[512,2304]{1,0:T(8,128)(2,1)S(1)} %copy-done.20, s32[2304]{0:T(1024)S(1)} %copy-done.51), kind=kOutput, calls=%fused_computation.98 | convolution fusion | flops 5442306048 | bytes 4727808 | tf_op jit(solution)/shard_map/dot_general | solution.py:28
  624.3 7.5 convolution_convert_fusion
  635.5 9.1 %all-to-all-done.2 = bf16[4,1,512,512]{2,3,1,0:T(8,128)(2,1)} async-done(((bf16[4,1,512,512]{2,3,1,0:T(8,128)(2,1)}), bf16[4,1,512,512]{2,3,1,0:T(8,128)(2,1)}, u32[]{:S(2)}, u32[]{:S(2)}) %all-to-all-start.2) | async-done | bytes 2097184 | tf_op jit(solution)/shard_map/all_to_all | solution.py:306
  659.4 12.4 %collective-permute-done.28 = bf16[128,2304]{1,0:T(8,128)(2,1)S(1)} collective-permute-done((bf16[128,2304]{1,0:T(8,128)(2,1)S(1)}, bf16[128,2304]{1,0:T(8,128)(2,1)S(1)}, u32[]{:S(2)}, u32[]{:S(2)}) %collective-permute-start.28) | collective-permute-done | bytes 589856 | tf_op jit(solution)/shard_map/ppermute | solution.py:69
  671.9 12.4 %collective-permute-done.29 = bf16[288,2304]{1,0:T(8,128)(2,1)S(1)} collective-permute-done((bf16[288,2304]{1,0:T(8,128)(2,1)S(1)}, bf16[288,2304]{1,0:T(8,128)(2,1)S(1)}, u32[]{:S(2)}, u32[]{:S(2)}) %collective-permute-start.29) | collective-permute-done | bytes 1327136 | tf_op jit(solution)/shard_map/ppermute | solution.py:64
  699.4 8.3 %collective-permute-done.32 = bf16[128,2304]{1,0:T(8,128)(2,1)S(1)} collective-permute-done((bf16[128,2304]{1,0:T(8,128)(2,1)S(1)}, bf16[128,2304]{1,0:T(8,128)(2,1)S(1)}, u32[]{:S(2)}, u32[]{:S(2)}) %collective-permute-start.32) | collective-permute-done | bytes 589856 | tf_op jit(solution)/shard_map/ppermute | solution.py:69
  741.4 7.7 collective-permute-done.41
  754.8 10.0 %collective-permute-done.46 = bf16[128,2304]{1,0:T(8,128)(2,1)S(1)} collective-permute-done((bf16[128,2304]{1,0:T(8,128)(2,1)S(1)}, bf16[128,2304]{1,0:T(8,128)(2,1)S(1)}, u32[]{:S(2)}, u32[]{:S(2)}) %collective-permute-start.46) | collective-permute-done | bytes 589856 | tf_op jit(solution)/shard_map/ppermute | solution.py:69
  767.5 10.5 %collective-permute-done.49 = bf16[128,2304]{1,0:T(8,128)(2,1)S(1)} collective-permute-done((bf16[128,2304]{1,0:T(8,128)(2,1)S(1)}, bf16[128,2304]{1,0:T(8,128)(2,1)S(1)}, u32[]{:S(2)}, u32[]{:S(2)}) %collective-permute-start.49) | collective-permute-done | bytes 589856 | tf_op jit(solution)/shard_map/ppermute | solution.py:69
  (400 shorter events, 294.5 us)
Async XLA Ops:
  7.2 54.9 %all-gather.5.cloned.1.call-start = ((), (), s32[]{:S(2)}) async-start(), calls=%async_computation.4 | async-start | bytes 7962624 | tf_op jit(solution)/shard_map/all_gather | solution.py:169
  15.5 134.8 %all-gather.7.cloned.1.call-start = ((), (), s32[]{:S(2)}) async-start(), calls=%async_computation.5 | async-start | bytes 11943936 | tf_op jit(solution)/shard_map/all_gather | solution.py:169
  70.2 41.8 %all-to-all-start.1 = ((bf16[4,1,512,512]{3,2,1,0:T(8,128)(2,1)}), bf16[4,1,512,512]{3,2,1,0:T(8,128)(2,1)}, u32[]{:S(2)}, u32[]{:S(2)}) async-start(bf16[4,1,512,512]{3,2,1,0:T(8,128)(2,1)} %broadcast_in_dim.15), calls=%async_computation.1 | async-start | bytes 4194304 | tf_op jit(solution)/shard_map/all_to_all | solution.py:198
  74.7 146.7 %all-gather.9.cloned.1.call-start = ((), (), s32[]{:S(2)}) async-start(), calls=%async_computation.6 | async-start | bytes 11943936 | tf_op jit(solution)/shard_map/all_gather | solution.py:169
  150.3 137.9 %all-gather.11.cloned.1.call-start = ((), (), s32[]{:S(2)}) async-start(), calls=%async_computation.7 | async-start | bytes 11943936 | tf_op jit(solution)/shard_map/all_gather | solution.py:169
  151.6 17.3 %collective-permute-start.1 = (bf16[128,2304]{1,0:T(8,128)(2,1)S(1)}, bf16[128,2304]{1,0:T(8,128)(2,1)S(1)}, u32[]{:S(2)}, u32[]{:S(2)}) collective-permute-start(bf16[128,2304]{1,0:T(8,128)(2,1)S(1)} %add_convert_fusion.14), channel_id=1, source_target_pairs={{0,1},{1,2},{2,3},{3,0},{4,5},{5,6},{6,7},{7,4},{8,9},{9,10},{10,1... | collective-permute-start | bytes 1769480 | tf_op jit(solution)/shard_map/ppermute | solution.py:69
  221.4 171.5 %all-reduce.2.cloned.1.call-start = ((), (), s32[]{:S(2)}) async-start(), calls=%async_computation.8 | async-start | bytes 4718592 | tf_op jit(solution)/shard_map/psum | solution.py:237
  233.8 71.6 %collective-permute-start.9 = (bf16[512,1152]{1,0:T(8,128)(2,1)}, bf16[512,1152]{1,0:T(8,128)(2,1)}, u32[]{:S(2)}, u32[]{:S(2)}) collective-permute-start(bf16[512,1152]{1,0:T(8,128)(2,1)} %get-tuple-element.218), channel_id=1, source_target_pairs={{0,16},{16,0},{1,17},{17,1},{2,18},{18,2},{3,19},{19,3},{4,20},{20... | collective-permute-start | bytes 3538952 | tf_op jit(solution)/shard_map/ppermute | solution.py:64
  233.8 17.7 %collective-permute-start.5 = (bf16[128,2304]{1,0:T(8,128)(2,1)}, bf16[128,2304]{1,0:T(8,128)(2,1)S(1)}, u32[]{:S(2)}, u32[]{:S(2)}) collective-permute-start(bf16[128,2304]{1,0:T(8,128)(2,1)} %collective-permute-done.4), channel_id=1, source_target_pairs={{0,1},{1,2},{2,3},{3,0},{4,5},{5,6},{6,7},{7,4},{8,9},{9,10},{10,1... | collective-permute-start | bytes 1769480 | tf_op jit(solution)/shard_map/ppermute | solution.py:69
  288.2 25.5 %collective-permute-start.6 = (bf16[512,2304]{1,0:T(8,128)(2,1)}, bf16[512,2304]{1,0:T(8,128)(2,1)}, u32[]{:S(2)}, u32[]{:S(2)}) collective-permute-start(bf16[512,2304]{1,0:T(8,128)(2,1)} %get-tuple-element.98), channel_id=1, source_target_pairs={{0,16},{16,0},{1,17},{17,1},{2,18},{18,2},{3,19},{19,3},{4,20},{20... | collective-permute-start | bytes 7077896 | tf_op jit(solution)/shard_map/ppermute | solution.py:64
  453.2 17.6 %collective-permute-start.10 = (bf16[128,2304]{1,0:T(8,128)(2,1)S(1)}, bf16[128,2304]{1,0:T(8,128)(2,1)S(1)}, u32[]{:S(2)}, u32[]{:S(2)}) collective-permute-start(bf16[128,2304]{1,0:T(8,128)(2,1)S(1)} %constant_dynamic-slice_fusion.1), channel_id=1, source_target_pairs={{0,1},{1,2},{2,3},{3,0},{4,5},{5,6},{6,7},{7,4},{8,9},{9,10},{10,1... | collective-permute-start | bytes 1769480 | tf_op jit(solution)/shard_map/ppermute | solution.py:69
  470.8 18.3 %collective-permute-start.17 = (bf16[512,2304]{1,0:T(8,128)(2,1)S(1)}, bf16[512,2304]{1,0:T(8,128)(2,1)}, u32[]{:S(2)}, u32[]{:S(2)}) collective-permute-start(bf16[512,2304]{1,0:T(8,128)(2,1)S(1)} %copy-done.17), channel_id=1, source_target_pairs={{0,16},{16,0},{1,17},{17,1},{2,18},{18,2},{3,19},{19,3},{4,20},{20... | collective-permute-start | bytes 7077896 | tf_op jit(solution)/shard_map/ppermute | solution.py:64
  471.4 17.2 %collective-permute-start.12 = (bf16[128,2304]{1,0:T(8,128)(2,1)S(1)}, bf16[128,2304]{1,0:T(8,128)(2,1)S(1)}, u32[]{:S(2)}, u32[]{:S(2)}) collective-permute-start(bf16[128,2304]{1,0:T(8,128)(2,1)S(1)} %add_convert_fusion.11), channel_id=1, source_target_pairs={{0,1},{1,2},{2,3},{3,0},{4,5},{5,6},{6,7},{7,4},{8,9},{9,10},{10,1... | collective-permute-start | bytes 1769480 | tf_op jit(solution)/shard_map/ppermute | solution.py:69
  473.2 31.4 %collective-permute-start.15 = (bf16[288,2304]{1,0:T(8,128)(2,1)}, bf16[288,2304]{1,0:T(8,128)(2,1)}, u32[]{:S(2)}, u32[]{:S(2)}) collective-permute-start(bf16[288,2304]{1,0:T(8,128)(2,1)} %get-tuple-element.205), channel_id=1, source_target_pairs={{0,4},{4,0},{8,12},{12,8},{1,5},{5,1},{9,13},{13,9},{2,6},{6,2},{1... | collective-permute-start | bytes 3981320 | tf_op jit(solution)/shard_map/ppermute | solution.py:64
  474.7 31.1 %collective-permute-start.16 = (bf16[288,2304]{1,0:T(8,128)(2,1)}, bf16[288,2304]{1,0:T(8,128)(2,1)}, u32[]{:S(2)}, u32[]{:S(2)}) collective-permute-start(bf16[288,2304]{1,0:T(8,128)(2,1)} %get-tuple-element.204), channel_id=1, source_target_pairs={{0,8},{8,0},{4,12},{12,4},{1,9},{9,1},{5,13},{13,5},{2,10},{10,2},... | collective-permute-start | bytes 3981320 | tf_op jit(solution)/shard_map/ppermute | solution.py:64
  488.8 17.0 %collective-permute-start.14 = (bf16[128,2304]{1,0:T(8,128)(2,1)S(1)}, bf16[128,2304]{1,0:T(8,128)(2,1)S(1)}, u32[]{:S(2)}, u32[]{:S(2)}) collective-permute-start(bf16[128,2304]{1,0:T(8,128)(2,1)S(1)} %add_convert_fusion.10), channel_id=1, source_target_pairs={{0,1},{1,2},{2,3},{3,0},{4,5},{5,6},{6,7},{7,4},{8,9},{9,10},{10,1... | collective-permute-start | bytes 1769480 | tf_op jit(solution)/shard_map/ppermute | solution.py:69
  507.8 16.7 %collective-permute-start.20 = (bf16[144,2304]{1,0:T(8,128)(2,1)S(1)}, bf16[144,2304]{1,0:T(8,128)(2,1)S(1)}, u32[]{:S(2)}, u32[]{:S(2)}) collective-permute-start(bf16[144,2304]{1,0:T(8,128)(2,1)S(1)} %get-tuple-element.203), channel_id=1, source_target_pairs={{0,8},{8,0},{4,12},{12,4},{1,9},{9,1},{5,13},{13,5},{2,10},{10,2},... | collective-permute-start | bytes 1990664 | tf_op jit(solution)/shard_map/ppermute | solution.py:64
  509.4 17.3 %collective-permute-start.21 = (bf16[144,2304]{1,0:T(8,128)(2,1)S(1)}, bf16[144,2304]{1,0:T(8,128)(2,1)S(1)}, u32[]{:S(2)}, u32[]{:S(2)}) collective-permute-start(bf16[144,2304]{1,0:T(8,128)(2,1)S(1)} %get-tuple-element.202), channel_id=1, source_target_pairs={{0,4},{4,0},{8,12},{12,8},{1,5},{5,1},{9,13},{13,9},{2,6},{6,2},{1... | collective-permute-start | bytes 1990664 | tf_op jit(solution)/shard_map/ppermute | solution.py:64
  522.3 31.0 %collective-permute-start.23 = (bf16[288,2304]{1,0:T(8,128)(2,1)S(1)}, bf16[288,2304]{1,0:T(8,128)(2,1)S(1)}, u32[]{:S(2)}, u32[]{:S(2)}) collective-permute-start(bf16[288,2304]{1,0:T(8,128)(2,1)S(1)} %get-tuple-element.201), channel_id=1, source_target_pairs={{0,4},{4,0},{8,12},{12,8},{1,5},{5,1},{9,13},{13,9},{2,6},{6,2},{1... | collective-permute-start | bytes 3981320 | tf_op jit(solution)/shard_map/ppermute | solution.py:64
  523.0 30.3 %collective-permute-start.24 = (bf16[288,2304]{1,0:T(8,128)(2,1)S(1)}, bf16[288,2304]{1,0:T(8,128)(2,1)S(1)}, u32[]{:S(2)}, u32[]{:S(2)}) collective-permute-start(bf16[288,2304]{1,0:T(8,128)(2,1)S(1)} %get-tuple-element.200), channel_id=1, source_target_pairs={{0,8},{8,0},{4,12},{12,4},{1,9},{9,1},{5,13},{13,5},{2,10},{10,2},... | collective-permute-start | bytes 3981320 | tf_op jit(solution)/shard_map/ppermute | solution.py:64
  583.2 20.0 %collective-permute-start.25 = (bf16[144,2304]{1,0:T(8,128)(2,1)}, bf16[144,2304]{1,0:T(8,128)(2,1)}, u32[]{:S(2)}, u32[]{:S(2)}) collective-permute-start(bf16[144,2304]{1,0:T(8,128)(2,1)} %get-tuple-element.197), channel_id=1, source_target_pairs={{0,8},{8,0},{4,12},{12,4},{1,9},{9,1},{5,13},{13,5},{2,10},{10,2},... | collective-permute-start | bytes 1990664 | tf_op jit(solution)/shard_map/ppermute | solution.py:64
  583.7 19.4 %collective-permute-start.26 = (bf16[144,2304]{1,0:T(8,128)(2,1)}, bf16[144,2304]{1,0:T(8,128)(2,1)}, u32[]{:S(2)}, u32[]{:S(2)}) collective-permute-start(bf16[144,2304]{1,0:T(8,128)(2,1)} %get-tuple-element.196), channel_id=1, source_target_pairs={{0,4},{4,0},{8,12},{12,8},{1,5},{5,1},{9,13},{13,9},{2,6},{6,2},{1... | collective-permute-start | bytes 1990664 | tf_op jit(solution)/shard_map/ppermute | solution.py:64
  613.8 18.0 %collective-permute-start.27 = (bf16[512,1152]{1,0:T(8,128)(2,1)}, bf16[512,1152]{1,0:T(8,128)(2,1)}, u32[]{:S(2)}, u32[]{:S(2)}) collective-permute-start(bf16[512,1152]{1,0:T(8,128)(2,1)} %get-tuple-element.214), channel_id=1, source_target_pairs={{0,16},{16,0},{1,17},{17,1},{2,18},{18,2},{3,19},{19,3},{4,20},{20... | collective-permute-start | bytes 3538952 | tf_op jit(solution)/shard_map/ppermute | solution.py:64
  613.8 30.9 %all-to-all-start.2 = ((bf16[4,1,512,512]{2,3,1,0:T(8,128)(2,1)}), bf16[4,1,512,512]{2,3,1,0:T(8,128)(2,1)}, u32[]{:S(2)}, u32[]{:S(2)}) async-start(bf16[4,1,512,512]{2,3,1,0:T(8,128)(2,1)} %maximum_bitcast_fusion.1), calls=%async_computation.2 | async-start | bytes 4194304 | tf_op jit(solution)/shard_map/all_to_all | solution.py:306
  652.7 31.6 %collective-permute-start.29 = (bf16[288,2304]{1,0:T(8,128)(2,1)S(1)}, bf16[288,2304]{1,0:T(8,128)(2,1)S(1)}, u32[]{:S(2)}, u32[]{:S(2)}) collective-permute-start(bf16[288,2304]{1,0:T(8,128)(2,1)S(1)} %get-tuple-element.193), channel_id=1, source_target_pairs={{0,4},{4,0},{8,12},{12,8},{1,5},{5,1},{9,13},{13,9},{2,6},{6,2},{1... | collective-permute-start | bytes 3981320 | tf_op jit(solution)/shard_map/ppermute | solution.py:64
  654.3 31.2 %collective-permute-start.30 = (bf16[288,2304]{1,0:T(8,128)(2,1)S(1)}, bf16[288,2304]{1,0:T(8,128)(2,1)S(1)}, u32[]{:S(2)}, u32[]{:S(2)}) collective-permute-start(bf16[288,2304]{1,0:T(8,128)(2,1)S(1)} %get-tuple-element.192), channel_id=1, source_target_pairs={{0,8},{8,0},{4,12},{12,4},{1,9},{9,1},{5,13},{13,5},{2,10},{10,2},... | collective-permute-start | bytes 3981320 | tf_op jit(solution)/shard_map/ppermute | solution.py:64
  654.9 17.0 %collective-permute-start.28 = (bf16[128,2304]{1,0:T(8,128)(2,1)S(1)}, bf16[128,2304]{1,0:T(8,128)(2,1)S(1)}, u32[]{:S(2)}, u32[]{:S(2)}) collective-permute-start(bf16[128,2304]{1,0:T(8,128)(2,1)S(1)} %constant_dynamic-slice_fusion), channel_id=1, source_target_pairs={{0,1},{1,2},{2,3},{3,0},{4,5},{5,6},{6,7},{7,4},{8,9},{9,10},{10,1... | collective-permute-start | bytes 1769480 | tf_op jit(solution)/shard_map/ppermute | solution.py:69
  693.6 34.0 %collective-permute-start.37 = (bf16[144,2304]{1,0:T(8,128)(2,1)}, bf16[144,2304]{1,0:T(8,128)(2,1)}, u32[]{:S(2)}, u32[]{:S(2)}) collective-permute-start(bf16[144,2304]{1,0:T(8,128)(2,1)} %get-tuple-element.191), channel_id=1, source_target_pairs={{0,8},{8,0},{4,12},{12,4},{1,9},{9,1},{5,13},{13,5},{2,10},{10,2},... | collective-permute-start | bytes 1990664 | tf_op jit(solution)/shard_map/ppermute | solution.py:64
  695.3 32.3 %collective-permute-start.38 = (bf16[144,2304]{1,0:T(8,128)(2,1)}, bf16[144,2304]{1,0:T(8,128)(2,1)}, u32[]{:S(2)}, u32[]{:S(2)}) collective-permute-start(bf16[144,2304]{1,0:T(8,128)(2,1)} %get-tuple-element.190), channel_id=1, source_target_pairs={{0,4},{4,0},{8,12},{12,8},{1,5},{5,1},{9,13},{13,9},{2,6},{6,2},{1... | collective-permute-start | bytes 1990664 | tf_op jit(solution)/shard_map/ppermute | solution.py:64
  696.8 28.7 %collective-permute-start.39 = (bf16[288,1024]{1,0:T(8,128)(2,1)}, bf16[288,1024]{1,0:T(8,128)(2,1)}, u32[]{:S(2)}, u32[]{:S(2)}) collective-permute-start(bf16[288,1024]{1,0:T(8,128)(2,1)} %get-tuple-element.212), channel_id=1, source_target_pairs={{0,4},{4,0},{8,12},{12,8},{1,5},{5,1},{9,13},{13,9},{2,6},{6,2},{1... | collective-permute-start | bytes 1769480 | tf_op jit(solution)/shard_map/ppermute | solution.py:64
  697.3 28.9 %collective-permute-start.40 = (bf16[288,1024]{1,0:T(8,128)(2,1)}, bf16[288,1024]{1,0:T(8,128)(2,1)}, u32[]{:S(2)}, u32[]{:S(2)}) collective-permute-start(bf16[288,1024]{1,0:T(8,128)(2,1)} %get-tuple-element.211), channel_id=1, source_target_pairs={{0,8},{8,0},{4,12},{12,4},{1,9},{9,1},{5,13},{13,5},{2,10},{10,2},... | collective-permute-start | bytes 1769480 | tf_op jit(solution)/shard_map/ppermute | solution.py:64
  708.6 18.9 %collective-permute-start.36 = (bf16[128,2304]{1,0:T(8,128)(2,1)}, bf16[128,2304]{1,0:T(8,128)(2,1)}, u32[]{:S(2)}, u32[]{:S(2)}) collective-permute-start(bf16[128,2304]{1,0:T(8,128)(2,1)} %add_convert_fusion.7), channel_id=1, source_target_pairs={{0,1},{1,2},{2,3},{3,0},{4,5},{5,6},{6,7},{7,4},{8,9},{9,10},{10,1... | collective-permute-start | bytes 1769480 | tf_op jit(solution)/shard_map/ppermute | solution.py:69
  (103 other events, 1434.7 us)
Sparse Core Ops, SparseCore 0:
  10.5 51.5 all-gather.4
  64.0 86.2 all-gather.6
  152.2 63.7 all-gather.8
  221.5 61.0 all-gather.10
  299.9 93.0 all-reduce.1

commit v3 on v2

--- a/solution.py
+++ b/solution.py
@@ -1,6 +1,8 @@
 import jax
 import jax.numpy as jnp
 from jax import lax
+from jax.experimental import pallas as pl
+from jax.experimental.pallas import tpu as pltpu
 from jax.sharding import PartitionSpec as P
 
 QUERY_HEADS = 8
@@ -75,11 +77,10 @@
 
 
 class Scatter:
-    def __init__(self, partial):
-        block = partial.shape[0] // 4
-        self.half = block // 2
-        self.kept = partial[: 2 * block]
-        self.first = (send("x", partial[2 * block : 3 * block]), send("y", partial[3 * block :]))
+    def __init__(self, blocks):
+        self.kept, to_x, to_y = blocks
+        self.half = to_x.shape[0] // 2
+        self.first = (send("x", to_x), send("y", to_y))
 
     def second(self):
         half, (from_x, from_y) = self.half, self.first
@@ -129,13 +130,263 @@
         return self.whole
 
 
-def column_order(width):
-    core, me = lax.axis_index("fsdp"), lax.axis_index("ctx")
-    half_width, half = width // 2, width // 16
-    run = jnp.arange(half, dtype=jnp.int32)
-    place = jnp.concatenate([(me ^ k) * (2 * half) + low * half + run for k, low in ORDER])
-    place = jnp.concatenate([core * half_width + place, (1 - core) * half_width + place])
-    return (jnp.arange(width, dtype=jnp.int32)[:, None] == place[None, :]).astype(BF)
+VMEM_BYTES = 56 * 2**20
+
+
+def kernel_params():
+    return pltpu.CompilerParams(vmem_limit_bytes=VMEM_BYTES)
+
+
+def cut_of(size):
+    return next((cut for cut in (768, 512) if size % cut == 0), size)
+
+
+def rowwise(fn, rows, vectors, dtypes, sums=0, block=128):
+    count, width = rows[0].shape
+    n_in, n_out = len(rows) + len(vectors), len(dtypes)
+
+    def kernel(*refs):
+        results = fn(*(ref[...] for ref in refs[:n_in]))
+        for ref, value in zip(refs[n_in : n_in + n_out], results):
+            ref[...] = value.astype(ref.dtype)
+        for ref, value in zip(refs[n_in + n_out :], results[n_out:]):
+            part = jnp.sum(value.reshape(block // 8, 8, width), 0)
+
+            @pl.when(pl.program_id(0) == 0)
+            def _():
+                ref[...] = part
+
+            @pl.when(pl.program_id(0) > 0)
+            def _():
+                ref[...] += part
+
+    by_row = pl.BlockSpec((block, width), lambda i: (i, 0))
+    return pl.pallas_call(
+        kernel,
+        grid=(count // block,),
+        in_specs=[by_row] * len(rows) + [pl.BlockSpec((1, width), lambda i: (0, 0))] * len(vectors),
+        out_specs=[by_row] * n_out + [pl.BlockSpec((8, width), lambda i: (0, 0))] * sums,
+        out_shape=[jax.ShapeDtypeStruct((count, width), dtype) for dtype in dtypes]
+        + [jax.ShapeDtypeStruct((8, width), F32)] * sums,
+        compiler_params=kernel_params(),
+        cost_estimate=pl.CostEstimate(
+            flops=20 * count * width, bytes_accessed=4 * count * width * n_in, transcendentals=0
+        ),
+    )(*rows, *vectors)
+
+
+ROOT = 0.7978845608028654
+
+
+def gelu_parts(z):
+    bend = jnp.tanh(ROOT * (z + 0.044715 * (z * z * z)))
+    value = 0.5 * z * (1.0 + bend)
+    slope = 0.5 * (1.0 + bend) + 0.5 * z * (1.0 - bend * bend) * (
+        ROOT * (1.0 + (3.0 * 0.044715) * (z * z))
+    )
+    return value, slope
+
+
+def ffn_hidden(x, weights):
+    count, width = x.shape
+    units = weights.shape[1] // 3
+    cut = cut_of(units)
+
+    def kernel(x_ref, gate_w, up_w, gate_ref, up_ref, hidden_ref):
+        gate = plain_dot(x_ref[...], gate_w[...])
+        up = plain_dot(x_ref[...], up_w[...])
+        gate_ref[...] = gate
+        up_ref[...] = up
+        hidden_ref[...] = (gelu_parts(gate)[0] * up).astype(BF)
+
+    out = pl.BlockSpec((count, cut), lambda j: (0, j))
+    return pl.pallas_call(
+        kernel,
+        grid=(units // cut,),
+        in_specs=[
+            pl.BlockSpec((count, width), lambda j: (0, 0)),
+            pl.BlockSpec((width, cut), lambda j: (0, j)),
+            pl.BlockSpec((width, cut), lambda j: (0, j + units // cut)),
+        ],
+        out_specs=[out] * 3,
+        out_shape=[
+            jax.ShapeDtypeStruct((count, units), F32),
+            jax.ShapeDtypeStruct((count, units), F32),
+            jax.ShapeDtypeStruct((count, units), BF),
+        ],
+        compiler_params=kernel_params(),
+        cost_estimate=pl.CostEstimate(
+            flops=4 * count * width * units,
+            bytes_accessed=4 * width * units + 10 * count * units,
+            transcendentals=count * units,
+        ),
+    )(x, weights, weights)
+
+
+def ffn_down(hidden, weights):
+    count, units = hidden.shape
+    width = weights.shape[0]
+    cut = cut_of(width)
+
+    def kernel(x_ref, w_ref, out_ref):
+        out_ref[...] = right_dot(x_ref[...], w_ref[...]).astype(BF)
+
+    return pl.pallas_call(
+        kernel,
+        grid=(width // cut,),
+        in_specs=[
+            pl.BlockSpec((count, units), lambda j: (0, 0)),
+            pl.BlockSpec((cut, units), lambda j: (j, 2)),
+        ],
+        out_specs=pl.BlockSpec((count, cut), lambda j: (0, j)),
+        out_shape=jax.ShapeDtypeStruct((count, width), BF),
+        compiler_params=kernel_params(),
+        cost_estimate=pl.CostEstimate(
+            flops=2 * count * width * units, bytes_accessed=2 * width * units, transcendentals=0
+        ),
+    )(hidden, weights)
+
+
+def ffn_hidden_back(dffn, weights, gate, up):
+    count, width = dffn.shape
+    units = gate.shape[1]
+    cut = cut_of(units)
+
+    def kernel(d_ref, w_ref, gate_ref, up_ref, dgate_ref, dup_ref):
+        dhidden = plain_dot(d_ref[...], w_ref[...])
+        value, slope = gelu_parts(gate_ref[...])
+        dgate_ref[...] = (dhidden * up_ref[...] * slope).astype(BF)
+        dup_ref[...] = (dhidden * value).astype(BF)
+
+    out = pl.BlockSpec((count, cut), lambda j: (0, j))
+    return pl.pallas_call(
+        kernel,
+        grid=(units // cut,),
+        in_specs=[
+            pl.BlockSpec((count, width), lambda j: (0, 0)),
+            pl.BlockSpec((width, cut), lambda j: (0, j + 2 * (units // cut))),
+            out,
+            out,
+        ],
+        out_specs=[out] * 2,
+        out_shape=[jax.ShapeDtypeStruct((count, units), BF)] * 2,
+        compiler_params=kernel_params(),
+        cost_estimate=pl.CostEstimate(
+            flops=2 * count * width * units,
+            bytes_accessed=2 * width * units + 12 * count * units,
+            transcendentals=count * units,
+        ),
+    )(dffn, weights, gate, up)
+
+
+def ffn_input_back(dgate, dup, weights):
+    count, units = dgate.shape
+    width = weights.shape[0]
+    cut = cut_of(width)
+
+    def kernel(dgate_ref, dup_ref, gate_w, up_w, out_ref):
+        out_ref[...] = (
+            right_dot(dgate_ref[...], gate_w[...]) + right_dot(dup_ref[...], up_w[...])
+        ).astype(BF)
+
+    whole = pl.BlockSpec((count, units), lambda j: (0, 0))
+    return pl.pallas_call(
+        kernel,
+        grid=(width // cut,),
+        in_specs=[
+            whole,
+            whole,
+            pl.BlockSpec((cut, units), lambda j: (j, 0)),
+            pl.BlockSpec((cut, units), lambda j: (j, 1)),
+        ],
+        out_specs=pl.BlockSpec((count, cut), lambda j: (0, j)),
+        out_shape=jax.ShapeDtypeStruct((count, width), BF),
+        compiler_params=kernel_params(),
+        cost_estimate=pl.CostEstimate(
+            flops=4 * count * width * units, bytes_accessed=4 * width * units, transcendentals=0
+        ),
+    )(dgate, dup, weights, weights)
+
+
+def weight_grad(rows, rows_far, cols, cols_far):
+    count, half_width = rows_far.shape
+    width = cols.shape[1]
+    cut = cut_of(width)
+    half = half_width // 8
+    place = jnp.stack([lax.axis_index("fsdp"), lax.axis_index("ctx")]).astype(jnp.int32)
+
+    def kernel(
+        place_ref, near_ref, far_ref, cols_ref, cols_far_ref, *rest
+    ):
+        outs, (near_t, far_t, total) = rest[:3], rest[3:]
+
+        @pl.when(pl.program_id(0) == 0)
+        def _():
+            near_t[...] = near_ref[...].T
+            far_t[...] = far_ref[...].T
+
+        total[...] = plain_dot(near_t[...], cols_ref[...]) + plain_dot(
+            far_t[...], cols_far_ref[...]
+        )
+        for index, (k, low) in enumerate(ORDER):
+            start = (lax.bitwise_xor(place_ref[1], k) * 2 + low) * half
+            block = total[pl.ds(pl.multiple_of(start, 16), half), :].astype(BF)
+            out, at = (outs[0], index) if index < 4 else (outs[1 + (index - 4) // 2], index % 2)
+            out[at * half : (at + 1) * half, :] = block
+
+    by_cut = pl.BlockSpec((count, cut), lambda j, place: (0, j))
+    sizes = (4 * half, 2 * half, 2 * half)
+    return pl.pallas_call(
+        kernel,
+        grid_spec=pltpu.PrefetchScalarGridSpec(
+            num_scalar_prefetch=1,
+            grid=(width // cut,),
+            in_specs=[
+                pl.BlockSpec((count, half_width), lambda j, place: (0, place[0])),
+                pl.BlockSpec((count, half_width), lambda j, place: (0, 0)),
+                by_cut,
+                by_cut,
+            ],
+            out_specs=[pl.BlockSpec((size, cut), lambda j, place: (0, j)) for size in sizes],
+            scratch_shapes=[
+                pltpu.VMEM((half_width, count), BF),
+                pltpu.VMEM((half_width, count), BF),
+                pltpu.VMEM((half_width, cut), F32),
+            ],
+        ),
+        out_shape=[jax.ShapeDtypeStruct((size, width), BF) for size in sizes],
+        compiler_params=kernel_params(),
+        cost_estimate=pl.CostEstimate(
+            flops=4 * count * half_width * width,
+            bytes_accessed=2 * half_width * width + 4 * count * (width + half_width),
+            transcendentals=0,
+        ),
+    )(place, rows, rows_far, cols, cols_far)
+
+
+def residual_rows(attn, hidden, scale_two, scale_three):
+    attn, hidden = attn.astype(F32), hidden.astype(F32)
+    after = hidden + normalize(attn)[0] * scale_two
+    return after, normalize(after)[0] * scale_three
+
+
+def output_rows(ffn_out, after, cot, scale_four):
+    normed, factor = normalize(ffn_out.astype(F32))
+    cot = cot.astype(F32)
+    return (
+        after + normed * scale_four,
+        norm_back(cot * scale_four, normed, factor),
+        cot * normed,
+    )
+
+
+def residual_back_rows(dffn_in, after, attn, cot, scale_three, scale_two):
+    dffn_in = dffn_in.astype(F32)
+    normed, factor = normalize(after)
+    dafter = cot.astype(F32) + norm_back(dffn_in * scale_three, normed, factor)
+    normed_two, factor_two = normalize(attn.astype(F32))
+    dattn = norm_back(dafter * scale_two, normed_two, factor_two)
+    return dafter, dattn, dffn_in * normed, dafter * normed_two
 
 
 def plane_body(
@@ -159,17 +410,21 @@
     head_groups = QUERY_HEADS // KEY_VALUE_HEADS
     half_width = width // 2
     q_cols, kv_cols = query_weight.shape[1], key_weight.shape[1]
+    size = lax.axis_size("tp")
     kv_local = kv_cols // HEAD_SIZE
     planes, me = lax.axis_size("ctx"), lax.axis_index("ctx")
 
-    def both_cores(mine):
-        return jnp.concatenate([mine, send("core", mine)], 0)
-
-    def gather(shard, axis):
-        return lax.all_gather(shard, ("fsdp", "ctx"), axis=axis, tiled=True)
+    core = lax.axis_index("fsdp")
+
+    def gather(shard):
+        return lax.all_gather(shard, ("fsdp", "ctx"), axis=0, tiled=True)
+
+    def far_half(rows):
+        return send("core", lax.dynamic_slice_in_dim(rows, (1 - core) * half_width, half_width, 1))
 
     attention_shards = jnp.concatenate([query_weight, key_weight, value_weight, w_out.T], 1)
-    attention_w = gather(attention_shards, 0)
+    attention_w = gather(attention_shards)
+    ffn_shards = jnp.concatenate([w_gate, w_up, w_down.T], 1)
     gains = jnp.stack([gain_attn_in, gain_attn_out, gain_ffn_in, gain_ffn_out])[None]
     gains = jnp.broadcast_to(gains, (2 * planes,) + gains.shape[1:])
     gains = lax.all_to_all(gains, ("fsdp", "ctx"), 0, 0, tiled=True)
@@ -178,15 +433,14 @@
     flat_in = hidden_in.astype(F32).reshape(row_count, width)
     normed_one, factor_one = normalize(flat_in)
     attention_input = (normed_one * scale_one).astype(BF)
-    to_blocks = column_order(width)
-
-    attention_w, attention_input, gate_t = tied(attention_w, attention_input, w_gate)
-    gate_w = gather(gate_t, 0)
+
+    attention_w, attention_input, ffn_shards = tied(attention_w, attention_input, ffn_shards)
+    ffn_w = gather(ffn_shards)
     qkv_cols = q_cols + 2 * kv_cols
     qkv_w, out_w = attention_w[:, :qkv_cols], attention_w[:, qkv_cols:]
     run = jnp.arange(tok_here, dtype=jnp.int32)
     query_pos = me * tok_here + run
-    key_pos = jnp.arange(planes * tok_here, dtype=jnp.int32)
+    key_pos = jnp.concatenate([(me ^ k) * tok_here + run for k in range(planes)])
     valid = query_pos[None, :] < lengths[:, None]
     allowed = (
         (key_pos[None, None, :] <= query_pos[None, :, None])
@@ -194,10 +448,8 @@
     )[:, None, None]
     qkv = plain_dot(attention_input, qkv_w).astype(BF)
     query_b = qkv[:, :q_cols]
-    kv = qkv[:, q_cols:].reshape(1, seqs_here, tok_here, 2 * kv_cols)
-    kv = lax.all_to_all(jnp.broadcast_to(kv, (planes,) + kv.shape[1:]), "ctx", 0, 0, tiled=True)
-
-    kv_all = kv.transpose(1, 0, 2, 3).reshape(seqs_here, SEQUENCE_SLOTS, 2 * kv_cols)
+    kv = qkv[:, q_cols:].reshape(seqs_here, tok_here, 2 * kv_cols)
+    kv_all = jnp.concatenate([kv, send("x", kv), send("y", kv), send("diagonal", kv)], 1)
     query_five = query_b.reshape(seqs_here, tok_here, kv_local, head_groups, HEAD_SIZE)
     key_four = kv_all[:, :, :kv_cols].reshape(seqs_here, SEQUENCE_SLOTS, kv_local, HEAD_SIZE)
     value_four = kv_all[:, :, kv_cols:].reshape(seqs_here, SEQUENCE_SLOTS, kv_local, HEAD_SIZE)
@@ -215,78 +467,65 @@
     )
     attn = right_dot(attended, out_w).astype(BF)
     ring = Ring(attn)
-
-    ring.going, gate_w, up_t = tied(ring.going, gate_w, w_up)
-    up_w = gather(up_t, 0)
-    ring.go()
-    ring.go()
-    ring.go()
-    ring.go()
-    ring.going, up_w, down_t = tied(ring.going, up_w, w_down)
-    down_w = gather(down_t, 1)
-    attn = ring.finish().astype(F32)
-    normed_two, factor_two = normalize(attn)
-    after_attn = flat_in + normed_two * scale_two
-    normed_three, factor_three = normalize(after_attn)
-    ffn_in = (normed_three * scale_three).astype(BF)
-    gate = plain_dot(ffn_in, gate_w)
-    upward = plain_dot(ffn_in, up_w)
-    activated, gelu_pull = jax.vjp(gelu_tanh, gate)
-    hidden_b = (activated * upward).astype(BF)
-    hidden_b, down_w = tied(hidden_b, down_w)
-    ffn_out = lax.psum(plain_dot(hidden_b, down_w).astype(BF), "tp")
-    cot = cotangent.astype(F32).reshape(row_count, width) * valid.reshape(row_count, 1).astype(F32)
-
-    def near_far(rows_from):
-        blocks = plain_dot(rows_from, to_blocks).astype(BF)
-        return jnp.concatenate([blocks[:, :half_width], send("core", blocks[:, half_width:])], 0)
-
-    def weight_grad(rows_both, cols_both):
-        return left_dot(rows_both, cols_both).astype(BF)
-
-    hidden_both, attended_both = both_cores(hidden_b), both_cores(attended)
-    ffn_in_both, attention_input_both = near_far(ffn_in), near_far(attention_input)
-    ffn_out, hidden_both, attended_both, ffn_in_both, attention_input_both = tied(
-        ffn_out, hidden_both, attended_both, ffn_in_both, attention_input_both
-    )
-    ffn_out = ffn_out.astype(F32)
-    normed_four, factor_four = normalize(ffn_out)
-    result = after_attn + normed_four * scale_four
-    grad_gain_four = jnp.sum(cot * normed_four, 0)
-    dffn_b = norm_back(cot * scale_four, normed_four, factor_four).astype(BF)
-    dhidden = right_dot(dffn_b, down_w)
-    dgate_b = gelu_pull(dhidden * upward)[0].astype(BF)
-    dup_b = (dhidden * activated).astype(BF)
-    dffn_in = (right_dot(dgate_b, gate_w) + right_dot(dup_b, up_w)).astype(BF)
-    dffn_in, dgate_b, dup_b, dffn_b = tied(dffn_in, dgate_b, dup_b, dffn_b)
-
+    for _ in range(2 * size - 3):
+        ring.go()
+    attn = ring.finish()
+    hidden_rows = hidden_in.reshape(row_count, width)
+    after_attn, ffn_in = rowwise(
+        residual_rows, [attn, hidden_rows], [scale_two, scale_three], [F32, BF]
+    )
+    gate, upward, hidden_b = ffn_hidden(ffn_in, ffn_w)
+    ffn_out = ffn_down(hidden_b, ffn_w)
+    ffn_out, hidden_b, attended, ffn_in, attention_input, cotangent = tied(
+        ffn_out, hidden_b, attended, ffn_in, attention_input, cotangent
+    )
+    ffn_out = lax.psum(ffn_out, "tp")
+
+    hidden_far, attended_far = send("core", hidden_b), send("core", attended)
+    ffn_in_far, attention_input_far = far_half(ffn_in), far_half(attention_input)
+    cot = jnp.where(
+        valid.reshape(row_count, 1), cotangent.reshape(row_count, width), jnp.zeros((), BF)
+    )
+    ffn_out, hidden_far, attended_far, ffn_in_far, attention_input_far, cot = tied(
+        ffn_out, hidden_far, attended_far, ffn_in_far, attention_input_far, cot
+    )
+    output, dffn_b, gain_four_rows = rowwise(
+        output_rows, [ffn_out, after_attn, cot], [scale_four], [BF, BF], 1
+    )
+    dgate_b, dup_b = ffn_hidden_back(dffn_b, ffn_w, gate, upward)
+    dffn_in = ffn_input_back(dgate_b, dup_b, ffn_w)
+    dffn_far = far_half(dffn_b)
+
+    dffn_in, dffn_far, dgate_b, dup_b = tied(dffn_in, dffn_far, dgate_b, dup_b)
     ring = Ring(dffn_in)
-    down_part = weight_grad(near_far(dffn_b), hidden_both)
-    ring.going, down_part, dgate_b = tied(ring.going, down_part, dgate_b)
+    dgate_far = send("core", dgate_b)
+    down_part = weight_grad(dffn_b, dffn_far, hidden_b, hidden_far)
+    ring.going, down_part, dgate_far = tied(ring.going, down_part, dgate_far)
     ring.go()
     down_s = Scatter(down_part)
-    gate_part = weight_grad(ffn_in_both, both_cores(dgate_b))
-    ring.going, gate_part = tied(ring.going, gate_part)
-    ring.go()
-    dup_both = both_cores(dup_b)
-    ring.going, down_s.first, dup_both = tied(ring.going, down_s.first, dup_both)
+    dup_far = send("core", dup_b)
+    gate_part = weight_grad(ffn_in, ffn_in_far, dgate_b, dgate_far)
+    ring.going, gate_part, dup_far = tied(ring.going, gate_part, dup_far)
+    ring.go()
+    up_part = weight_grad(ffn_in, ffn_in_far, dup_b, dup_far)
+    ring.going, up_part = tied(ring.going, up_part)
+    ring.go()
+    ring.going, down_s.first, gate_part = tied(ring.going, down_s.first, gate_part)
     ring.go()
     down_s.second()
     gate_s = Scatter(gate_part)
-    output = result.astype(BF)
-    ring.going, output = tied(ring.going, output)
-    ring.go()
-    ring.going, down_s.last = tied(ring.going, down_s.last)
-    ring.go()
-    grad_down = down_s.result().T
-    ring.going, gate_s.first, grad_down = tied(ring.going, gate_s.first, grad_down)
+    ring.go()
+    dffn_in, gate_s.first, down_s.last, up_part = tied(
+        ring.finish(), gate_s.first, down_s.last, up_part
+    )
     gate_s.second()
-    dffn_in = ring.finish()
-    dffn_in = dffn_in.astype(F32)
-    grad_gain_three = jnp.sum(dffn_in * normed_three, 0)
-    dafter = cot + norm_back(dffn_in * scale_three, normed_three, factor_three)
-    grad_gain_two = jnp.sum(dafter * normed_two, 0)
-    dattn_b = norm_back(dafter * scale_two, normed_two, factor_two).astype(BF)
+    dafter, dattn_b, gain_three_rows, gain_two_rows = rowwise(
+        residual_back_rows,
+        [dffn_in, after_attn, attn, cot],
+        [scale_three, scale_two],
+        [F32, BF],
+        2,
+    )
     dattended = plain_dot(dattn_b, out_w).astype(BF).reshape(query_five.shape)
     dprobs = jnp.einsum("stkgd,sukd->skgtu", dattended, value_four, preferred_element_type=F32)
     weighted = jnp.sum(probs * dprobs, -1, keepdims=True)
@@ -295,73 +534,73 @@
     dkey_part = (
         jnp.einsum("skgtu,stkgd->sukd", draw_b, query_five, preferred_element_type=F32) * QSCALE
     )
-    dkv = jnp.concatenate(
-        [
-            part.astype(BF).reshape(seqs_here, planes, tok_here, kv_cols)
-            for part in (dkey_part, dvalue_part)
-        ],
-        3,
-    ).transpose(1, 0, 2, 3)
-    dkv, dattn_b, dup_both, gate_s.last = tied(dkv, dattn_b, dup_both, gate_s.last)
-    dkv = lax.all_to_all(dkv, "ctx", 0, 0, tiled=True)
-    up_part = weight_grad(ffn_in_both, dup_both)
-    out_part = weight_grad(near_far(dattn_b), attended_both)
+    dkv = [
+        jnp.concatenate(
+            [
+                part[:, k * tok_here : (k + 1) * tok_here].astype(BF).reshape(row_count, kv_cols)
+                for part in (dkey_part, dvalue_part)
+            ],
+            1,
+        )
+        for k in range(planes)
+    ]
+    dattn_far = far_half(dattn_b)
+    dkv, dattn_far, gate_s.last = tied(dkv, dattn_far, gate_s.last)
+    dkv = [dkv[0], send("x", dkv[1]), send("y", dkv[2]), send("diagonal", dkv[3])]
+    out_part = weight_grad(dattn_b, dattn_far, attended, attended_far)
     dquery_b = (
         (jnp.einsum("skgtu,sukd->stkgd", draw_b, key_four, preferred_element_type=F32) * QSCALE)
         .astype(BF)
         .reshape(row_count, -1)
     )
+    grad_down = down_s.result().T
     grad_gate = gate_s.result()
-    dkv, dquery_b, up_part, out_part, grad_gate = tied(dkv, dquery_b, up_part, out_part, grad_gate)
+    dkv, dquery_b, out_part, grad_down, grad_gate, up_part = tied(
+        dkv, dquery_b, out_part, grad_down, grad_gate, up_part
+    )
     up_s = Scatter(up_part)
-    dkv_b = jnp.sum(dkv.astype(F32), 0).astype(BF).reshape(row_count, -1)
+    dkv_b = sum(part.astype(F32) for part in dkv).astype(BF)
     dqkv_b = jnp.concatenate([dquery_b, dkv_b], 1)
     dattn_in = right_dot(dqkv_b, qkv_w)
     dattn_in, dqkv_b, dafter = tied(dattn_in.astype(BF), dqkv_b, dafter)
 
     ring = Ring(dattn_in)
-    grad_gain_one = jnp.sum(dattn_in.astype(F32) * normed_one, 0)[None]
-    qkv_part = weight_grad(attention_input_both, both_cores(dqkv_b))
-    ring.going, up_s.first, qkv_part, grad_gain_one = tied(
-        ring.going, up_s.first, qkv_part, grad_gain_one
-    )
-    ring.go()
+    dqkv_far = send("core", dqkv_b)
+    grad_gain_one = jnp.sum(dattn_in.astype(F32) * normed_one, 0)
+    qkv_part = weight_grad(attention_input, attention_input_far, dqkv_b, dqkv_far)
+    grad_gains = jnp.stack(
+        [grad_gain_one]
+        + [jnp.sum(rows, 0) / size for rows in (gain_two_rows, gain_three_rows, gain_four_rows)]
+    )
+    grad_gains = grad_gains.reshape(4, 2 * planes, 1, -1).transpose(1, 2, 0, 3)
+    grad_gains = jnp.broadcast_to(grad_gains, (2 * planes, size) + grad_gains.shape[2:])
+    grad_gains = grad_gains.reshape((-1,) + grad_gains.shape[2:])
+    ring.going, qkv_part = tied(ring.going, qkv_part)
+    ring.go()
+    ring.going, grad_gains = tied(ring.going, grad_gains)
+    ring.go()
+    grad_gains = lax.all_to_all(grad_gains, ("fsdp", "ctx", "tp"), 0, 0, tiled=True)
+    ring.going, up_s.first = tied(ring.going, up_s.first)
     up_s.second()
     qkv_s = Scatter(qkv_part)
-    grad_gain_one = grad_gain_one + sum(
-        around(grad_gain_one, by) for by in range(1, lax.axis_size("tp"))
-    )
-    ring.going, grad_gain_one = tied(ring.going, grad_gain_one)
+    ring.go()
+    ring.going, out_part = tied(ring.going, out_part)
     ring.go()
     ring.going, up_s.last, qkv_s.first = tied(ring.going, up_s.last, qkv_s.first)
-    ring.go()
     qkv_s.second()
     out_s = Scatter(out_part)
+    ring.go()
     grad_up = up_s.result()
     ring.going, qkv_s.last, out_s.first, grad_up = tied(
         ring.going, qkv_s.last, out_s.first, grad_up
     )
-    ring.go()
     out_s.second()
     grad_qkv = qkv_s.result()
-    grad_gains = jnp.concatenate(
-        [grad_gain_one, grad_gain_two[None], grad_gain_three[None], grad_gain_four[None]], 0
-    )
-    grad_gains = jnp.sum(
-        lax.all_to_all(
-            grad_gains.reshape(4, 2 * planes, -1).transpose(1, 0, 2),
-            ("fsdp", "ctx"),
-            0,
-            0,
-            tiled=True,
-        ),
-        0,
-    )
-    ring.going, out_s.last, grad_qkv = tied(ring.going, out_s.last, grad_qkv)
-    ring.go()
+    dattn_in, out_s.last, grad_gains, grad_qkv = tied(
+        ring.finish(), out_s.last, grad_gains, grad_qkv
+    )
+    grad_gains = jnp.sum(grad_gains, 0)
     grad_out = out_s.result().T
-    ring.going, grad_out, grad_gains = tied(ring.going, grad_out, grad_gains)
-    dattn_in = ring.finish()
     dattn_in = dattn_in.astype(F32)
     grad_input = dafter + norm_back(dattn_in * scale_one, normed_one, factor_one)
     grad_input = grad_input.astype(BF)

time: 799 us -> 748 us (0.936)
  matrix products: 174 us -> 32.8 us
  Pallas kernels: 0 us -> 130 us
  other arithmetic: 107 us -> 80.7 us
  waiting for transfers between devices: 398 us -> 390 us
    pallas_call x0 -> x12, Pallas kernels: none -> 130 us  [the longest x5 46.1 us: weight_grad(): pl.pallas_call(kernel, grid_spec=pltpu.PrefetchScalarGridSpec(num_scalar_...]
    dot_general x9 -> x2, matrix products: 77.3 us -> 8.89 us  [plain_dot(): return jnp.dot(first, second, preferred_element_type=jnp.float32)]
    ppermute x29 -> x35, waiting for transfers between devices: 52.7 us -> 111 us  [send(): return lax.ppermute(value, *LINKS[link])]
    all_to_all x3 -> x1, waiting for transfers between devices: 46.4 us -> 0.01 us  [plane_body(): lax.all_to_all(grad_gains, ('fsdp', 'ctx', 'tp'), 0, 0, tiled=True)]
    dot_general x5 -> x2, matrix products: 47.2 us -> 8.55 us  [right_dot(): lax.dot_general(first, second, (((1,), (1,)), ((), ())), preferred_elemen...]
    ppermute x21 -> x18, waiting for transfers between devices: 176 us -> 139 us  [around(): lax.ppermute(value, 'tp', [(i, (i + by) % size) for i in range(size)])]
    dot_general x5 -> x0, matrix products: 26.6 us -> none  [left_dot(): lax.dot_general(first, second, (((0,), (0,)), ((), ())), preferred_elemen...]
    reduce_sum x6 -> x5, other arithmetic: 22.3 us -> 7.16 us  [the longest x3 3.03 us: plane_body(): jnp.sum(rows, 0) / size]
  transfers between devices with their start and end apart: 59 -> 58, of which waited for: 33 -> 33; matrix products, arithmetic and copies ran while one was open for 25% -> 12% of each run, Pallas kernels for 0% -> 11%
where the time goes in v3:
time: 748 us; the launch traced here: 736 us
  waiting for transfers between devices  390 us (52%)
  Pallas kernels  130 us (17%)
  other arithmetic  80.7 us (11%)
  starting transfers between devices  48.1 us (6%)
  local copies, waits for them, and re-layouts  38.3 us (5%)
  matrix products  32.8 us (4%)
  between operations  15.9 us (2%)
    ppermute x18, waiting for transfers between devices, around(): lax.ppermute(value, 'tp', [(i, (i + by) % size) for i in range(size)])  139 us
    ppermute x35, waiting for transfers between devices, send(): return lax.ppermute(value, *LINKS[link])  111 us
    psum x1, waiting for transfers between devices, plane_body(): ffn_out = lax.psum(ffn_out, 'tp')  87.1 us
    all_gather x2, waiting for transfers between devices, gather(): return lax.all_gather(shard, ('fsdp', 'ctx'), axis=0, tiled=True)  52.7 us
    pallas_call x5, Pallas kernels, weight_grad(): pl.pallas_call(kernel, grid_spec=pltpu.PrefetchScalarGridSpec(num_scalar_...  46.1 us
    ppermute x35, starting transfers between devices, send(): return lax.ppermute(value, *LINKS[link])  31.3 us
    pallas_call x3, Pallas kernels, rowwise(): pl.pallas_call(kernel, grid=(count // block,), in_specs=[by_row] * len(ro...  25.1 us
    pallas_call x1, Pallas kernels, ffn_hidden(): pl.pallas_call(kernel, grid=(units // cut,), in_specs=[pl.BlockSpec((coun...  17.4 us
  transfers between devices with their start and end apart: 58, of which 33 were waited for; matrix products, arithmetic and copies ran while one was open for 12% of the time, Pallas kernels for 11%

profile of v3, /device:TPU:0, one launch (start us, length us, event | category | flops | bytes accessed | tf_op | source)
XLA Modules:
  0.0 735.8 jit_solution(5323521363253317488)
XLA Ops:
  22.5 39.6 %all-gather.3.cloned.1.call-done = bf16[2304,1536]{1,0:T(8,128)(2,1)} async-done(((bf16[288,1536]{1,0:T(8,128)(2,1)}), bf16[2304,1536]{1,0:T(8,128)(2,1)}) %all-gather.3.cloned.1.call-update) | async-done | bytes 7077904 | tf_op jit(solution)/shard_map/all_gather | solution.py:420
  73.3 14.2 %collective-permute-done = bf16[1,512,512]{2,1,0:T(8,128)(2,1)S(1)} collective-permute-done((bf16[1,512,512]{2,1,0:T(8,128)(2,1)S(1)}, bf16[1,512,512]{2,1,0:T(8,128)(2,1)S(1)}, u32[]{:S(2)}, u32[]{:S(2)}) %collective-permute-start) | collective-permute-done | bytes 524320 | tf_op jit(solution)/shard_map/ppermute | solution.py:66
  91.7 17.9 %collective-permute-done.2 = bf16[1,512,512]{2,1,0:T(8,128)(2,1)} collective-permute-done((bf16[1,512,512]{2,1,0:T(8,128)(2,1)S(1)}, bf16[1,512,512]{2,1,0:T(8,128)(2,1)}, u32[]{:S(2)}, u32[]{:S(2)}) %collective-permute-start.2) | collective-permute-done | bytes 524320 | tf_op jit(solution)/shard_map/ppermute | solution.py:66
  125.7 13.9 %collective-permute-done.3 = bf16[128,2304]{1,0:T(8,128)(2,1)} collective-permute-done((bf16[128,2304]{1,0:T(8,128)(2,1)}, bf16[128,2304]{1,0:T(8,128)(2,1)}, u32[]{:S(2)}, u32[]{:S(2)}) %collective-permute-start.3) | collective-permute-done | bytes 589856 | tf_op jit(solution)/shard_map/ppermute | solution.py:71
  141.6 14.5 %collective-permute-done.4 = bf16[128,2304]{1,0:T(8,128)(2,1)} collective-permute-done((bf16[128,2304]{1,0:T(8,128)(2,1)}, bf16[128,2304]{1,0:T(8,128)(2,1)}, u32[]{:S(2)}, u32[]{:S(2)}) %collective-permute-start.4) | collective-permute-done | bytes 589856 | tf_op jit(solution)/shard_map/ppermute | solution.py:71
  158.4 13.5 %collective-permute-done.5 = bf16[128,2304]{1,0:T(8,128)(2,1)} collective-permute-done((bf16[128,2304]{1,0:T(8,128)(2,1)}, bf16[128,2304]{1,0:T(8,128)(2,1)}, u32[]{:S(2)}, u32[]{:S(2)}) %collective-permute-start.5) | collective-permute-done | bytes 589856 | tf_op jit(solution)/shard_map/ppermute | solution.py:71
  173.4 13.3 %collective-permute-done.6 = bf16[128,2304]{1,0:T(8,128)(2,1)} collective-permute-done((bf16[128,2304]{1,0:T(8,128)(2,1)S(1)}, bf16[128,2304]{1,0:T(8,128)(2,1)}, u32[]{:S(2)}, u32[]{:S(2)}) %collective-permute-start.6) | collective-permute-done | bytes 589856 | tf_op jit(solution)/shard_map/ppermute | solution.py:71
  190.3 10.4 %collective-permute-done.7 = bf16[128,2304]{1,0:T(8,128)(2,1)} collective-permute-done((bf16[128,2304]{1,0:T(8,128)(2,1)}, bf16[128,2304]{1,0:T(8,128)(2,1)}, u32[]{:S(2)}, u32[]{:S(2)}) %collective-permute-start.7) | collective-permute-done | bytes 589856 | tf_op jit(solution)/shard_map/ppermute | solution.py:71
  202.9 9.7 %collective-permute-done.8 = bf16[128,2304]{1,0:T(8,128)(2,1)S(1)} collective-permute-done((bf16[128,2304]{1,0:T(8,128)(2,1)}, bf16[128,2304]{1,0:T(8,128)(2,1)S(1)}, u32[]{:S(2)}, u32[]{:S(2)}) %collective-permute-start.8) | collective-permute-done | bytes 589856 | tf_op jit(solution)/shard_map/ppermute | solution.py:71
  214.1 6.2 shard_map.237
  220.3 13.1 %all-gather.5.cloned.1.call-done.gate_w.up_w.w_ref = bf16[2304,6912]{1,0:T(8,128)(2,1)} async-done(((bf16[288,6912]{1,0:T(8,128)(2,1)}), bf16[2304,6912]{1,0:T(8,128)(2,1)}) %all-gather.5.cloned.1.call-update) | async-done | bytes 31850512 | tf_op jit(solution)/shard_map/all_gather | solution.py:420
  233.4 17.4 %shard_map.238 = (f32[512,2304]{1,0:T(8,128)}, f32[512,2304]{1,0:T(8,128)}, bf16[512,2304]{1,0:T(8,128)(2,1)}) custom-call(bf16[512,2304]{1,0:T(8,128)(2,1)} %get-tuple-element.149.x_ref.near_ref, bf16[2304,6912]{1,0:T(8,128)(2,1)} %all-gather.5.cloned.1.call-done.gate_w.up_w.w_ref, bf16[2304,6912]{1,0:T(8,128)(2,1)} %all-gather.5.cloned.1.call-done.gate_w.up_w.w_ref), custom_call_target="tpu_custom_call" | custom-call | flops 10871635968 | bytes 33030144 | tf_op jit(solution)/shard_map/pallas_call | solution.py:203
  250.8 10.0 %shard_map.239 = bf16[512,2304]{1,0:T(8,128)(2,1)} custom-call(bf16[512,2304]{1,0:T(8,128)(2,1)} %get-tuple-element.147.x_ref.cols_ref, bf16[2304,6912]{1,0:T(8,128)(2,1)} %all-gather.5.cloned.1.call-done.gate_w.up_w.w_ref), custom_call_target="tpu_custom_call" | custom-call | flops 5435817984 | bytes 10616832 | tf_op jit(solution)/shard_map/pallas_call | solution.py:234
  269.7 87.1 %all-reduce.2.cloned.1.call-done.refs_0_ = bf16[512,2304]{1,0:T(8,128)(2,1)} async-done(((bf16[512,2304]{1,0:T(8,128)(2,1)}), bf16[512,2304]{1,0:T(8,128)(2,1)}) %all-reduce.2.cloned.1.call-update) | async-done | bytes 2359312 | tf_op jit(solution)/shard_map/psum | solution.py:482
  356.8 8.3 %shard_map.240 = (bf16[512,2304]{1,0:T(8,128)(2,1)}, bf16[512,2304]{1,0:T(8,128)(2,1)}, f32[8,2304]{1,0:T(8,128)}) custom-call(bf16[512,2304]{1,0:T(8,128)(2,1)} %all-reduce.2.cloned.1.call-done.refs_0_, f32[512,2304]{1,0:T(8,128)} %get-tuple-element.153.refs_1_, bf16[512,2304]{1,0:T(8,128)(2,1)} %bitcast_select_fusion.1.refs_2_.refs_3_, f32[1,2304]{1,0:T(1,128)} %add.373.refs_3_), custom_call_target="tpu_custom_call" | custom-call | flops 23592960 | bytes 18874368 | tf_op jit(solution)/shard_map/pallas_call | solution.py:164
  366.6 14.4 %shard_map.241 = (bf16[512,2304]{1,0:T(8,128)(2,1)}, bf16[512,2304]{1,0:T(8,128)(2,1)}) custom-call(bf16[512,2304]{1,0:T(8,128)(2,1)} %get-tuple-element.156.d_ref.near_ref, bf16[2304,6912]{1,0:T(8,128)(2,1)} %all-gather.5.cloned.1.call-done.gate_w.up_w.w_ref, f32[512,2304]{1,0:T(8,128)} %get-tuple-element.157.gate_ref, f32[512,2304]{1,0:T(8,128)} %get-tuple-element.158.up_ref), custom_call_target="tpu_custom_call" | custom-call | flops 5435817984 | bytes 24772608 | tf_op jit(solution)/shard_map/pallas_call | solution.py:262
  381.0 17.1 %shard_map.242 = bf16[512,2304]{1,0:T(8,128)(2,1)} custom-call(bf16[512,2304]{1,0:T(8,128)(2,1)} %get-tuple-element.167.dgate_ref.cols_ref, bf16[512,2304]{1,0:T(8,128)(2,1)} %get-tuple-element.174.dup_ref.cols_ref, bf16[2304,6912]{1,0:T(8,128)(2,1)} %all-gather.5.cloned.1.call-done.gate_w.up_w.w_ref, ...), custom_call_target="tpu_custom_call" | custom-call | flops 10871635968 | bytes 21233664 | tf_op jit(solution)/shard_map/pallas_call | solution.py:293
  401.7 11.3 %shard_map.243 = (bf16[576,2304]{1,0:T(8,128)(2,1)}, bf16[288,2304]{1,0:T(8,128)(2,1)}, bf16[288,2304]{1,0:T(8,128)(2,1)}) custom-call(s32[2]{0:T(128)} %pad_add_fusion.1.place_ref, bf16[512,2304]{1,0:T(8,128)(2,1)} %get-tuple-element.156.d_ref.near_ref, bf16[512,1152]{1,0:T(8,128)(2,1)} %copy-done.57, bf16[512,2304]{1,0:T(8,128)(2,1)} %get-tuple-element.147.x_ref.cols_ref, ...), custom_call_target="tpu_custom_call" | custom-call | flops 5435817984 | bytes 12386304 | tf_op jit(solution)/shard_map/pallas_call | solution.py:339
  420.1 11.2 %shard_map.244 = (bf16[576,2304]{1,0:T(8,128)(2,1)}, bf16[288,2304]{1,0:T(8,128)(2,1)}, bf16[288,2304]{1,0:T(8,128)(2,1)}) custom-call(s32[2]{0:T(128)} %pad_add_fusion.1.place_ref, bf16[512,2304]{1,0:T(8,128)(2,1)} %get-tuple-element.149.x_ref.near_ref, bf16[512,1152]{1,0:T(8,128)(2,1)} %collective-permute-done.11.far_ref, ...), custom_call_target="tpu_custom_call" | custom-call | flops 5435817984 | bytes 12386304 | tf_op jit(solution)/shard_map/pallas_call | solution.py:339
  440.0 11.2 %shard_map.245 = (bf16[576,2304]{1,0:T(8,128)(2,1)}, bf16[288,2304]{1,0:T(8,128)(2,1)}, bf16[288,2304]{1,0:T(8,128)(2,1)}) custom-call(s32[2]{0:T(128)} %pad_add_fusion.1.place_ref, bf16[512,2304]{1,0:T(8,128)(2,1)} %get-tuple-element.149.x_ref.near_ref, bf16[512,1152]{1,0:T(8,128)(2,1)} %collective-permute-done.11.far_ref, ...), custom_call_target="tpu_custom_call" | custom-call | flops 5435817984 | bytes 12386304 | tf_op jit(solution)/shard_map/pallas_call | solution.py:339
  453.1 13.9 %collective-permute-done.20 = bf16[288,2304]{1,0:T(8,128)(2,1)S(1)} collective-permute-done((bf16[288,2304]{1,0:T(8,128)(2,1)}, bf16[288,2304]{1,0:T(8,128)(2,1)S(1)}, u32[]{:S(2)}, u32[]{:S(2)}) %collective-permute-start.20) | collective-permute-done | bytes 1327136 | tf_op jit(solution)/shard_map/ppermute | solution.py:66
  473.9 9.0 %collective-permute-done.22 = bf16[128,2304]{1,0:T(8,128)(2,1)S(1)} collective-permute-done((bf16[128,2304]{1,0:T(8,128)(2,1)S(1)}, bf16[128,2304]{1,0:T(8,128)(2,1)S(1)}, u32[]{:S(2)}, u32[]{:S(2)}) %collective-permute-start.22) | collective-permute-done | bytes 589856 | tf_op jit(solution)/shard_map/ppermute | solution.py:71
  483.2 13.5 %collective-permute-done.23 = bf16[128,2304]{1,0:T(8,128)(2,1)S(1)} collective-permute-done((bf16[128,2304]{1,0:T(8,128)(2,1)S(1)}, bf16[128,2304]{1,0:T(8,128)(2,1)S(1)}, u32[]{:S(2)}, u32[]{:S(2)}) %collective-permute-start.23) | collective-permute-done | bytes 589856 | tf_op jit(solution)/shard_map/ppermute | solution.py:71
  496.8 14.8 %collective-permute-done.26 = bf16[144,2304]{1,0:T(8,128)(2,1)S(1)} collective-permute-done((bf16[144,2304]{1,0:T(8,128)(2,1)S(1)}, bf16[144,2304]{1,0:T(8,128)(2,1)S(1)}, u32[]{:S(2)}, u32[]{:S(2)}) %collective-permute-start.26) | collective-permute-done | bytes 663584 | tf_op jit(solution)/shard_map/ppermute | solution.py:66
  513.7 10.6 %shard_map.246 = (f32[512,2304]{1,0:T(8,128)}, bf16[512,2304]{1,0:T(8,128)(2,1)}, f32[8,2304]{1,0:T(8,128)}, f32[8,2304]{1,0:T(8,128)}) custom-call(bf16[512,2304]{1,0:T(8,128)(2,1)} %copy-done.5, f32[512,2304]{1,0:T(8,128)} %get-tuple-element.153.refs_1_, bf16[512,2304]{1,0:T(8,128)(2,1)} %copy-done.3, ...), custom_call_target="tpu_custom_call" | custom-call | flops 23592960 | bytes 28311552 | tf_op jit(solution)/shard_map/pallas_call | solution.py:164
  575.9 11.2 %collective-permute-done.32 = bf16[512,512]{1,0:T(8,128)(2,1)} collective-permute-done((bf16[512,512]{1,0:T(8,128)(2,1)}, bf16[512,512]{1,0:T(8,128)(2,1)}, u32[]{:S(2)}, u32[]{:S(2)}) %collective-permute-start.32) | collective-permute-done | bytes 524320 | tf_op jit(solution)/shard_map/ppermute | solution.py:66
  601.4 7.4 %shard_map.248 = (bf16[576,1024]{1,0:T(8,128)(2,1)}, bf16[288,1024]{1,0:T(8,128)(2,1)}, bf16[288,1024]{1,0:T(8,128)(2,1)}) custom-call(s32[2]{0:T(128)} %pad_add_fusion.1.place_ref, bf16[512,2304]{1,0:T(8,128)(2,1)} %fusion.8.near_ref, bf16[512,1152]{1,0:T(8,128)(2,1)} %collective-permute-done.12.far_ref, bf16[512,1024]{1,0:T(8,128)(2,1)} %pad_maximum_fusion.5.cols_ref, ...), custom_call_target="tpu_custom_call" | custom-call | flops 2415919104 | bytes 6815744 | tf_op jit(solution)/shard_map/pallas_call | solution.py:339
  620.5 11.3 %collective-permute-done.36 = bf16[128,2304]{1,0:T(8,128)(2,1)S(1)} collective-permute-done((bf16[128,2304]{1,0:T(8,128)(2,1)}, bf16[128,2304]{1,0:T(8,128)(2,1)S(1)}, u32[]{:S(2)}, u32[]{:S(2)}) %collective-permute-start.36) | collective-permute-done | bytes 589856 | tf_op jit(solution)/shard_map/ppermute | solution.py:71
  633.9 15.7 %collective-permute-done.38 = bf16[288,2304]{1,0:T(8,128)(2,1)S(1)} collective-permute-done((bf16[288,2304]{1,0:T(8,128)(2,1)}, bf16[288,2304]{1,0:T(8,128)(2,1)S(1)}, u32[]{:S(2)}, u32[]{:S(2)}) %collective-permute-start.38) | collective-permute-done | bytes 1327136 | tf_op jit(solution)/shard_map/ppermute | solution.py:66
  662.0 8.2 %collective-permute-done.40 = bf16[128,2304]{1,0:T(8,128)(2,1)} collective-permute-done((bf16[128,2304]{1,0:T(8,128)(2,1)S(1)}, bf16[128,2304]{1,0:T(8,128)(2,1)}, u32[]{:S(2)}, u32[]{:S(2)}) %collective-permute-start.40) | collective-permute-done | bytes 589856 | tf_op jit(solution)/shard_map/ppermute | solution.py:71
  677.2 10.6 %collective-permute-done.44 = bf16[288,1024]{1,0:T(8,128)(2,1)} collective-permute-done((bf16[288,1024]{1,0:T(8,128)(2,1)}, bf16[288,1024]{1,0:T(8,128)(2,1)}, u32[]{:S(2)}, u32[]{:S(2)}) %collective-permute-start.44) | collective-permute-done | bytes 589856 | tf_op jit(solution)/shard_map/ppermute | solution.py:66
  722.9 6.0 fusion.39
  (336 shorter events, 233.6 us)
Async XLA Ops:
  7.2 54.9 %all-gather.3.cloned.1.call-start = ((), (), s32[]{:S(2)}) async-start(), calls=%async_computation.2 | async-start | bytes 7962624 | tf_op jit(solution)/shard_map/all_gather | solution.py:420
  15.5 217.9 %all-gather.5.cloned.1.call-start = ((), (), s32[]{:S(2)}) async-start(), calls=%async_computation.3 | async-start | bytes 35831808 | tf_op jit(solution)/shard_map/all_gather | solution.py:420
  62.1 294.7 %all-reduce.2.cloned.1.call-start = ((), (), s32[]{:S(2)}) async-start(), calls=%async_computation.4 | async-start | bytes 4718592 | tf_op jit(solution)/shard_map/psum | solution.py:482
  67.9 19.6 %collective-permute-start = (bf16[1,512,512]{2,1,0:T(8,128)(2,1)S(1)}, bf16[1,512,512]{2,1,0:T(8,128)(2,1)S(1)}, u32[]{:S(2)}, u32[]{:S(2)}) collective-permute-start(bf16[1,512,512]{2,1,0:T(8,128)(2,1)S(1)} %get-tuple-element.310), channel_id=1, source_target_pairs={{0,4},{4,0},{8,12},{12,8},{1,5},{5,1},{9,13},{13,9},{2,6},{6,2},{1... | collective-permute-start | bytes 1572872 | tf_op jit(solution)/shard_map/ppermute | solution.py:66
  69.5 22.2 %collective-permute-start.1 = (bf16[1,512,512]{2,1,0:T(8,128)(2,1)S(1)}, bf16[1,512,512]{2,1,0:T(8,128)(2,1)}, u32[]{:S(2)}, u32[]{:S(2)}) collective-permute-start(bf16[1,512,512]{2,1,0:T(8,128)(2,1)S(1)} %get-tuple-element.310), channel_id=1, source_target_pairs={{0,8},{8,0},{4,12},{12,4},{1,9},{9,1},{5,13},{13,5},{2,10},{10,2},... | collective-permute-start | bytes 1572872 | tf_op jit(solution)/shard_map/ppermute | solution.py:66
  70.0 39.6 %collective-permute-start.2 = (bf16[1,512,512]{2,1,0:T(8,128)(2,1)S(1)}, bf16[1,512,512]{2,1,0:T(8,128)(2,1)}, u32[]{:S(2)}, u32[]{:S(2)}) collective-permute-start(bf16[1,512,512]{2,1,0:T(8,128)(2,1)S(1)} %get-tuple-element.310), channel_id=1, source_target_pairs={{0,12},{12,0},{4,8},{8,4},{1,13},{13,1},{5,9},{9,5},{2,14},{14,2},... | collective-permute-start | bytes 1572872 | tf_op jit(solution)/shard_map/ppermute | solution.py:66
  366.5 31.6 %collective-permute-start.13 = (bf16[512,1152]{1,0:T(8,128)(2,1)S(1)}, bf16[512,1152]{1,0:T(8,128)(2,1)S(1)}, u32[]{:S(2)}, u32[]{:S(2)}) collective-permute-start(bf16[512,1152]{1,0:T(8,128)(2,1)S(1)} %constant_dynamic-slice_fusion.3), channel_id=1, source_target_pairs={{0,16},{16,0},{1,17},{17,1},{2,18},{18,2},{3,19},{19,3},{4,20},{20... | collective-permute-start | bytes 3538952 | tf_op jit(solution)/shard_map/ppermute | solution.py:66
  398.1 20.7 %collective-permute-start.15 = (bf16[512,2304]{1,0:T(8,128)(2,1)S(1)}, bf16[512,2304]{1,0:T(8,128)(2,1)}, u32[]{:S(2)}, u32[]{:S(2)}) collective-permute-start(bf16[512,2304]{1,0:T(8,128)(2,1)S(1)} %copy-done.16), channel_id=1, source_target_pairs={{0,16},{16,0},{1,17},{17,1},{2,18},{18,2},{3,19},{19,3},{4,20},{20... | collective-permute-start | bytes 7077896 | tf_op jit(solution)/shard_map/ppermute | solution.py:66
  398.7 32.6 %collective-permute-start.17 = (bf16[512,2304]{1,0:T(8,128)(2,1)S(1)}, bf16[512,2304]{1,0:T(8,128)(2,1)}, u32[]{:S(2)}, u32[]{:S(2)}) collective-permute-start(bf16[512,2304]{1,0:T(8,128)(2,1)S(1)} %copy-done.15), channel_id=1, source_target_pairs={{0,16},{16,0},{1,17},{17,1},{2,18},{18,2},{3,19},{19,3},{4,20},{20... | collective-permute-start | bytes 7077896 | tf_op jit(solution)/shard_map/ppermute | solution.py:66
  400.7 18.2 %collective-permute-start.14 = (bf16[128,2304]{1,0:T(8,128)(2,1)}, bf16[128,2304]{1,0:T(8,128)(2,1)}, u32[]{:S(2)}, u32[]{:S(2)}) collective-permute-start(bf16[128,2304]{1,0:T(8,128)(2,1)} %constant_dynamic-slice_fusion.2), channel_id=1, source_target_pairs={{0,1},{1,2},{2,3},{3,0},{4,5},{5,6},{6,7},{7,4},{8,9},{9,10},{10,1... | collective-permute-start | bytes 1769480 | tf_op jit(solution)/shard_map/ppermute | solution.py:71
  420.0 16.7 %collective-permute-start.16 = (bf16[128,2304]{1,0:T(8,128)(2,1)S(1)}, bf16[128,2304]{1,0:T(8,128)(2,1)S(1)}, u32[]{:S(2)}, u32[]{:S(2)}) collective-permute-start(bf16[128,2304]{1,0:T(8,128)(2,1)S(1)} %add_convert_fusion.11), channel_id=1, source_target_pairs={{0,1},{1,2},{2,3},{3,0},{4,5},{5,6},{6,7},{7,4},{8,9},{9,10},{10,1... | collective-permute-start | bytes 1769480 | tf_op jit(solution)/shard_map/ppermute | solution.py:71
  436.9 15.8 %collective-permute-start.18 = (bf16[128,2304]{1,0:T(8,128)(2,1)S(1)}, bf16[128,2304]{1,0:T(8,128)(2,1)S(1)}, u32[]{:S(2)}, u32[]{:S(2)}) collective-permute-start(bf16[128,2304]{1,0:T(8,128)(2,1)S(1)} %add_convert_fusion.10), channel_id=1, source_target_pairs={{0,1},{1,2},{2,3},{3,0},{4,5},{5,6},{6,7},{7,4},{8,9},{9,10},{10,1... | collective-permute-start | bytes 1769480 | tf_op jit(solution)/shard_map/ppermute | solution.py:71
  437.0 30.1 %collective-permute-start.20 = (bf16[288,2304]{1,0:T(8,128)(2,1)}, bf16[288,2304]{1,0:T(8,128)(2,1)S(1)}, u32[]{:S(2)}, u32[]{:S(2)}) collective-permute-start(bf16[288,2304]{1,0:T(8,128)(2,1)} %get-tuple-element.181), channel_id=1, source_target_pairs={{0,4},{4,0},{8,12},{12,8},{1,5},{5,1},{9,13},{13,9},{2,6},{6,2},{1... | collective-permute-start | bytes 3981320 | tf_op jit(solution)/shard_map/ppermute | solution.py:66
  438.5 29.8 %collective-permute-start.21 = (bf16[288,2304]{1,0:T(8,128)(2,1)}, bf16[288,2304]{1,0:T(8,128)(2,1)}, u32[]{:S(2)}, u32[]{:S(2)}) collective-permute-start(bf16[288,2304]{1,0:T(8,128)(2,1)} %get-tuple-element.182), channel_id=1, source_target_pairs={{0,8},{8,0},{4,12},{12,4},{1,9},{9,1},{5,13},{13,5},{2,10},{10,2},... | collective-permute-start | bytes 3981320 | tf_op jit(solution)/shard_map/ppermute | solution.py:66
  468.3 43.2 %collective-permute-start.24 = (bf16[288,2304]{1,0:T(8,128)(2,1)}, bf16[288,2304]{1,0:T(8,128)(2,1)S(1)}, u32[]{:S(2)}, u32[]{:S(2)}) collective-permute-start(bf16[288,2304]{1,0:T(8,128)(2,1)} %get-tuple-element.187), channel_id=1, source_target_pairs={{0,4},{4,0},{8,12},{12,8},{1,5},{5,1},{9,13},{13,9},{2,6},{6,2},{1... | collective-permute-start | bytes 3981320 | tf_op jit(solution)/shard_map/ppermute | solution.py:66
  469.4 44.2 %collective-permute-start.25 = (bf16[288,2304]{1,0:T(8,128)(2,1)S(1)}, bf16[288,2304]{1,0:T(8,128)(2,1)}, u32[]{:S(2)}, u32[]{:S(2)}) collective-permute-start(bf16[288,2304]{1,0:T(8,128)(2,1)S(1)} %copy-done.56), channel_id=1, source_target_pairs={{0,8},{8,0},{4,12},{12,4},{1,9},{9,1},{5,13},{13,5},{2,10},{10,2},... | collective-permute-start | bytes 3981320 | tf_op jit(solution)/shard_map/ppermute | solution.py:66
  472.4 39.2 %collective-permute-start.26 = (bf16[144,2304]{1,0:T(8,128)(2,1)S(1)}, bf16[144,2304]{1,0:T(8,128)(2,1)S(1)}, u32[]{:S(2)}, u32[]{:S(2)}) collective-permute-start(bf16[144,2304]{1,0:T(8,128)(2,1)S(1)} %get-tuple-element.294), channel_id=1, source_target_pairs={{0,8},{8,0},{4,12},{12,4},{1,9},{9,1},{5,13},{13,5},{2,10},{10,2},... | collective-permute-start | bytes 1990664 | tf_op jit(solution)/shard_map/ppermute | solution.py:66
  473.0 38.6 %collective-permute-start.27 = (bf16[144,2304]{1,0:T(8,128)(2,1)S(1)}, bf16[144,2304]{1,0:T(8,128)(2,1)S(1)}, u32[]{:S(2)}, u32[]{:S(2)}) collective-permute-start(bf16[144,2304]{1,0:T(8,128)(2,1)S(1)} %get-tuple-element.293), channel_id=1, source_target_pairs={{0,4},{4,0},{8,12},{12,8},{1,5},{5,1},{9,13},{13,9},{2,6},{6,2},{1... | collective-permute-start | bytes 1990664 | tf_op jit(solution)/shard_map/ppermute | solution.py:66
  562.1 25.0 %collective-permute-start.32 = (bf16[512,512]{1,0:T(8,128)(2,1)}, bf16[512,512]{1,0:T(8,128)(2,1)}, u32[]{:S(2)}, u32[]{:S(2)}) collective-permute-start(bf16[512,512]{1,0:T(8,128)(2,1)} %pad_maximum_fusion.9), channel_id=1, source_target_pairs={{0,8},{8,0},{4,12},{12,4},{1,9},{9,1},{5,13},{13,5},{2,10},{10,2},... | collective-permute-start | bytes 1572872 | tf_op jit(solution)/shard_map/ppermute | solution.py:66
  562.6 24.5 %collective-permute-start.33 = (bf16[512,512]{1,0:T(8,128)(2,1)}, bf16[512,512]{1,0:T(8,128)(2,1)}, u32[]{:S(2)}, u32[]{:S(2)}) collective-permute-start(bf16[512,512]{1,0:T(8,128)(2,1)} %pad_maximum_fusion.10), channel_id=1, source_target_pairs={{0,12},{12,0},{4,8},{8,4},{1,13},{13,1},{5,9},{9,5},{2,14},{14,2},... | collective-permute-start | bytes 1572872 | tf_op jit(solution)/shard_map/ppermute | solution.py:66
  595.4 17.6 %collective-permute-start.34 = (bf16[128,2304]{1,0:T(8,128)(2,1)S(1)}, bf16[128,2304]{1,0:T(8,128)(2,1)S(1)}, u32[]{:S(2)}, u32[]{:S(2)}) collective-permute-start(bf16[128,2304]{1,0:T(8,128)(2,1)S(1)} %constant_dynamic-slice_fusion), channel_id=1, source_target_pairs={{0,1},{1,2},{2,3},{3,0},{4,5},{5,6},{6,7},{7,4},{8,9},{9,10},{10,1... | collective-permute-start | bytes 1769480 | tf_op jit(solution)/shard_map/ppermute | solution.py:71
  614.9 16.9 %collective-permute-start.36 = (bf16[128,2304]{1,0:T(8,128)(2,1)}, bf16[128,2304]{1,0:T(8,128)(2,1)S(1)}, u32[]{:S(2)}, u32[]{:S(2)}) collective-permute-start(bf16[128,2304]{1,0:T(8,128)(2,1)} %add_convert_fusion.8), channel_id=1, source_target_pairs={{0,1},{1,2},{2,3},{3,0},{4,5},{5,6},{6,7},{7,4},{8,9},{9,10},{10,1... | collective-permute-start | bytes 1769480 | tf_op jit(solution)/shard_map/ppermute | solution.py:71
  618.5 31.0 %collective-permute-start.38 = (bf16[288,2304]{1,0:T(8,128)(2,1)}, bf16[288,2304]{1,0:T(8,128)(2,1)S(1)}, u32[]{:S(2)}, u32[]{:S(2)}) collective-permute-start(bf16[288,2304]{1,0:T(8,128)(2,1)} %get-tuple-element.234), channel_id=1, source_target_pairs={{0,4},{4,0},{8,12},{12,8},{1,5},{5,1},{9,13},{13,9},{2,6},{6,2},{1... | collective-permute-start | bytes 3981320 | tf_op jit(solution)/shard_map/ppermute | solution.py:66
  619.9 30.7 %collective-permute-start.39 = (bf16[288,2304]{1,0:T(8,128)(2,1)}, bf16[288,2304]{1,0:T(8,128)(2,1)S(1)}, u32[]{:S(2)}, u32[]{:S(2)}) collective-permute-start(bf16[288,2304]{1,0:T(8,128)(2,1)} %get-tuple-element.235), channel_id=1, source_target_pairs={{0,8},{8,0},{4,12},{12,4},{1,9},{9,1},{5,13},{13,5},{2,10},{10,2},... | collective-permute-start | bytes 3981320 | tf_op jit(solution)/shard_map/ppermute | solution.py:66
  633.8 16.8 %collective-permute-start.37 = (bf16[128,2304]{1,0:T(8,128)(2,1)S(1)}, bf16[128,2304]{1,0:T(8,128)(2,1)S(1)}, u32[]{:S(2)}, u32[]{:S(2)}) collective-permute-start(bf16[128,2304]{1,0:T(8,128)(2,1)S(1)} %add_convert_fusion.7), channel_id=1, source_target_pairs={{0,1},{1,2},{2,3},{3,0},{4,5},{5,6},{6,7},{7,4},{8,9},{9,10},{10,1... | collective-permute-start | bytes 1769480 | tf_op jit(solution)/shard_map/ppermute | solution.py:71
  654.3 15.9 %collective-permute-start.40 = (bf16[128,2304]{1,0:T(8,128)(2,1)S(1)}, bf16[128,2304]{1,0:T(8,128)(2,1)}, u32[]{:S(2)}, u32[]{:S(2)}) collective-permute-start(bf16[128,2304]{1,0:T(8,128)(2,1)S(1)} %get-tuple-element.278), channel_id=1, source_target_pairs={{0,1},{1,2},{2,3},{3,0},{4,5},{5,6},{6,7},{7,4},{8,9},{9,10},{10,1... | collective-permute-start | bytes 1769480 | tf_op jit(solution)/shard_map/ppermute | solution.py:71
  657.9 32.3 %collective-permute-start.42 = (bf16[144,2304]{1,0:T(8,128)(2,1)}, bf16[144,2304]{1,0:T(8,128)(2,1)}, u32[]{:S(2)}, u32[]{:S(2)}) collective-permute-start(bf16[144,2304]{1,0:T(8,128)(2,1)} %get-tuple-element.286), channel_id=1, source_target_pairs={{0,8},{8,0},{4,12},{12,4},{1,9},{9,1},{5,13},{13,5},{2,10},{10,2},... | collective-permute-start | bytes 1990664 | tf_op jit(solution)/shard_map/ppermute | solution.py:66
  658.4 31.7 %collective-permute-start.43 = (bf16[144,2304]{1,0:T(8,128)(2,1)}, bf16[144,2304]{1,0:T(8,128)(2,1)}, u32[]{:S(2)}, u32[]{:S(2)}) collective-permute-start(bf16[144,2304]{1,0:T(8,128)(2,1)} %get-tuple-element.285), channel_id=1, source_target_pairs={{0,4},{4,0},{8,12},{12,8},{1,5},{5,1},{9,13},{13,9},{2,6},{6,2},{1... | collective-permute-start | bytes 1990664 | tf_op jit(solution)/shard_map/ppermute | solution.py:66
  659.6 28.1 %collective-permute-start.44 = (bf16[288,1024]{1,0:T(8,128)(2,1)}, bf16[288,1024]{1,0:T(8,128)(2,1)}, u32[]{:S(2)}, u32[]{:S(2)}) collective-permute-start(bf16[288,1024]{1,0:T(8,128)(2,1)} %get-tuple-element.244), channel_id=1, source_target_pairs={{0,4},{4,0},{8,12},{12,8},{1,5},{5,1},{9,13},{13,9},{2,6},{6,2},{1... | collective-permute-start | bytes 1769480 | tf_op jit(solution)/shard_map/ppermute | solution.py:66
  660.5 28.8 %collective-permute-start.45 = (bf16[288,1024]{1,0:T(8,128)(2,1)}, bf16[288,1024]{1,0:T(8,128)(2,1)}, u32[]{:S(2)}, u32[]{:S(2)}) collective-permute-start(bf16[288,1024]{1,0:T(8,128)(2,1)} %get-tuple-element.245), channel_id=1, source_target_pairs={{0,8},{8,0},{4,12},{12,4},{1,9},{9,1},{5,13},{13,5},{2,10},{10,2},... | collective-permute-start | bytes 1769480 | tf_op jit(solution)/shard_map/ppermute | solution.py:66
  670.2 20.0 %collective-permute-start.41 = (bf16[128,2304]{1,0:T(8,128)(2,1)}, bf16[128,2304]{1,0:T(8,128)(2,1)}, u32[]{:S(2)}, u32[]{:S(2)}) collective-permute-start(bf16[128,2304]{1,0:T(8,128)(2,1)} %collective-permute-done.40), channel_id=1, source_target_pairs={{0,1},{1,2},{2,3},{3,0},{4,5},{5,6},{6,7},{7,4},{8,9},{9,10},{10,1... | collective-permute-start | bytes 1769480 | tf_op jit(solution)/shard_map/ppermute | solution.py:71
  670.2 40.4 %all-to-all-start.1 = ((f32[32,4,288]{2,1,0:T(4,128)}), f32[32,4,288]{2,1,0:T(4,128)}, u32[]{:S(2)}, u32[]{:S(2)}) async-start(f32[32,4,288]{2,1,0:T(4,128)} %bitcast.167), calls=%async_computation.1 | async-start | bytes 393216 | tf_op jit(solution)/shard_map/all_to_all | solution.py:582
  (86 other events, 822.4 us)
Sparse Core Ops, SparseCore 0:
  10.5 51.5 all-gather.2
  64.0 169.3 all-gather.4
  261.1 95.6 all-reduce.1

commit v4 on v3

--- a/solution.py
+++ b/solution.py
@@ -78,51 +78,61 @@
 
 class Scatter:
     def __init__(self, blocks):
-        self.kept, to_x, to_y = blocks
-        self.half = to_x.shape[0] // 2
-        self.first = (send("x", to_x), send("y", to_y))
-
-    def second(self):
-        half, (from_x, from_y) = self.half, self.first
-        x_low, y_top = self.kept[2 * half : 3 * half], self.kept[3 * half :]
+        self.blocks = blocks
+        self.half = blocks[1].shape[0]
+
+    def diagonal(self):
+        self.first = (send("x", self.blocks[2]), send("y", self.blocks[3]))
+
+    def direct(self):
+        self.middle = (send("x", self.blocks[1]), send("y", self.blocks[4]))
+
+    def sums(self):
+        half, kept, (d_top, d_low) = self.half, self.blocks[0], self.first
+        x_low, y_top = kept[2 * half : 3 * half], kept[3 * half :]
         self.last = (
-            send("y", (y_top.astype(F32) + from_x[half:].astype(F32)).astype(BF)),
-            send("x", (x_low.astype(F32) + from_y[:half].astype(F32)).astype(BF)),
+            send("x", (x_low.astype(F32) + d_low.astype(F32)).astype(BF)),
+            send("y", (y_top.astype(F32) + d_top.astype(F32)).astype(BF)),
         )
 
     def result(self):
-        half, (from_x, from_y), (y_top, x_low) = self.half, self.first, self.last
-        kept = self.kept
-        top = kept[:half].astype(F32) + from_x[:half].astype(F32) + y_top.astype(F32)
-        low = kept[half : 2 * half].astype(F32) + from_y[half:].astype(F32) + x_low.astype(F32)
+        half, kept = self.half, self.blocks[0]
+        (x_top, y_low), (x_low, y_top) = self.middle, self.last
+        top = kept[:half].astype(F32) + x_top.astype(F32) + y_top.astype(F32)
+        low = kept[half : 2 * half].astype(F32) + y_low.astype(F32) + x_low.astype(F32)
         return jnp.concatenate([top, low], 0)
 
 
 class Ring:
-    def __init__(self, value):
-        self.value, self.step = value, 0
+    def __init__(self, value, parts=1):
+        self.value, self.step, self.parts = value, 0, parts
         self.size, self.me = lax.axis_size("tp"), lax.axis_index("tp")
-        self.rows = value.shape[0] // self.size
+        self.rows = value.shape[0] // (parts * self.size)
         self.whole = jnp.zeros_like(value)
-        self.going = around(self.block(self.me - 1))
-
-    def block(self, index):
-        start = (index + self.size) % self.size * self.rows
-        return lax.dynamic_slice_in_dim(self.value, start, self.rows, 0)
-
-    def put(self):
-        index = (self.me - (self.step - self.size + 1) + self.size) % self.size
-        self.whole = lax.dynamic_update_slice_in_dim(self.whole, self.going, index * self.rows, 0)
+        self.sent = [self.block(part, self.me - 1) for part in range(parts)]
+        self.going = [around(sent) for sent in self.sent]
+
+    def start(self, part, index):
+        return (part * self.size + (index + self.size) % self.size) * self.rows
+
+    def block(self, part, index):
+        return lax.dynamic_slice_in_dim(self.value, self.start(part, index), self.rows, 0)
 
     def go(self):
-        if self.step < self.size - 1:
-            own = self.block(self.me - 2 - self.step)
-            self.going = (self.going.astype(F32) + own.astype(F32)).astype(BF)
         self.step += 1
-        if self.step >= self.size - 1:
-            self.put()
-        if self.step < 2 * self.size - 2:
-            self.going = around(self.going)
+        for part in range(self.parts):
+            going = self.going[part]
+            if self.parts > 1:
+                going, _ = tied(going, self.sent[1 - part])
+            if self.step < self.size:
+                own = self.block(part, self.me - 1 - self.step)
+                going = (going.astype(F32) + own.astype(F32)).astype(BF)
+            if self.step >= self.size - 1:
+                at = self.start(part, self.me - self.step + self.size - 1)
+                self.whole = lax.dynamic_update_slice_in_dim(self.whole, going, at, 0)
+            if self.step < 2 * self.size - 2:
+                self.sent[part] = going
+                self.going[part] = around(going)
 
     def finish(self):
         while self.step < 2 * self.size - 2:
@@ -318,7 +328,7 @@
     def kernel(
         place_ref, near_ref, far_ref, cols_ref, cols_far_ref, *rest
     ):
-        outs, (near_t, far_t, total) = rest[:3], rest[3:]
+        outs, (near_t, far_t, total) = rest[:5], rest[5:]
 
         @pl.when(pl.program_id(0) == 0)
         def _():
@@ -331,11 +341,11 @@
         for index, (k, low) in enumerate(ORDER):
             start = (lax.bitwise_xor(place_ref[1], k) * 2 + low) * half
             block = total[pl.ds(pl.multiple_of(start, 16), half), :].astype(BF)
-            out, at = (outs[0], index) if index < 4 else (outs[1 + (index - 4) // 2], index % 2)
+            out, at = (outs[0], index) if index < 4 else (outs[index - 3], 0)
             out[at * half : (at + 1) * half, :] = block
 
     by_cut = pl.BlockSpec((count, cut), lambda j, place: (0, j))
-    sizes = (4 * half, 2 * half, 2 * half)
+    sizes = (4 * half,) + (half,) * 4
     return pl.pallas_call(
         kernel,
         grid_spec=pltpu.PrefetchScalarGridSpec(
@@ -466,7 +476,7 @@
         .reshape(row_count, -1)
     )
     attn = right_dot(attended, out_w).astype(BF)
-    ring = Ring(attn)
+    ring = Ring(attn, 2)
     for _ in range(2 * size - 3):
         ring.go()
     attn = ring.finish()
@@ -479,16 +489,18 @@
     ffn_out, hidden_b, attended, ffn_in, attention_input, cotangent = tied(
         ffn_out, hidden_b, attended, ffn_in, attention_input, cotangent
     )
-    ffn_out = lax.psum(ffn_out, "tp")
+    ring = Ring(ffn_out, 2)
 
     hidden_far, attended_far = send("core", hidden_b), send("core", attended)
     ffn_in_far, attention_input_far = far_half(ffn_in), far_half(attention_input)
     cot = jnp.where(
         valid.reshape(row_count, 1), cotangent.reshape(row_count, width), jnp.zeros((), BF)
     )
-    ffn_out, hidden_far, attended_far, ffn_in_far, attention_input_far, cot = tied(
-        ffn_out, hidden_far, attended_far, ffn_in_far, attention_input_far, cot
-    )
+    ring.go()
+    ring.going, hidden_far, attended_far, ffn_in_far, attention_input_far, cot = tied(
+        ring.going, hidden_far, attended_far, ffn_in_far, attention_input_far, cot
+    )
+    ffn_out = ring.finish()
     output, dffn_b, gain_four_rows = rowwise(
         output_rows, [ffn_out, after_attn, cot], [scale_four], [BF, BF], 1
     )
@@ -499,26 +511,30 @@
     dffn_in, dffn_far, dgate_b, dup_b = tied(dffn_in, dffn_far, dgate_b, dup_b)
     ring = Ring(dffn_in)
     dgate_far = send("core", dgate_b)
-    down_part = weight_grad(dffn_b, dffn_far, hidden_b, hidden_far)
-    ring.going, down_part, dgate_far = tied(ring.going, down_part, dgate_far)
-    ring.go()
-    down_s = Scatter(down_part)
+    down_s = Scatter(weight_grad(dffn_b, dffn_far, hidden_b, hidden_far))
+    ring.going, down_s.blocks, dgate_far = tied(ring.going, down_s.blocks, dgate_far)
+    ring.go()
+    down_s.diagonal()
     dup_far = send("core", dup_b)
-    gate_part = weight_grad(ffn_in, ffn_in_far, dgate_b, dgate_far)
-    ring.going, gate_part, dup_far = tied(ring.going, gate_part, dup_far)
-    ring.go()
-    up_part = weight_grad(ffn_in, ffn_in_far, dup_b, dup_far)
-    ring.going, up_part = tied(ring.going, up_part)
-    ring.go()
-    ring.going, down_s.first, gate_part = tied(ring.going, down_s.first, gate_part)
-    ring.go()
-    down_s.second()
-    gate_s = Scatter(gate_part)
-    ring.go()
-    dffn_in, gate_s.first, down_s.last, up_part = tied(
-        ring.finish(), gate_s.first, down_s.last, up_part
-    )
-    gate_s.second()
+    gate_s = Scatter(weight_grad(ffn_in, ffn_in_far, dgate_b, dgate_far))
+    ring.going, gate_s.blocks, dup_far, down_s.first = tied(
+        ring.going, gate_s.blocks, dup_far, down_s.first
+    )
+    ring.go()
+    down_s.direct()
+    up_s = Scatter(weight_grad(ffn_in, ffn_in_far, dup_b, dup_far))
+    ring.going, up_s.blocks, down_s.middle = tied(ring.going, up_s.blocks, down_s.middle)
+    ring.go()
+    down_s.sums()
+    ring.going, down_s.last, gate_s.blocks = tied(ring.going, down_s.last, gate_s.blocks)
+    ring.go()
+    gate_s.diagonal()
+    grad_down = down_s.result().T
+    ring.going, gate_s.first, grad_down = tied(ring.going, gate_s.first, grad_down)
+    ring.go()
+    gate_s.direct()
+    dffn_in, up_s.blocks, gate_s.first = tied(ring.finish(), up_s.blocks, gate_s.first)
+    gate_s.sums()
     dafter, dattn_b, gain_three_rows, gain_two_rows = rowwise(
         residual_back_rows,
         [dffn_in, after_attn, attn, cot],
@@ -527,9 +543,12 @@
         2,
     )
     dattended = plain_dot(dattn_b, out_w).astype(BF).reshape(query_five.shape)
+    dattended, gate_s.middle = tied(dattended, gate_s.middle)
     dprobs = jnp.einsum("stkgd,sukd->skgtu", dattended, value_four, preferred_element_type=F32)
     weighted = jnp.sum(probs * dprobs, -1, keepdims=True)
     draw_b = (probs * (dprobs - weighted) * (1.0 - bent * bent)).astype(BF)
+    draw_b, gate_s.last, up_s.blocks = tied(draw_b, gate_s.last, up_s.blocks)
+    up_s.diagonal()
     dvalue_part = jnp.einsum("skgtu,stkgd->sukd", probs_b, dattended, preferred_element_type=F32)
     dkey_part = (
         jnp.einsum("skgtu,stkgd->sukd", draw_b, query_five, preferred_element_type=F32) * QSCALE
@@ -545,29 +564,33 @@
         for k in range(planes)
     ]
     dattn_far = far_half(dattn_b)
-    dkv, dattn_far, gate_s.last = tied(dkv, dattn_far, gate_s.last)
+    dkv, dattn_far, up_s.first = tied(dkv, dattn_far, up_s.first)
     dkv = [dkv[0], send("x", dkv[1]), send("y", dkv[2]), send("diagonal", dkv[3])]
-    out_part = weight_grad(dattn_b, dattn_far, attended, attended_far)
+    out_s = Scatter(weight_grad(dattn_b, dattn_far, attended, attended_far))
     dquery_b = (
         (jnp.einsum("skgtu,sukd->stkgd", draw_b, key_four, preferred_element_type=F32) * QSCALE)
         .astype(BF)
         .reshape(row_count, -1)
     )
-    grad_down = down_s.result().T
     grad_gate = gate_s.result()
-    dkv, dquery_b, out_part, grad_down, grad_gate, up_part = tied(
-        dkv, dquery_b, out_part, grad_down, grad_gate, up_part
-    )
-    up_s = Scatter(up_part)
+    dkv, dquery_b, out_s.blocks, grad_gate, up_s.blocks = tied(
+        dkv, dquery_b, out_s.blocks, grad_gate, up_s.blocks
+    )
     dkv_b = sum(part.astype(F32) for part in dkv).astype(BF)
     dqkv_b = jnp.concatenate([dquery_b, dkv_b], 1)
     dattn_in = right_dot(dqkv_b, qkv_w)
-    dattn_in, dqkv_b, dafter = tied(dattn_in.astype(BF), dqkv_b, dafter)
+    dattn_in, dqkv_b, dafter, up_s.blocks = tied(
+        dattn_in.astype(BF), dqkv_b, dafter, up_s.blocks
+    )
 
     ring = Ring(dattn_in)
     dqkv_far = send("core", dqkv_b)
+    up_s.direct()
+    qkv_s = Scatter(weight_grad(attention_input, attention_input_far, dqkv_b, dqkv_far))
+    ring.going, qkv_s.blocks, up_s.middle = tied(ring.going, qkv_s.blocks, up_s.middle)
+    ring.go()
+    up_s.sums()
     grad_gain_one = jnp.sum(dattn_in.astype(F32) * normed_one, 0)
-    qkv_part = weight_grad(attention_input, attention_input_far, dqkv_b, dqkv_far)
     grad_gains = jnp.stack(
         [grad_gain_one]
         + [jnp.sum(rows, 0) / size for rows in (gain_two_rows, gain_three_rows, gain_four_rows)]
@@ -575,32 +598,31 @@
     grad_gains = grad_gains.reshape(4, 2 * planes, 1, -1).transpose(1, 2, 0, 3)
     grad_gains = jnp.broadcast_to(grad_gains, (2 * planes, size) + grad_gains.shape[2:])
     grad_gains = grad_gains.reshape((-1,) + grad_gains.shape[2:])
-    ring.going, qkv_part = tied(ring.going, qkv_part)
-    ring.go()
-    ring.going, grad_gains = tied(ring.going, grad_gains)
+    ring.going, grad_gains, up_s.last = tied(ring.going, grad_gains, up_s.last)
     ring.go()
     grad_gains = lax.all_to_all(grad_gains, ("fsdp", "ctx", "tp"), 0, 0, tiled=True)
-    ring.going, up_s.first = tied(ring.going, up_s.first)
-    up_s.second()
-    qkv_s = Scatter(qkv_part)
-    ring.go()
-    ring.going, out_part = tied(ring.going, out_part)
-    ring.go()
-    ring.going, up_s.last, qkv_s.first = tied(ring.going, up_s.last, qkv_s.first)
-    qkv_s.second()
-    out_s = Scatter(out_part)
-    ring.go()
+    qkv_s.diagonal()
+    qkv_s.direct()
     grad_up = up_s.result()
-    ring.going, qkv_s.last, out_s.first, grad_up = tied(
-        ring.going, qkv_s.last, out_s.first, grad_up
-    )
-    out_s.second()
+    ring.going, qkv_s.first, qkv_s.middle, grad_up = tied(
+        ring.going, qkv_s.first, qkv_s.middle, grad_up
+    )
+    ring.go()
+    qkv_s.sums()
+    out_s.diagonal()
+    ring.going, qkv_s.last, out_s.first = tied(ring.going, qkv_s.last, out_s.first)
+    ring.go()
+    out_s.direct()
+    out_s.sums()
     grad_qkv = qkv_s.result()
-    dattn_in, out_s.last, grad_gains, grad_qkv = tied(
-        ring.finish(), out_s.last, grad_gains, grad_qkv
-    )
+    ring.going, out_s.middle, out_s.last, grad_qkv = tied(
+        ring.going, out_s.middle, out_s.last, grad_qkv
+    )
+    ring.go()
+    grad_out = out_s.result().T
+    ring.going, grad_out = tied(ring.going, grad_out)
+    dattn_in, grad_gains = tied(ring.finish(), grad_gains)
     grad_gains = jnp.sum(grad_gains, 0)
-    grad_out = out_s.result().T
     dattn_in = dattn_in.astype(F32)
     grad_input = dafter + norm_back(dattn_in * scale_one, normed_one, factor_one)
     grad_input = grad_input.astype(BF)

time: 748 us -> 716 us (0.957)
  waiting for transfers between devices: 390 us -> 354 us
  starting transfers between devices: 48.1 us -> 59.6 us
    psum x1 -> x0, waiting for transfers between devices: 87.1 us -> none  [plane_body(): ffn_out = lax.psum(ffn_out, 'tp')]
    ppermute x18 -> x36, waiting for transfers between devices: 139 us -> 208 us  [around(): lax.ppermute(value, 'tp', [(i, (i + by) % size) for i in range(size)])]
    ppermute x35 -> x45, waiting for transfers between devices: 111 us -> 83.7 us  [send(): return lax.ppermute(value, *LINKS[link])]
    all_gather x2, waiting for transfers between devices: 52.7 us -> 62.4 us  [gather(): return lax.all_gather(shard, ('fsdp', 'ctx'), axis=0, tiled=True)]
    ppermute x35 -> x45, starting transfers between devices: 31.3 us -> 40.3 us  [send(): return lax.ppermute(value, *LINKS[link])]
    convert_element_type x11 -> x17, other arithmetic: 16 us -> 17 us  [the longest x5 8.82 us: sums(): (y_top.astype(F32) + d_top.astype(F32)).astype(BF)]
  transfers between devices with their start and end apart: 58 -> 85, of which waited for: 33 -> 55; matrix products, arithmetic and copies ran while one was open for 12% -> 15% of each run, Pallas kernels for 11% -> 13%
where the time goes in v4:
time: 716 us; the launch traced here: 708 us
  waiting for transfers between devices  354 us (49%)
  Pallas kernels  130 us (18%)
  other arithmetic  74.1 us (10%)
  starting transfers between devices  59.6 us (8%)
  local copies, waits for them, and re-layouts  37.2 us (5%)
  matrix products  36.4 us (5%)
  between operations  16.6 us (2%)
    ppermute x36, waiting for transfers between devices, around(): lax.ppermute(value, 'tp', [(i, (i + by) % size) for i in range(size)])  208 us
    ppermute x45, waiting for transfers between devices, send(): return lax.ppermute(value, *LINKS[link])  83.7 us
    all_gather x2, waiting for transfers between devices, gather(): return lax.all_gather(shard, ('fsdp', 'ctx'), axis=0, tiled=True)  62.4 us
    pallas_call x5, Pallas kernels, weight_grad(): pl.pallas_call(kernel, grid_spec=pltpu.PrefetchScalarGridSpec(num_scalar_...  46.3 us
    ppermute x45, starting transfers between devices, send(): return lax.ppermute(value, *LINKS[link])  40.3 us
    pallas_call x3, Pallas kernels, rowwise(): pl.pallas_call(kernel, grid=(count // block,), in_specs=[by_row] * len(ro...  25 us
    pallas_call x1, Pallas kernels, ffn_hidden(): pl.pallas_call(kernel, grid=(units // cut,), in_specs=[pl.BlockSpec((coun...  17.4 us
    pallas_call x1, Pallas kernels, ffn_input_back(): pl.pallas_call(kernel, grid=(width // cut,), in_specs=[whole, whole, pl.B...  16.9 us
  transfers between devices with their start and end apart: 85, of which 55 were waited for; matrix products, arithmetic and copies ran while one was open for 15% of the time, Pallas kernels for 13%

profile of v4, /device:TPU:0, one launch (start us, length us, event | category | flops | bytes accessed | tf_op | source)
XLA Modules:
  0.0 708.1 jit_solution(3424618724165985348)
XLA Ops:
  22.5 39.6 %all-gather.3.cloned.1.call-done = bf16[2304,1536]{1,0:T(8,128)(2,1)} async-done(((bf16[288,1536]{1,0:T(8,128)(2,1)}), bf16[2304,1536]{1,0:T(8,128)(2,1)}) %all-gather.3.cloned.1.call-update) | async-done | bytes 7077904 | tf_op jit(solution)/shard_map/all_gather | solution.py:430
  73.2 14.2 %collective-permute-done = bf16[1,512,512]{2,1,0:T(8,128)(2,1)S(1)} collective-permute-done((bf16[1,512,512]{2,1,0:T(8,128)(2,1)S(1)}, bf16[1,512,512]{2,1,0:T(8,128)(2,1)S(1)}, u32[]{:S(2)}, u32[]{:S(2)}) %collective-permute-start) | collective-permute-done | bytes 524320 | tf_op jit(solution)/shard_map/ppermute | solution.py:66
  91.6 17.9 %collective-permute-done.2 = bf16[1,512,512]{2,1,0:T(8,128)(2,1)} collective-permute-done((bf16[1,512,512]{2,1,0:T(8,128)(2,1)S(1)}, bf16[1,512,512]{2,1,0:T(8,128)(2,1)}, u32[]{:S(2)}, u32[]{:S(2)}) %collective-permute-start.2) | collective-permute-done | bytes 524320 | tf_op jit(solution)/shard_map/ppermute | solution.py:66
  127.1 9.1 %collective-permute-done.3 = bf16[64,2304]{1,0:T(8,128)(2,1)} collective-permute-done((bf16[64,2304]{1,0:T(8,128)(2,1)}, bf16[64,2304]{1,0:T(8,128)(2,1)}, u32[]{:S(2)}, u32[]{:S(2)}) %collective-permute-start.3) | collective-permute-done | bytes 294944 | tf_op jit(solution)/shard_map/ppermute | solution.py:71
  142.6 6.5 collective-permute-done.4
  175.5 6.3 collective-permute-done.10
  188.0 6.3 collective-permute-done.12
  194.4 8.5 %collective-permute-done.14 = bf16[64,2304]{1,0:T(8,128)(2,1)S(1)} collective-permute-done((bf16[64,2304]{1,0:T(8,128)(2,1)S(1)}, bf16[64,2304]{1,0:T(8,128)(2,1)S(1)}, u32[]{:S(2)}, u32[]{:S(2)}) %collective-permute-start.14) | collective-permute-done | bytes 294944 | tf_op jit(solution)/shard_map/ppermute | solution.py:71
  210.6 22.8 %all-gather.5.cloned.1.call-done.gate_w.up_w.w_ref = bf16[2304,6912]{1,0:T(8,128)(2,1)} async-done(((bf16[288,6912]{1,0:T(8,128)(2,1)}), bf16[2304,6912]{1,0:T(8,128)(2,1)}) %all-gather.5.cloned.1.call-update) | async-done | bytes 31850512 | tf_op jit(solution)/shard_map/all_gather | solution.py:430
  233.4 17.4 %shard_map.238 = (f32[512,2304]{1,0:T(8,128)}, f32[512,2304]{1,0:T(8,128)}, bf16[512,2304]{1,0:T(8,128)(2,1)}) custom-call(bf16[512,2304]{1,0:T(8,128)(2,1)} %get-tuple-element.233.x_ref.near_ref, bf16[2304,6912]{1,0:T(8,128)(2,1)} %all-gather.5.cloned.1.call-done.gate_w.up_w.w_ref, bf16[2304,6912]{1,0:T(8,128)(2,1)} %all-gather.5.cloned.1.call-done.gate_w.up_w.w_ref), custom_call_target="tpu_custom_call" | custom-call | flops 10871635968 | bytes 33030144 | tf_op jit(solution)/shard_map/pallas_call | solution.py:213
  250.8 10.1 %shard_map.239 = bf16[512,2304]{1,0:T(8,128)(2,1)} custom-call(bf16[512,2304]{1,0:T(8,128)(2,1)} %get-tuple-element.231.x_ref.cols_ref, bf16[2304,6912]{1,0:T(8,128)(2,1)} %all-gather.5.cloned.1.call-done.gate_w.up_w.w_ref), custom_call_target="tpu_custom_call" | custom-call | flops 5435817984 | bytes 10616832 | tf_op jit(solution)/shard_map/pallas_call | solution.py:244
  266.5 7.3 %collective-permute-done.15 = bf16[64,2304]{1,0:T(8,128)(2,1)S(1)} collective-permute-done((bf16[64,2304]{1,0:T(8,128)(2,1)S(1)}, bf16[64,2304]{1,0:T(8,128)(2,1)S(1)}, u32[]{:S(2)}, u32[]{:S(2)}) %collective-permute-start.15) | collective-permute-done | bytes 294944 | tf_op jit(solution)/shard_map/ppermute | solution.py:71
  283.2 12.8 %collective-permute-done.18 = bf16[64,2304]{1,0:T(8,128)(2,1)S(1)} collective-permute-done((bf16[64,2304]{1,0:T(8,128)(2,1)S(1)}, bf16[64,2304]{1,0:T(8,128)(2,1)S(1)}, u32[]{:S(2)}, u32[]{:S(2)}) %collective-permute-start.18) | collective-permute-done | bytes 294944 | tf_op jit(solution)/shard_map/ppermute | solution.py:71
  297.5 10.5 %collective-permute-done.23 = bf16[64,2304]{1,0:T(8,128)(2,1)S(1)} collective-permute-done((bf16[64,2304]{1,0:T(8,128)(2,1)S(1)}, bf16[64,2304]{1,0:T(8,128)(2,1)S(1)}, u32[]{:S(2)}, u32[]{:S(2)}) %collective-permute-start.23) | collective-permute-done | bytes 294944 | tf_op jit(solution)/shard_map/ppermute | solution.py:71
  320.9 6.3 collective-permute-done.26
  339.9 9.8 %collective-permute-done.30 = bf16[64,2304]{1,0:T(8,128)(2,1)S(1)} collective-permute-done((bf16[64,2304]{1,0:T(8,128)(2,1)S(1)}, bf16[64,2304]{1,0:T(8,128)(2,1)S(1)}, u32[]{:S(2)}, u32[]{:S(2)}) %collective-permute-start.30) | collective-permute-done | bytes 294944 | tf_op jit(solution)/shard_map/ppermute | solution.py:71
  351.1 8.2 %shard_map.240 = (bf16[512,2304]{1,0:T(8,128)(2,1)}, bf16[512,2304]{1,0:T(8,128)(2,1)}, f32[8,2304]{1,0:T(8,128)}) custom-call(bf16[512,2304]{1,0:T(8,128)(2,1)} %copy-done.10, f32[512,2304]{1,0:T(8,128)} %get-tuple-element.248.refs_1_, bf16[512,2304]{1,0:T(8,128)(2,1)} %bitcast_select_fusion.1.refs_2_.refs_3_, f32[1,2304]{1,0:T(1,128)} %add.588.refs_3_), custom_call_target="tpu_custom_call" | custom-call | flops 23592960 | bytes 18874368 | tf_op jit(solution)/shard_map/pallas_call | solution.py:174
  360.8 14.3 %shard_map.241 = (bf16[512,2304]{1,0:T(8,128)(2,1)}, bf16[512,2304]{1,0:T(8,128)(2,1)}) custom-call(bf16[512,2304]{1,0:T(8,128)(2,1)} %get-tuple-element.251.d_ref.near_ref, bf16[2304,6912]{1,0:T(8,128)(2,1)} %all-gather.5.cloned.1.call-done.gate_w.up_w.w_ref, f32[512,2304]{1,0:T(8,128)} %get-tuple-element.252.gate_ref, f32[512,2304]{1,0:T(8,128)} %get-tuple-element.253.up_ref), custom_call_target="tpu_custom_call" | custom-call | flops 5435817984 | bytes 24772608 | tf_op jit(solution)/shard_map/pallas_call | solution.py:272
  375.1 16.9 %shard_map.242 = bf16[512,2304]{1,0:T(8,128)(2,1)} custom-call(bf16[512,2304]{1,0:T(8,128)(2,1)} %get-tuple-element.264.dgate_ref.cols_ref, bf16[512,2304]{1,0:T(8,128)(2,1)} %get-tuple-element.273.dup_ref.cols_ref, bf16[2304,6912]{1,0:T(8,128)(2,1)} %all-gather.5.cloned.1.call-done.gate_w.up_w.w_ref, ...), custom_call_target="tpu_custom_call" | custom-call | flops 10871635968 | bytes 21233664 | tf_op jit(solution)/shard_map/pallas_call | solution.py:303
  395.4 11.3 %shard_map.243 = (bf16[576,2304]{1,0:T(8,128)(2,1)}, bf16[144,2304]{1,0:T(8,128)(2,1)}, bf16[144,2304]{1,0:T(8,128)(2,1)}, bf16[144,2304]{1,0:T(8,128)(2,1)}, bf16[144,2304]{1,0:T(8,128)(2,1)}) custom-call(s32[2]{0:T(128)} %pad_add_fusion.1.place_ref, bf16[512,2304]{1,0:T(8,128)(2,1)} %get-tuple-element.251.d_ref.near_ref, bf16[512,1152]{1,0:T(8,128)(2,1)} %copy-done.60, ...), custom_call_target="tpu_custom_call" | custom-call | flops 5435817984 | bytes 12386304 | tf_op jit(solution)/shard_map/pallas_call | solution.py:349
  415.9 11.3 %shard_map.244 = (bf16[576,2304]{1,0:T(8,128)(2,1)}, bf16[144,2304]{1,0:T(8,128)(2,1)}, bf16[144,2304]{1,0:T(8,128)(2,1)}, bf16[144,2304]{1,0:T(8,128)(2,1)}, bf16[144,2304]{1,0:T(8,128)(2,1)}) custom-call(s32[2]{0:T(128)} %pad_add_fusion.1.place_ref, bf16[512,2304]{1,0:T(8,128)(2,1)} %get-tuple-element.233.x_ref.near_ref, bf16[512,1152]{1,0:T(8,128)(2,1)} %copy-done.59, ...), custom_call_target="tpu_custom_call" | custom-call | flops 5435817984 | bytes 12386304 | tf_op jit(solution)/shard_map/pallas_call | solution.py:349
  438.6 11.3 %shard_map.245 = (bf16[576,2304]{1,0:T(8,128)(2,1)}, bf16[144,2304]{1,0:T(8,128)(2,1)}, bf16[144,2304]{1,0:T(8,128)(2,1)}, bf16[144,2304]{1,0:T(8,128)(2,1)}, bf16[144,2304]{1,0:T(8,128)(2,1)}) custom-call(s32[2]{0:T(128)} %pad_add_fusion.1.place_ref, bf16[512,2304]{1,0:T(8,128)(2,1)} %get-tuple-element.233.x_ref.near_ref, bf16[512,1152]{1,0:T(8,128)(2,1)} %copy-done.59, ...), custom_call_target="tpu_custom_call" | custom-call | flops 5435817984 | bytes 12386304 | tf_op jit(solution)/shard_map/pallas_call | solution.py:349
  458.7 8.7 %collective-permute-done.41 = bf16[128,2304]{1,0:T(8,128)(2,1)S(1)} collective-permute-done((bf16[128,2304]{1,0:T(8,128)(2,1)}, bf16[128,2304]{1,0:T(8,128)(2,1)S(1)}, u32[]{:S(2)}, u32[]{:S(2)}) %collective-permute-start.41) | collective-permute-done | bytes 589856 | tf_op jit(solution)/shard_map/ppermute | solution.py:71
  475.6 7.0 collective-permute-done.44
  487.2 11.5 %collective-permute-done.47 = bf16[128,2304]{1,0:T(8,128)(2,1)S(1)} collective-permute-done((bf16[128,2304]{1,0:T(8,128)(2,1)S(1)}, bf16[128,2304]{1,0:T(8,128)(2,1)S(1)}, u32[]{:S(2)}, u32[]{:S(2)}) %collective-permute-start.47) | collective-permute-done | bytes 589856 | tf_op jit(solution)/shard_map/ppermute | solution.py:71
  500.3 10.6 %shard_map.246 = (f32[512,2304]{1,0:T(8,128)}, bf16[512,2304]{1,0:T(8,128)(2,1)}, f32[8,2304]{1,0:T(8,128)}, f32[8,2304]{1,0:T(8,128)}) custom-call(bf16[512,2304]{1,0:T(8,128)(2,1)} %copy-done.8, f32[512,2304]{1,0:T(8,128)} %get-tuple-element.248.refs_1_, bf16[512,2304]{1,0:T(8,128)(2,1)} %copy-done.3, ...), custom_call_target="tpu_custom_call" | custom-call | flops 23592960 | bytes 28311552 | tf_op jit(solution)/shard_map/pallas_call | solution.py:174
  546.2 9.8 %collective-permute-done.53 = bf16[144,2304]{1,0:T(8,128)(2,1)} collective-permute-done((bf16[144,2304]{1,0:T(8,128)(2,1)}, bf16[144,2304]{1,0:T(8,128)(2,1)}, u32[]{:S(2)}, u32[]{:S(2)}) %collective-permute-start.53) | collective-permute-done | bytes 663584 | tf_op jit(solution)/shard_map/ppermute | solution.py:66
  572.1 7.0 collective-permute-done.56
  594.8 7.4 %shard_map.248 = (bf16[576,1024]{1,0:T(8,128)(2,1)}, bf16[144,1024]{1,0:T(8,128)(2,1)}, bf16[144,1024]{1,0:T(8,128)(2,1)}, bf16[144,1024]{1,0:T(8,128)(2,1)}, bf16[144,1024]{1,0:T(8,128)(2,1)}) custom-call(s32[2]{0:T(128)} %pad_add_fusion.1.place_ref, bf16[512,2304]{1,0:T(8,128)(2,1)} %fusion.8.near_ref, bf16[512,1152]{1,0:T(8,128)(2,1)} %copy-done.58, ...), custom_call_target="tpu_custom_call" | custom-call | flops 2415919104 | bytes 6815744 | tf_op jit(solution)/shard_map/pallas_call | solution.py:349
  631.7 9.5 %collective-permute-done.65 = bf16[128,2304]{1,0:T(8,128)(2,1)S(1)} collective-permute-done((bf16[128,2304]{1,0:T(8,128)(2,1)S(1)}, bf16[128,2304]{1,0:T(8,128)(2,1)S(1)}, u32[]{:S(2)}, u32[]{:S(2)}) %collective-permute-start.65) | collective-permute-done | bytes 589856 | tf_op jit(solution)/shard_map/ppermute | solution.py:71
  668.1 9.1 %collective-permute-done.75 = bf16[128,2304]{1,0:T(8,128)(2,1)S(1)} collective-permute-done((bf16[128,2304]{1,0:T(8,128)(2,1)}, bf16[128,2304]{1,0:T(8,128)(2,1)S(1)}, u32[]{:S(2)}, u32[]{:S(2)}) %collective-permute-start.75) | collective-permute-done | bytes 589856 | tf_op jit(solution)/shard_map/ppermute | solution.py:71
  680.8 9.8 %collective-permute-done.80 = bf16[128,2304]{1,0:T(8,128)(2,1)S(1)} collective-permute-done((bf16[128,2304]{1,0:T(8,128)(2,1)S(1)}, bf16[128,2304]{1,0:T(8,128)(2,1)S(1)}, u32[]{:S(2)}, u32[]{:S(2)}) %collective-permute-start.80) | collective-permute-done | bytes 589856 | tf_op jit(solution)/shard_map/ppermute | solution.py:71
  (417 shorter events, 322.5 us)
Async XLA Ops:
  7.2 54.9 %all-gather.3.cloned.1.call-start = ((), (), s32[]{:S(2)}) async-start(), calls=%async_computation.2 | async-start | bytes 7962624 | tf_op jit(solution)/shard_map/all_gather | solution.py:430
  15.5 217.9 %all-gather.5.cloned.1.call-start = ((), (), s32[]{:S(2)}) async-start(), calls=%async_computation.3 | async-start | bytes 35831808 | tf_op jit(solution)/shard_map/all_gather | solution.py:430
  67.9 19.6 %collective-permute-start = (bf16[1,512,512]{2,1,0:T(8,128)(2,1)S(1)}, bf16[1,512,512]{2,1,0:T(8,128)(2,1)S(1)}, u32[]{:S(2)}, u32[]{:S(2)}) collective-permute-start(bf16[1,512,512]{2,1,0:T(8,128)(2,1)S(1)} %get-tuple-element.460), channel_id=1, source_target_pairs={{0,4},{4,0},{8,12},{12,8},{1,5},{5,1},{9,13},{13,9},{2,6},{6,2},{1... | collective-permute-start | bytes 1572872 | tf_op jit(solution)/shard_map/ppermute | solution.py:66
  69.4 22.2 %collective-permute-start.1 = (bf16[1,512,512]{2,1,0:T(8,128)(2,1)S(1)}, bf16[1,512,512]{2,1,0:T(8,128)(2,1)}, u32[]{:S(2)}, u32[]{:S(2)}) collective-permute-start(bf16[1,512,512]{2,1,0:T(8,128)(2,1)S(1)} %get-tuple-element.460), channel_id=1, source_target_pairs={{0,8},{8,0},{4,12},{12,4},{1,9},{9,1},{5,13},{13,5},{2,10},{10,2},... | collective-permute-start | bytes 1572872 | tf_op jit(solution)/shard_map/ppermute | solution.py:66
  70.0 39.6 %collective-permute-start.2 = (bf16[1,512,512]{2,1,0:T(8,128)(2,1)S(1)}, bf16[1,512,512]{2,1,0:T(8,128)(2,1)}, u32[]{:S(2)}, u32[]{:S(2)}) collective-permute-start(bf16[1,512,512]{2,1,0:T(8,128)(2,1)S(1)} %get-tuple-element.460), channel_id=1, source_target_pairs={{0,12},{12,0},{4,8},{8,4},{1,13},{13,1},{5,9},{9,5},{2,14},{14,2},... | collective-permute-start | bytes 1572872 | tf_op jit(solution)/shard_map/ppermute | solution.py:66
  265.7 30.3 %collective-permute-start.21 = (bf16[512,1152]{1,0:T(8,128)(2,1)S(1)}, bf16[512,1152]{1,0:T(8,128)(2,1)S(1)}, u32[]{:S(2)}, u32[]{:S(2)}) collective-permute-start(bf16[512,1152]{1,0:T(8,128)(2,1)S(1)} %constant_dynamic-slice_fusion.5), channel_id=1, source_target_pairs={{0,16},{16,0},{1,17},{17,1},{2,18},{18,2},{3,19},{19,3},{4,20},{20... | collective-permute-start | bytes 3538952 | tf_op jit(solution)/shard_map/ppermute | solution.py:66
  265.8 30.2 %collective-permute-start.19 = (bf16[512,2304]{1,0:T(8,128)(2,1)S(1)}, bf16[512,2304]{1,0:T(8,128)(2,1)S(1)}, u32[]{:S(2)}, u32[]{:S(2)}) collective-permute-start(bf16[512,2304]{1,0:T(8,128)(2,1)S(1)} %copy-done.19), channel_id=1, source_target_pairs={{0,16},{16,0},{1,17},{17,1},{2,18},{18,2},{3,19},{19,3},{4,20},{20... | collective-permute-start | bytes 7077896 | tf_op jit(solution)/shard_map/ppermute | solution.py:66
  266.4 29.6 %collective-permute-start.22 = (bf16[512,1152]{1,0:T(8,128)(2,1)S(1)}, bf16[512,1152]{1,0:T(8,128)(2,1)S(1)}, u32[]{:S(2)}, u32[]{:S(2)}) collective-permute-start(bf16[512,1152]{1,0:T(8,128)(2,1)S(1)} %constant_dynamic-slice_fusion.4), channel_id=1, source_target_pairs={{0,16},{16,0},{1,17},{17,1},{2,18},{18,2},{3,19},{19,3},{4,20},{20... | collective-permute-start | bytes 3538952 | tf_op jit(solution)/shard_map/ppermute | solution.py:66
  296.3 18.0 %collective-permute-start.24 = (bf16[64,2304]{1,0:T(8,128)(2,1)S(1)}, bf16[64,2304]{1,0:T(8,128)(2,1)S(1)}, u32[]{:S(2)}, u32[]{:S(2)}) collective-permute-start(bf16[64,2304]{1,0:T(8,128)(2,1)S(1)} %add_convert_fusion.17), channel_id=1, source_target_pairs={{0,1},{1,2},{2,3},{3,0},{4,5},{5,6},{6,7},{7,4},{8,9},{9,10},{10,1... | collective-permute-start | bytes 884744 | tf_op jit(solution)/shard_map/ppermute | solution.py:71
  360.7 31.3 %collective-permute-start.31 = (bf16[512,1152]{1,0:T(8,128)(2,1)S(1)}, bf16[512,1152]{1,0:T(8,128)(2,1)S(1)}, u32[]{:S(2)}, u32[]{:S(2)}) collective-permute-start(bf16[512,1152]{1,0:T(8,128)(2,1)S(1)} %constant_dynamic-slice_fusion.3), channel_id=1, source_target_pairs={{0,16},{16,0},{1,17},{17,1},{2,18},{18,2},{3,19},{19,3},{4,20},{20... | collective-permute-start | bytes 3538952 | tf_op jit(solution)/shard_map/ppermute | solution.py:66
  393.1 19.2 %collective-permute-start.33 = (bf16[512,2304]{1,0:T(8,128)(2,1)}, bf16[512,2304]{1,0:T(8,128)(2,1)}, u32[]{:S(2)}, u32[]{:S(2)}) collective-permute-start(bf16[512,2304]{1,0:T(8,128)(2,1)} %get-tuple-element.264.dgate_ref.cols_ref), channel_id=1, source_target_pairs={{0,16},{16,0},{1,17},{17,1},{2,18},{18,2},{3,19},{19,3},{4,20},{20... | collective-permute-start | bytes 7077896 | tf_op jit(solution)/shard_map/ppermute | solution.py:66
  393.6 33.6 %collective-permute-start.35 = (bf16[512,2304]{1,0:T(8,128)(2,1)}, bf16[512,2304]{1,0:T(8,128)(2,1)}, u32[]{:S(2)}, u32[]{:S(2)}) collective-permute-start(bf16[512,2304]{1,0:T(8,128)(2,1)} %get-tuple-element.273.dup_ref.cols_ref), channel_id=1, source_target_pairs={{0,16},{16,0},{1,17},{17,1},{2,18},{18,2},{3,19},{19,3},{4,20},{20... | collective-permute-start | bytes 7077896 | tf_op jit(solution)/shard_map/ppermute | solution.py:66
  412.3 19.6 %collective-permute-start.36 = (bf16[144,2304]{1,0:T(8,128)(2,1)}, bf16[144,2304]{1,0:T(8,128)(2,1)}, u32[]{:S(2)}, u32[]{:S(2)}) collective-permute-start(bf16[144,2304]{1,0:T(8,128)(2,1)} %get-tuple-element.274), channel_id=1, source_target_pairs={{0,4},{4,0},{8,12},{12,8},{1,5},{5,1},{9,13},{13,9},{2,6},{6,2},{1... | collective-permute-start | bytes 1990664 | tf_op jit(solution)/shard_map/ppermute | solution.py:66
  413.7 18.1 %collective-permute-start.37 = (bf16[144,2304]{1,0:T(8,128)(2,1)}, bf16[144,2304]{1,0:T(8,128)(2,1)}, u32[]{:S(2)}, u32[]{:S(2)}) collective-permute-start(bf16[144,2304]{1,0:T(8,128)(2,1)} %get-tuple-element.275), channel_id=1, source_target_pairs={{0,8},{8,0},{4,12},{12,4},{1,9},{9,1},{5,13},{13,5},{2,10},{10,2},... | collective-permute-start | bytes 1990664 | tf_op jit(solution)/shard_map/ppermute | solution.py:66
  415.4 34.4 %collective-permute-start.39 = (bf16[144,2304]{1,0:T(8,128)(2,1)}, bf16[144,2304]{1,0:T(8,128)(2,1)S(1)}, u32[]{:S(2)}, u32[]{:S(2)}) collective-permute-start(bf16[144,2304]{1,0:T(8,128)(2,1)} %get-tuple-element.283), channel_id=1, source_target_pairs={{0,4},{4,0},{8,12},{12,8},{1,5},{5,1},{9,13},{13,9},{2,6},{6,2},{1... | collective-permute-start | bytes 1990664 | tf_op jit(solution)/shard_map/ppermute | solution.py:66
  427.2 22.7 %collective-permute-start.40 = (bf16[144,2304]{1,0:T(8,128)(2,1)}, bf16[144,2304]{1,0:T(8,128)(2,1)S(1)}, u32[]{:S(2)}, u32[]{:S(2)}) collective-permute-start(bf16[144,2304]{1,0:T(8,128)(2,1)} %get-tuple-element.284), channel_id=1, source_target_pairs={{0,8},{8,0},{4,12},{12,4},{1,9},{9,1},{5,13},{13,5},{2,10},{10,2},... | collective-permute-start | bytes 1990664 | tf_op jit(solution)/shard_map/ppermute | solution.py:66
  436.5 21.0 %collective-permute-start.42 = (bf16[144,2304]{1,0:T(8,128)(2,1)}, bf16[144,2304]{1,0:T(8,128)(2,1)}, u32[]{:S(2)}, u32[]{:S(2)}) collective-permute-start(bf16[144,2304]{1,0:T(8,128)(2,1)} %get-tuple-element.440), channel_id=1, source_target_pairs={{0,4},{4,0},{8,12},{12,8},{1,5},{5,1},{9,13},{13,9},{2,6},{6,2},{1... | collective-permute-start | bytes 1990664 | tf_op jit(solution)/shard_map/ppermute | solution.py:66
  436.9 21.8 %collective-permute-start.43 = (bf16[144,2304]{1,0:T(8,128)(2,1)}, bf16[144,2304]{1,0:T(8,128)(2,1)}, u32[]{:S(2)}, u32[]{:S(2)}) collective-permute-start(bf16[144,2304]{1,0:T(8,128)(2,1)} %get-tuple-element.439), channel_id=1, source_target_pairs={{0,8},{8,0},{4,12},{12,4},{1,9},{9,1},{5,13},{13,5},{2,10},{10,2},... | collective-permute-start | bytes 1990664 | tf_op jit(solution)/shard_map/ppermute | solution.py:66
  467.4 18.1 %collective-permute-start.45 = (bf16[144,2304]{1,0:T(8,128)(2,1)}, bf16[144,2304]{1,0:T(8,128)(2,1)S(1)}, u32[]{:S(2)}, u32[]{:S(2)}) collective-permute-start(bf16[144,2304]{1,0:T(8,128)(2,1)} %get-tuple-element.295), channel_id=1, source_target_pairs={{0,4},{4,0},{8,12},{12,8},{1,5},{5,1},{9,13},{13,9},{2,6},{6,2},{1... | collective-permute-start | bytes 1990664 | tf_op jit(solution)/shard_map/ppermute | solution.py:66
  468.8 18.1 %collective-permute-start.46 = (bf16[144,2304]{1,0:T(8,128)(2,1)}, bf16[144,2304]{1,0:T(8,128)(2,1)S(1)}, u32[]{:S(2)}, u32[]{:S(2)}) collective-permute-start(bf16[144,2304]{1,0:T(8,128)(2,1)} %get-tuple-element.296), channel_id=1, source_target_pairs={{0,8},{8,0},{4,12},{12,4},{1,9},{9,1},{5,13},{13,5},{2,10},{10,2},... | collective-permute-start | bytes 1990664 | tf_op jit(solution)/shard_map/ppermute | solution.py:66
  469.4 45.4 %collective-permute-start.48 = (bf16[144,2304]{1,0:T(8,128)(2,1)}, bf16[144,2304]{1,0:T(8,128)(2,1)}, u32[]{:S(2)}, u32[]{:S(2)}) collective-permute-start(bf16[144,2304]{1,0:T(8,128)(2,1)} %get-tuple-element.311), channel_id=1, source_target_pairs={{0,4},{4,0},{8,12},{12,8},{1,5},{5,1},{9,13},{13,9},{2,6},{6,2},{1... | collective-permute-start | bytes 1990664 | tf_op jit(solution)/shard_map/ppermute | solution.py:66
  469.8 45.0 %collective-permute-start.49 = (bf16[144,2304]{1,0:T(8,128)(2,1)}, bf16[144,2304]{1,0:T(8,128)(2,1)}, u32[]{:S(2)}, u32[]{:S(2)}) collective-permute-start(bf16[144,2304]{1,0:T(8,128)(2,1)} %get-tuple-element.312), channel_id=1, source_target_pairs={{0,8},{8,0},{4,12},{12,4},{1,9},{9,1},{5,13},{13,5},{2,10},{10,2},... | collective-permute-start | bytes 1990664 | tf_op jit(solution)/shard_map/ppermute | solution.py:66
  557.9 21.2 %collective-permute-start.56 = (bf16[512,512]{1,0:T(8,128)(2,1)S(1)}, bf16[512,512]{1,0:T(8,128)(2,1)S(1)}, u32[]{:S(2)}, u32[]{:S(2)}) collective-permute-start(bf16[512,512]{1,0:T(8,128)(2,1)S(1)} %pad_maximum_fusion.9), channel_id=1, source_target_pairs={{0,8},{8,0},{4,12},{12,4},{1,9},{9,1},{5,13},{13,5},{2,10},{10,2},... | collective-permute-start | bytes 1572872 | tf_op jit(solution)/shard_map/ppermute | solution.py:66
  559.2 21.4 %collective-permute-start.57 = (bf16[512,512]{1,0:T(8,128)(2,1)S(1)}, bf16[512,512]{1,0:T(8,128)(2,1)S(1)}, u32[]{:S(2)}, u32[]{:S(2)}) collective-permute-start(bf16[512,512]{1,0:T(8,128)(2,1)S(1)} %pad_maximum_fusion.10), channel_id=1, source_target_pairs={{0,12},{12,0},{4,8},{8,4},{1,13},{13,1},{5,9},{9,5},{2,14},{14,2},... | collective-permute-start | bytes 1572872 | tf_op jit(solution)/shard_map/ppermute | solution.py:66
  586.8 17.7 %collective-permute-start.58 = (bf16[128,2304]{1,0:T(8,128)(2,1)S(1)}, bf16[128,2304]{1,0:T(8,128)(2,1)}, u32[]{:S(2)}, u32[]{:S(2)}) collective-permute-start(bf16[128,2304]{1,0:T(8,128)(2,1)S(1)} %constant_dynamic-slice_fusion), channel_id=1, source_target_pairs={{0,1},{1,2},{2,3},{3,0},{4,5},{5,6},{6,7},{7,4},{8,9},{9,10},{10,1... | collective-permute-start | bytes 1769480 | tf_op jit(solution)/shard_map/ppermute | solution.py:71
  586.9 18.0 %collective-permute-start.60 = (bf16[144,2304]{1,0:T(8,128)(2,1)}, bf16[144,2304]{1,0:T(8,128)(2,1)S(1)}, u32[]{:S(2)}, u32[]{:S(2)}) collective-permute-start(bf16[144,2304]{1,0:T(8,128)(2,1)} %get-tuple-element.361), channel_id=1, source_target_pairs={{0,4},{4,0},{8,12},{12,8},{1,5},{5,1},{9,13},{13,9},{2,6},{6,2},{1... | collective-permute-start | bytes 1990664 | tf_op jit(solution)/shard_map/ppermute | solution.py:66
  587.7 18.0 %collective-permute-start.61 = (bf16[144,2304]{1,0:T(8,128)(2,1)}, bf16[144,2304]{1,0:T(8,128)(2,1)S(1)}, u32[]{:S(2)}, u32[]{:S(2)}) collective-permute-start(bf16[144,2304]{1,0:T(8,128)(2,1)} %get-tuple-element.362), channel_id=1, source_target_pairs={{0,8},{8,0},{4,12},{12,4},{1,9},{9,1},{5,13},{13,5},{2,10},{10,2},... | collective-permute-start | bytes 1990664 | tf_op jit(solution)/shard_map/ppermute | solution.py:66
  592.0 27.2 %collective-permute-start.63 = (bf16[144,2304]{1,0:T(8,128)(2,1)}, bf16[144,2304]{1,0:T(8,128)(2,1)}, u32[]{:S(2)}, u32[]{:S(2)}) collective-permute-start(bf16[144,2304]{1,0:T(8,128)(2,1)} %get-tuple-element.432), channel_id=1, source_target_pairs={{0,4},{4,0},{8,12},{12,8},{1,5},{5,1},{9,13},{13,9},{2,6},{6,2},{1... | collective-permute-start | bytes 1990664 | tf_op jit(solution)/shard_map/ppermute | solution.py:66
  593.7 26.2 %collective-permute-start.64 = (bf16[144,2304]{1,0:T(8,128)(2,1)}, bf16[144,2304]{1,0:T(8,128)(2,1)}, u32[]{:S(2)}, u32[]{:S(2)}) collective-permute-start(bf16[144,2304]{1,0:T(8,128)(2,1)} %get-tuple-element.431), channel_id=1, source_target_pairs={{0,8},{8,0},{4,12},{12,4},{1,9},{9,1},{5,13},{13,5},{2,10},{10,2},... | collective-permute-start | bytes 1990664 | tf_op jit(solution)/shard_map/ppermute | solution.py:66
  610.8 19.4 %collective-permute-start.66 = (bf16[144,1024]{1,0:T(8,128)(2,1)}, bf16[144,1024]{1,0:T(8,128)(2,1)S(1)}, u32[]{:S(2)}, u32[]{:S(2)}) collective-permute-start(bf16[144,1024]{1,0:T(8,128)(2,1)} %get-tuple-element.371), channel_id=1, source_target_pairs={{0,4},{4,0},{8,12},{12,8},{1,5},{5,1},{9,13},{13,9},{2,6},{6,2},{1... | collective-permute-start | bytes 884744 | tf_op jit(solution)/shard_map/ppermute | solution.py:66
  612.2 18.0 %collective-permute-start.67 = (bf16[144,1024]{1,0:T(8,128)(2,1)}, bf16[144,1024]{1,0:T(8,128)(2,1)S(1)}, u32[]{:S(2)}, u32[]{:S(2)}) collective-permute-start(bf16[144,1024]{1,0:T(8,128)(2,1)} %get-tuple-element.372), channel_id=1, source_target_pairs={{0,8},{8,0},{4,12},{12,4},{1,9},{9,1},{5,13},{13,5},{2,10},{10,2},... | collective-permute-start | bytes 884744 | tf_op jit(solution)/shard_map/ppermute | solution.py:66
  650.3 41.1 %all-to-all-start.1 = ((f32[32,4,288]{2,1,0:T(4,128)}), f32[32,4,288]{2,1,0:T(4,128)S(1)}, u32[]{:S(2)}, u32[]{:S(2)}) async-start(f32[32,4,288]{2,1,0:T(4,128)} %bitcast.52), calls=%async_computation.1 | async-start | bytes 393216 | tf_op jit(solution)/shard_map/all_to_all | solution.py:603
  (117 other events, 1218.4 us)
Sparse Core Ops, SparseCore 0:
  10.5 51.5 all-gather.2
  64.0 169.3 all-gather.4

commit v5 on v4

--- a/solution.py
+++ b/solution.py
@@ -83,6 +83,11 @@
 
     def diagonal(self):
         self.first = (send("x", self.blocks[2]), send("y", self.blocks[3]))
+
+    def both(self):
+        half = self.half = self.blocks[1].shape[0] // 2
+        from_x, from_y = send("x", self.blocks[1]), send("y", self.blocks[2])
+        self.first, self.middle = (from_x[half:], from_y[:half]), (from_x[:half], from_y[half:])
 
     def direct(self):
         self.middle = (send("x", self.blocks[1]), send("y", self.blocks[4]))
@@ -318,17 +323,18 @@
     )(dgate, dup, weights, weights)
 
 
-def weight_grad(rows, rows_far, cols, cols_far):
+def weight_grad(rows, rows_far, cols, cols_far, joined=False):
     count, half_width = rows_far.shape
     width = cols.shape[1]
     cut = cut_of(width)
     half = half_width // 8
     place = jnp.stack([lax.axis_index("fsdp"), lax.axis_index("ctx")]).astype(jnp.int32)
+    sizes = (4 * half, 2 * half, 2 * half) if joined else (4 * half,) + (half,) * 4
 
     def kernel(
         place_ref, near_ref, far_ref, cols_ref, cols_far_ref, *rest
     ):
-        outs, (near_t, far_t, total) = rest[:5], rest[5:]
+        outs, (near_t, far_t, total) = rest[: len(sizes)], rest[len(sizes) :]
 
         @pl.when(pl.program_id(0) == 0)
         def _():
@@ -341,11 +347,15 @@
         for index, (k, low) in enumerate(ORDER):
             start = (lax.bitwise_xor(place_ref[1], k) * 2 + low) * half
             block = total[pl.ds(pl.multiple_of(start, 16), half), :].astype(BF)
-            out, at = (outs[0], index) if index < 4 else (outs[index - 3], 0)
+            if index < 4:
+                out, at = outs[0], index
+            elif joined:
+                out, at = outs[1 + (index - 4) // 2], index % 2
+            else:
+                out, at = outs[index - 3], 0
             out[at * half : (at + 1) * half, :] = block
 
     by_cut = pl.BlockSpec((count, cut), lambda j, place: (0, j))
-    sizes = (4 * half,) + (half,) * 4
     return pl.pallas_call(
         kernel,
         grid_spec=pltpu.PrefetchScalarGridSpec(
@@ -372,6 +382,91 @@
             transcendentals=0,
         ),
     )(place, rows, rows_far, cols, cols_far)
+
+
+def attention_back(query, dattended, attended, kv, logsum, length):
+    tokens, columns = query.shape
+    heads, blocks = columns // HEAD_SIZE, kv.shape[0] // tokens
+    scalars = jnp.stack([lax.axis_index("ctx").astype(jnp.int32), length])
+
+    def kernel(scalars_ref, q_ref, d_ref, a_ref, kv_ref, log_ref, dq_ref, dkv_ref, dq, dk, dv):
+        block, head = pl.program_id(0), pl.program_id(1)
+        q, d = q_ref[...], d_ref[...]
+        key, value = kv_ref[:, :HEAD_SIZE], kv_ref[:, HEAD_SIZE:]
+        me = scalars_ref[0]
+        bent = jnp.tanh(right_dot(q, key) * (QSCALE / CAP))
+        shape = (tokens, tokens)
+        key_pos = lax.bitwise_xor(me, block) * tokens + lax.broadcasted_iota(jnp.int32, shape, 1)
+        query_pos = me * tokens + lax.broadcasted_iota(jnp.int32, shape, 0)
+        allowed = (key_pos <= query_pos) & (key_pos < scalars_ref[1])
+        probs = jnp.where(allowed, jnp.exp(CAP * bent - log_ref[...]), 0.0)
+        weighted = jnp.sum(d.astype(F32) * a_ref[...].astype(F32), -1, keepdims=True)
+        draw = (probs * (right_dot(d, value) - weighted) * (1.0 - bent * bent)).astype(BF)
+        dk_part, dv_part = left_dot(draw, q), left_dot(probs.astype(BF), d)
+        dq_part = plain_dot(draw, key)
+
+        @pl.when(head == 0)
+        def _():
+            dk[...] = dk_part
+            dv[...] = dv_part
+
+        @pl.when(head > 0)
+        def _():
+            dk[...] += dk_part
+            dv[...] += dv_part
+
+        @pl.when(block == 0)
+        def _():
+            dq[head] = dq_part
+
+        @pl.when(block > 0)
+        def _():
+            dq[head] += dq_part
+
+        @pl.when(head == heads - 1)
+        def _():
+            dkv_ref[:, :HEAD_SIZE] = (dk[...] * QSCALE).astype(BF)
+            dkv_ref[:, HEAD_SIZE:] = dv[...].astype(BF)
+
+        @pl.when((block == blocks - 1) & (head == heads - 1))
+        def _():
+            for i in range(heads):
+                dq_ref[:, i * HEAD_SIZE : (i + 1) * HEAD_SIZE] = (dq[i] * QSCALE).astype(BF)
+
+    by_head = pl.BlockSpec((tokens, HEAD_SIZE), lambda b, h, scalars: (0, h))
+    return pl.pallas_call(
+        kernel,
+        grid_spec=pltpu.PrefetchScalarGridSpec(
+            num_scalar_prefetch=1,
+            grid=(blocks, heads),
+            in_specs=[
+                by_head,
+                by_head,
+                by_head,
+                pl.BlockSpec((tokens, 2 * HEAD_SIZE), lambda b, h, scalars: (b, 0)),
+                pl.BlockSpec((None, tokens, 1), lambda b, h, scalars: (h, 0, 0)),
+            ],
+            out_specs=[
+                pl.BlockSpec((tokens, columns), lambda b, h, scalars: (0, 0)),
+                pl.BlockSpec((None, tokens, 2 * HEAD_SIZE), lambda b, h, scalars: (b, 0, 0)),
+            ],
+            scratch_shapes=[
+                pltpu.VMEM((heads, tokens, HEAD_SIZE), F32),
+                pltpu.VMEM((tokens, HEAD_SIZE), F32),
+                pltpu.VMEM((tokens, HEAD_SIZE), F32),
+            ],
+        ),
+        out_shape=[
+            jax.ShapeDtypeStruct((tokens, columns), BF),
+            jax.ShapeDtypeStruct((blocks, tokens, 2 * HEAD_SIZE), BF),
+        ],
+        compiler_params=kernel_params(),
+        cost_estimate=pl.CostEstimate(
+            flops=10 * tokens * tokens * blocks * columns,
+            bytes_accessed=8 * tokens * columns * blocks,
+            transcendentals=2 * tokens * tokens * blocks * heads,
+        ),
+    )(scalars, query, dattended, attended, kv, logsum)
 
 
 def residual_rows(attn, hidden, scale_two, scale_three):
@@ -533,8 +628,11 @@
     ring.going, gate_s.first, grad_down = tied(ring.going, gate_s.first, grad_down)
     ring.go()
     gate_s.direct()
-    dffn_in, up_s.blocks, gate_s.first = tied(ring.finish(), up_s.blocks, gate_s.first)
+    dffn_in, up_s.blocks, gate_s.first, gate_s.middle = tied(
+        ring.finish(), up_s.blocks, gate_s.first, gate_s.middle
+    )
     gate_s.sums()
+    up_s.diagonal()
     dafter, dattn_b, gain_three_rows, gain_two_rows = rowwise(
         residual_back_rows,
         [dffn_in, after_attn, attn, cot],
@@ -542,36 +640,18 @@
         [F32, BF],
         2,
     )
-    dattended = plain_dot(dattn_b, out_w).astype(BF).reshape(query_five.shape)
-    dattended, gate_s.middle = tied(dattended, gate_s.middle)
-    dprobs = jnp.einsum("stkgd,sukd->skgtu", dattended, value_four, preferred_element_type=F32)
-    weighted = jnp.sum(probs * dprobs, -1, keepdims=True)
-    draw_b = (probs * (dprobs - weighted) * (1.0 - bent * bent)).astype(BF)
-    draw_b, gate_s.last, up_s.blocks = tied(draw_b, gate_s.last, up_s.blocks)
-    up_s.diagonal()
-    dvalue_part = jnp.einsum("skgtu,stkgd->sukd", probs_b, dattended, preferred_element_type=F32)
-    dkey_part = (
-        jnp.einsum("skgtu,stkgd->sukd", draw_b, query_five, preferred_element_type=F32) * QSCALE
-    )
-    dkv = [
-        jnp.concatenate(
-            [
-                part[:, k * tok_here : (k + 1) * tok_here].astype(BF).reshape(row_count, kv_cols)
-                for part in (dkey_part, dvalue_part)
-            ],
-            1,
-        )
-        for k in range(planes)
-    ]
+    dattended = plain_dot(dattn_b, out_w).astype(BF)
     dattn_far = far_half(dattn_b)
-    dkv, dattn_far, up_s.first = tied(dkv, dattn_far, up_s.first)
+    dattended, gate_s.last, up_s.first, up_s.blocks = tied(
+        dattended, gate_s.last, up_s.first, up_s.blocks
+    )
+    up_s.direct()
+    dquery_b, dkv = attention_back(
+        query_b, dattended, attended, kv_all[0], logsum.reshape(head_groups, row_count, 1), lengths[0]
+    )
+    dkv, dattn_far, up_s.middle = tied(dkv, dattn_far, up_s.middle)
     dkv = [dkv[0], send("x", dkv[1]), send("y", dkv[2]), send("diagonal", dkv[3])]
-    out_s = Scatter(weight_grad(dattn_b, dattn_far, attended, attended_far))
-    dquery_b = (
-        (jnp.einsum("skgtu,sukd->stkgd", draw_b, key_four, preferred_element_type=F32) * QSCALE)
-        .astype(BF)
-        .reshape(row_count, -1)
-    )
+    out_s = Scatter(weight_grad(dattn_b, dattn_far, attended, attended_far, True))
     grad_gate = gate_s.result()
     dkv, dquery_b, out_s.blocks, grad_gate, up_s.blocks = tied(
         dkv, dquery_b, out_s.blocks, grad_gate, up_s.blocks
@@ -585,42 +665,40 @@
 
     ring = Ring(dattn_in)
     dqkv_far = send("core", dqkv_b)
-    up_s.direct()
-    qkv_s = Scatter(weight_grad(attention_input, attention_input_far, dqkv_b, dqkv_far))
-    ring.going, qkv_s.blocks, up_s.middle = tied(ring.going, qkv_s.blocks, up_s.middle)
-    ring.go()
+    qkv_s = Scatter(
+        weight_grad(attention_input, attention_input_far, dqkv_b, dqkv_far, True)
+    )
     up_s.sums()
+    gain_rows = gain_two_rows, gain_three_rows, gain_four_rows
+    ring.going, qkv_s.blocks, up_s.last, gain_rows = tied(
+        ring.going, qkv_s.blocks, up_s.last, gain_rows
+    )
+    ring.go()
+    qkv_s.both()
     grad_gain_one = jnp.sum(dattn_in.astype(F32) * normed_one, 0)
-    grad_gains = jnp.stack(
-        [grad_gain_one]
-        + [jnp.sum(rows, 0) / size for rows in (gain_two_rows, gain_three_rows, gain_four_rows)]
-    )
+    grad_gains = jnp.stack([grad_gain_one] + [jnp.sum(rows, 0) / size for rows in gain_rows])
     grad_gains = grad_gains.reshape(4, 2 * planes, 1, -1).transpose(1, 2, 0, 3)
     grad_gains = jnp.broadcast_to(grad_gains, (2 * planes, size) + grad_gains.shape[2:])
     grad_gains = grad_gains.reshape((-1,) + grad_gains.shape[2:])
-    ring.going, grad_gains, up_s.last = tied(ring.going, grad_gains, up_s.last)
-    ring.go()
+    ring.going, qkv_s.first, qkv_s.middle, out_s.blocks = tied(
+        ring.going, qkv_s.first, qkv_s.middle, out_s.blocks
+    )
+    ring.go()
+    qkv_s.sums()
+    out_s.both()
+    grad_up = up_s.result()
+    ring.going, qkv_s.last, out_s.first, out_s.middle, grad_up, grad_gains = tied(
+        ring.going, qkv_s.last, out_s.first, out_s.middle, grad_up, grad_gains
+    )
+    ring.go()
+    out_s.sums()
     grad_gains = lax.all_to_all(grad_gains, ("fsdp", "ctx", "tp"), 0, 0, tiled=True)
-    qkv_s.diagonal()
-    qkv_s.direct()
-    grad_up = up_s.result()
-    ring.going, qkv_s.first, qkv_s.middle, grad_up = tied(
-        ring.going, qkv_s.first, qkv_s.middle, grad_up
-    )
-    ring.go()
-    qkv_s.sums()
-    out_s.diagonal()
-    ring.going, qkv_s.last, out_s.first = tied(ring.going, qkv_s.last, out_s.first)
-    ring.go()
-    out_s.direct()
-    out_s.sums()
     grad_qkv = qkv_s.result()
-    ring.going, out_s.middle, out_s.last, grad_qkv = tied(
-        ring.going, out_s.middle, out_s.last, grad_qkv
-    )
+    ring.going, out_s.last, grad_qkv = tied(ring.going, out_s.last, grad_qkv)
     ring.go()
     grad_out = out_s.result().T
     ring.going, grad_out = tied(ring.going, grad_out)
+    ring.go()
     dattn_in, grad_gains = tied(ring.finish(), grad_gains)
     grad_gains = jnp.sum(grad_gains, 0)
     dattn_in = dattn_in.astype(F32)

time: 716 us -> 702 us (0.980)
  Pallas kernels: 130 us -> 145 us
  other arithmetic: 74.1 us -> 60.3 us
  matrix products: 36.4 us -> 23.3 us
  waiting for transfers between devices: 354 us -> 363 us
    pallas_call x0 -> x1, Pallas kernels: none -> 15.6 us  [attention_back(): pl.pallas_call(kernel, grid_spec=pltpu.PrefetchScalarGridSpec(num_scalar_...]
    ppermute x36, waiting for transfers between devices: 208 us -> 221 us  [around(): lax.ppermute(value, 'tp', [(i, (i + by) % size) for i in range(size)])]
    dot_general x4 -> x0, matrix products: 12.8 us -> none  [the longest x1 3.64 us: plane_body(): jnp.einsum('skgtu,stkgd->sukd', draw_b, query_five, preferred_element_typ...]
    ppermute x45 -> x41, starting transfers between devices: 40.3 us -> 35.6 us  [send(): return lax.ppermute(value, *LINKS[link])]
    ppermute x45 -> x41, waiting for transfers between devices: 83.7 us -> 79.2 us  [send(): return lax.ppermute(value, *LINKS[link])]
  transfers between devices with their start and end apart: 85 -> 81, of which waited for: 55 -> 49; matrix products, arithmetic and copies ran while one was open for 15% -> 12% of each run, Pallas kernels for 13% -> 16%
where the time goes in v5:
time: 702 us; the launch traced here: 694 us
  waiting for transfers between devices  363 us (52%)
  Pallas kernels  145 us (21%)
  other arithmetic  60.3 us (9%)
  starting transfers between devices  54.9 us (8%)
  local copies, waits for them, and re-layouts  31.6 us (5%)
  matrix products  23.3 us (3%)
  between operations  16.3 us (2%)
    ppermute x36, waiting for transfers between devices, around(): lax.ppermute(value, 'tp', [(i, (i + by) % size) for i in range(size)])  221 us
    ppermute x41, waiting for transfers between devices, send(): return lax.ppermute(value, *LINKS[link])  79.2 us
    all_gather x2, waiting for transfers between devices, gather(): return lax.all_gather(shard, ('fsdp', 'ctx'), axis=0, tiled=True)  62.3 us
    pallas_call x5, Pallas kernels, weight_grad(): pl.pallas_call(kernel, grid_spec=pltpu.PrefetchScalarGridSpec(num_scalar_...  46.3 us
    ppermute x41, starting transfers between devices, send(): return lax.ppermute(value, *LINKS[link])  35.6 us
    pallas_call x3, Pallas kernels, rowwise(): pl.pallas_call(kernel, grid=(count // block,), in_specs=[by_row] * len(ro...  24.9 us
    pallas_call x1, Pallas kernels, ffn_hidden(): pl.pallas_call(kernel, grid=(units // cut,), in_specs=[pl.BlockSpec((coun...  17.4 us
    pallas_call x1, Pallas kernels, ffn_input_back(): pl.pallas_call(kernel, grid=(width // cut,), in_specs=[whole, whole, pl.B...  16.9 us
  transfers between devices with their start and end apart: 81, of which 49 were waited for; matrix products, arithmetic and copies ran while one was open for 12% of the time, Pallas kernels for 16%

profile of v5, /device:TPU:0, one launch (start us, length us, event | category | flops | bytes accessed | tf_op | source)
XLA Modules:
  0.0 694.5 jit_solution(17449514954250778490)
XLA Ops:
  23.1 39.1 %all-gather.3.cloned.1.call-done = bf16[2304,1536]{1,0:T(8,128)(2,1)} async-done(((bf16[288,1536]{1,0:T(8,128)(2,1)}), bf16[2304,1536]{1,0:T(8,128)(2,1)}) %all-gather.3.cloned.1.call-update) | async-done | bytes 7077904 | tf_op jit(solution)/shard_map/all_gather | solution.py:525
  73.0 14.4 %collective-permute-done = bf16[1,512,512]{2,1,0:T(8,128)(2,1)S(1)} collective-permute-done((bf16[1,512,512]{2,1,0:T(8,128)(2,1)S(1)}, bf16[1,512,512]{2,1,0:T(8,128)(2,1)S(1)}, u32[]{:S(2)}, u32[]{:S(2)}) %collective-permute-start) | collective-permute-done | bytes 524320 | tf_op jit(solution)/shard_map/ppermute | solution.py:66
  91.5 17.9 %collective-permute-done.2 = bf16[1,512,512]{2,1,0:T(8,128)(2,1)S(1)} collective-permute-done((bf16[1,512,512]{2,1,0:T(8,128)(2,1)S(1)}, bf16[1,512,512]{2,1,0:T(8,128)(2,1)S(1)}, u32[]{:S(2)}, u32[]{:S(2)}) %collective-permute-start.2) | collective-permute-done | bytes 524320 | tf_op jit(solution)/shard_map/ppermute | solution.py:66
  126.6 9.0 %collective-permute-done.3 = bf16[64,2304]{1,0:T(8,128)(2,1)S(1)} collective-permute-done((bf16[64,2304]{1,0:T(8,128)(2,1)}, bf16[64,2304]{1,0:T(8,128)(2,1)S(1)}, u32[]{:S(2)}, u32[]{:S(2)}) %collective-permute-start.3) | collective-permute-done | bytes 294944 | tf_op jit(solution)/shard_map/ppermute | solution.py:71
  187.3 6.3 collective-permute-done.12
  193.7 8.8 %collective-permute-done.14 = bf16[64,2304]{1,0:T(8,128)(2,1)S(1)} collective-permute-done((bf16[64,2304]{1,0:T(8,128)(2,1)S(1)}, bf16[64,2304]{1,0:T(8,128)(2,1)S(1)}, u32[]{:S(2)}, u32[]{:S(2)}) %collective-permute-start.14) | collective-permute-done | bytes 294944 | tf_op jit(solution)/shard_map/ppermute | solution.py:71
  210.2 23.2 %all-gather.5.cloned.1.call-done.gate_w.up_w.w_ref = bf16[2304,6912]{1,0:T(8,128)(2,1)} async-done(((bf16[288,6912]{1,0:T(8,128)(2,1)}), bf16[2304,6912]{1,0:T(8,128)(2,1)}) %all-gather.5.cloned.1.call-update) | async-done | bytes 31850512 | tf_op jit(solution)/shard_map/all_gather | solution.py:525
  233.4 17.4 %shard_map.238 = (f32[512,2304]{1,0:T(8,128)}, f32[512,2304]{1,0:T(8,128)}, bf16[512,2304]{1,0:T(8,128)(2,1)}) custom-call(bf16[512,2304]{1,0:T(8,128)(2,1)} %get-tuple-element.222.x_ref.near_ref, bf16[2304,6912]{1,0:T(8,128)(2,1)} %all-gather.5.cloned.1.call-done.gate_w.up_w.w_ref, bf16[2304,6912]{1,0:T(8,128)(2,1)} %all-gather.5.cloned.1.call-done.gate_w.up_w.w_ref), custom_call_target="tpu_custom_call" | custom-call | flops 10871635968 | bytes 33030144 | tf_op jit(solution)/shard_map/pallas_call | solution.py:218
  250.7 10.1 %shard_map.239 = bf16[512,2304]{1,0:T(8,128)(2,1)} custom-call(bf16[512,2304]{1,0:T(8,128)(2,1)} %get-tuple-element.220.x_ref.cols_ref, bf16[2304,6912]{1,0:T(8,128)(2,1)} %all-gather.5.cloned.1.call-done.gate_w.up_w.w_ref), custom_call_target="tpu_custom_call" | custom-call | flops 5435817984 | bytes 10616832 | tf_op jit(solution)/shard_map/pallas_call | solution.py:249
  266.2 7.5 %collective-permute-done.15 = bf16[64,2304]{1,0:T(8,128)(2,1)S(1)} collective-permute-done((bf16[64,2304]{1,0:T(8,128)(2,1)S(1)}, bf16[64,2304]{1,0:T(8,128)(2,1)S(1)}, u32[]{:S(2)}, u32[]{:S(2)}) %collective-permute-start.15) | collective-permute-done | bytes 294944 | tf_op jit(solution)/shard_map/ppermute | solution.py:71
  282.4 13.5 %collective-permute-done.18 = bf16[64,2304]{1,0:T(8,128)(2,1)S(1)} collective-permute-done((bf16[64,2304]{1,0:T(8,128)(2,1)S(1)}, bf16[64,2304]{1,0:T(8,128)(2,1)S(1)}, u32[]{:S(2)}, u32[]{:S(2)}) %collective-permute-start.18) | collective-permute-done | bytes 294944 | tf_op jit(solution)/shard_map/ppermute | solution.py:71
  296.3 11.6 %collective-permute-done.23 = bf16[64,2304]{1,0:T(8,128)(2,1)S(1)} collective-permute-done((bf16[64,2304]{1,0:T(8,128)(2,1)S(1)}, bf16[64,2304]{1,0:T(8,128)(2,1)S(1)}, u32[]{:S(2)}, u32[]{:S(2)}) %collective-permute-start.23) | collective-permute-done | bytes 294944 | tf_op jit(solution)/shard_map/ppermute | solution.py:71
  320.5 6.3 collective-permute-done.26
  333.1 6.3 collective-permute-done.28
  339.5 10.1 %collective-permute-done.30 = bf16[64,2304]{1,0:T(8,128)(2,1)S(1)} collective-permute-done((bf16[64,2304]{1,0:T(8,128)(2,1)S(1)}, bf16[64,2304]{1,0:T(8,128)(2,1)S(1)}, u32[]{:S(2)}, u32[]{:S(2)}) %collective-permute-start.30) | collective-permute-done | bytes 294944 | tf_op jit(solution)/shard_map/ppermute | solution.py:71
  351.1 8.3 %shard_map.240 = (bf16[512,2304]{1,0:T(8,128)(2,1)}, bf16[512,2304]{1,0:T(8,128)(2,1)}, f32[8,2304]{1,0:T(8,128)}) custom-call(bf16[512,2304]{1,0:T(8,128)(2,1)} %copy-done.10, f32[512,2304]{1,0:T(8,128)} %get-tuple-element.237.refs_1_, bf16[512,2304]{1,0:T(8,128)(2,1)} %bitcast_select_fusion.1.refs_2_.refs_3_, f32[1,2304]{1,0:T(1,128)} %add.598.refs_3_), custom_call_target="tpu_custom_call" | custom-call | flops 23592960 | bytes 18874368 | tf_op jit(solution)/shard_map/pallas_call | solution.py:179
  360.8 14.3 %shard_map.241 = (bf16[512,2304]{1,0:T(8,128)(2,1)}, bf16[512,2304]{1,0:T(8,128)(2,1)}) custom-call(bf16[512,2304]{1,0:T(8,128)(2,1)} %get-tuple-element.240.d_ref.near_ref, bf16[2304,6912]{1,0:T(8,128)(2,1)} %all-gather.5.cloned.1.call-done.gate_w.up_w.w_ref, f32[512,2304]{1,0:T(8,128)} %get-tuple-element.241.gate_ref, f32[512,2304]{1,0:T(8,128)} %get-tuple-element.242.up_ref), custom_call_target="tpu_custom_call" | custom-call | flops 5435817984 | bytes 24772608 | tf_op jit(solution)/shard_map/pallas_call | solution.py:277
  375.1 16.9 %shard_map.242 = bf16[512,2304]{1,0:T(8,128)(2,1)} custom-call(bf16[512,2304]{1,0:T(8,128)(2,1)} %get-tuple-element.253.dgate_ref.cols_ref, bf16[512,2304]{1,0:T(8,128)(2,1)} %get-tuple-element.262.dup_ref.cols_ref, bf16[2304,6912]{1,0:T(8,128)(2,1)} %all-gather.5.cloned.1.call-done.gate_w.up_w.w_ref, ...), custom_call_target="tpu_custom_call" | custom-call | flops 10871635968 | bytes 21233664 | tf_op jit(solution)/shard_map/pallas_call | solution.py:308
  394.5 11.3 %shard_map.243 = (bf16[576,2304]{1,0:T(8,128)(2,1)}, bf16[144,2304]{1,0:T(8,128)(2,1)}, bf16[144,2304]{1,0:T(8,128)(2,1)}, bf16[144,2304]{1,0:T(8,128)(2,1)}, bf16[144,2304]{1,0:T(8,128)(2,1)}) custom-call(s32[2]{0:T(128)} %pad_add_fusion.2.place_ref, bf16[512,2304]{1,0:T(8,128)(2,1)} %get-tuple-element.240.d_ref.near_ref, bf16[512,1152]{1,0:T(8,128)(2,1)} %copy-done.59, ...), custom_call_target="tpu_custom_call" | custom-call | flops 5435817984 | bytes 12386304 | tf_op jit(solution)/shard_map/pallas_call | solution.py:359
  415.1 11.3 %shard_map.244 = (bf16[576,2304]{1,0:T(8,128)(2,1)}, bf16[144,2304]{1,0:T(8,128)(2,1)}, bf16[144,2304]{1,0:T(8,128)(2,1)}, bf16[144,2304]{1,0:T(8,128)(2,1)}, bf16[144,2304]{1,0:T(8,128)(2,1)}) custom-call(s32[2]{0:T(128)} %pad_add_fusion.2.place_ref, bf16[512,2304]{1,0:T(8,128)(2,1)} %get-tuple-element.222.x_ref.near_ref, bf16[512,1152]{1,0:T(8,128)(2,1)} %copy-done.58, ...), custom_call_target="tpu_custom_call" | custom-call | flops 5435817984 | bytes 12386304 | tf_op jit(solution)/shard_map/pallas_call | solution.py:359
  437.1 11.2 %shard_map.245 = (bf16[576,2304]{1,0:T(8,128)(2,1)}, bf16[144,2304]{1,0:T(8,128)(2,1)}, bf16[144,2304]{1,0:T(8,128)(2,1)}, bf16[144,2304]{1,0:T(8,128)(2,1)}, bf16[144,2304]{1,0:T(8,128)(2,1)}) custom-call(s32[2]{0:T(128)} %pad_add_fusion.2.place_ref, bf16[512,2304]{1,0:T(8,128)(2,1)} %get-tuple-element.222.x_ref.near_ref, bf16[512,1152]{1,0:T(8,128)(2,1)} %copy-done.58, ...), custom_call_target="tpu_custom_call" | custom-call | flops 5435817984 | bytes 12386304 | tf_op jit(solution)/shard_map/pallas_call | solution.py:359
  457.7 8.1 %collective-permute-done.41 = bf16[128,2304]{1,0:T(8,128)(2,1)} collective-permute-done((bf16[128,2304]{1,0:T(8,128)(2,1)}, bf16[128,2304]{1,0:T(8,128)(2,1)}, u32[]{:S(2)}, u32[]{:S(2)}) %collective-permute-start.41) | collective-permute-done | bytes 589856 | tf_op jit(solution)/shard_map/ppermute | solution.py:71
  473.9 7.5 %collective-permute-done.44 = bf16[128,2304]{1,0:T(8,128)(2,1)S(1)} collective-permute-done((bf16[128,2304]{1,0:T(8,128)(2,1)}, bf16[128,2304]{1,0:T(8,128)(2,1)S(1)}, u32[]{:S(2)}, u32[]{:S(2)}) %collective-permute-start.44) | collective-permute-done | bytes 589856 | tf_op jit(solution)/shard_map/ppermute | solution.py:71
  486.7 10.5 %collective-permute-done.47 = bf16[128,2304]{1,0:T(8,128)(2,1)S(1)} collective-permute-done((bf16[128,2304]{1,0:T(8,128)(2,1)S(1)}, bf16[128,2304]{1,0:T(8,128)(2,1)S(1)}, u32[]{:S(2)}, u32[]{:S(2)}) %collective-permute-start.47) | collective-permute-done | bytes 589856 | tf_op jit(solution)/shard_map/ppermute | solution.py:71
  500.0 10.4 %shard_map.246 = (f32[512,2304]{1,0:T(8,128)}, bf16[512,2304]{1,0:T(8,128)(2,1)}, f32[8,2304]{1,0:T(8,128)}, f32[8,2304]{1,0:T(8,128)}) custom-call(bf16[512,2304]{1,0:T(8,128)(2,1)} %copy-done.7, f32[512,2304]{1,0:T(8,128)} %get-tuple-element.237.refs_1_, bf16[512,2304]{1,0:T(8,128)(2,1)} %copy-done.2, ...), custom_call_target="tpu_custom_call" | custom-call | flops 23592960 | bytes 28311552 | tf_op jit(solution)/shard_map/pallas_call | solution.py:179
  529.3 15.6 %shard_map.247 = (bf16[512,512]{1,0:T(8,128)(2,1)}, bf16[4,512,512]{2,1,0:T(8,128)(2,1)}) custom-call(s32[2]{0:T(128)} %pad_add_fusion.1.scalars_ref, bf16[512,512]{1,0:T(8,128)(2,1)} %copy-done.38, bf16[512,512]{1,0:T(8,128)(2,1)} %fusion.30.d_ref, bf16[512,512]{1,0:T(8,128)(2,1)} %copy-done.21, bf16[2048,512]{1,0:T(8,128)(2,1)} %get-tuple-element.427.kv_ref, ...), custom_call_target="tpu_custom_call" | custom-call | flops 5368709120 | bytes 8388608 | tf_op jit(solution)/shard_map/pallas_call | solution.py:437
  560.5 6.9 collective-permute-done.58
  580.1 7.4 %shard_map.249 = (bf16[576,1024]{1,0:T(8,128)(2,1)}, bf16[288,1024]{1,0:T(8,128)(2,1)}, bf16[288,1024]{1,0:T(8,128)(2,1)}) custom-call(s32[2]{0:T(128)} %pad_add_fusion.2.place_ref, bf16[512,2304]{1,0:T(8,128)(2,1)} %fusion.4.near_ref, bf16[512,1152]{1,0:T(8,128)(2,1)} %copy-done.57, bf16[512,1024]{1,0:T(8,128)(2,1)} %copy-done.25, ...), custom_call_target="tpu_custom_call" | custom-call | flops 2415919104 | bytes 6815744 | tf_op jit(solution)/shard_map/pallas_call | solution.py:359
  587.5 8.0 %collective-permute-done.60 = bf16[128,2304]{1,0:T(8,128)(2,1)} collective-permute-done((bf16[128,2304]{1,0:T(8,128)(2,1)}, bf16[128,2304]{1,0:T(8,128)(2,1)}, u32[]{:S(2)}, u32[]{:S(2)}) %collective-permute-start.60) | collective-permute-done | bytes 589856 | tf_op jit(solution)/shard_map/ppermute | solution.py:71
  603.7 6.9 collective-permute-done.66
  653.5 10.0 %collective-permute-done.75 = bf16[128,2304]{1,0:T(8,128)(2,1)S(1)} collective-permute-done((bf16[128,2304]{1,0:T(8,128)(2,1)}, bf16[128,2304]{1,0:T(8,128)(2,1)S(1)}, u32[]{:S(2)}, u32[]{:S(2)}) %collective-permute-start.75) | collective-permute-done | bytes 589856 | tf_op jit(solution)/shard_map/ppermute | solution.py:71
  665.2 12.0 %collective-permute-done.76 = bf16[128,2304]{1,0:T(8,128)(2,1)S(1)} collective-permute-done((bf16[128,2304]{1,0:T(8,128)(2,1)S(1)}, bf16[128,2304]{1,0:T(8,128)(2,1)S(1)}, u32[]{:S(2)}, u32[]{:S(2)}) %collective-permute-start.76) | collective-permute-done | bytes 589856 | tf_op jit(solution)/shard_map/ppermute | solution.py:71
  (399 shorter events, 300.1 us)
Async XLA Ops:
  7.2 54.9 %all-gather.3.cloned.1.call-start = ((), (), s32[]{:S(2)}) async-start(), calls=%async_computation.2 | async-start | bytes 7962624 | tf_op jit(solution)/shard_map/all_gather | solution.py:525
  15.5 217.9 %all-gather.5.cloned.1.call-start = ((), (), s32[]{:S(2)}) async-start(), calls=%async_computation.3 | async-start | bytes 35831808 | tf_op jit(solution)/shard_map/all_gather | solution.py:525
  67.9 19.6 %collective-permute-start = (bf16[1,512,512]{2,1,0:T(8,128)(2,1)S(1)}, bf16[1,512,512]{2,1,0:T(8,128)(2,1)S(1)}, u32[]{:S(2)}, u32[]{:S(2)}) collective-permute-start(bf16[1,512,512]{2,1,0:T(8,128)(2,1)S(1)} %get-tuple-element.436), channel_id=1, source_target_pairs={{0,4},{4,0},{8,12},{12,8},{1,5},{5,1},{9,13},{13,9},{2,6},{6,2},{1... | collective-permute-start | bytes 1572872 | tf_op jit(solution)/shard_map/ppermute | solution.py:66
  69.4 22.1 %collective-permute-start.1 = (bf16[1,512,512]{2,1,0:T(8,128)(2,1)S(1)}, bf16[1,512,512]{2,1,0:T(8,128)(2,1)S(1)}, u32[]{:S(2)}, u32[]{:S(2)}) collective-permute-start(bf16[1,512,512]{2,1,0:T(8,128)(2,1)S(1)} %get-tuple-element.436), channel_id=1, source_target_pairs={{0,8},{8,0},{4,12},{12,4},{1,9},{9,1},{5,13},{13,5},{2,10},{10,2},... | collective-permute-start | bytes 1572872 | tf_op jit(solution)/shard_map/ppermute | solution.py:66
  70.0 39.5 %collective-permute-start.2 = (bf16[1,512,512]{2,1,0:T(8,128)(2,1)S(1)}, bf16[1,512,512]{2,1,0:T(8,128)(2,1)S(1)}, u32[]{:S(2)}, u32[]{:S(2)}) collective-permute-start(bf16[1,512,512]{2,1,0:T(8,128)(2,1)S(1)} %get-tuple-element.436), channel_id=1, source_target_pairs={{0,12},{12,0},{4,8},{8,4},{1,13},{13,1},{5,9},{9,5},{2,14},{14,2},... | collective-permute-start | bytes 1572872 | tf_op jit(solution)/shard_map/ppermute | solution.py:66
  265.4 30.5 %collective-permute-start.21 = (bf16[512,1152]{1,0:T(8,128)(2,1)S(1)}, bf16[512,1152]{1,0:T(8,128)(2,1)S(1)}, u32[]{:S(2)}, u32[]{:S(2)}) collective-permute-start(bf16[512,1152]{1,0:T(8,128)(2,1)S(1)} %constant_dynamic-slice_fusion.5), channel_id=1, source_target_pairs={{0,16},{16,0},{1,17},{17,1},{2,18},{18,2},{3,19},{19,3},{4,20},{20... | collective-permute-start | bytes 3538952 | tf_op jit(solution)/shard_map/ppermute | solution.py:66
  265.5 30.4 %collective-permute-start.19 = (bf16[512,2304]{1,0:T(8,128)(2,1)S(1)}, bf16[512,2304]{1,0:T(8,128)(2,1)S(1)}, u32[]{:S(2)}, u32[]{:S(2)}) collective-permute-start(bf16[512,2304]{1,0:T(8,128)(2,1)S(1)} %copy-done.18), channel_id=1, source_target_pairs={{0,16},{16,0},{1,17},{17,1},{2,18},{18,2},{3,19},{19,3},{4,20},{20... | collective-permute-start | bytes 7077896 | tf_op jit(solution)/shard_map/ppermute | solution.py:66
  266.1 29.8 %collective-permute-start.22 = (bf16[512,1152]{1,0:T(8,128)(2,1)S(1)}, bf16[512,1152]{1,0:T(8,128)(2,1)S(1)}, u32[]{:S(2)}, u32[]{:S(2)}) collective-permute-start(bf16[512,1152]{1,0:T(8,128)(2,1)S(1)} %constant_dynamic-slice_fusion.4), channel_id=1, source_target_pairs={{0,16},{16,0},{1,17},{17,1},{2,18},{18,2},{3,19},{19,3},{4,20},{20... | collective-permute-start | bytes 3538952 | tf_op jit(solution)/shard_map/ppermute | solution.py:66
  296.2 18.0 %collective-permute-start.24 = (bf16[64,2304]{1,0:T(8,128)(2,1)S(1)}, bf16[64,2304]{1,0:T(8,128)(2,1)S(1)}, u32[]{:S(2)}, u32[]{:S(2)}) collective-permute-start(bf16[64,2304]{1,0:T(8,128)(2,1)S(1)} %add_convert_fusion.17), channel_id=1, source_target_pairs={{0,1},{1,2},{2,3},{3,0},{4,5},{5,6},{6,7},{7,4},{8,9},{9,10},{10,1... | collective-permute-start | bytes 884744 | tf_op jit(solution)/shard_map/ppermute | solution.py:71
  360.7 31.3 %collective-permute-start.31 = (bf16[512,1152]{1,0:T(8,128)(2,1)S(1)}, bf16[512,1152]{1,0:T(8,128)(2,1)S(1)}, u32[]{:S(2)}, u32[]{:S(2)}) collective-permute-start(bf16[512,1152]{1,0:T(8,128)(2,1)S(1)} %constant_dynamic-slice_fusion.3), channel_id=1, source_target_pairs={{0,16},{16,0},{1,17},{17,1},{2,18},{18,2},{3,19},{19,3},{4,20},{20... | collective-permute-start | bytes 3538952 | tf_op jit(solution)/shard_map/ppermute | solution.py:66
  392.0 19.3 %collective-permute-start.33 = (bf16[512,2304]{1,0:T(8,128)(2,1)}, bf16[512,2304]{1,0:T(8,128)(2,1)}, u32[]{:S(2)}, u32[]{:S(2)}) collective-permute-start(bf16[512,2304]{1,0:T(8,128)(2,1)} %get-tuple-element.253.dgate_ref.cols_ref), channel_id=1, source_target_pairs={{0,16},{16,0},{1,17},{17,1},{2,18},{18,2},{3,19},{19,3},{4,20},{20... | collective-permute-start | bytes 7077896 | tf_op jit(solution)/shard_map/ppermute | solution.py:66
  392.6 33.9 %collective-permute-start.35 = (bf16[512,2304]{1,0:T(8,128)(2,1)}, bf16[512,2304]{1,0:T(8,128)(2,1)}, u32[]{:S(2)}, u32[]{:S(2)}) collective-permute-start(bf16[512,2304]{1,0:T(8,128)(2,1)} %get-tuple-element.262.dup_ref.cols_ref), channel_id=1, source_target_pairs={{0,16},{16,0},{1,17},{17,1},{2,18},{18,2},{3,19},{19,3},{4,20},{20... | collective-permute-start | bytes 7077896 | tf_op jit(solution)/shard_map/ppermute | solution.py:66
  411.3 19.8 %collective-permute-start.36 = (bf16[144,2304]{1,0:T(8,128)(2,1)}, bf16[144,2304]{1,0:T(8,128)(2,1)}, u32[]{:S(2)}, u32[]{:S(2)}) collective-permute-start(bf16[144,2304]{1,0:T(8,128)(2,1)} %get-tuple-element.263), channel_id=1, source_target_pairs={{0,4},{4,0},{8,12},{12,8},{1,5},{5,1},{9,13},{13,9},{2,6},{6,2},{1... | collective-permute-start | bytes 1990664 | tf_op jit(solution)/shard_map/ppermute | solution.py:66
  412.7 18.4 %collective-permute-start.37 = (bf16[144,2304]{1,0:T(8,128)(2,1)}, bf16[144,2304]{1,0:T(8,128)(2,1)}, u32[]{:S(2)}, u32[]{:S(2)}) collective-permute-start(bf16[144,2304]{1,0:T(8,128)(2,1)} %get-tuple-element.264), channel_id=1, source_target_pairs={{0,8},{8,0},{4,12},{12,4},{1,9},{9,1},{5,13},{13,5},{2,10},{10,2},... | collective-permute-start | bytes 1990664 | tf_op jit(solution)/shard_map/ppermute | solution.py:66
  414.7 33.6 %collective-permute-start.39 = (bf16[144,2304]{1,0:T(8,128)(2,1)}, bf16[144,2304]{1,0:T(8,128)(2,1)S(1)}, u32[]{:S(2)}, u32[]{:S(2)}) collective-permute-start(bf16[144,2304]{1,0:T(8,128)(2,1)} %get-tuple-element.272), channel_id=1, source_target_pairs={{0,4},{4,0},{8,12},{12,8},{1,5},{5,1},{9,13},{13,9},{2,6},{6,2},{1... | collective-permute-start | bytes 1990664 | tf_op jit(solution)/shard_map/ppermute | solution.py:66
  426.4 21.9 %collective-permute-start.40 = (bf16[144,2304]{1,0:T(8,128)(2,1)}, bf16[144,2304]{1,0:T(8,128)(2,1)S(1)}, u32[]{:S(2)}, u32[]{:S(2)}) collective-permute-start(bf16[144,2304]{1,0:T(8,128)(2,1)} %get-tuple-element.273), channel_id=1, source_target_pairs={{0,8},{8,0},{4,12},{12,4},{1,9},{9,1},{5,13},{13,5},{2,10},{10,2},... | collective-permute-start | bytes 1990664 | tf_op jit(solution)/shard_map/ppermute | solution.py:66
  435.0 21.5 %collective-permute-start.42 = (bf16[144,2304]{1,0:T(8,128)(2,1)}, bf16[144,2304]{1,0:T(8,128)(2,1)}, u32[]{:S(2)}, u32[]{:S(2)}) collective-permute-start(bf16[144,2304]{1,0:T(8,128)(2,1)} %get-tuple-element.418), channel_id=1, source_target_pairs={{0,4},{4,0},{8,12},{12,8},{1,5},{5,1},{9,13},{13,9},{2,6},{6,2},{1... | collective-permute-start | bytes 1990664 | tf_op jit(solution)/shard_map/ppermute | solution.py:66
  435.4 22.3 %collective-permute-start.43 = (bf16[144,2304]{1,0:T(8,128)(2,1)}, bf16[144,2304]{1,0:T(8,128)(2,1)}, u32[]{:S(2)}, u32[]{:S(2)}) collective-permute-start(bf16[144,2304]{1,0:T(8,128)(2,1)} %get-tuple-element.417), channel_id=1, source_target_pairs={{0,8},{8,0},{4,12},{12,4},{1,9},{9,1},{5,13},{13,5},{2,10},{10,2},... | collective-permute-start | bytes 1990664 | tf_op jit(solution)/shard_map/ppermute | solution.py:66
  465.8 18.1 %collective-permute-start.45 = (bf16[144,2304]{1,0:T(8,128)(2,1)}, bf16[144,2304]{1,0:T(8,128)(2,1)S(1)}, u32[]{:S(2)}, u32[]{:S(2)}) collective-permute-start(bf16[144,2304]{1,0:T(8,128)(2,1)} %get-tuple-element.284), channel_id=1, source_target_pairs={{0,4},{4,0},{8,12},{12,8},{1,5},{5,1},{9,13},{13,9},{2,6},{6,2},{1... | collective-permute-start | bytes 1990664 | tf_op jit(solution)/shard_map/ppermute | solution.py:66
  467.3 18.1 %collective-permute-start.46 = (bf16[144,2304]{1,0:T(8,128)(2,1)}, bf16[144,2304]{1,0:T(8,128)(2,1)S(1)}, u32[]{:S(2)}, u32[]{:S(2)}) collective-permute-start(bf16[144,2304]{1,0:T(8,128)(2,1)} %get-tuple-element.285), channel_id=1, source_target_pairs={{0,8},{8,0},{4,12},{12,4},{1,9},{9,1},{5,13},{13,5},{2,10},{10,2},... | collective-permute-start | bytes 1990664 | tf_op jit(solution)/shard_map/ppermute | solution.py:66
  467.8 29.4 %collective-permute-start.48 = (bf16[144,2304]{1,0:T(8,128)(2,1)}, bf16[144,2304]{1,0:T(8,128)(2,1)S(1)}, u32[]{:S(2)}, u32[]{:S(2)}) collective-permute-start(bf16[144,2304]{1,0:T(8,128)(2,1)} %get-tuple-element.298), channel_id=1, source_target_pairs={{0,4},{4,0},{8,12},{12,8},{1,5},{5,1},{9,13},{13,9},{2,6},{6,2},{1... | collective-permute-start | bytes 1990664 | tf_op jit(solution)/shard_map/ppermute | solution.py:66
  468.2 29.0 %collective-permute-start.49 = (bf16[144,2304]{1,0:T(8,128)(2,1)}, bf16[144,2304]{1,0:T(8,128)(2,1)S(1)}, u32[]{:S(2)}, u32[]{:S(2)}) collective-permute-start(bf16[144,2304]{1,0:T(8,128)(2,1)} %get-tuple-element.299), channel_id=1, source_target_pairs={{0,8},{8,0},{4,12},{12,4},{1,9},{9,1},{5,13},{13,5},{2,10},{10,2},... | collective-permute-start | bytes 1990664 | tf_op jit(solution)/shard_map/ppermute | solution.py:66
  499.0 20.0 %collective-permute-start.50 = (bf16[144,2304]{1,0:T(8,128)(2,1)}, bf16[144,2304]{1,0:T(8,128)(2,1)}, u32[]{:S(2)}, u32[]{:S(2)}) collective-permute-start(bf16[144,2304]{1,0:T(8,128)(2,1)} %get-tuple-element.414), channel_id=1, source_target_pairs={{0,4},{4,0},{8,12},{12,8},{1,5},{5,1},{9,13},{13,9},{2,6},{6,2},{1... | collective-permute-start | bytes 1990664 | tf_op jit(solution)/shard_map/ppermute | solution.py:66
  499.6 19.4 %collective-permute-start.51 = (bf16[144,2304]{1,0:T(8,128)(2,1)}, bf16[144,2304]{1,0:T(8,128)(2,1)}, u32[]{:S(2)}, u32[]{:S(2)}) collective-permute-start(bf16[144,2304]{1,0:T(8,128)(2,1)} %get-tuple-element.413), channel_id=1, source_target_pairs={{0,8},{8,0},{4,12},{12,4},{1,9},{9,1},{5,13},{13,5},{2,10},{10,2},... | collective-permute-start | bytes 1990664 | tf_op jit(solution)/shard_map/ppermute | solution.py:66
  515.0 29.9 %collective-permute-start.54 = (bf16[512,1152]{1,0:T(8,128)(2,1)S(1)}, bf16[512,1152]{1,0:T(8,128)(2,1)S(1)}, u32[]{:S(2)}, u32[]{:S(2)}) collective-permute-start(bf16[512,1152]{1,0:T(8,128)(2,1)S(1)} %constant_dynamic-slice_fusion.1), channel_id=1, source_target_pairs={{0,16},{16,0},{1,17},{17,1},{2,18},{18,2},{3,19},{19,3},{4,20},{20... | collective-permute-start | bytes 3538952 | tf_op jit(solution)/shard_map/ppermute | solution.py:66
  525.3 19.6 %collective-permute-start.55 = (bf16[144,2304]{1,0:T(8,128)(2,1)}, bf16[144,2304]{1,0:T(8,128)(2,1)}, u32[]{:S(2)}, u32[]{:S(2)}) collective-permute-start(bf16[144,2304]{1,0:T(8,128)(2,1)} %get-tuple-element.312), channel_id=1, source_target_pairs={{0,4},{4,0},{8,12},{12,8},{1,5},{5,1},{9,13},{13,9},{2,6},{6,2},{1... | collective-permute-start | bytes 1990664 | tf_op jit(solution)/shard_map/ppermute | solution.py:66
  526.7 18.2 %collective-permute-start.56 = (bf16[144,2304]{1,0:T(8,128)(2,1)}, bf16[144,2304]{1,0:T(8,128)(2,1)}, u32[]{:S(2)}, u32[]{:S(2)}) collective-permute-start(bf16[144,2304]{1,0:T(8,128)(2,1)} %get-tuple-element.313), channel_id=1, source_target_pairs={{0,8},{8,0},{4,12},{12,4},{1,9},{9,1},{5,13},{13,5},{2,10},{10,2},... | collective-permute-start | bytes 1990664 | tf_op jit(solution)/shard_map/ppermute | solution.py:66
  548.0 19.4 %collective-permute-start.58 = (bf16[512,512]{1,0:T(8,128)(2,1)S(1)}, bf16[512,512]{1,0:T(8,128)(2,1)S(1)}, u32[]{:S(2)}, u32[]{:S(2)}) collective-permute-start(bf16[512,512]{1,0:T(8,128)(2,1)S(1)} %get-tuple-element.424), channel_id=1, source_target_pairs={{0,8},{8,0},{4,12},{12,4},{1,9},{9,1},{5,13},{13,5},{2,10},{10,2},... | collective-permute-start | bytes 1572872 | tf_op jit(solution)/shard_map/ppermute | solution.py:66
  549.1 18.3 %collective-permute-start.59 = (bf16[512,512]{1,0:T(8,128)(2,1)S(1)}, bf16[512,512]{1,0:T(8,128)(2,1)S(1)}, u32[]{:S(2)}, u32[]{:S(2)}) collective-permute-start(bf16[512,512]{1,0:T(8,128)(2,1)S(1)} %get-tuple-element.423), channel_id=1, source_target_pairs={{0,12},{12,0},{4,8},{8,4},{1,13},{13,1},{5,9},{9,5},{2,14},{14,2},... | collective-permute-start | bytes 1572872 | tf_op jit(solution)/shard_map/ppermute | solution.py:66
  575.1 20.5 %collective-permute-start.62 = (bf16[144,2304]{1,0:T(8,128)(2,1)}, bf16[144,2304]{1,0:T(8,128)(2,1)}, u32[]{:S(2)}, u32[]{:S(2)}) collective-permute-start(bf16[144,2304]{1,0:T(8,128)(2,1)} %get-tuple-element.410), channel_id=1, source_target_pairs={{0,4},{4,0},{8,12},{12,8},{1,5},{5,1},{9,13},{13,9},{2,6},{6,2},{1... | collective-permute-start | bytes 1990664 | tf_op jit(solution)/shard_map/ppermute | solution.py:66
  576.3 19.2 %collective-permute-start.63 = (bf16[144,2304]{1,0:T(8,128)(2,1)}, bf16[144,2304]{1,0:T(8,128)(2,1)}, u32[]{:S(2)}, u32[]{:S(2)}) collective-permute-start(bf16[144,2304]{1,0:T(8,128)(2,1)} %get-tuple-element.409), channel_id=1, source_target_pairs={{0,8},{8,0},{4,12},{12,4},{1,9},{9,1},{5,13},{13,5},{2,10},{10,2},... | collective-permute-start | bytes 1990664 | tf_op jit(solution)/shard_map/ppermute | solution.py:66
  636.9 41.2 %all-to-all-start.1 = ((f32[32,4,288]{2,1,0:T(4,128)}), f32[32,4,288]{2,1,0:T(4,128)S(1)}, u32[]{:S(2)}, u32[]{:S(2)}) async-start(f32[32,4,288]{2,1,0:T(4,128)} %bitcast.29), calls=%async_computation.1 | async-start | bytes 393216 | tf_op jit(solution)/shard_map/all_to_all | solution.py:695
  (111 other events, 1358.0 us)
Sparse Core Ops, SparseCore 0:
  10.5 51.5 all-gather.2
  64.0 169.3 all-gather.4

commit v6 on v5

--- a/solution.py
+++ b/solution.py
@@ -69,6 +69,14 @@
 def around(value, by=1):
     size = lax.axis_size("tp")
     return lax.ppermute(value, "tp", [(i, (i + by) % size) for i in range(size)])
+
+
+def place(pieces, starts):
+    rows = sum(piece.shape[0] for piece in pieces)
+    whole = jnp.zeros((rows,) + pieces[0].shape[1:], pieces[0].dtype)
+    for piece, start in zip(pieces, starts):
+        whole = lax.dynamic_update_slice_in_dim(whole, piece, start, 0)
+    return whole
 
 
 def halves(block):
@@ -202,125 +210,139 @@
     return value, slope
 
 
-def ffn_hidden(x, weights):
+def ffn_forward(x, weights, down_rest):
     count, width = x.shape
-    units = weights.shape[1] // 3
-    cut = cut_of(units)
-
-    def kernel(x_ref, gate_w, up_w, gate_ref, up_ref, hidden_ref):
-        gate = plain_dot(x_ref[...], gate_w[...])
-        up = plain_dot(x_ref[...], up_w[...])
-        gate_ref[...] = gate
-        up_ref[...] = up
-        hidden_ref[...] = (gelu_parts(gate)[0] * up).astype(BF)
-
-    out = pl.BlockSpec((count, cut), lambda j: (0, j))
+    cut, out_cut = down_rest.shape[1], cut_of(width)
+    units = (weights.shape[1] + cut) // 3
+    first = units // cut
+
+    def kernel(x_ref, gate_w, up_w, down_w, rest_w, gate_ref, up_ref, hidden_ref, out_ref, kept):
+        step = pl.program_id(0)
+
+        @pl.when(step < first)
+        def _():
+            gate = plain_dot(x_ref[...], gate_w[...])
+            up = plain_dot(x_ref[...], up_w[...])
+            hidden = (gelu_parts(gate)[0] * up).astype(BF)
+            gate_ref[...] = gate
+            up_ref[...] = up
+            hidden_ref[...] = hidden
+            kept[step] = hidden
+
+        @pl.when(step >= first)
+        def _():
+            total = right_dot(kept[first - 1], rest_w[...])
+            for i in range(first - 1):
+                total += right_dot(kept[i], down_w[:, i * cut : (i + 1) * cut])
+            out_ref[...] = total.astype(BF)
+
+    def early(j):
+        return jnp.minimum(j, first - 1)
+
+    def late(j):
+        return jnp.maximum(j - first, 0)
+
+    out = pl.BlockSpec((count, cut), lambda j: (0, early(j)))
     return pl.pallas_call(
         kernel,
-        grid=(units // cut,),
+        grid=(first + width // out_cut,),
         in_specs=[
             pl.BlockSpec((count, width), lambda j: (0, 0)),
-            pl.BlockSpec((width, cut), lambda j: (0, j)),
-            pl.BlockSpec((width, cut), lambda j: (0, j + units // cut)),
+            pl.BlockSpec((width, cut), lambda j: (0, early(j))),
+            pl.BlockSpec((width, cut), lambda j: (0, early(j) + first)),
+            pl.BlockSpec((out_cut, units - cut), lambda j: (late(j), 3)),
+            pl.BlockSpec((out_cut, cut), lambda j: (late(j), 0)),
         ],
-        out_specs=[out] * 3,
+        out_specs=[out] * 3 + [pl.BlockSpec((count, out_cut), lambda j: (0, late(j)))],
         out_shape=[
             jax.ShapeDtypeStruct((count, units), F32),
             jax.ShapeDtypeStruct((count, units), F32),
             jax.ShapeDtypeStruct((count, units), BF),
+            jax.ShapeDtypeStruct((count, width), BF),
         ],
+        scratch_shapes=[pltpu.VMEM((first, count, cut), BF)],
         compiler_params=kernel_params(),
         cost_estimate=pl.CostEstimate(
-            flops=4 * count * width * units,
-            bytes_accessed=4 * width * units + 10 * count * units,
+            flops=6 * count * width * units,
+            bytes_accessed=6 * width * units + 10 * count * units,
             transcendentals=count * units,
         ),
-    )(x, weights, weights)
-
-
-def ffn_down(hidden, weights):
-    count, units = hidden.shape
-    width = weights.shape[0]
-    cut = cut_of(width)
-
-    def kernel(x_ref, w_ref, out_ref):
-        out_ref[...] = right_dot(x_ref[...], w_ref[...]).astype(BF)
-
+    )(x, weights, weights, weights, down_rest)
+
+
+def ffn_backward(dffn, weights, down_rest, gate, up):
+    count, width = dffn.shape
+    units = gate.shape[1]
+    cut, out_cut = down_rest.shape[1], cut_of(width)
+    first = units // cut
+
+    def kernel(
+        d_ref,
+        down_w,
+        rest_w,
+        gate_ref,
+        up_ref,
+        gate_w,
+        up_w,
+        dgate_ref,
+        dup_ref,
+        out_ref,
+        kept,
+        kept_up,
+    ):
+        step = pl.program_id(0)
+
+        def make(weight):
+            dhidden = plain_dot(d_ref[...], weight[...])
+            value, slope = gelu_parts(gate_ref[...])
+            dgate = (dhidden * up_ref[...] * slope).astype(BF)
+            dup = (dhidden * value).astype(BF)
+            dgate_ref[...] = dgate
+            dup_ref[...] = dup
+            kept[step] = dgate
+            kept_up[step] = dup
+
+        pl.when(step < first - 1)(lambda: make(down_w))
+        pl.when(step == first - 1)(lambda: make(rest_w))
+
+        @pl.when(step >= first)
+        def _():
+            out_ref[...] = sum(
+                right_dot(terms[i], weight[:, i * cut : (i + 1) * cut])
+                for i in range(first)
+                for terms, weight in ((kept, gate_w), (kept_up, up_w))
+            ).astype(BF)
+
+    def early(j):
+        return jnp.minimum(j, first - 1)
+
+    def late(j):
+        return jnp.maximum(j - first, 0)
+
+    by_cut = pl.BlockSpec((count, cut), lambda j: (0, early(j)))
     return pl.pallas_call(
         kernel,
-        grid=(width // cut,),
+        grid=(first + width // out_cut,),
         in_specs=[
-            pl.BlockSpec((count, units), lambda j: (0, 0)),
-            pl.BlockSpec((cut, units), lambda j: (j, 2)),
+            pl.BlockSpec((count, width), lambda j: (0, 0)),
+            pl.BlockSpec((width, cut), lambda j: (0, jnp.minimum(j, first - 2) + 2 * first)),
+            pl.BlockSpec((width, cut), lambda j: (0, 0)),
+            by_cut,
+            by_cut,
+            pl.BlockSpec((out_cut, units), lambda j: (late(j), 0)),
+            pl.BlockSpec((out_cut, units), lambda j: (late(j), 1)),
         ],
-        out_specs=pl.BlockSpec((count, cut), lambda j: (0, j)),
-        out_shape=jax.ShapeDtypeStruct((count, width), BF),
+        out_specs=[by_cut] * 2 + [pl.BlockSpec((count, out_cut), lambda j: (0, late(j)))],
+        out_shape=[jax.ShapeDtypeStruct((count, units), BF)] * 2
+        + [jax.ShapeDtypeStruct((count, width), BF)],
+        scratch_shapes=[pltpu.VMEM((first, count, cut), BF)] * 2,
         compiler_params=kernel_params(),
         cost_estimate=pl.CostEstimate(
-            flops=2 * count * width * units, bytes_accessed=2 * width * units, transcendentals=0
-        ),
-    )(hidden, weights)
-
-
-def ffn_hidden_back(dffn, weights, gate, up):
-    count, width = dffn.shape
-    units = gate.shape[1]
-    cut = cut_of(units)
-
-    def kernel(d_ref, w_ref, gate_ref, up_ref, dgate_ref, dup_ref):
-        dhidden = plain_dot(d_ref[...], w_ref[...])
-        value, slope = gelu_parts(gate_ref[...])
-        dgate_ref[...] = (dhidden * up_ref[...] * slope).astype(BF)
-        dup_ref[...] = (dhidden * value).astype(BF)
-
-    out = pl.BlockSpec((count, cut), lambda j: (0, j))
-    return pl.pallas_call(
-        kernel,
-        grid=(units // cut,),
-        in_specs=[
-            pl.BlockSpec((count, width), lambda j: (0, 0)),
-            pl.BlockSpec((width, cut), lambda j: (0, j + 2 * (units // cut))),
-            out,
-            out,
-        ],
-        out_specs=[out] * 2,
-        out_shape=[jax.ShapeDtypeStruct((count, units), BF)] * 2,
-        compiler_params=kernel_params(),
-        cost_estimate=pl.CostEstimate(
-            flops=2 * count * width * units,
-            bytes_accessed=2 * width * units + 12 * count * units,
+            flops=6 * count * width * units,
+            bytes_accessed=6 * width * units + 12 * count * units,
             transcendentals=count * units,
         ),
-    )(dffn, weights, gate, up)
-
-
-def ffn_input_back(dgate, dup, weights):
-    count, units = dgate.shape
-    width = weights.shape[0]
-    cut = cut_of(width)
-
-    def kernel(dgate_ref, dup_ref, gate_w, up_w, out_ref):
-        out_ref[...] = (
-            right_dot(dgate_ref[...], gate_w[...]) + right_dot(dup_ref[...], up_w[...])
-        ).astype(BF)
-
-    whole = pl.BlockSpec((count, units), lambda j: (0, 0))
-    return pl.pallas_call(
-        kernel,
-        grid=(width // cut,),
-        in_specs=[
-            whole,
-            whole,
-            pl.BlockSpec((cut, units), lambda j: (j, 0)),
-            pl.BlockSpec((cut, units), lambda j: (j, 1)),
-        ],
-        out_specs=pl.BlockSpec((count, cut), lambda j: (0, j)),
-        out_shape=jax.ShapeDtypeStruct((count, width), BF),
-        compiler_params=kernel_params(),
-        cost_estimate=pl.CostEstimate(
-            flops=4 * count * width * units, bytes_accessed=4 * width * units, transcendentals=0
-        ),
-    )(dgate, dup, weights, weights)
+    )(dffn, weights, down_rest, gate, up, weights, weights)
 
 
 def weight_grad(rows, rows_far, cols, cols_far, joined=False):
@@ -529,7 +551,10 @@
 
     attention_shards = jnp.concatenate([query_weight, key_weight, value_weight, w_out.T], 1)
     attention_w = gather(attention_shards)
-    ffn_shards = jnp.concatenate([w_gate, w_up, w_down.T], 1)
+    late = w_down.shape[0] - cut_of(w_down.shape[0])
+    ffn_shards = jnp.concatenate([w_gate, w_up, w_down[:late].T], 1)
+    rest_t = w_down[late:].T
+    rest_x, rest_y = send("x", rest_t), send("y", rest_t)
     gains = jnp.stack([gain_attn_in, gain_attn_out, gain_ffn_in, gain_ffn_out])[None]
     gains = jnp.broadcast_to(gains, (2 * planes,) + gains.shape[1:])
     gains = lax.all_to_all(gains, ("fsdp", "ctx"), 0, 0, tiled=True)
@@ -539,7 +564,9 @@
     normed_one, factor_one = normalize(flat_in)
     attention_input = (normed_one * scale_one).astype(BF)
 
-    attention_w, attention_input, ffn_shards = tied(attention_w, attention_input, ffn_shards)
+    attention_w, attention_input, ffn_shards, rest_x, rest_y = tied(
+        attention_w, attention_input, ffn_shards, rest_x, rest_y
+    )
     ffn_w = gather(ffn_shards)
     qkv_cols = q_cols + 2 * kv_cols
     qkv_w, out_w = attention_w[:, :qkv_cols], attention_w[:, qkv_cols:]
@@ -555,6 +582,8 @@
     query_b = qkv[:, :q_cols]
     kv = qkv[:, q_cols:].reshape(seqs_here, tok_here, 2 * kv_cols)
     kv_all = jnp.concatenate([kv, send("x", kv), send("y", kv), send("diagonal", kv)], 1)
+    kv_all, rest_x, rest_y = tied(kv_all, rest_x, rest_y)
+    rest_last = [send("y", halves(rest_x)[0]), send("x", halves(rest_y)[1])]
     query_five = query_b.reshape(seqs_here, tok_here, kv_local, head_groups, HEAD_SIZE)
     key_four = kv_all[:, :, :kv_cols].reshape(seqs_here, SEQUENCE_SLOTS, kv_local, HEAD_SIZE)
     value_four = kv_all[:, :, kv_cols:].reshape(seqs_here, SEQUENCE_SLOTS, kv_local, HEAD_SIZE)
@@ -570,17 +599,26 @@
         .astype(BF)
         .reshape(row_count, -1)
     )
+    attended, rest_last = tied(attended, rest_last)
     attn = right_dot(attended, out_w).astype(BF)
     ring = Ring(attn, 2)
-    for _ in range(2 * size - 3):
-        ring.go()
+    ring.go()
+    rows, start = rest_t.shape[0], [(me ^ k) * rest_t.shape[0] for k in range(4)]
+    rest_near = place([rest_t, rest_x, rest_y, *rest_last], [*start, start[3] + rows // 2])
+    ring.go()
+    ring.going, rest_near = tied(ring.going, rest_near)
+    rest_far = send("core", rest_near)
+    ring.go()
+    ring.go()
+    ring.going, rest_far = tied(ring.going, rest_far)
+    ring.go()
+    down_rest = place([rest_near, rest_far], [core * half_width, (1 - core) * half_width])
     attn = ring.finish()
     hidden_rows = hidden_in.reshape(row_count, width)
     after_attn, ffn_in = rowwise(
         residual_rows, [attn, hidden_rows], [scale_two, scale_three], [F32, BF]
     )
-    gate, upward, hidden_b = ffn_hidden(ffn_in, ffn_w)
-    ffn_out = ffn_down(hidden_b, ffn_w)
+    gate, upward, hidden_b, ffn_out = ffn_forward(ffn_in, ffn_w, down_rest)
     ffn_out, hidden_b, attended, ffn_in, attention_input, cotangent = tied(
         ffn_out, hidden_b, attended, ffn_in, attention_input, cotangent
     )
@@ -599,8 +637,9 @@
     output, dffn_b, gain_four_rows = rowwise(
         output_rows, [ffn_out, after_attn, cot], [scale_four], [BF, BF], 1
     )
-    dgate_b, dup_b = ffn_hidden_back(dffn_b, ffn_w, gate, upward)
-    dffn_in = ffn_input_back(dgate_b, dup_b, ffn_w)
+    dgate_b, dup_b, dffn_in = ffn_backward(
+        dffn_b, ffn_w, down_rest, gate, upward
+    )
     dffn_far = far_half(dffn_b)
 
     dffn_in, dffn_far, dgate_b, dup_b = tied(dffn_in, dffn_far, dgate_b, dup_b)

time: 702 us -> 693 us (0.987)
  waiting for transfers between devices: 363 us -> 338 us
  local copies, waits for them, and re-layouts: 31.6 us -> 44.8 us
  starting transfers between devices: 54.9 us -> 62.6 us
    all_gather x2, waiting for transfers between devices: 62.3 us -> 31.7 us  [gather(): return lax.all_gather(shard, ('fsdp', 'ctx'), axis=0, tiled=True)]
    ppermute x41 -> x46, starting transfers between devices: 35.6 us -> 43.2 us  [send(): return lax.ppermute(value, *LINKS[link])]
    dynamic_update_slice x0 -> x7, local copies, waits for them, and re-layouts: none -> 7.58 us  [place(): whole = lax.dynamic_update_slice_in_dim(whole, piece, start, 0)]
    pallas_call x4 -> x2, Pallas kernels: 58.7 us -> 55.6 us  [the longest x1 28.8 us: ffn_backward(): pl.pallas_call(kernel, grid=(first + width // out_cut,), in_specs=[pl.Blo...]
    ppermute x41 -> x46, waiting for transfers between devices: 79.2 us -> 81.5 us  [send(): return lax.ppermute(value, *LINKS[link])]
  transfers between devices with their start and end apart: 81 -> 86, of which waited for: 49 -> 49; matrix products, arithmetic and copies ran while one was open for 12% -> 13% of each run, Pallas kernels for 16% -> 16%
where the time goes in v6:
time: 693 us; the launch traced here: 683 us
  waiting for transfers between devices  338 us (49%)
  Pallas kernels  143 us (21%)
  starting transfers between devices  62.6 us (9%)
  other arithmetic  55 us (8%)
  local copies, waits for them, and re-layouts  44.8 us (6%)
  matrix products  23.4 us (3%)
  between operations  16.7 us (2%)
    ppermute x36, waiting for transfers between devices, around(): lax.ppermute(value, 'tp', [(i, (i + by) % size) for i in range(size)])  218 us
    ppermute x46, waiting for transfers between devices, send(): return lax.ppermute(value, *LINKS[link])  81.5 us
    pallas_call x5, Pallas kernels, weight_grad(): pl.pallas_call(kernel, grid_spec=pltpu.PrefetchScalarGridSpec(num_scalar_...  46.4 us
    ppermute x46, starting transfers between devices, send(): return lax.ppermute(value, *LINKS[link])  43.2 us
    all_gather x2, waiting for transfers between devices, gather(): return lax.all_gather(shard, ('fsdp', 'ctx'), axis=0, tiled=True)  31.7 us
    pallas_call x1, Pallas kernels, ffn_backward(): pl.pallas_call(kernel, grid=(first + width // out_cut,), in_specs=[pl.Blo...  28.8 us
    pallas_call x1, Pallas kernels, ffn_forward(): pl.pallas_call(kernel, grid=(first + width // out_cut,), in_specs=[pl.Blo...  26.8 us
    pallas_call x3, Pallas kernels, rowwise(): pl.pallas_call(kernel, grid=(count // block,), in_specs=[by_row] * len(ro...  25 us
  transfers between devices with their start and end apart: 86, of which 49 were waited for; matrix products, arithmetic and copies ran while one was open for 13% of the time, Pallas kernels for 16%

profile of v6, /device:TPU:0, one launch (start us, length us, event | category | flops | bytes accessed | tf_op | source)
XLA Modules:
  0.0 682.7 jit_solution(16385311715336814278)
XLA Ops:
  33.1 31.7 %all-gather.3.cloned.1.call-done = bf16[2304,1536]{1,0:T(8,128)(2,1)} async-done(((bf16[288,1536]{1,0:T(8,128)(2,1)}), bf16[2304,1536]{1,0:T(8,128)(2,1)}) %all-gather.3.cloned.1.call-update) | async-done | bytes 7077904 | tf_op jit(solution)/shard_map/all_gather | solution.py:547
  75.7 14.9 %collective-permute-done.2 = bf16[1,512,512]{2,1,0:T(8,128)(2,1)S(1)} collective-permute-done((bf16[1,512,512]{2,1,0:T(8,128)(2,1)S(1)}, bf16[1,512,512]{2,1,0:T(8,128)(2,1)S(1)}, u32[]{:S(2)}, u32[]{:S(2)}) %collective-permute-start.2) | collective-permute-done | bytes 524320 | tf_op jit(solution)/shard_map/ppermute | solution.py:66
  94.7 18.0 %collective-permute-done.4 = bf16[1,512,512]{2,1,0:T(8,128)(2,1)} collective-permute-done((bf16[1,512,512]{2,1,0:T(8,128)(2,1)S(1)}, bf16[1,512,512]{2,1,0:T(8,128)(2,1)}, u32[]{:S(2)}, u32[]{:S(2)}) %collective-permute-start.4) | collective-permute-done | bytes 524320 | tf_op jit(solution)/shard_map/ppermute | solution.py:66
  143.3 7.9 %collective-permute-done.9 = bf16[64,2304]{1,0:T(8,128)(2,1)S(1)} collective-permute-done((bf16[64,2304]{1,0:T(8,128)(2,1)}, bf16[64,2304]{1,0:T(8,128)(2,1)S(1)}, u32[]{:S(2)}, u32[]{:S(2)}) %collective-permute-start.9) | collective-permute-done | bytes 294944 | tf_op jit(solution)/shard_map/ppermute | solution.py:71
  175.9 8.5 %collective-permute-done.13 = bf16[64,2304]{1,0:T(8,128)(2,1)S(1)} collective-permute-done((bf16[64,2304]{1,0:T(8,128)(2,1)S(1)}, bf16[64,2304]{1,0:T(8,128)(2,1)S(1)}, u32[]{:S(2)}, u32[]{:S(2)}) %collective-permute-start.13) | collective-permute-done | bytes 294944 | tf_op jit(solution)/shard_map/ppermute | solution.py:71
  184.4 6.3 collective-permute-done.14
  190.8 12.2 %collective-permute-done.16 = bf16[64,2304]{1,0:T(8,128)(2,1)S(1)} collective-permute-done((bf16[64,2304]{1,0:T(8,128)(2,1)S(1)}, bf16[64,2304]{1,0:T(8,128)(2,1)S(1)}, u32[]{:S(2)}, u32[]{:S(2)}) %collective-permute-start.16) | collective-permute-done | bytes 294944 | tf_op jit(solution)/shard_map/ppermute | solution.py:71
  203.4 16.4 %collective-permute-done.19 = bf16[64,2304]{1,0:T(8,128)(2,1)S(1)} collective-permute-done((bf16[64,2304]{1,0:T(8,128)(2,1)S(1)}, bf16[64,2304]{1,0:T(8,128)(2,1)S(1)}, u32[]{:S(2)}, u32[]{:S(2)}) %collective-permute-start.19) | collective-permute-done | bytes 294944 | tf_op jit(solution)/shard_map/ppermute | solution.py:71
  221.2 6.3 shard_map.237
  227.5 26.8 %shard_map.238 = (f32[512,2304]{1,0:T(8,128)}, f32[512,2304]{1,0:T(8,128)}, bf16[512,2304]{1,0:T(8,128)(2,1)}, bf16[512,2304]{1,0:T(8,128)(2,1)}) custom-call(bf16[512,2304]{1,0:T(8,128)(2,1)} %get-tuple-element.253.x_ref.near_ref, bf16[2304,6144]{1,0:T(8,128)(2,1)} %all-gather.5.cloned.1.call-done.gate_w.up_w.down_w, ...), custom_call_target="tpu_custom_call" | custom-call | flops 16307453952 | bytes 43646976 | tf_op jit(solution)/shard_map/pallas_call | solution.py:246
  258.3 9.0 %collective-permute-done.20 = bf16[64,2304]{1,0:T(8,128)(2,1)S(1)} collective-permute-done((bf16[64,2304]{1,0:T(8,128)(2,1)S(1)}, bf16[64,2304]{1,0:T(8,128)(2,1)S(1)}, u32[]{:S(2)}, u32[]{:S(2)}) %collective-permute-start.20) | collective-permute-done | bytes 294944 | tf_op jit(solution)/shard_map/ppermute | solution.py:71
  274.7 12.2 %collective-permute-done.23 = bf16[64,2304]{1,0:T(8,128)(2,1)S(1)} collective-permute-done((bf16[64,2304]{1,0:T(8,128)(2,1)S(1)}, bf16[64,2304]{1,0:T(8,128)(2,1)S(1)}, u32[]{:S(2)}, u32[]{:S(2)}) %collective-permute-start.23) | collective-permute-done | bytes 294944 | tf_op jit(solution)/shard_map/ppermute | solution.py:71
  287.9 10.9 %collective-permute-done.28 = bf16[64,2304]{1,0:T(8,128)(2,1)S(1)} collective-permute-done((bf16[64,2304]{1,0:T(8,128)(2,1)S(1)}, bf16[64,2304]{1,0:T(8,128)(2,1)S(1)}, u32[]{:S(2)}, u32[]{:S(2)}) %collective-permute-start.28) | collective-permute-done | bytes 294944 | tf_op jit(solution)/shard_map/ppermute | solution.py:71
  311.5 6.3 collective-permute-done.31
  317.9 6.3 collective-permute-done.32
  324.1 6.3 collective-permute-done.33
  330.9 8.4 %collective-permute-done.35 = bf16[64,2304]{1,0:T(8,128)(2,1)S(1)} collective-permute-done((bf16[64,2304]{1,0:T(8,128)(2,1)S(1)}, bf16[64,2304]{1,0:T(8,128)(2,1)S(1)}, u32[]{:S(2)}, u32[]{:S(2)}) %collective-permute-start.35) | collective-permute-done | bytes 294944 | tf_op jit(solution)/shard_map/ppermute | solution.py:71
  340.8 8.2 %shard_map.239 = (bf16[512,2304]{1,0:T(8,128)(2,1)}, bf16[512,2304]{1,0:T(8,128)(2,1)}, f32[8,2304]{1,0:T(8,128)}) custom-call(bf16[512,2304]{1,0:T(8,128)(2,1)} %copy-done.7, f32[512,2304]{1,0:T(8,128)} %get-tuple-element.268.refs_1_, bf16[512,2304]{1,0:T(8,128)(2,1)} %bitcast_select_fusion.1.refs_2_.refs_3_, f32[1,2304]{1,0:T(1,128)} %add.629.refs_3_), custom_call_target="tpu_custom_call" | custom-call | flops 23592960 | bytes 18874368 | tf_op jit(solution)/shard_map/pallas_call | solution.py:187
  350.5 28.8 %shard_map.240 = (bf16[512,2304]{1,0:T(8,128)(2,1)}, bf16[512,2304]{1,0:T(8,128)(2,1)}, bf16[512,2304]{1,0:T(8,128)(2,1)}) custom-call(bf16[512,2304]{1,0:T(8,128)(2,1)} %get-tuple-element.271.d_ref.near_ref, bf16[2304,6144]{1,0:T(8,128)(2,1)} %all-gather.5.cloned.1.call-done.gate_w.up_w.down_w, bf16[2304,768]{1,0:T(8,128)(2,1)} %copy-done.2, ...), custom_call_target="tpu_custom_call" | custom-call | flops 16307453952 | bytes 46006272 | tf_op jit(solution)/shard_map/pallas_call | solution.py:323
  381.8 11.3 %shard_map.241 = (bf16[576,2304]{1,0:T(8,128)(2,1)}, bf16[144,2304]{1,0:T(8,128)(2,1)}, bf16[144,2304]{1,0:T(8,128)(2,1)}, bf16[144,2304]{1,0:T(8,128)(2,1)}, bf16[144,2304]{1,0:T(8,128)(2,1)}) custom-call(s32[2]{0:T(128)} %get-tuple-element.482.place_ref, bf16[512,2304]{1,0:T(8,128)(2,1)} %get-tuple-element.271.d_ref.near_ref, ...), custom_call_target="tpu_custom_call" | custom-call | flops 5435817984 | bytes 12386304 | tf_op jit(solution)/shard_map/pallas_call | solution.py:381
  402.1 11.3 %shard_map.242 = (bf16[576,2304]{1,0:T(8,128)(2,1)}, bf16[144,2304]{1,0:T(8,128)(2,1)}, bf16[144,2304]{1,0:T(8,128)(2,1)}, bf16[144,2304]{1,0:T(8,128)(2,1)}, bf16[144,2304]{1,0:T(8,128)(2,1)}) custom-call(s32[2]{0:T(128)} %get-tuple-element.482.place_ref, bf16[512,2304]{1,0:T(8,128)(2,1)} %get-tuple-element.253.x_ref.near_ref, ...), custom_call_target="tpu_custom_call" | custom-call | flops 5435817984 | bytes 12386304 | tf_op jit(solution)/shard_map/pallas_call | solution.py:381
  424.2 11.3 %shard_map.243 = (bf16[576,2304]{1,0:T(8,128)(2,1)}, bf16[144,2304]{1,0:T(8,128)(2,1)}, bf16[144,2304]{1,0:T(8,128)(2,1)}, bf16[144,2304]{1,0:T(8,128)(2,1)}, bf16[144,2304]{1,0:T(8,128)(2,1)}) custom-call(s32[2]{0:T(128)} %get-tuple-element.482.place_ref, bf16[512,2304]{1,0:T(8,128)(2,1)} %get-tuple-element.253.x_ref.near_ref, ...), custom_call_target="tpu_custom_call" | custom-call | flops 5435817984 | bytes 12386304 | tf_op jit(solution)/shard_map/pallas_call | solution.py:381
  445.1 7.6 %collective-permute-done.46 = bf16[128,2304]{1,0:T(8,128)(2,1)} collective-permute-done((bf16[128,2304]{1,0:T(8,128)(2,1)}, bf16[128,2304]{1,0:T(8,128)(2,1)}, u32[]{:S(2)}, u32[]{:S(2)}) %collective-permute-start.46) | collective-permute-done | bytes 589856 | tf_op jit(solution)/shard_map/ppermute | solution.py:71
  460.7 7.5 %collective-permute-done.49 = bf16[128,2304]{1,0:T(8,128)(2,1)S(1)} collective-permute-done((bf16[128,2304]{1,0:T(8,128)(2,1)}, bf16[128,2304]{1,0:T(8,128)(2,1)S(1)}, u32[]{:S(2)}, u32[]{:S(2)}) %collective-permute-start.49) | collective-permute-done | bytes 589856 | tf_op jit(solution)/shard_map/ppermute | solution.py:71
  473.7 10.5 %collective-permute-done.52 = bf16[128,2304]{1,0:T(8,128)(2,1)S(1)} collective-permute-done((bf16[128,2304]{1,0:T(8,128)(2,1)S(1)}, bf16[128,2304]{1,0:T(8,128)(2,1)S(1)}, u32[]{:S(2)}, u32[]{:S(2)}) %collective-permute-start.52) | collective-permute-done | bytes 589856 | tf_op jit(solution)/shard_map/ppermute | solution.py:71
  486.1 10.5 %shard_map.244 = (f32[512,2304]{1,0:T(8,128)}, bf16[512,2304]{1,0:T(8,128)(2,1)}, f32[8,2304]{1,0:T(8,128)}, f32[8,2304]{1,0:T(8,128)}) custom-call(bf16[512,2304]{1,0:T(8,128)(2,1)} %copy-done.4, f32[512,2304]{1,0:T(8,128)} %get-tuple-element.268.refs_1_, bf16[512,2304]{1,0:T(8,128)(2,1)} %copy-done.3, ...), custom_call_target="tpu_custom_call" | custom-call | flops 23592960 | bytes 28311552 | tf_op jit(solution)/shard_map/pallas_call | solution.py:187
  515.2 15.6 %shard_map.245 = (bf16[512,512]{1,0:T(8,128)(2,1)}, bf16[4,512,512]{2,1,0:T(8,128)(2,1)}) custom-call(s32[2]{0:T(128)} %get-tuple-element.481.scalars_ref, bf16[512,512]{1,0:T(8,128)(2,1)} %copy-done.46, bf16[512,512]{1,0:T(8,128)(2,1)} %fusion.30.d_ref, bf16[512,512]{1,0:T(8,128)(2,1)} %copy-done.20, bf16[2048,512]{1,0:T(8,128)(2,1)} %bitcast.93, ...), custom_call_target="tpu_custom_call" | custom-call | flops 5368709120 | bytes 8388608 | tf_op jit(solution)/shard_map/pallas_call | solution.py:459
  568.6 7.5 %shard_map.247 = (bf16[576,1024]{1,0:T(8,128)(2,1)}, bf16[288,1024]{1,0:T(8,128)(2,1)}, bf16[288,1024]{1,0:T(8,128)(2,1)}) custom-call(s32[2]{0:T(128)} %get-tuple-element.482.place_ref, bf16[512,2304]{1,0:T(8,128)(2,1)} %fusion.4.near_ref, bf16[512,1152]{1,0:T(8,128)(2,1)} %copy-done.66, bf16[512,1024]{1,0:T(8,128)(2,1)} %copy-done.27, ...), custom_call_target="tpu_custom_call" | custom-call | flops 2415919104 | bytes 6815744 | tf_op jit(solution)/shard_map/pallas_call | solution.py:381
  576.0 8.0 %collective-permute-done.65 = bf16[128,2304]{1,0:T(8,128)(2,1)} collective-permute-done((bf16[128,2304]{1,0:T(8,128)(2,1)}, bf16[128,2304]{1,0:T(8,128)(2,1)}, u32[]{:S(2)}, u32[]{:S(2)}) %collective-permute-start.65) | collective-permute-done | bytes 589856 | tf_op jit(solution)/shard_map/ppermute | solution.py:71
  591.8 7.2 %collective-permute-done.71 = bf16[288,1024]{1,0:T(8,128)(2,1)S(1)} collective-permute-done((bf16[288,1024]{1,0:T(8,128)(2,1)}, bf16[288,1024]{1,0:T(8,128)(2,1)S(1)}, u32[]{:S(2)}, u32[]{:S(2)}) %collective-permute-start.71) | collective-permute-done | bytes 589856 | tf_op jit(solution)/shard_map/ppermute | solution.py:66
  641.4 10.0 %collective-permute-done.80 = bf16[128,2304]{1,0:T(8,128)(2,1)S(1)} collective-permute-done((bf16[128,2304]{1,0:T(8,128)(2,1)}, bf16[128,2304]{1,0:T(8,128)(2,1)S(1)}, u32[]{:S(2)}, u32[]{:S(2)}) %collective-permute-start.80) | collective-permute-done | bytes 589856 | tf_op jit(solution)/shard_map/ppermute | solution.py:71
  653.2 12.0 %collective-permute-done.81 = bf16[128,2304]{1,0:T(8,128)(2,1)S(1)} collective-permute-done((bf16[128,2304]{1,0:T(8,128)(2,1)S(1)}, bf16[128,2304]{1,0:T(8,128)(2,1)S(1)}, u32[]{:S(2)}, u32[]{:S(2)}) %collective-permute-start.81) | collective-permute-done | bytes 589856 | tf_op jit(solution)/shard_map/ppermute | solution.py:71
  (438 shorter events, 290.3 us)
Async XLA Ops:
  7.2 57.6 %all-gather.3.cloned.1.call-start = ((), (), s32[]{:S(2)}) async-start(), calls=%async_computation.2 | async-start | bytes 7962624 | tf_op jit(solution)/shard_map/all_gather | solution.py:547
  11.4 21.7 %collective-permute-start = (bf16[288,768]{1,0:T(8,128)(2,1)}, bf16[288,768]{1,0:T(8,128)(2,1)S(1)}, u32[]{:S(2)}, u32[]{:S(2)}) collective-permute-start(bf16[288,768]{1,0:T(8,128)(2,1)} %slice_bitcast_fusion.6), channel_id=1, source_target_pairs={{0,4},{4,0},{8,12},{12,8},{1,5},{5,1},{9,13},{13,9},{2,6},{6,2},{1... | collective-permute-start | bytes 1327112 | tf_op jit(solution)/shard_map/ppermute | solution.py:66
  14.4 18.7 %collective-permute-start.1 = (bf16[288,768]{1,0:T(8,128)(2,1)}, bf16[288,768]{1,0:T(8,128)(2,1)S(1)}, u32[]{:S(2)}, u32[]{:S(2)}) collective-permute-start(bf16[288,768]{1,0:T(8,128)(2,1)} %slice_bitcast_fusion.6), channel_id=1, source_target_pairs={{0,8},{8,0},{4,12},{12,4},{1,9},{9,1},{5,13},{13,5},{2,10},{10,2},... | collective-permute-start | bytes 1327112 | tf_op jit(solution)/shard_map/ppermute | solution.py:66
  19.9 207.6 %all-gather.5.cloned.1.call-start = ((), (), s32[]{:S(2)}) async-start(), calls=%async_computation.3 | async-start | bytes 31850496 | tf_op jit(solution)/shard_map/all_gather | solution.py:547
  70.6 20.1 %collective-permute-start.2 = (bf16[1,512,512]{2,1,0:T(8,128)(2,1)S(1)}, bf16[1,512,512]{2,1,0:T(8,128)(2,1)S(1)}, u32[]{:S(2)}, u32[]{:S(2)}) collective-permute-start(bf16[1,512,512]{2,1,0:T(8,128)(2,1)S(1)} %get-tuple-element.466), channel_id=1, source_target_pairs={{0,4},{4,0},{8,12},{12,8},{1,5},{5,1},{9,13},{13,9},{2,6},{6,2},{1... | collective-permute-start | bytes 1572872 | tf_op jit(solution)/shard_map/ppermute | solution.py:66
  72.1 22.6 %collective-permute-start.3 = (bf16[1,512,512]{2,1,0:T(8,128)(2,1)S(1)}, bf16[1,512,512]{2,1,0:T(8,128)(2,1)S(1)}, u32[]{:S(2)}, u32[]{:S(2)}) collective-permute-start(bf16[1,512,512]{2,1,0:T(8,128)(2,1)S(1)} %get-tuple-element.466), channel_id=1, source_target_pairs={{0,8},{8,0},{4,12},{12,4},{1,9},{9,1},{5,13},{13,5},{2,10},{10,2},... | collective-permute-start | bytes 1572872 | tf_op jit(solution)/shard_map/ppermute | solution.py:66
  72.7 40.1 %collective-permute-start.4 = (bf16[1,512,512]{2,1,0:T(8,128)(2,1)S(1)}, bf16[1,512,512]{2,1,0:T(8,128)(2,1)}, u32[]{:S(2)}, u32[]{:S(2)}) collective-permute-start(bf16[1,512,512]{2,1,0:T(8,128)(2,1)S(1)} %get-tuple-element.466), channel_id=1, source_target_pairs={{0,12},{12,0},{4,8},{8,4},{1,13},{13,1},{5,9},{9,5},{2,14},{14,2},... | collective-permute-start | bytes 1572872 | tf_op jit(solution)/shard_map/ppermute | solution.py:66
  172.5 30.5 %collective-permute-start.17 = (bf16[1152,768]{1,0:T(8,128)(2,1)}, bf16[1152,768]{1,0:T(8,128)(2,1)S(1)}, u32[]{:S(2)}, u32[]{:S(2)}) collective-permute-start(bf16[1152,768]{1,0:T(8,128)(2,1)} %constant_dynamic-update-slice_fusion.26), channel_id=1, source_target_pairs={{0,16},{16,0},{1,17},{17,1},{2,18},{18,2},{3,19},{19,3},{4,20},{20... | collective-permute-start | bytes 5308424 | tf_op jit(solution)/shard_map/ppermute | solution.py:66
  184.4 18.6 %collective-permute-start.15 = (bf16[64,2304]{1,0:T(8,128)(2,1)S(1)}, bf16[64,2304]{1,0:T(8,128)(2,1)S(1)}, u32[]{:S(2)}, u32[]{:S(2)}) collective-permute-start(bf16[64,2304]{1,0:T(8,128)(2,1)S(1)} %collective-permute-done.13), channel_id=1, source_target_pairs={{0,1},{1,2},{2,3},{3,0},{4,5},{5,6},{6,7},{7,4},{8,9},{9,10},{10,1... | collective-permute-start | bytes 884744 | tf_op jit(solution)/shard_map/ppermute | solution.py:71
  257.5 29.4 %collective-permute-start.26 = (bf16[512,1152]{1,0:T(8,128)(2,1)S(1)}, bf16[512,1152]{1,0:T(8,128)(2,1)S(1)}, u32[]{:S(2)}, u32[]{:S(2)}) collective-permute-start(bf16[512,1152]{1,0:T(8,128)(2,1)S(1)} %constant_dynamic-slice_fusion.5), channel_id=1, source_target_pairs={{0,16},{16,0},{1,17},{17,1},{2,18},{18,2},{3,19},{19,3},{4,20},{20... | collective-permute-start | bytes 3538952 | tf_op jit(solution)/shard_map/ppermute | solution.py:66
  257.6 29.3 %collective-permute-start.24 = (bf16[512,2304]{1,0:T(8,128)(2,1)}, bf16[512,2304]{1,0:T(8,128)(2,1)S(1)}, u32[]{:S(2)}, u32[]{:S(2)}) collective-permute-start(bf16[512,2304]{1,0:T(8,128)(2,1)} %get-tuple-element.251.cols_ref), channel_id=1, source_target_pairs={{0,16},{16,0},{1,17},{17,1},{2,18},{18,2},{3,19},{19,3},{4,20},{20... | collective-permute-start | bytes 7077896 | tf_op jit(solution)/shard_map/ppermute | solution.py:66
  258.2 28.7 %collective-permute-start.27 = (bf16[512,1152]{1,0:T(8,128)(2,1)S(1)}, bf16[512,1152]{1,0:T(8,128)(2,1)S(1)}, u32[]{:S(2)}, u32[]{:S(2)}) collective-permute-start(bf16[512,1152]{1,0:T(8,128)(2,1)S(1)} %constant_dynamic-slice_fusion.4), channel_id=1, source_target_pairs={{0,16},{16,0},{1,17},{17,1},{2,18},{18,2},{3,19},{19,3},{4,20},{20... | collective-permute-start | bytes 3538952 | tf_op jit(solution)/shard_map/ppermute | solution.py:66
  350.4 28.9 %collective-permute-start.36 = (bf16[512,1152]{1,0:T(8,128)(2,1)S(1)}, bf16[512,1152]{1,0:T(8,128)(2,1)S(1)}, u32[]{:S(2)}, u32[]{:S(2)}) collective-permute-start(bf16[512,1152]{1,0:T(8,128)(2,1)S(1)} %constant_dynamic-slice_fusion.3), channel_id=1, source_target_pairs={{0,16},{16,0},{1,17},{17,1},{2,18},{18,2},{3,19},{19,3},{4,20},{20... | collective-permute-start | bytes 3538952 | tf_op jit(solution)/shard_map/ppermute | solution.py:66
  379.3 19.2 %collective-permute-start.38 = (bf16[512,2304]{1,0:T(8,128)(2,1)}, bf16[512,2304]{1,0:T(8,128)(2,1)}, u32[]{:S(2)}, u32[]{:S(2)}) collective-permute-start(bf16[512,2304]{1,0:T(8,128)(2,1)} %get-tuple-element.285.cols_ref), channel_id=1, source_target_pairs={{0,16},{16,0},{1,17},{17,1},{2,18},{18,2},{3,19},{19,3},{4,20},{20... | collective-permute-start | bytes 7077896 | tf_op jit(solution)/shard_map/ppermute | solution.py:66
  379.9 33.5 %collective-permute-start.40 = (bf16[512,2304]{1,0:T(8,128)(2,1)}, bf16[512,2304]{1,0:T(8,128)(2,1)}, u32[]{:S(2)}, u32[]{:S(2)}) collective-permute-start(bf16[512,2304]{1,0:T(8,128)(2,1)} %get-tuple-element.294.cols_ref), channel_id=1, source_target_pairs={{0,16},{16,0},{1,17},{17,1},{2,18},{18,2},{3,19},{19,3},{4,20},{20... | collective-permute-start | bytes 7077896 | tf_op jit(solution)/shard_map/ppermute | solution.py:66
  398.6 19.6 %collective-permute-start.41 = (bf16[144,2304]{1,0:T(8,128)(2,1)}, bf16[144,2304]{1,0:T(8,128)(2,1)}, u32[]{:S(2)}, u32[]{:S(2)}) collective-permute-start(bf16[144,2304]{1,0:T(8,128)(2,1)} %get-tuple-element.295), channel_id=1, source_target_pairs={{0,4},{4,0},{8,12},{12,8},{1,5},{5,1},{9,13},{13,9},{2,6},{6,2},{1... | collective-permute-start | bytes 1990664 | tf_op jit(solution)/shard_map/ppermute | solution.py:66
  401.8 33.6 %collective-permute-start.44 = (bf16[144,2304]{1,0:T(8,128)(2,1)}, bf16[144,2304]{1,0:T(8,128)(2,1)S(1)}, u32[]{:S(2)}, u32[]{:S(2)}) collective-permute-start(bf16[144,2304]{1,0:T(8,128)(2,1)} %get-tuple-element.304), channel_id=1, source_target_pairs={{0,4},{4,0},{8,12},{12,8},{1,5},{5,1},{9,13},{13,9},{2,6},{6,2},{1... | collective-permute-start | bytes 1990664 | tf_op jit(solution)/shard_map/ppermute | solution.py:66
  413.4 22.0 %collective-permute-start.45 = (bf16[144,2304]{1,0:T(8,128)(2,1)}, bf16[144,2304]{1,0:T(8,128)(2,1)S(1)}, u32[]{:S(2)}, u32[]{:S(2)}) collective-permute-start(bf16[144,2304]{1,0:T(8,128)(2,1)} %get-tuple-element.305), channel_id=1, source_target_pairs={{0,8},{8,0},{4,12},{12,4},{1,9},{9,1},{5,13},{13,5},{2,10},{10,2},... | collective-permute-start | bytes 1990664 | tf_op jit(solution)/shard_map/ppermute | solution.py:66
  422.1 21.7 %collective-permute-start.47 = (bf16[144,2304]{1,0:T(8,128)(2,1)}, bf16[144,2304]{1,0:T(8,128)(2,1)}, u32[]{:S(2)}, u32[]{:S(2)}) collective-permute-start(bf16[144,2304]{1,0:T(8,128)(2,1)} %get-tuple-element.450), channel_id=1, source_target_pairs={{0,4},{4,0},{8,12},{12,8},{1,5},{5,1},{9,13},{13,9},{2,6},{6,2},{1... | collective-permute-start | bytes 1990664 | tf_op jit(solution)/shard_map/ppermute | solution.py:66
  422.4 22.7 %collective-permute-start.48 = (bf16[144,2304]{1,0:T(8,128)(2,1)}, bf16[144,2304]{1,0:T(8,128)(2,1)}, u32[]{:S(2)}, u32[]{:S(2)}) collective-permute-start(bf16[144,2304]{1,0:T(8,128)(2,1)} %get-tuple-element.449), channel_id=1, source_target_pairs={{0,8},{8,0},{4,12},{12,4},{1,9},{9,1},{5,13},{13,5},{2,10},{10,2},... | collective-permute-start | bytes 1990664 | tf_op jit(solution)/shard_map/ppermute | solution.py:66
  452.7 18.1 %collective-permute-start.50 = (bf16[144,2304]{1,0:T(8,128)(2,1)}, bf16[144,2304]{1,0:T(8,128)(2,1)S(1)}, u32[]{:S(2)}, u32[]{:S(2)}) collective-permute-start(bf16[144,2304]{1,0:T(8,128)(2,1)} %get-tuple-element.316), channel_id=1, source_target_pairs={{0,4},{4,0},{8,12},{12,8},{1,5},{5,1},{9,13},{13,9},{2,6},{6,2},{1... | collective-permute-start | bytes 1990664 | tf_op jit(solution)/shard_map/ppermute | solution.py:66
  454.7 29.5 %collective-permute-start.53 = (bf16[144,2304]{1,0:T(8,128)(2,1)}, bf16[144,2304]{1,0:T(8,128)(2,1)S(1)}, u32[]{:S(2)}, u32[]{:S(2)}) collective-permute-start(bf16[144,2304]{1,0:T(8,128)(2,1)} %get-tuple-element.330), channel_id=1, source_target_pairs={{0,4},{4,0},{8,12},{12,8},{1,5},{5,1},{9,13},{13,9},{2,6},{6,2},{1... | collective-permute-start | bytes 1990664 | tf_op jit(solution)/shard_map/ppermute | solution.py:66
  455.0 29.2 %collective-permute-start.54 = (bf16[144,2304]{1,0:T(8,128)(2,1)}, bf16[144,2304]{1,0:T(8,128)(2,1)S(1)}, u32[]{:S(2)}, u32[]{:S(2)}) collective-permute-start(bf16[144,2304]{1,0:T(8,128)(2,1)} %get-tuple-element.331), channel_id=1, source_target_pairs={{0,8},{8,0},{4,12},{12,4},{1,9},{9,1},{5,13},{13,5},{2,10},{10,2},... | collective-permute-start | bytes 1990664 | tf_op jit(solution)/shard_map/ppermute | solution.py:66
  485.3 20.1 %collective-permute-start.55 = (bf16[144,2304]{1,0:T(8,128)(2,1)S(1)}, bf16[144,2304]{1,0:T(8,128)(2,1)S(1)}, u32[]{:S(2)}, u32[]{:S(2)}) collective-permute-start(bf16[144,2304]{1,0:T(8,128)(2,1)S(1)} %get-tuple-element.446), channel_id=1, source_target_pairs={{0,4},{4,0},{8,12},{12,8},{1,5},{5,1},{9,13},{13,9},{2,6},{6,2},{1... | collective-permute-start | bytes 1990664 | tf_op jit(solution)/shard_map/ppermute | solution.py:66
  485.8 19.6 %collective-permute-start.56 = (bf16[144,2304]{1,0:T(8,128)(2,1)S(1)}, bf16[144,2304]{1,0:T(8,128)(2,1)S(1)}, u32[]{:S(2)}, u32[]{:S(2)}) collective-permute-start(bf16[144,2304]{1,0:T(8,128)(2,1)S(1)} %get-tuple-element.445), channel_id=1, source_target_pairs={{0,8},{8,0},{4,12},{12,4},{1,9},{9,1},{5,13},{13,5},{2,10},{10,2},... | collective-permute-start | bytes 1990664 | tf_op jit(solution)/shard_map/ppermute | solution.py:66
  501.3 29.5 %collective-permute-start.59 = (bf16[512,1152]{1,0:T(8,128)(2,1)S(1)}, bf16[512,1152]{1,0:T(8,128)(2,1)S(1)}, u32[]{:S(2)}, u32[]{:S(2)}) collective-permute-start(bf16[512,1152]{1,0:T(8,128)(2,1)S(1)} %constant_dynamic-slice_fusion.1), channel_id=1, source_target_pairs={{0,16},{16,0},{1,17},{17,1},{2,18},{18,2},{3,19},{19,3},{4,20},{20... | collective-permute-start | bytes 3538952 | tf_op jit(solution)/shard_map/ppermute | solution.py:66
  511.9 18.9 %collective-permute-start.60 = (bf16[144,2304]{1,0:T(8,128)(2,1)}, bf16[144,2304]{1,0:T(8,128)(2,1)S(1)}, u32[]{:S(2)}, u32[]{:S(2)}) collective-permute-start(bf16[144,2304]{1,0:T(8,128)(2,1)} %get-tuple-element.344), channel_id=1, source_target_pairs={{0,4},{4,0},{8,12},{12,8},{1,5},{5,1},{9,13},{13,9},{2,6},{6,2},{1... | collective-permute-start | bytes 1990664 | tf_op jit(solution)/shard_map/ppermute | solution.py:66
  535.1 19.2 %collective-permute-start.63 = (bf16[512,512]{1,0:T(8,128)(2,1)}, bf16[512,512]{1,0:T(8,128)(2,1)S(1)}, u32[]{:S(2)}, u32[]{:S(2)}) collective-permute-start(bf16[512,512]{1,0:T(8,128)(2,1)} %get-tuple-element.456), channel_id=1, source_target_pairs={{0,8},{8,0},{4,12},{12,4},{1,9},{9,1},{5,13},{13,5},{2,10},{10,2},... | collective-permute-start | bytes 1572872 | tf_op jit(solution)/shard_map/ppermute | solution.py:66
  536.6 19.1 %collective-permute-start.64 = (bf16[512,512]{1,0:T(8,128)(2,1)S(1)}, bf16[512,512]{1,0:T(8,128)(2,1)S(1)}, u32[]{:S(2)}, u32[]{:S(2)}) collective-permute-start(bf16[512,512]{1,0:T(8,128)(2,1)S(1)} %get-tuple-element.455), channel_id=1, source_target_pairs={{0,12},{12,0},{4,8},{8,4},{1,13},{13,1},{5,9},{9,5},{2,14},{14,2},... | collective-permute-start | bytes 1572872 | tf_op jit(solution)/shard_map/ppermute | solution.py:66
  563.3 20.7 %collective-permute-start.67 = (bf16[144,2304]{1,0:T(8,128)(2,1)}, bf16[144,2304]{1,0:T(8,128)(2,1)}, u32[]{:S(2)}, u32[]{:S(2)}) collective-permute-start(bf16[144,2304]{1,0:T(8,128)(2,1)} %get-tuple-element.442), channel_id=1, source_target_pairs={{0,4},{4,0},{8,12},{12,8},{1,5},{5,1},{9,13},{13,9},{2,6},{6,2},{1... | collective-permute-start | bytes 1990664 | tf_op jit(solution)/shard_map/ppermute | solution.py:66
  564.2 19.9 %collective-permute-start.68 = (bf16[144,2304]{1,0:T(8,128)(2,1)}, bf16[144,2304]{1,0:T(8,128)(2,1)}, u32[]{:S(2)}, u32[]{:S(2)}) collective-permute-start(bf16[144,2304]{1,0:T(8,128)(2,1)} %get-tuple-element.441), channel_id=1, source_target_pairs={{0,8},{8,0},{4,12},{12,4},{1,9},{9,1},{5,13},{13,5},{2,10},{10,2},... | collective-permute-start | bytes 1990664 | tf_op jit(solution)/shard_map/ppermute | solution.py:66
  624.8 41.3 %all-to-all-start.1 = ((f32[32,4,288]{2,1,0:T(4,128)}), f32[32,4,288]{2,1,0:T(4,128)S(1)}, u32[]{:S(2)}, u32[]{:S(2)}) async-start(f32[32,4,288]{2,1,0:T(4,128)} %bitcast.30), calls=%async_computation.1 | async-start | bytes 393216 | tf_op jit(solution)/shard_map/all_to_all | solution.py:734
  (126 other events, 2046.8 us)
Sparse Core Ops, SparseCore 0:
  10.5 54.2 all-gather.2
  66.7 159.6 all-gather.4

commit v7 on v6

--- a/solution.py
+++ b/solution.py
@@ -516,6 +516,11 @@
     return dafter, dattn, dffn_in * normed, dafter * normed_two
 
 
+def input_back_rows(dattn_in, hidden, dafter, scale_one):
+    normed, factor = normalize(hidden.astype(F32))
+    return (dafter + norm_back(dattn_in.astype(F32) * scale_one, normed, factor),)
+
+
 def plane_body(
     hidden_in,
     lengths,
@@ -610,7 +615,7 @@
     rest_far = send("core", rest_near)
     ring.go()
     ring.go()
-    ring.going, rest_far = tied(ring.going, rest_far)
+    ring.going[1], rest_far = tied(ring.going[1], rest_far)
     ring.go()
     down_rest = place([rest_near, rest_far], [core * half_width, (1 - core) * half_width])
     attn = ring.finish()
@@ -630,8 +635,8 @@
         valid.reshape(row_count, 1), cotangent.reshape(row_count, width), jnp.zeros((), BF)
     )
     ring.go()
-    ring.going, hidden_far, attended_far, ffn_in_far, attention_input_far, cot = tied(
-        ring.going, hidden_far, attended_far, ffn_in_far, attention_input_far, cot
+    ring.going[0], hidden_far, attended_far, ffn_in_far, attention_input_far, cot = tied(
+        ring.going[0], hidden_far, attended_far, ffn_in_far, attention_input_far, cot
     )
     ffn_out = ring.finish()
     output, dffn_b, gain_four_rows = rowwise(
@@ -740,9 +745,7 @@
     ring.go()
     dattn_in, grad_gains = tied(ring.finish(), grad_gains)
     grad_gains = jnp.sum(grad_gains, 0)
-    dattn_in = dattn_in.astype(F32)
-    grad_input = dafter + norm_back(dattn_in * scale_one, normed_one, factor_one)
-    grad_input = grad_input.astype(BF)
+    (grad_input,) = rowwise(input_back_rows, [dattn_in, hidden_rows, dafter], [scale_one], [BF])
     return (
         output.reshape(hidden_in.shape),
         grad_input.reshape(hidden_in.shape),

time: 693 us -> 692 us (level)
  Pallas kernels: 143 us -> 150 us
    ppermute x36, waiting for transfers between devices: 218 us -> 211 us  [around(): lax.ppermute(value, 'tp', [(i, (i + by) % size) for i in range(size)])]
    pallas_call x3 -> x4, Pallas kernels: 25 us -> 32.1 us  [rowwise(): pl.pallas_call(kernel, grid=(count // block,), in_specs=[by_row] * len(ro...]
  transfers between devices with their start and end apart: 86 -> 86, of which waited for: 49 -> 53; matrix products, arithmetic and copies ran while one was open for 13% -> 13% of each run, Pallas kernels for 16% -> 16%
where the time goes in v7:
time: 692 us; the launch traced here: 681 us
  waiting for transfers between devices  335 us (48%)
  Pallas kernels  150 us (22%)
  starting transfers between devices  64.2 us (9%)
  other arithmetic  48.3 us (7%)
  local copies, waits for them, and re-layouts  44 us (6%)
  matrix products  23.4 us (3%)
  between operations  16.6 us (2%)
    ppermute x36, waiting for transfers between devices, around(): lax.ppermute(value, 'tp', [(i, (i + by) % size) for i in range(size)])  211 us
    ppermute x46, waiting for transfers between devices, send(): return lax.ppermute(value, *LINKS[link])  81.2 us
    pallas_call x5, Pallas kernels, weight_grad(): pl.pallas_call(kernel, grid_spec=pltpu.PrefetchScalarGridSpec(num_scalar_...  46.3 us
    ppermute x46, starting transfers between devices, send(): return lax.ppermute(value, *LINKS[link])  43.6 us
    all_gather x2, waiting for transfers between devices, gather(): return lax.all_gather(shard, ('fsdp', 'ctx'), axis=0, tiled=True)  37.4 us
    pallas_call x4, Pallas kernels, rowwise(): pl.pallas_call(kernel, grid=(count // block,), in_specs=[by_row] * len(ro...  32.1 us
    pallas_call x1, Pallas kernels, ffn_backward(): pl.pallas_call(kernel, grid=(first + width // out_cut,), in_specs=[pl.Blo...  28.8 us
    pallas_call x1, Pallas kernels, ffn_forward(): pl.pallas_call(kernel, grid=(first + width // out_cut,), in_specs=[pl.Blo...  26.8 us
  transfers between devices with their start and end apart: 86, of which 53 were waited for; matrix products, arithmetic and copies ran while one was open for 13% of the time, Pallas kernels for 16%

profile of v7, /device:TPU:0, one launch (start us, length us, event | category | flops | bytes accessed | tf_op | source)
XLA Modules:
  0.0 681.2 jit_solution(4803271589240070651)
XLA Ops:
  33.1 31.7 %all-gather.3.cloned.1.call-done = bf16[2304,1536]{1,0:T(8,128)(2,1)} async-done(((bf16[288,1536]{1,0:T(8,128)(2,1)}), bf16[2304,1536]{1,0:T(8,128)(2,1)}) %all-gather.3.cloned.1.call-update) | async-done | bytes 7077904 | tf_op jit(solution)/shard_map/all_gather | solution.py:552
  75.7 14.9 %collective-permute-done.2 = bf16[1,512,512]{2,1,0:T(8,128)(2,1)S(1)} collective-permute-done((bf16[1,512,512]{2,1,0:T(8,128)(2,1)S(1)}, bf16[1,512,512]{2,1,0:T(8,128)(2,1)S(1)}, u32[]{:S(2)}, u32[]{:S(2)}) %collective-permute-start.2) | collective-permute-done | bytes 524320 | tf_op jit(solution)/shard_map/ppermute | solution.py:66
  94.7 18.0 %collective-permute-done.4 = bf16[1,512,512]{2,1,0:T(8,128)(2,1)} collective-permute-done((bf16[1,512,512]{2,1,0:T(8,128)(2,1)S(1)}, bf16[1,512,512]{2,1,0:T(8,128)(2,1)}, u32[]{:S(2)}, u32[]{:S(2)}) %collective-permute-start.4) | collective-permute-done | bytes 524320 | tf_op jit(solution)/shard_map/ppermute | solution.py:66
  143.3 7.9 %collective-permute-done.9 = bf16[64,2304]{1,0:T(8,128)(2,1)S(1)} collective-permute-done((bf16[64,2304]{1,0:T(8,128)(2,1)}, bf16[64,2304]{1,0:T(8,128)(2,1)S(1)}, u32[]{:S(2)}, u32[]{:S(2)}) %collective-permute-start.9) | collective-permute-done | bytes 294944 | tf_op jit(solution)/shard_map/ppermute | solution.py:71
  176.8 7.7 %collective-permute-done.13 = bf16[64,2304]{1,0:T(8,128)(2,1)S(1)} collective-permute-done((bf16[64,2304]{1,0:T(8,128)(2,1)S(1)}, bf16[64,2304]{1,0:T(8,128)(2,1)S(1)}, u32[]{:S(2)}, u32[]{:S(2)}) %collective-permute-start.13) | collective-permute-done | bytes 294944 | tf_op jit(solution)/shard_map/ppermute | solution.py:71
  184.5 6.3 collective-permute-done.14
  190.9 6.3 collective-permute-done.15
  197.2 6.3 collective-permute-done.16
  203.5 6.3 collective-permute-done.18
  214.3 6.3 shard_map.237
  226.3 26.8 %shard_map.238 = (f32[512,2304]{1,0:T(8,128)}, f32[512,2304]{1,0:T(8,128)}, bf16[512,2304]{1,0:T(8,128)(2,1)}, bf16[512,2304]{1,0:T(8,128)(2,1)}) custom-call(bf16[512,2304]{1,0:T(8,128)(2,1)} %get-tuple-element.249.x_ref.near_ref, bf16[2304,6144]{1,0:T(8,128)(2,1)} %all-gather.5.cloned.1.call-done.gate_w.up_w.down_w, ...), custom_call_target="tpu_custom_call" | custom-call | flops 16307453952 | bytes 43646976 | tf_op jit(solution)/shard_map/pallas_call | solution.py:246
  273.1 10.4 %collective-permute-done.21 = bf16[64,2304]{1,0:T(8,128)(2,1)S(1)} collective-permute-done((bf16[64,2304]{1,0:T(8,128)(2,1)S(1)}, bf16[64,2304]{1,0:T(8,128)(2,1)S(1)}, u32[]{:S(2)}, u32[]{:S(2)}) %collective-permute-start.21) | collective-permute-done | bytes 294944 | tf_op jit(solution)/shard_map/ppermute | solution.py:71
  309.0 6.3 collective-permute-done.31
  315.4 6.3 collective-permute-done.32
  321.7 6.3 collective-permute-done.33
  328.4 10.3 %collective-permute-done.35 = bf16[64,2304]{1,0:T(8,128)(2,1)S(1)} collective-permute-done((bf16[64,2304]{1,0:T(8,128)(2,1)S(1)}, bf16[64,2304]{1,0:T(8,128)(2,1)S(1)}, u32[]{:S(2)}, u32[]{:S(2)}) %collective-permute-start.35) | collective-permute-done | bytes 294944 | tf_op jit(solution)/shard_map/ppermute | solution.py:71
  340.2 8.3 %shard_map.239 = (bf16[512,2304]{1,0:T(8,128)(2,1)}, bf16[512,2304]{1,0:T(8,128)(2,1)}, f32[8,2304]{1,0:T(8,128)}) custom-call(bf16[512,2304]{1,0:T(8,128)(2,1)} %copy-done.10, f32[512,2304]{1,0:T(8,128)} %get-tuple-element.264.refs_1_, bf16[512,2304]{1,0:T(8,128)(2,1)} %bitcast_select_fusion.1.refs_2_.refs_3_, f32[1,2304]{1,0:T(1,128)} %add.627.refs_3_), custom_call_target="tpu_custom_call" | custom-call | flops 23592960 | bytes 18874368 | tf_op jit(solution)/shard_map/pallas_call | solution.py:187
  350.0 28.8 %shard_map.240 = (bf16[512,2304]{1,0:T(8,128)(2,1)}, bf16[512,2304]{1,0:T(8,128)(2,1)}, bf16[512,2304]{1,0:T(8,128)(2,1)}) custom-call(bf16[512,2304]{1,0:T(8,128)(2,1)} %get-tuple-element.267.d_ref.near_ref, bf16[2304,6144]{1,0:T(8,128)(2,1)} %all-gather.5.cloned.1.call-done.gate_w.up_w.down_w, bf16[2304,768]{1,0:T(8,128)(2,1)} %copy-done.2, ...), custom_call_target="tpu_custom_call" | custom-call | flops 16307453952 | bytes 46006272 | tf_op jit(solution)/shard_map/pallas_call | solution.py:323
  381.3 11.3 %shard_map.241 = (bf16[576,2304]{1,0:T(8,128)(2,1)}, bf16[144,2304]{1,0:T(8,128)(2,1)}, bf16[144,2304]{1,0:T(8,128)(2,1)}, bf16[144,2304]{1,0:T(8,128)(2,1)}, bf16[144,2304]{1,0:T(8,128)(2,1)}) custom-call(s32[2]{0:T(128)} %get-tuple-element.478.place_ref, bf16[512,2304]{1,0:T(8,128)(2,1)} %get-tuple-element.267.d_ref.near_ref, ...), custom_call_target="tpu_custom_call" | custom-call | flops 5435817984 | bytes 12386304 | tf_op jit(solution)/shard_map/pallas_call | solution.py:381
  401.8 11.3 %shard_map.242 = (bf16[576,2304]{1,0:T(8,128)(2,1)}, bf16[144,2304]{1,0:T(8,128)(2,1)}, bf16[144,2304]{1,0:T(8,128)(2,1)}, bf16[144,2304]{1,0:T(8,128)(2,1)}, bf16[144,2304]{1,0:T(8,128)(2,1)}) custom-call(s32[2]{0:T(128)} %get-tuple-element.478.place_ref, bf16[512,2304]{1,0:T(8,128)(2,1)} %get-tuple-element.249.x_ref.near_ref, ...), custom_call_target="tpu_custom_call" | custom-call | flops 5435817984 | bytes 12386304 | tf_op jit(solution)/shard_map/pallas_call | solution.py:381
  423.7 11.2 %shard_map.243 = (bf16[576,2304]{1,0:T(8,128)(2,1)}, bf16[144,2304]{1,0:T(8,128)(2,1)}, bf16[144,2304]{1,0:T(8,128)(2,1)}, bf16[144,2304]{1,0:T(8,128)(2,1)}, bf16[144,2304]{1,0:T(8,128)(2,1)}) custom-call(s32[2]{0:T(128)} %get-tuple-element.478.place_ref, bf16[512,2304]{1,0:T(8,128)(2,1)} %get-tuple-element.249.x_ref.near_ref, ...), custom_call_target="tpu_custom_call" | custom-call | flops 5435817984 | bytes 12386304 | tf_op jit(solution)/shard_map/pallas_call | solution.py:381
  444.6 7.7 %collective-permute-done.46 = bf16[128,2304]{1,0:T(8,128)(2,1)} collective-permute-done((bf16[128,2304]{1,0:T(8,128)(2,1)}, bf16[128,2304]{1,0:T(8,128)(2,1)}, u32[]{:S(2)}, u32[]{:S(2)}) %collective-permute-start.46) | collective-permute-done | bytes 589856 | tf_op jit(solution)/shard_map/ppermute | solution.py:71
  460.3 7.4 %collective-permute-done.49 = bf16[128,2304]{1,0:T(8,128)(2,1)S(1)} collective-permute-done((bf16[128,2304]{1,0:T(8,128)(2,1)}, bf16[128,2304]{1,0:T(8,128)(2,1)S(1)}, u32[]{:S(2)}, u32[]{:S(2)}) %collective-permute-start.49) | collective-permute-done | bytes 589856 | tf_op jit(solution)/shard_map/ppermute | solution.py:71
  473.2 10.5 %collective-permute-done.52 = bf16[128,2304]{1,0:T(8,128)(2,1)S(1)} collective-permute-done((bf16[128,2304]{1,0:T(8,128)(2,1)S(1)}, bf16[128,2304]{1,0:T(8,128)(2,1)S(1)}, u32[]{:S(2)}, u32[]{:S(2)}) %collective-permute-start.52) | collective-permute-done | bytes 589856 | tf_op jit(solution)/shard_map/ppermute | solution.py:71
  486.5 10.4 %shard_map.244 = (f32[512,2304]{1,0:T(8,128)}, bf16[512,2304]{1,0:T(8,128)(2,1)}, f32[8,2304]{1,0:T(8,128)}, f32[8,2304]{1,0:T(8,128)}) custom-call(bf16[512,2304]{1,0:T(8,128)(2,1)} %copy-done.4, f32[512,2304]{1,0:T(8,128)} %get-tuple-element.264.refs_1_, bf16[512,2304]{1,0:T(8,128)(2,1)} %copy-done.3, ...), custom_call_target="tpu_custom_call" | custom-call | flops 23592960 | bytes 28311552 | tf_op jit(solution)/shard_map/pallas_call | solution.py:187
  515.9 15.6 %shard_map.245 = (bf16[512,512]{1,0:T(8,128)(2,1)}, bf16[4,512,512]{2,1,0:T(8,128)(2,1)}) custom-call(s32[2]{0:T(128)} %get-tuple-element.477.scalars_ref, bf16[512,512]{1,0:T(8,128)(2,1)} %copy-done.49, bf16[512,512]{1,0:T(8,128)(2,1)} %fusion.22.d_ref, bf16[512,512]{1,0:T(8,128)(2,1)} %copy-done.23, bf16[2048,512]{1,0:T(8,128)(2,1)} %bitcast.92, ...), custom_call_target="tpu_custom_call" | custom-call | flops 5368709120 | bytes 8388608 | tf_op jit(solution)/shard_map/pallas_call | solution.py:459
  569.0 7.5 %shard_map.247 = (bf16[576,1024]{1,0:T(8,128)(2,1)}, bf16[288,1024]{1,0:T(8,128)(2,1)}, bf16[288,1024]{1,0:T(8,128)(2,1)}) custom-call(s32[2]{0:T(128)} %get-tuple-element.478.place_ref, bf16[512,2304]{1,0:T(8,128)(2,1)} %fusion.2.near_ref, bf16[512,1152]{1,0:T(8,128)(2,1)} %copy-done.67, bf16[512,1024]{1,0:T(8,128)(2,1)} %copy-done.30, ...), custom_call_target="tpu_custom_call" | custom-call | flops 2415919104 | bytes 6815744 | tf_op jit(solution)/shard_map/pallas_call | solution.py:381
  576.5 7.9 %collective-permute-done.65 = bf16[128,2304]{1,0:T(8,128)(2,1)} collective-permute-done((bf16[128,2304]{1,0:T(8,128)(2,1)}, bf16[128,2304]{1,0:T(8,128)(2,1)}, u32[]{:S(2)}, u32[]{:S(2)}) %collective-permute-start.65) | collective-permute-done | bytes 589856 | tf_op jit(solution)/shard_map/ppermute | solution.py:71
  592.0 7.4 %collective-permute-done.71 = bf16[288,1024]{1,0:T(8,128)(2,1)S(1)} collective-permute-done((bf16[288,1024]{1,0:T(8,128)(2,1)}, bf16[288,1024]{1,0:T(8,128)(2,1)S(1)}, u32[]{:S(2)}, u32[]{:S(2)}) %collective-permute-start.71) | collective-permute-done | bytes 589856 | tf_op jit(solution)/shard_map/ppermute | solution.py:66
  640.9 10.9 %collective-permute-done.80 = bf16[128,2304]{1,0:T(8,128)(2,1)S(1)} collective-permute-done((bf16[128,2304]{1,0:T(8,128)(2,1)}, bf16[128,2304]{1,0:T(8,128)(2,1)S(1)}, u32[]{:S(2)}, u32[]{:S(2)}) %collective-permute-start.80) | collective-permute-done | bytes 589856 | tf_op jit(solution)/shard_map/ppermute | solution.py:71
  652.6 12.8 %collective-permute-done.81 = bf16[128,2304]{1,0:T(8,128)(2,1)S(1)} collective-permute-done((bf16[128,2304]{1,0:T(8,128)(2,1)S(1)}, bf16[128,2304]{1,0:T(8,128)(2,1)S(1)}, u32[]{:S(2)}, u32[]{:S(2)}) %collective-permute-start.81) | collective-permute-done | bytes 589856 | tf_op jit(solution)/shard_map/ppermute | solution.py:71
  666.9 7.0 %shard_map.248 = bf16[512,2304]{1,0:T(8,128)(2,1)} custom-call(bf16[512,2304]{1,0:T(8,128)(2,1)} %copy-done.9, bf16[512,2304]{1,0:T(8,128)(2,1)} %bitcast.90, f32[512,2304]{1,0:T(8,128)} %get-tuple-element.408.refs_2_, f32[1,2304]{1,0:T(1,128)} %add.673.refs_3_), custom_call_target="tpu_custom_call" | custom-call | flops 23592960 | bytes 18874368 | tf_op jit(solution)/shard_map/pallas_call | solution.py:187
  (437 shorter events, 310.4 us)
Async XLA Ops:
  7.2 57.6 %all-gather.3.cloned.1.call-start = ((), (), s32[]{:S(2)}) async-start(), calls=%async_computation.2 | async-start | bytes 7962624 | tf_op jit(solution)/shard_map/all_gather | solution.py:552
  11.4 21.7 %collective-permute-start = (bf16[288,768]{1,0:T(8,128)(2,1)}, bf16[288,768]{1,0:T(8,128)(2,1)S(1)}, u32[]{:S(2)}, u32[]{:S(2)}) collective-permute-start(bf16[288,768]{1,0:T(8,128)(2,1)} %slice_bitcast_fusion.6), channel_id=1, source_target_pairs={{0,4},{4,0},{8,12},{12,8},{1,5},{5,1},{9,13},{13,9},{2,6},{6,2},{1... | collective-permute-start | bytes 1327112 | tf_op jit(solution)/shard_map/ppermute | solution.py:66
  14.4 18.7 %collective-permute-start.1 = (bf16[288,768]{1,0:T(8,128)(2,1)}, bf16[288,768]{1,0:T(8,128)(2,1)S(1)}, u32[]{:S(2)}, u32[]{:S(2)}) collective-permute-start(bf16[288,768]{1,0:T(8,128)(2,1)} %slice_bitcast_fusion.6), channel_id=1, source_target_pairs={{0,8},{8,0},{4,12},{12,4},{1,9},{9,1},{5,13},{13,5},{2,10},{10,2},... | collective-permute-start | bytes 1327112 | tf_op jit(solution)/shard_map/ppermute | solution.py:66
  19.9 206.4 %all-gather.5.cloned.1.call-start = ((), (), s32[]{:S(2)}) async-start(), calls=%async_computation.3 | async-start | bytes 31850496 | tf_op jit(solution)/shard_map/all_gather | solution.py:552
  70.6 20.1 %collective-permute-start.2 = (bf16[1,512,512]{2,1,0:T(8,128)(2,1)S(1)}, bf16[1,512,512]{2,1,0:T(8,128)(2,1)S(1)}, u32[]{:S(2)}, u32[]{:S(2)}) collective-permute-start(bf16[1,512,512]{2,1,0:T(8,128)(2,1)S(1)} %get-tuple-element.462), channel_id=1, source_target_pairs={{0,4},{4,0},{8,12},{12,8},{1,5},{5,1},{9,13},{13,9},{2,6},{6,2},{1... | collective-permute-start | bytes 1572872 | tf_op jit(solution)/shard_map/ppermute | solution.py:66
  72.1 22.6 %collective-permute-start.3 = (bf16[1,512,512]{2,1,0:T(8,128)(2,1)S(1)}, bf16[1,512,512]{2,1,0:T(8,128)(2,1)S(1)}, u32[]{:S(2)}, u32[]{:S(2)}) collective-permute-start(bf16[1,512,512]{2,1,0:T(8,128)(2,1)S(1)} %get-tuple-element.462), channel_id=1, source_target_pairs={{0,8},{8,0},{4,12},{12,4},{1,9},{9,1},{5,13},{13,5},{2,10},{10,2},... | collective-permute-start | bytes 1572872 | tf_op jit(solution)/shard_map/ppermute | solution.py:66
  72.7 40.1 %collective-permute-start.4 = (bf16[1,512,512]{2,1,0:T(8,128)(2,1)S(1)}, bf16[1,512,512]{2,1,0:T(8,128)(2,1)}, u32[]{:S(2)}, u32[]{:S(2)}) collective-permute-start(bf16[1,512,512]{2,1,0:T(8,128)(2,1)S(1)} %get-tuple-element.462), channel_id=1, source_target_pairs={{0,12},{12,0},{4,8},{8,4},{1,13},{13,1},{5,9},{9,5},{2,14},{14,2},... | collective-permute-start | bytes 1572872 | tf_op jit(solution)/shard_map/ppermute | solution.py:66
  172.8 30.6 %collective-permute-start.17 = (bf16[1152,768]{1,0:T(8,128)(2,1)}, bf16[1152,768]{1,0:T(8,128)(2,1)S(1)}, u32[]{:S(2)}, u32[]{:S(2)}) collective-permute-start(bf16[1152,768]{1,0:T(8,128)(2,1)} %constant_dynamic-update-slice_fusion.26), channel_id=1, source_target_pairs={{0,16},{16,0},{1,17},{17,1},{2,18},{18,2},{3,19},{19,3},{4,20},{20... | collective-permute-start | bytes 5308424 | tf_op jit(solution)/shard_map/ppermute | solution.py:66
  257.5 26.0 %collective-permute-start.24 = (bf16[512,1152]{1,0:T(8,128)(2,1)S(1)}, bf16[512,1152]{1,0:T(8,128)(2,1)S(1)}, u32[]{:S(2)}, u32[]{:S(2)}) collective-permute-start(bf16[512,1152]{1,0:T(8,128)(2,1)S(1)} %constant_dynamic-slice_fusion.5), channel_id=1, source_target_pairs={{0,16},{16,0},{1,17},{17,1},{2,18},{18,2},{3,19},{19,3},{4,20},{20... | collective-permute-start | bytes 3538952 | tf_op jit(solution)/shard_map/ppermute | solution.py:66
  257.6 25.9 %collective-permute-start.22 = (bf16[512,2304]{1,0:T(8,128)(2,1)}, bf16[512,2304]{1,0:T(8,128)(2,1)S(1)}, u32[]{:S(2)}, u32[]{:S(2)}) collective-permute-start(bf16[512,2304]{1,0:T(8,128)(2,1)} %get-tuple-element.247.cols_ref), channel_id=1, source_target_pairs={{0,16},{16,0},{1,17},{17,1},{2,18},{18,2},{3,19},{19,3},{4,20},{20... | collective-permute-start | bytes 7077896 | tf_op jit(solution)/shard_map/ppermute | solution.py:66
  258.2 25.3 %collective-permute-start.25 = (bf16[512,1152]{1,0:T(8,128)(2,1)S(1)}, bf16[512,1152]{1,0:T(8,128)(2,1)S(1)}, u32[]{:S(2)}, u32[]{:S(2)}) collective-permute-start(bf16[512,1152]{1,0:T(8,128)(2,1)S(1)} %constant_dynamic-slice_fusion.4), channel_id=1, source_target_pairs={{0,16},{16,0},{1,17},{17,1},{2,18},{18,2},{3,19},{19,3},{4,20},{20... | collective-permute-start | bytes 3538952 | tf_op jit(solution)/shard_map/ppermute | solution.py:66
  349.9 28.9 %collective-permute-start.36 = (bf16[512,1152]{1,0:T(8,128)(2,1)S(1)}, bf16[512,1152]{1,0:T(8,128)(2,1)S(1)}, u32[]{:S(2)}, u32[]{:S(2)}) collective-permute-start(bf16[512,1152]{1,0:T(8,128)(2,1)S(1)} %constant_dynamic-slice_fusion.3), channel_id=1, source_target_pairs={{0,16},{16,0},{1,17},{17,1},{2,18},{18,2},{3,19},{19,3},{4,20},{20... | collective-permute-start | bytes 3538952 | tf_op jit(solution)/shard_map/ppermute | solution.py:66
  378.9 19.2 %collective-permute-start.38 = (bf16[512,2304]{1,0:T(8,128)(2,1)}, bf16[512,2304]{1,0:T(8,128)(2,1)}, u32[]{:S(2)}, u32[]{:S(2)}) collective-permute-start(bf16[512,2304]{1,0:T(8,128)(2,1)} %get-tuple-element.281.cols_ref), channel_id=1, source_target_pairs={{0,16},{16,0},{1,17},{17,1},{2,18},{18,2},{3,19},{19,3},{4,20},{20... | collective-permute-start | bytes 7077896 | tf_op jit(solution)/shard_map/ppermute | solution.py:66
  379.4 33.6 %collective-permute-start.40 = (bf16[512,2304]{1,0:T(8,128)(2,1)}, bf16[512,2304]{1,0:T(8,128)(2,1)}, u32[]{:S(2)}, u32[]{:S(2)}) collective-permute-start(bf16[512,2304]{1,0:T(8,128)(2,1)} %get-tuple-element.290.cols_ref), channel_id=1, source_target_pairs={{0,16},{16,0},{1,17},{17,1},{2,18},{18,2},{3,19},{19,3},{4,20},{20... | collective-permute-start | bytes 7077896 | tf_op jit(solution)/shard_map/ppermute | solution.py:66
  398.1 19.6 %collective-permute-start.41 = (bf16[144,2304]{1,0:T(8,128)(2,1)}, bf16[144,2304]{1,0:T(8,128)(2,1)}, u32[]{:S(2)}, u32[]{:S(2)}) collective-permute-start(bf16[144,2304]{1,0:T(8,128)(2,1)} %get-tuple-element.291), channel_id=1, source_target_pairs={{0,4},{4,0},{8,12},{12,8},{1,5},{5,1},{9,13},{13,9},{2,6},{6,2},{1... | collective-permute-start | bytes 1990664 | tf_op jit(solution)/shard_map/ppermute | solution.py:66
  399.6 18.1 %collective-permute-start.42 = (bf16[144,2304]{1,0:T(8,128)(2,1)}, bf16[144,2304]{1,0:T(8,128)(2,1)}, u32[]{:S(2)}, u32[]{:S(2)}) collective-permute-start(bf16[144,2304]{1,0:T(8,128)(2,1)} %get-tuple-element.292), channel_id=1, source_target_pairs={{0,8},{8,0},{4,12},{12,4},{1,9},{9,1},{5,13},{13,5},{2,10},{10,2},... | collective-permute-start | bytes 1990664 | tf_op jit(solution)/shard_map/ppermute | solution.py:66
  401.3 33.7 %collective-permute-start.44 = (bf16[144,2304]{1,0:T(8,128)(2,1)}, bf16[144,2304]{1,0:T(8,128)(2,1)S(1)}, u32[]{:S(2)}, u32[]{:S(2)}) collective-permute-start(bf16[144,2304]{1,0:T(8,128)(2,1)} %get-tuple-element.300), channel_id=1, source_target_pairs={{0,4},{4,0},{8,12},{12,8},{1,5},{5,1},{9,13},{13,9},{2,6},{6,2},{1... | collective-permute-start | bytes 1990664 | tf_op jit(solution)/shard_map/ppermute | solution.py:66
  413.1 21.9 %collective-permute-start.45 = (bf16[144,2304]{1,0:T(8,128)(2,1)}, bf16[144,2304]{1,0:T(8,128)(2,1)S(1)}, u32[]{:S(2)}, u32[]{:S(2)}) collective-permute-start(bf16[144,2304]{1,0:T(8,128)(2,1)} %get-tuple-element.301), channel_id=1, source_target_pairs={{0,8},{8,0},{4,12},{12,4},{1,9},{9,1},{5,13},{13,5},{2,10},{10,2},... | collective-permute-start | bytes 1990664 | tf_op jit(solution)/shard_map/ppermute | solution.py:66
  421.7 21.7 %collective-permute-start.47 = (bf16[144,2304]{1,0:T(8,128)(2,1)}, bf16[144,2304]{1,0:T(8,128)(2,1)}, u32[]{:S(2)}, u32[]{:S(2)}) collective-permute-start(bf16[144,2304]{1,0:T(8,128)(2,1)} %get-tuple-element.446), channel_id=1, source_target_pairs={{0,4},{4,0},{8,12},{12,8},{1,5},{5,1},{9,13},{13,9},{2,6},{6,2},{1... | collective-permute-start | bytes 1990664 | tf_op jit(solution)/shard_map/ppermute | solution.py:66
  422.1 22.5 %collective-permute-start.48 = (bf16[144,2304]{1,0:T(8,128)(2,1)}, bf16[144,2304]{1,0:T(8,128)(2,1)}, u32[]{:S(2)}, u32[]{:S(2)}) collective-permute-start(bf16[144,2304]{1,0:T(8,128)(2,1)} %get-tuple-element.445), channel_id=1, source_target_pairs={{0,8},{8,0},{4,12},{12,4},{1,9},{9,1},{5,13},{13,5},{2,10},{10,2},... | collective-permute-start | bytes 1990664 | tf_op jit(solution)/shard_map/ppermute | solution.py:66
  452.3 18.1 %collective-permute-start.50 = (bf16[144,2304]{1,0:T(8,128)(2,1)}, bf16[144,2304]{1,0:T(8,128)(2,1)S(1)}, u32[]{:S(2)}, u32[]{:S(2)}) collective-permute-start(bf16[144,2304]{1,0:T(8,128)(2,1)} %get-tuple-element.312), channel_id=1, source_target_pairs={{0,4},{4,0},{8,12},{12,8},{1,5},{5,1},{9,13},{13,9},{2,6},{6,2},{1... | collective-permute-start | bytes 1990664 | tf_op jit(solution)/shard_map/ppermute | solution.py:66
  454.3 29.5 %collective-permute-start.53 = (bf16[144,2304]{1,0:T(8,128)(2,1)}, bf16[144,2304]{1,0:T(8,128)(2,1)S(1)}, u32[]{:S(2)}, u32[]{:S(2)}) collective-permute-start(bf16[144,2304]{1,0:T(8,128)(2,1)} %get-tuple-element.326), channel_id=1, source_target_pairs={{0,4},{4,0},{8,12},{12,8},{1,5},{5,1},{9,13},{13,9},{2,6},{6,2},{1... | collective-permute-start | bytes 1990664 | tf_op jit(solution)/shard_map/ppermute | solution.py:66
  454.7 29.1 %collective-permute-start.54 = (bf16[144,2304]{1,0:T(8,128)(2,1)}, bf16[144,2304]{1,0:T(8,128)(2,1)S(1)}, u32[]{:S(2)}, u32[]{:S(2)}) collective-permute-start(bf16[144,2304]{1,0:T(8,128)(2,1)} %get-tuple-element.327), channel_id=1, source_target_pairs={{0,8},{8,0},{4,12},{12,4},{1,9},{9,1},{5,13},{13,5},{2,10},{10,2},... | collective-permute-start | bytes 1990664 | tf_op jit(solution)/shard_map/ppermute | solution.py:66
  485.6 20.1 %collective-permute-start.55 = (bf16[144,2304]{1,0:T(8,128)(2,1)}, bf16[144,2304]{1,0:T(8,128)(2,1)S(1)}, u32[]{:S(2)}, u32[]{:S(2)}) collective-permute-start(bf16[144,2304]{1,0:T(8,128)(2,1)} %get-tuple-element.442), channel_id=1, source_target_pairs={{0,4},{4,0},{8,12},{12,8},{1,5},{5,1},{9,13},{13,9},{2,6},{6,2},{1... | collective-permute-start | bytes 1990664 | tf_op jit(solution)/shard_map/ppermute | solution.py:66
  486.1 19.5 %collective-permute-start.56 = (bf16[144,2304]{1,0:T(8,128)(2,1)}, bf16[144,2304]{1,0:T(8,128)(2,1)S(1)}, u32[]{:S(2)}, u32[]{:S(2)}) collective-permute-start(bf16[144,2304]{1,0:T(8,128)(2,1)} %get-tuple-element.441), channel_id=1, source_target_pairs={{0,8},{8,0},{4,12},{12,4},{1,9},{9,1},{5,13},{13,5},{2,10},{10,2},... | collective-permute-start | bytes 1990664 | tf_op jit(solution)/shard_map/ppermute | solution.py:66
  501.6 29.9 %collective-permute-start.59 = (bf16[512,1152]{1,0:T(8,128)(2,1)S(1)}, bf16[512,1152]{1,0:T(8,128)(2,1)S(1)}, u32[]{:S(2)}, u32[]{:S(2)}) collective-permute-start(bf16[512,1152]{1,0:T(8,128)(2,1)S(1)} %constant_dynamic-slice_fusion.1), channel_id=1, source_target_pairs={{0,16},{16,0},{1,17},{17,1},{2,18},{18,2},{3,19},{19,3},{4,20},{20... | collective-permute-start | bytes 3538952 | tf_op jit(solution)/shard_map/ppermute | solution.py:66
  512.4 19.1 %collective-permute-start.60 = (bf16[144,2304]{1,0:T(8,128)(2,1)}, bf16[144,2304]{1,0:T(8,128)(2,1)S(1)}, u32[]{:S(2)}, u32[]{:S(2)}) collective-permute-start(bf16[144,2304]{1,0:T(8,128)(2,1)} %get-tuple-element.340), channel_id=1, source_target_pairs={{0,4},{4,0},{8,12},{12,8},{1,5},{5,1},{9,13},{13,9},{2,6},{6,2},{1... | collective-permute-start | bytes 1990664 | tf_op jit(solution)/shard_map/ppermute | solution.py:66
  535.7 19.2 %collective-permute-start.63 = (bf16[512,512]{1,0:T(8,128)(2,1)}, bf16[512,512]{1,0:T(8,128)(2,1)S(1)}, u32[]{:S(2)}, u32[]{:S(2)}) collective-permute-start(bf16[512,512]{1,0:T(8,128)(2,1)} %get-tuple-element.452), channel_id=1, source_target_pairs={{0,8},{8,0},{4,12},{12,4},{1,9},{9,1},{5,13},{13,5},{2,10},{10,2},... | collective-permute-start | bytes 1572872 | tf_op jit(solution)/shard_map/ppermute | solution.py:66
  537.1 19.0 %collective-permute-start.64 = (bf16[512,512]{1,0:T(8,128)(2,1)S(1)}, bf16[512,512]{1,0:T(8,128)(2,1)S(1)}, u32[]{:S(2)}, u32[]{:S(2)}) collective-permute-start(bf16[512,512]{1,0:T(8,128)(2,1)S(1)} %get-tuple-element.451), channel_id=1, source_target_pairs={{0,12},{12,0},{4,8},{8,4},{1,13},{13,1},{5,9},{9,5},{2,14},{14,2},... | collective-permute-start | bytes 1572872 | tf_op jit(solution)/shard_map/ppermute | solution.py:66
  563.8 20.7 %collective-permute-start.67 = (bf16[144,2304]{1,0:T(8,128)(2,1)}, bf16[144,2304]{1,0:T(8,128)(2,1)}, u32[]{:S(2)}, u32[]{:S(2)}) collective-permute-start(bf16[144,2304]{1,0:T(8,128)(2,1)} %get-tuple-element.438), channel_id=1, source_target_pairs={{0,4},{4,0},{8,12},{12,8},{1,5},{5,1},{9,13},{13,9},{2,6},{6,2},{1... | collective-permute-start | bytes 1990664 | tf_op jit(solution)/shard_map/ppermute | solution.py:66
  564.8 19.6 %collective-permute-start.68 = (bf16[144,2304]{1,0:T(8,128)(2,1)}, bf16[144,2304]{1,0:T(8,128)(2,1)}, u32[]{:S(2)}, u32[]{:S(2)}) collective-permute-start(bf16[144,2304]{1,0:T(8,128)(2,1)} %get-tuple-element.437), channel_id=1, source_target_pairs={{0,8},{8,0},{4,12},{12,4},{1,9},{9,1},{5,13},{13,5},{2,10},{10,2},... | collective-permute-start | bytes 1990664 | tf_op jit(solution)/shard_map/ppermute | solution.py:66
  625.1 40.4 %all-to-all-start.1 = ((f32[32,4,288]{2,1,0:T(4,128)}), f32[32,4,288]{2,1,0:T(4,128)S(1)}, u32[]{:S(2)}, u32[]{:S(2)}) async-start(f32[32,4,288]{2,1,0:T(4,128)} %bitcast.30), calls=%async_computation.1 | async-start | bytes 393216 | tf_op jit(solution)/shard_map/all_to_all | solution.py:739
  (126 other events, 1410.4 us)
Sparse Core Ops, SparseCore 0:
  10.5 54.2 all-gather.2
  66.7 159.6 all-gather.4

commit v8 on v7

--- a/solution.py
+++ b/solution.py
@@ -648,28 +648,28 @@
     dffn_far = far_half(dffn_b)
 
     dffn_in, dffn_far, dgate_b, dup_b = tied(dffn_in, dffn_far, dgate_b, dup_b)
-    ring = Ring(dffn_in)
+    ring = Ring(dffn_in, 2)
     dgate_far = send("core", dgate_b)
     down_s = Scatter(weight_grad(dffn_b, dffn_far, hidden_b, hidden_far))
-    ring.going, down_s.blocks, dgate_far = tied(ring.going, down_s.blocks, dgate_far)
+    ring.going[0], down_s.blocks, dgate_far = tied(ring.going[0], down_s.blocks, dgate_far)
     ring.go()
     down_s.diagonal()
     dup_far = send("core", dup_b)
     gate_s = Scatter(weight_grad(ffn_in, ffn_in_far, dgate_b, dgate_far))
-    ring.going, gate_s.blocks, dup_far, down_s.first = tied(
-        ring.going, gate_s.blocks, dup_far, down_s.first
+    ring.going[0], gate_s.blocks, dup_far, down_s.first = tied(
+        ring.going[0], gate_s.blocks, dup_far, down_s.first
     )
     ring.go()
     down_s.direct()
     up_s = Scatter(weight_grad(ffn_in, ffn_in_far, dup_b, dup_far))
-    ring.going, up_s.blocks, down_s.middle = tied(ring.going, up_s.blocks, down_s.middle)
+    ring.going[0], up_s.blocks, down_s.middle = tied(ring.going[0], up_s.blocks, down_s.middle)
     ring.go()
     down_s.sums()
-    ring.going, down_s.last, gate_s.blocks = tied(ring.going, down_s.last, gate_s.blocks)
+    ring.going[0], down_s.last, gate_s.blocks = tied(ring.going[0], down_s.last, gate_s.blocks)
     ring.go()
     gate_s.diagonal()
     grad_down = down_s.result().T
-    ring.going, gate_s.first, grad_down = tied(ring.going, gate_s.first, grad_down)
+    ring.going[0], gate_s.first, grad_down = tied(ring.going[0], gate_s.first, grad_down)
     ring.go()
     gate_s.direct()
     dffn_in, up_s.blocks, gate_s.first, gate_s.middle = tied(

time: 692 us -> 686 us (level)
  waiting for transfers between devices: 335 us -> 320 us
  starting transfers between devices: 64.2 us -> 71.7 us
    ppermute x36 -> x42, waiting for transfers between devices: 211 us -> 199 us  [around(): lax.ppermute(value, 'tp', [(i, (i + by) % size) for i in range(size)])]
    ppermute x36 -> x42, starting transfers between devices: 12 us -> 19.1 us  [around(): lax.ppermute(value, 'tp', [(i, (i + by) % size) for i in range(size)])]
  transfers between devices with their start and end apart: 86 -> 92, of which waited for: 53 -> 52; matrix products, arithmetic and copies ran while one was open for 13% -> 13% of each run, Pallas kernels for 16% -> 16%
where the time goes in v8:
time: 686 us; the launch traced here: 675 us
  waiting for transfers between devices  320 us (47%)
  Pallas kernels  150 us (22%)
  starting transfers between devices  71.7 us (10%)
  other arithmetic  48.3 us (7%)
  local copies, waits for them, and re-layouts  45 us (7%)
  matrix products  23.4 us (3%)
  between operations  16.6 us (2%)
    ppermute x42, waiting for transfers between devices, around(): lax.ppermute(value, 'tp', [(i, (i + by) % size) for i in range(size)])  199 us
    ppermute x46, waiting for transfers between devices, send(): return lax.ppermute(value, *LINKS[link])  77.9 us
    pallas_call x5, Pallas kernels, weight_grad(): pl.pallas_call(kernel, grid_spec=pltpu.PrefetchScalarGridSpec(num_scalar_...  46.1 us
    ppermute x46, starting transfers between devices, send(): return lax.ppermute(value, *LINKS[link])  44.2 us
    all_gather x2, waiting for transfers between devices, gather(): return lax.all_gather(shard, ('fsdp', 'ctx'), axis=0, tiled=True)  37.4 us
    pallas_call x4, Pallas kernels, rowwise(): pl.pallas_call(kernel, grid=(count // block,), in_specs=[by_row] * len(ro...  32.1 us
    pallas_call x1, Pallas kernels, ffn_backward(): pl.pallas_call(kernel, grid=(first + width // out_cut,), in_specs=[pl.Blo...  29.3 us
    pallas_call x1, Pallas kernels, ffn_forward(): pl.pallas_call(kernel, grid=(first + width // out_cut,), in_specs=[pl.Blo...  27 us
  transfers between devices with their start and end apart: 92, of which 52 were waited for; matrix products, arithmetic and copies ran while one was open for 13% of the time, Pallas kernels for 16%

profile of v8, /device:TPU:0, one launch (start us, length us, event | category | flops | bytes accessed | tf_op | source)
XLA Modules:
  0.0 675.3 jit_solution(15664752609868565046)
XLA Ops:
  33.1 31.7 %all-gather.3.cloned.1.call-done = bf16[2304,1536]{1,0:T(8,128)(2,1)} async-done(((bf16[288,1536]{1,0:T(8,128)(2,1)}), bf16[2304,1536]{1,0:T(8,128)(2,1)}) %all-gather.3.cloned.1.call-update) | async-done | bytes 7077904 | tf_op jit(solution)/shard_map/all_gather | solution.py:552
  75.7 14.9 %collective-permute-done.2 = bf16[1,512,512]{2,1,0:T(8,128)(2,1)S(1)} collective-permute-done((bf16[1,512,512]{2,1,0:T(8,128)(2,1)S(1)}, bf16[1,512,512]{2,1,0:T(8,128)(2,1)S(1)}, u32[]{:S(2)}, u32[]{:S(2)}) %collective-permute-start.2) | collective-permute-done | bytes 524320 | tf_op jit(solution)/shard_map/ppermute | solution.py:66
  94.7 18.0 %collective-permute-done.4 = bf16[1,512,512]{2,1,0:T(8,128)(2,1)} collective-permute-done((bf16[1,512,512]{2,1,0:T(8,128)(2,1)S(1)}, bf16[1,512,512]{2,1,0:T(8,128)(2,1)}, u32[]{:S(2)}, u32[]{:S(2)}) %collective-permute-start.4) | collective-permute-done | bytes 524320 | tf_op jit(solution)/shard_map/ppermute | solution.py:66
  143.3 7.9 %collective-permute-done.9 = bf16[64,2304]{1,0:T(8,128)(2,1)S(1)} collective-permute-done((bf16[64,2304]{1,0:T(8,128)(2,1)}, bf16[64,2304]{1,0:T(8,128)(2,1)S(1)}, u32[]{:S(2)}, u32[]{:S(2)}) %collective-permute-start.9) | collective-permute-done | bytes 294944 | tf_op jit(solution)/shard_map/ppermute | solution.py:71
  151.3 6.2 collective-permute-done.8
  176.8 7.7 %collective-permute-done.13 = bf16[64,2304]{1,0:T(8,128)(2,1)S(1)} collective-permute-done((bf16[64,2304]{1,0:T(8,128)(2,1)S(1)}, bf16[64,2304]{1,0:T(8,128)(2,1)S(1)}, u32[]{:S(2)}, u32[]{:S(2)}) %collective-permute-start.13) | collective-permute-done | bytes 294944 | tf_op jit(solution)/shard_map/ppermute | solution.py:71
  184.5 6.3 collective-permute-done.14
  190.9 6.3 collective-permute-done.15
  197.2 6.3 collective-permute-done.16
  203.5 6.3 collective-permute-done.18
  214.3 6.3 shard_map.237
  226.3 27.0 %shard_map.238 = (f32[512,2304]{1,0:T(8,128)}, f32[512,2304]{1,0:T(8,128)}, bf16[512,2304]{1,0:T(8,128)(2,1)}, bf16[512,2304]{1,0:T(8,128)(2,1)}) custom-call(bf16[512,2304]{1,0:T(8,128)(2,1)} %get-tuple-element.261.x_ref.near_ref, bf16[2304,6144]{1,0:T(8,128)(2,1)} %all-gather.5.cloned.1.call-done.gate_w.up_w.down_w, ...), custom_call_target="tpu_custom_call" | custom-call | flops 16307453952 | bytes 43646976 | tf_op jit(solution)/shard_map/pallas_call | solution.py:246
  273.3 10.4 %collective-permute-done.21 = bf16[64,2304]{1,0:T(8,128)(2,1)S(1)} collective-permute-done((bf16[64,2304]{1,0:T(8,128)(2,1)S(1)}, bf16[64,2304]{1,0:T(8,128)(2,1)S(1)}, u32[]{:S(2)}, u32[]{:S(2)}) %collective-permute-start.21) | collective-permute-done | bytes 294944 | tf_op jit(solution)/shard_map/ppermute | solution.py:71
  309.3 6.3 collective-permute-done.31
  315.6 6.3 collective-permute-done.32
  321.9 6.3 collective-permute-done.33
  328.7 10.3 %collective-permute-done.35 = bf16[64,2304]{1,0:T(8,128)(2,1)S(1)} collective-permute-done((bf16[64,2304]{1,0:T(8,128)(2,1)S(1)}, bf16[64,2304]{1,0:T(8,128)(2,1)S(1)}, u32[]{:S(2)}, u32[]{:S(2)}) %collective-permute-start.35) | collective-permute-done | bytes 294944 | tf_op jit(solution)/shard_map/ppermute | solution.py:71
  340.5 8.3 %shard_map.239 = (bf16[512,2304]{1,0:T(8,128)(2,1)}, bf16[512,2304]{1,0:T(8,128)(2,1)}, f32[8,2304]{1,0:T(8,128)}) custom-call(bf16[512,2304]{1,0:T(8,128)(2,1)} %copy-done.10, f32[512,2304]{1,0:T(8,128)} %get-tuple-element.276.refs_1_, bf16[512,2304]{1,0:T(8,128)(2,1)} %bitcast_select_fusion.1.refs_2_.refs_3_, f32[1,2304]{1,0:T(1,128)} %add.672.refs_3_), custom_call_target="tpu_custom_call" | custom-call | flops 23592960 | bytes 18874368 | tf_op jit(solution)/shard_map/pallas_call | solution.py:187
  350.2 29.3 %shard_map.240 = (bf16[512,2304]{1,0:T(8,128)(2,1)}, bf16[512,2304]{1,0:T(8,128)(2,1)}, bf16[512,2304]{1,0:T(8,128)(2,1)}) custom-call(bf16[512,2304]{1,0:T(8,128)(2,1)} %get-tuple-element.279.d_ref.near_ref, bf16[2304,6144]{1,0:T(8,128)(2,1)} %all-gather.5.cloned.1.call-done.gate_w.up_w.down_w, bf16[2304,768]{1,0:T(8,128)(2,1)} %copy-done.2, ...), custom_call_target="tpu_custom_call" | custom-call | flops 16307453952 | bytes 46006272 | tf_op jit(solution)/shard_map/pallas_call | solution.py:323
  382.2 11.3 %shard_map.241 = (bf16[576,2304]{1,0:T(8,128)(2,1)}, bf16[144,2304]{1,0:T(8,128)(2,1)}, bf16[144,2304]{1,0:T(8,128)(2,1)}, bf16[144,2304]{1,0:T(8,128)(2,1)}, bf16[144,2304]{1,0:T(8,128)(2,1)}) custom-call(s32[2]{0:T(128)} %get-tuple-element.506.place_ref, bf16[512,2304]{1,0:T(8,128)(2,1)} %get-tuple-element.279.d_ref.near_ref, ...), custom_call_target="tpu_custom_call" | custom-call | flops 5435817984 | bytes 12386304 | tf_op jit(solution)/shard_map/pallas_call | solution.py:381
  401.3 11.1 %shard_map.242 = (bf16[576,2304]{1,0:T(8,128)(2,1)}, bf16[144,2304]{1,0:T(8,128)(2,1)}, bf16[144,2304]{1,0:T(8,128)(2,1)}, bf16[144,2304]{1,0:T(8,128)(2,1)}, bf16[144,2304]{1,0:T(8,128)(2,1)}) custom-call(s32[2]{0:T(128)} %get-tuple-element.506.place_ref, bf16[512,2304]{1,0:T(8,128)(2,1)} %get-tuple-element.261.x_ref.near_ref, ...), custom_call_target="tpu_custom_call" | custom-call | flops 5435817984 | bytes 12386304 | tf_op jit(solution)/shard_map/pallas_call | solution.py:381
  419.7 11.2 %shard_map.243 = (bf16[576,2304]{1,0:T(8,128)(2,1)}, bf16[144,2304]{1,0:T(8,128)(2,1)}, bf16[144,2304]{1,0:T(8,128)(2,1)}, bf16[144,2304]{1,0:T(8,128)(2,1)}, bf16[144,2304]{1,0:T(8,128)(2,1)}) custom-call(s32[2]{0:T(128)} %get-tuple-element.506.place_ref, bf16[512,2304]{1,0:T(8,128)(2,1)} %get-tuple-element.261.x_ref.near_ref, ...), custom_call_target="tpu_custom_call" | custom-call | flops 5435817984 | bytes 12386304 | tf_op jit(solution)/shard_map/pallas_call | solution.py:381
  468.4 9.5 %collective-permute-done.58 = bf16[64,2304]{1,0:T(8,128)(2,1)S(1)} collective-permute-done((bf16[64,2304]{1,0:T(8,128)(2,1)S(1)}, bf16[64,2304]{1,0:T(8,128)(2,1)S(1)}, u32[]{:S(2)}, u32[]{:S(2)}) %collective-permute-start.58) | collective-permute-done | bytes 294944 | tf_op jit(solution)/shard_map/ppermute | solution.py:71
  481.5 10.5 %shard_map.244 = (f32[512,2304]{1,0:T(8,128)}, bf16[512,2304]{1,0:T(8,128)(2,1)}, f32[8,2304]{1,0:T(8,128)}, f32[8,2304]{1,0:T(8,128)}) custom-call(bf16[512,2304]{1,0:T(8,128)(2,1)} %copy-done.4, f32[512,2304]{1,0:T(8,128)} %get-tuple-element.276.refs_1_, bf16[512,2304]{1,0:T(8,128)(2,1)} %copy-done.3, ...), custom_call_target="tpu_custom_call" | custom-call | flops 23592960 | bytes 28311552 | tf_op jit(solution)/shard_map/pallas_call | solution.py:187
  511.0 15.6 %shard_map.245 = (bf16[512,512]{1,0:T(8,128)(2,1)}, bf16[4,512,512]{2,1,0:T(8,128)(2,1)}) custom-call(s32[2]{0:T(128)} %get-tuple-element.505.scalars_ref, bf16[512,512]{1,0:T(8,128)(2,1)} %copy-done.47, bf16[512,512]{1,0:T(8,128)(2,1)} %fusion.22.d_ref, bf16[512,512]{1,0:T(8,128)(2,1)} %copy-done.23, bf16[2048,512]{1,0:T(8,128)(2,1)} %bitcast.92, ...), custom_call_target="tpu_custom_call" | custom-call | flops 5368709120 | bytes 8388608 | tf_op jit(solution)/shard_map/pallas_call | solution.py:459
  544.8 6.2 collective-permute-done.69
  563.7 7.4 %shard_map.247 = (bf16[576,1024]{1,0:T(8,128)(2,1)}, bf16[288,1024]{1,0:T(8,128)(2,1)}, bf16[288,1024]{1,0:T(8,128)(2,1)}) custom-call(s32[2]{0:T(128)} %get-tuple-element.506.place_ref, bf16[512,2304]{1,0:T(8,128)(2,1)} %fusion.2.near_ref, bf16[512,1152]{1,0:T(8,128)(2,1)} %copy-done.66, bf16[512,1024]{1,0:T(8,128)(2,1)} %copy-done.30, ...), custom_call_target="tpu_custom_call" | custom-call | flops 2415919104 | bytes 6815744 | tf_op jit(solution)/shard_map/pallas_call | solution.py:381
  571.1 8.0 %collective-permute-done.71 = bf16[128,2304]{1,0:T(8,128)(2,1)} collective-permute-done((bf16[128,2304]{1,0:T(8,128)(2,1)}, bf16[128,2304]{1,0:T(8,128)(2,1)}, u32[]{:S(2)}, u32[]{:S(2)}) %collective-permute-start.71) | collective-permute-done | bytes 589856 | tf_op jit(solution)/shard_map/ppermute | solution.py:71
  587.0 8.4 %collective-permute-done.77 = bf16[288,1024]{1,0:T(8,128)(2,1)S(1)} collective-permute-done((bf16[288,1024]{1,0:T(8,128)(2,1)}, bf16[288,1024]{1,0:T(8,128)(2,1)S(1)}, u32[]{:S(2)}, u32[]{:S(2)}) %collective-permute-start.77) | collective-permute-done | bytes 589856 | tf_op jit(solution)/shard_map/ppermute | solution.py:66
  636.2 10.3 %collective-permute-done.86 = bf16[128,2304]{1,0:T(8,128)(2,1)S(1)} collective-permute-done((bf16[128,2304]{1,0:T(8,128)(2,1)}, bf16[128,2304]{1,0:T(8,128)(2,1)S(1)}, u32[]{:S(2)}, u32[]{:S(2)}) %collective-permute-start.86) | collective-permute-done | bytes 589856 | tf_op jit(solution)/shard_map/ppermute | solution.py:71
  647.4 12.1 %collective-permute-done.87 = bf16[128,2304]{1,0:T(8,128)(2,1)S(1)} collective-permute-done((bf16[128,2304]{1,0:T(8,128)(2,1)S(1)}, bf16[128,2304]{1,0:T(8,128)(2,1)S(1)}, u32[]{:S(2)}, u32[]{:S(2)}) %collective-permute-start.87) | collective-permute-done | bytes 589856 | tf_op jit(solution)/shard_map/ppermute | solution.py:71
  661.0 7.0 %shard_map.248 = bf16[512,2304]{1,0:T(8,128)(2,1)} custom-call(bf16[512,2304]{1,0:T(8,128)(2,1)} %copy-done.9, bf16[512,2304]{1,0:T(8,128)(2,1)} %bitcast.90, f32[512,2304]{1,0:T(8,128)} %get-tuple-element.432.refs_2_, f32[1,2304]{1,0:T(1,128)} %add.721.refs_3_), custom_call_target="tpu_custom_call" | custom-call | flops 23592960 | bytes 18874368 | tf_op jit(solution)/shard_map/pallas_call | solution.py:187
  (455 shorter events, 308.0 us)
Async XLA Ops:
  7.2 57.6 %all-gather.3.cloned.1.call-start = ((), (), s32[]{:S(2)}) async-start(), calls=%async_computation.2 | async-start | bytes 7962624 | tf_op jit(solution)/shard_map/all_gather | solution.py:552
  11.4 21.7 %collective-permute-start = (bf16[288,768]{1,0:T(8,128)(2,1)}, bf16[288,768]{1,0:T(8,128)(2,1)S(1)}, u32[]{:S(2)}, u32[]{:S(2)}) collective-permute-start(bf16[288,768]{1,0:T(8,128)(2,1)} %slice_bitcast_fusion.6), channel_id=1, source_target_pairs={{0,4},{4,0},{8,12},{12,8},{1,5},{5,1},{9,13},{13,9},{2,6},{6,2},{1... | collective-permute-start | bytes 1327112 | tf_op jit(solution)/shard_map/ppermute | solution.py:66
  14.4 18.7 %collective-permute-start.1 = (bf16[288,768]{1,0:T(8,128)(2,1)}, bf16[288,768]{1,0:T(8,128)(2,1)S(1)}, u32[]{:S(2)}, u32[]{:S(2)}) collective-permute-start(bf16[288,768]{1,0:T(8,128)(2,1)} %slice_bitcast_fusion.6), channel_id=1, source_target_pairs={{0,8},{8,0},{4,12},{12,4},{1,9},{9,1},{5,13},{13,5},{2,10},{10,2},... | collective-permute-start | bytes 1327112 | tf_op jit(solution)/shard_map/ppermute | solution.py:66
  19.9 206.4 %all-gather.5.cloned.1.call-start = ((), (), s32[]{:S(2)}) async-start(), calls=%async_computation.3 | async-start | bytes 31850496 | tf_op jit(solution)/shard_map/all_gather | solution.py:552
  70.6 20.1 %collective-permute-start.2 = (bf16[1,512,512]{2,1,0:T(8,128)(2,1)S(1)}, bf16[1,512,512]{2,1,0:T(8,128)(2,1)S(1)}, u32[]{:S(2)}, u32[]{:S(2)}) collective-permute-start(bf16[1,512,512]{2,1,0:T(8,128)(2,1)S(1)} %get-tuple-element.490), channel_id=1, source_target_pairs={{0,4},{4,0},{8,12},{12,8},{1,5},{5,1},{9,13},{13,9},{2,6},{6,2},{1... | collective-permute-start | bytes 1572872 | tf_op jit(solution)/shard_map/ppermute | solution.py:66
  72.1 22.6 %collective-permute-start.3 = (bf16[1,512,512]{2,1,0:T(8,128)(2,1)S(1)}, bf16[1,512,512]{2,1,0:T(8,128)(2,1)S(1)}, u32[]{:S(2)}, u32[]{:S(2)}) collective-permute-start(bf16[1,512,512]{2,1,0:T(8,128)(2,1)S(1)} %get-tuple-element.490), channel_id=1, source_target_pairs={{0,8},{8,0},{4,12},{12,4},{1,9},{9,1},{5,13},{13,5},{2,10},{10,2},... | collective-permute-start | bytes 1572872 | tf_op jit(solution)/shard_map/ppermute | solution.py:66
  72.7 40.1 %collective-permute-start.4 = (bf16[1,512,512]{2,1,0:T(8,128)(2,1)S(1)}, bf16[1,512,512]{2,1,0:T(8,128)(2,1)}, u32[]{:S(2)}, u32[]{:S(2)}) collective-permute-start(bf16[1,512,512]{2,1,0:T(8,128)(2,1)S(1)} %get-tuple-element.490), channel_id=1, source_target_pairs={{0,12},{12,0},{4,8},{8,4},{1,13},{13,1},{5,9},{9,5},{2,14},{14,2},... | collective-permute-start | bytes 1572872 | tf_op jit(solution)/shard_map/ppermute | solution.py:66
  172.8 30.6 %collective-permute-start.17 = (bf16[1152,768]{1,0:T(8,128)(2,1)}, bf16[1152,768]{1,0:T(8,128)(2,1)S(1)}, u32[]{:S(2)}, u32[]{:S(2)}) collective-permute-start(bf16[1152,768]{1,0:T(8,128)(2,1)} %constant_dynamic-update-slice_fusion.30), channel_id=1, source_target_pairs={{0,16},{16,0},{1,17},{17,1},{2,18},{18,2},{3,19},{19,3},{4,20},{20... | collective-permute-start | bytes 5308424 | tf_op jit(solution)/shard_map/ppermute | solution.py:66
  257.7 26.0 %collective-permute-start.24 = (bf16[512,1152]{1,0:T(8,128)(2,1)S(1)}, bf16[512,1152]{1,0:T(8,128)(2,1)S(1)}, u32[]{:S(2)}, u32[]{:S(2)}) collective-permute-start(bf16[512,1152]{1,0:T(8,128)(2,1)S(1)} %constant_dynamic-slice_fusion.6), channel_id=1, source_target_pairs={{0,16},{16,0},{1,17},{17,1},{2,18},{18,2},{3,19},{19,3},{4,20},{20... | collective-permute-start | bytes 3538952 | tf_op jit(solution)/shard_map/ppermute | solution.py:66
  257.8 25.9 %collective-permute-start.22 = (bf16[512,2304]{1,0:T(8,128)(2,1)}, bf16[512,2304]{1,0:T(8,128)(2,1)S(1)}, u32[]{:S(2)}, u32[]{:S(2)}) collective-permute-start(bf16[512,2304]{1,0:T(8,128)(2,1)} %get-tuple-element.259.cols_ref), channel_id=1, source_target_pairs={{0,16},{16,0},{1,17},{17,1},{2,18},{18,2},{3,19},{19,3},{4,20},{20... | collective-permute-start | bytes 7077896 | tf_op jit(solution)/shard_map/ppermute | solution.py:66
  258.4 25.3 %collective-permute-start.25 = (bf16[512,1152]{1,0:T(8,128)(2,1)S(1)}, bf16[512,1152]{1,0:T(8,128)(2,1)S(1)}, u32[]{:S(2)}, u32[]{:S(2)}) collective-permute-start(bf16[512,1152]{1,0:T(8,128)(2,1)S(1)} %constant_dynamic-slice_fusion.5), channel_id=1, source_target_pairs={{0,16},{16,0},{1,17},{17,1},{2,18},{18,2},{3,19},{19,3},{4,20},{20... | collective-permute-start | bytes 3538952 | tf_op jit(solution)/shard_map/ppermute | solution.py:66
  350.2 29.4 %collective-permute-start.36 = (bf16[512,1152]{1,0:T(8,128)(2,1)S(1)}, bf16[512,1152]{1,0:T(8,128)(2,1)S(1)}, u32[]{:S(2)}, u32[]{:S(2)}) collective-permute-start(bf16[512,1152]{1,0:T(8,128)(2,1)S(1)} %constant_dynamic-slice_fusion.4), channel_id=1, source_target_pairs={{0,16},{16,0},{1,17},{17,1},{2,18},{18,2},{3,19},{19,3},{4,20},{20... | collective-permute-start | bytes 3538952 | tf_op jit(solution)/shard_map/ppermute | solution.py:66
  381.9 30.6 %collective-permute-start.40 = (bf16[512,2304]{1,0:T(8,128)(2,1)}, bf16[512,2304]{1,0:T(8,128)(2,1)}, u32[]{:S(2)}, u32[]{:S(2)}) collective-permute-start(bf16[512,2304]{1,0:T(8,128)(2,1)} %get-tuple-element.303.cols_ref), channel_id=1, source_target_pairs={{0,16},{16,0},{1,17},{17,1},{2,18},{18,2},{3,19},{19,3},{4,20},{20... | collective-permute-start | bytes 7077896 | tf_op jit(solution)/shard_map/ppermute | solution.py:66
  393.6 21.0 %collective-permute-start.41 = (bf16[144,2304]{1,0:T(8,128)(2,1)}, bf16[144,2304]{1,0:T(8,128)(2,1)S(1)}, u32[]{:S(2)}, u32[]{:S(2)}) collective-permute-start(bf16[144,2304]{1,0:T(8,128)(2,1)} %get-tuple-element.304), channel_id=1, source_target_pairs={{0,4},{4,0},{8,12},{12,8},{1,5},{5,1},{9,13},{13,9},{2,6},{6,2},{1... | collective-permute-start | bytes 1990664 | tf_op jit(solution)/shard_map/ppermute | solution.py:66
  395.0 19.6 %collective-permute-start.42 = (bf16[144,2304]{1,0:T(8,128)(2,1)}, bf16[144,2304]{1,0:T(8,128)(2,1)S(1)}, u32[]{:S(2)}, u32[]{:S(2)}) collective-permute-start(bf16[144,2304]{1,0:T(8,128)(2,1)} %get-tuple-element.305), channel_id=1, source_target_pairs={{0,8},{8,0},{4,12},{12,4},{1,9},{9,1},{5,13},{13,5},{2,10},{10,2},... | collective-permute-start | bytes 1990664 | tf_op jit(solution)/shard_map/ppermute | solution.py:66
  399.9 18.3 %collective-permute-start.47 = (bf16[64,2304]{1,0:T(8,128)(2,1)}, bf16[64,2304]{1,0:T(8,128)(2,1)}, u32[]{:S(2)}, u32[]{:S(2)}) collective-permute-start(bf16[64,2304]{1,0:T(8,128)(2,1)} %add_convert_fusion.16), channel_id=1, source_target_pairs={{0,1},{1,2},{2,3},{3,0},{4,5},{5,6},{6,7},{7,4},{8,9},{9,10},{10,1... | collective-permute-start | bytes 884744 | tf_op jit(solution)/shard_map/ppermute | solution.py:71
  412.5 18.4 %collective-permute-start.45 = (bf16[144,2304]{1,0:T(8,128)(2,1)}, bf16[144,2304]{1,0:T(8,128)(2,1)S(1)}, u32[]{:S(2)}, u32[]{:S(2)}) collective-permute-start(bf16[144,2304]{1,0:T(8,128)(2,1)} %get-tuple-element.315), channel_id=1, source_target_pairs={{0,4},{4,0},{8,12},{12,8},{1,5},{5,1},{9,13},{13,9},{2,6},{6,2},{1... | collective-permute-start | bytes 1990664 | tf_op jit(solution)/shard_map/ppermute | solution.py:66
  413.1 18.6 %collective-permute-start.46 = (bf16[144,2304]{1,0:T(8,128)(2,1)}, bf16[144,2304]{1,0:T(8,128)(2,1)S(1)}, u32[]{:S(2)}, u32[]{:S(2)}) collective-permute-start(bf16[144,2304]{1,0:T(8,128)(2,1)} %get-tuple-element.316), channel_id=1, source_target_pairs={{0,8},{8,0},{4,12},{12,4},{1,9},{9,1},{5,13},{13,5},{2,10},{10,2},... | collective-permute-start | bytes 1990664 | tf_op jit(solution)/shard_map/ppermute | solution.py:66
  416.1 32.0 %collective-permute-start.50 = (bf16[144,2304]{1,0:T(8,128)(2,1)}, bf16[144,2304]{1,0:T(8,128)(2,1)}, u32[]{:S(2)}, u32[]{:S(2)}) collective-permute-start(bf16[144,2304]{1,0:T(8,128)(2,1)} %get-tuple-element.472), channel_id=1, source_target_pairs={{0,4},{4,0},{8,12},{12,8},{1,5},{5,1},{9,13},{13,9},{2,6},{6,2},{1... | collective-permute-start | bytes 1990664 | tf_op jit(solution)/shard_map/ppermute | solution.py:66
  417.5 30.6 %collective-permute-start.51 = (bf16[144,2304]{1,0:T(8,128)(2,1)}, bf16[144,2304]{1,0:T(8,128)(2,1)}, u32[]{:S(2)}, u32[]{:S(2)}) collective-permute-start(bf16[144,2304]{1,0:T(8,128)(2,1)} %get-tuple-element.471), channel_id=1, source_target_pairs={{0,8},{8,0},{4,12},{12,4},{1,9},{9,1},{5,13},{13,5},{2,10},{10,2},... | collective-permute-start | bytes 1990664 | tf_op jit(solution)/shard_map/ppermute | solution.py:66
  448.1 18.1 %collective-permute-start.54 = (bf16[144,2304]{1,0:T(8,128)(2,1)}, bf16[144,2304]{1,0:T(8,128)(2,1)S(1)}, u32[]{:S(2)}, u32[]{:S(2)}) collective-permute-start(bf16[144,2304]{1,0:T(8,128)(2,1)} %get-tuple-element.332), channel_id=1, source_target_pairs={{0,4},{4,0},{8,12},{12,8},{1,5},{5,1},{9,13},{13,9},{2,6},{6,2},{1... | collective-permute-start | bytes 1990664 | tf_op jit(solution)/shard_map/ppermute | solution.py:66
  454.3 23.6 %collective-permute-start.59 = (bf16[144,2304]{1,0:T(8,128)(2,1)}, bf16[144,2304]{1,0:T(8,128)(2,1)S(1)}, u32[]{:S(2)}, u32[]{:S(2)}) collective-permute-start(bf16[144,2304]{1,0:T(8,128)(2,1)} %get-tuple-element.350), channel_id=1, source_target_pairs={{0,4},{4,0},{8,12},{12,8},{1,5},{5,1},{9,13},{13,9},{2,6},{6,2},{1... | collective-permute-start | bytes 1990664 | tf_op jit(solution)/shard_map/ppermute | solution.py:66
  479.7 20.1 %collective-permute-start.61 = (bf16[144,2304]{1,0:T(8,128)(2,1)}, bf16[144,2304]{1,0:T(8,128)(2,1)S(1)}, u32[]{:S(2)}, u32[]{:S(2)}) collective-permute-start(bf16[144,2304]{1,0:T(8,128)(2,1)} %get-tuple-element.468), channel_id=1, source_target_pairs={{0,4},{4,0},{8,12},{12,8},{1,5},{5,1},{9,13},{13,9},{2,6},{6,2},{1... | collective-permute-start | bytes 1990664 | tf_op jit(solution)/shard_map/ppermute | solution.py:66
  480.2 19.5 %collective-permute-start.62 = (bf16[144,2304]{1,0:T(8,128)(2,1)}, bf16[144,2304]{1,0:T(8,128)(2,1)}, u32[]{:S(2)}, u32[]{:S(2)}) collective-permute-start(bf16[144,2304]{1,0:T(8,128)(2,1)} %get-tuple-element.467), channel_id=1, source_target_pairs={{0,8},{8,0},{4,12},{12,4},{1,9},{9,1},{5,13},{13,5},{2,10},{10,2},... | collective-permute-start | bytes 1990664 | tf_op jit(solution)/shard_map/ppermute | solution.py:66
  495.6 30.9 %collective-permute-start.65 = (bf16[512,1152]{1,0:T(8,128)(2,1)S(1)}, bf16[512,1152]{1,0:T(8,128)(2,1)S(1)}, u32[]{:S(2)}, u32[]{:S(2)}) collective-permute-start(bf16[512,1152]{1,0:T(8,128)(2,1)S(1)} %constant_dynamic-slice_fusion.1), channel_id=1, source_target_pairs={{0,16},{16,0},{1,17},{17,1},{2,18},{18,2},{3,19},{19,3},{4,20},{20... | collective-permute-start | bytes 3538952 | tf_op jit(solution)/shard_map/ppermute | solution.py:66
  507.3 19.2 %collective-permute-start.66 = (bf16[144,2304]{1,0:T(8,128)(2,1)}, bf16[144,2304]{1,0:T(8,128)(2,1)S(1)}, u32[]{:S(2)}, u32[]{:S(2)}) collective-permute-start(bf16[144,2304]{1,0:T(8,128)(2,1)} %get-tuple-element.364), channel_id=1, source_target_pairs={{0,4},{4,0},{8,12},{12,8},{1,5},{5,1},{9,13},{13,9},{2,6},{6,2},{1... | collective-permute-start | bytes 1990664 | tf_op jit(solution)/shard_map/ppermute | solution.py:66
  508.2 18.4 %collective-permute-start.67 = (bf16[144,2304]{1,0:T(8,128)(2,1)}, bf16[144,2304]{1,0:T(8,128)(2,1)S(1)}, u32[]{:S(2)}, u32[]{:S(2)}) collective-permute-start(bf16[144,2304]{1,0:T(8,128)(2,1)} %get-tuple-element.365), channel_id=1, source_target_pairs={{0,8},{8,0},{4,12},{12,4},{1,9},{9,1},{5,13},{13,5},{2,10},{10,2},... | collective-permute-start | bytes 1990664 | tf_op jit(solution)/shard_map/ppermute | solution.py:66
  531.0 20.1 %collective-permute-start.69 = (bf16[512,512]{1,0:T(8,128)(2,1)}, bf16[512,512]{1,0:T(8,128)(2,1)S(1)}, u32[]{:S(2)}, u32[]{:S(2)}) collective-permute-start(bf16[512,512]{1,0:T(8,128)(2,1)} %get-tuple-element.480), channel_id=1, source_target_pairs={{0,8},{8,0},{4,12},{12,4},{1,9},{9,1},{5,13},{13,5},{2,10},{10,2},... | collective-permute-start | bytes 1572872 | tf_op jit(solution)/shard_map/ppermute | solution.py:66
  532.2 18.8 %collective-permute-start.70 = (bf16[512,512]{1,0:T(8,128)(2,1)S(1)}, bf16[512,512]{1,0:T(8,128)(2,1)S(1)}, u32[]{:S(2)}, u32[]{:S(2)}) collective-permute-start(bf16[512,512]{1,0:T(8,128)(2,1)S(1)} %get-tuple-element.479), channel_id=1, source_target_pairs={{0,12},{12,0},{4,8},{8,4},{1,13},{13,1},{5,9},{9,5},{2,14},{14,2},... | collective-permute-start | bytes 1572872 | tf_op jit(solution)/shard_map/ppermute | solution.py:66
  558.7 20.4 %collective-permute-start.73 = (bf16[144,2304]{1,0:T(8,128)(2,1)}, bf16[144,2304]{1,0:T(8,128)(2,1)}, u32[]{:S(2)}, u32[]{:S(2)}) collective-permute-start(bf16[144,2304]{1,0:T(8,128)(2,1)} %get-tuple-element.464), channel_id=1, source_target_pairs={{0,4},{4,0},{8,12},{12,8},{1,5},{5,1},{9,13},{13,9},{2,6},{6,2},{1... | collective-permute-start | bytes 1990664 | tf_op jit(solution)/shard_map/ppermute | solution.py:66
  559.9 19.3 %collective-permute-start.74 = (bf16[144,2304]{1,0:T(8,128)(2,1)}, bf16[144,2304]{1,0:T(8,128)(2,1)}, u32[]{:S(2)}, u32[]{:S(2)}) collective-permute-start(bf16[144,2304]{1,0:T(8,128)(2,1)} %get-tuple-element.463), channel_id=1, source_target_pairs={{0,8},{8,0},{4,12},{12,4},{1,9},{9,1},{5,13},{13,5},{2,10},{10,2},... | collective-permute-start | bytes 1990664 | tf_op jit(solution)/shard_map/ppermute | solution.py:66
  619.3 40.2 %all-to-all-start.1 = ((f32[32,4,288]{2,1,0:T(4,128)}), f32[32,4,288]{2,1,0:T(4,128)S(1)}, u32[]{:S(2)}, u32[]{:S(2)}) async-start(f32[32,4,288]{2,1,0:T(4,128)} %bitcast.30), calls=%async_computation.1 | async-start | bytes 393216 | tf_op jit(solution)/shard_map/all_to_all | solution.py:739
  (132 other events, 1463.6 us)
Sparse Core Ops, SparseCore 0:
  10.5 54.2 all-gather.2
  66.7 159.6 all-gather.4

commit v9 on v8

--- a/solution.py
+++ b/solution.py
@@ -651,25 +651,25 @@
     ring = Ring(dffn_in, 2)
     dgate_far = send("core", dgate_b)
     down_s = Scatter(weight_grad(dffn_b, dffn_far, hidden_b, hidden_far))
-    ring.going[0], down_s.blocks, dgate_far = tied(ring.going[0], down_s.blocks, dgate_far)
+    ring.going[1], down_s.blocks, dgate_far = tied(ring.going[1], down_s.blocks, dgate_far)
     ring.go()
     down_s.diagonal()
     dup_far = send("core", dup_b)
     gate_s = Scatter(weight_grad(ffn_in, ffn_in_far, dgate_b, dgate_far))
-    ring.going[0], gate_s.blocks, dup_far, down_s.first = tied(
-        ring.going[0], gate_s.blocks, dup_far, down_s.first
+    ring.going[1], gate_s.blocks, dup_far, down_s.first = tied(
+        ring.going[1], gate_s.blocks, dup_far, down_s.first
     )
     ring.go()
     down_s.direct()
     up_s = Scatter(weight_grad(ffn_in, ffn_in_far, dup_b, dup_far))
-    ring.going[0], up_s.blocks, down_s.middle = tied(ring.going[0], up_s.blocks, down_s.middle)
+    ring.going[1], up_s.blocks, down_s.middle = tied(ring.going[1], up_s.blocks, down_s.middle)
     ring.go()
     down_s.sums()
-    ring.going[0], down_s.last, gate_s.blocks = tied(ring.going[0], down_s.last, gate_s.blocks)
+    ring.going[1], down_s.last, gate_s.blocks = tied(ring.going[1], down_s.last, gate_s.blocks)
     ring.go()
     gate_s.diagonal()
     grad_down = down_s.result().T
-    ring.going[0], gate_s.first, grad_down = tied(ring.going[0], gate_s.first, grad_down)
+    ring.going[1], gate_s.first, grad_down = tied(ring.going[1], gate_s.first, grad_down)
     ring.go()
     gate_s.direct()
     dffn_in, up_s.blocks, gate_s.first, gate_s.middle = tied(

time: 686 us -> 701 us (1.022)
  waiting for transfers between devices: 320 us -> 349 us
    ppermute x42, waiting for transfers between devices: 199 us -> 226 us  [around(): lax.ppermute(value, 'tp', [(i, (i + by) % size) for i in range(size)])]
  transfers between devices with their start and end apart: 92 -> 92, of which waited for: 52 -> 53; matrix products, arithmetic and copies ran while one was open for 13% -> 12% of each run, Pallas kernels for 16% -> 16%
where the time goes in v9:
time: 701 us; the launch traced here: 690 us
  waiting for transfers between devices  349 us (50%)
  Pallas kernels  149 us (21%)
  starting transfers between devices  65.5 us (9%)
  local copies, waits for them, and re-layouts  44.5 us (6%)
  other arithmetic  41.5 us (6%)
  matrix products  23.2 us (3%)
  between operations  16.7 us (2%)
    ppermute x42, waiting for transfers between devices, around(): lax.ppermute(value, 'tp', [(i, (i + by) % size) for i in range(size)])  226 us
    ppermute x46, waiting for transfers between devices, send(): return lax.ppermute(value, *LINKS[link])  79.7 us
    pallas_call x5, Pallas kernels, weight_grad(): pl.pallas_call(kernel, grid_spec=pltpu.PrefetchScalarGridSpec(num_scalar_...  46.1 us
    ppermute x46, starting transfers between devices, send(): return lax.ppermute(value, *LINKS[link])  43.4 us
    all_gather x2, waiting for transfers between devices, gather(): return lax.all_gather(shard, ('fsdp', 'ctx'), axis=0, tiled=True)  37.3 us
    pallas_call x4, Pallas kernels, rowwise(): pl.pallas_call(kernel, grid=(count // block,), in_specs=[by_row] * len(ro...  32 us
    pallas_call x1, Pallas kernels, ffn_backward(): pl.pallas_call(kernel, grid=(first + width // out_cut,), in_specs=[pl.Blo...  28.8 us
    pallas_call x1, Pallas kernels, ffn_forward(): pl.pallas_call(kernel, grid=(first + width // out_cut,), in_specs=[pl.Blo...  26.8 us
  transfers between devices with their start and end apart: 92, of which 53 were waited for; matrix products, arithmetic and copies ran while one was open for 12% of the time, Pallas kernels for 16%

profile of v9, /device:TPU:0, one launch (start us, length us, event | category | flops | bytes accessed | tf_op | source)
XLA Modules:
  0.0 690.0 jit_solution(17880373573092706456)
XLA Ops:
  33.1 31.7 %all-gather.3.cloned.1.call-done = bf16[2304,1536]{1,0:T(8,128)(2,1)} async-done(((bf16[288,1536]{1,0:T(8,128)(2,1)}), bf16[2304,1536]{1,0:T(8,128)(2,1)}) %all-gather.3.cloned.1.call-update) | async-done | bytes 7077904 | tf_op jit(solution)/shard_map/all_gather | solution.py:552
  75.7 14.9 %collective-permute-done.2 = bf16[1,512,512]{2,1,0:T(8,128)(2,1)S(1)} collective-permute-done((bf16[1,512,512]{2,1,0:T(8,128)(2,1)S(1)}, bf16[1,512,512]{2,1,0:T(8,128)(2,1)S(1)}, u32[]{:S(2)}, u32[]{:S(2)}) %collective-permute-start.2) | collective-permute-done | bytes 524320 | tf_op jit(solution)/shard_map/ppermute | solution.py:66
  94.7 17.9 %collective-permute-done.4 = bf16[1,512,512]{2,1,0:T(8,128)(2,1)S(1)} collective-permute-done((bf16[1,512,512]{2,1,0:T(8,128)(2,1)S(1)}, bf16[1,512,512]{2,1,0:T(8,128)(2,1)S(1)}, u32[]{:S(2)}, u32[]{:S(2)}) %collective-permute-start.4) | collective-permute-done | bytes 524320 | tf_op jit(solution)/shard_map/ppermute | solution.py:66
  142.6 8.8 %collective-permute-done.9 = bf16[64,2304]{1,0:T(8,128)(2,1)S(1)} collective-permute-done((bf16[64,2304]{1,0:T(8,128)(2,1)}, bf16[64,2304]{1,0:T(8,128)(2,1)S(1)}, u32[]{:S(2)}, u32[]{:S(2)}) %collective-permute-start.9) | collective-permute-done | bytes 294944 | tf_op jit(solution)/shard_map/ppermute | solution.py:71
  177.0 7.7 %collective-permute-done.13 = bf16[64,2304]{1,0:T(8,128)(2,1)S(1)} collective-permute-done((bf16[64,2304]{1,0:T(8,128)(2,1)S(1)}, bf16[64,2304]{1,0:T(8,128)(2,1)S(1)}, u32[]{:S(2)}, u32[]{:S(2)}) %collective-permute-start.13) | collective-permute-done | bytes 294944 | tf_op jit(solution)/shard_map/ppermute | solution.py:71
  184.7 6.3 collective-permute-done.14
  197.4 6.3 collective-permute-done.16
  203.7 6.3 collective-permute-done.18
  226.3 26.8 %shard_map.238 = (f32[512,2304]{1,0:T(8,128)}, f32[512,2304]{1,0:T(8,128)}, bf16[512,2304]{1,0:T(8,128)(2,1)}, bf16[512,2304]{1,0:T(8,128)(2,1)}) custom-call(bf16[512,2304]{1,0:T(8,128)(2,1)} %get-tuple-element.261.x_ref.near_ref, bf16[2304,6144]{1,0:T(8,128)(2,1)} %all-gather.5.cloned.1.call-done.gate_w.up_w.down_w, ...), custom_call_target="tpu_custom_call" | custom-call | flops 16307453952 | bytes 43646976 | tf_op jit(solution)/shard_map/pallas_call | solution.py:246
  273.1 10.4 %collective-permute-done.21 = bf16[64,2304]{1,0:T(8,128)(2,1)S(1)} collective-permute-done((bf16[64,2304]{1,0:T(8,128)(2,1)S(1)}, bf16[64,2304]{1,0:T(8,128)(2,1)S(1)}, u32[]{:S(2)}, u32[]{:S(2)}) %collective-permute-start.21) | collective-permute-done | bytes 294944 | tf_op jit(solution)/shard_map/ppermute | solution.py:71
  308.8 6.3 collective-permute-done.31
  315.1 6.3 collective-permute-done.32
  321.4 6.3 collective-permute-done.33
  328.2 10.6 %collective-permute-done.35 = bf16[64,2304]{1,0:T(8,128)(2,1)S(1)} collective-permute-done((bf16[64,2304]{1,0:T(8,128)(2,1)S(1)}, bf16[64,2304]{1,0:T(8,128)(2,1)S(1)}, u32[]{:S(2)}, u32[]{:S(2)}) %collective-permute-start.35) | collective-permute-done | bytes 294944 | tf_op jit(solution)/shard_map/ppermute | solution.py:71
  340.3 8.3 %shard_map.239 = (bf16[512,2304]{1,0:T(8,128)(2,1)}, bf16[512,2304]{1,0:T(8,128)(2,1)}, f32[8,2304]{1,0:T(8,128)}) custom-call(bf16[512,2304]{1,0:T(8,128)(2,1)} %copy-done.10, f32[512,2304]{1,0:T(8,128)} %get-tuple-element.276.refs_1_, bf16[512,2304]{1,0:T(8,128)(2,1)} %bitcast_select_fusion.1.refs_2_.refs_3_, f32[1,2304]{1,0:T(1,128)} %add.672.refs_3_), custom_call_target="tpu_custom_call" | custom-call | flops 23592960 | bytes 18874368 | tf_op jit(solution)/shard_map/pallas_call | solution.py:187
  350.0 28.8 %shard_map.240 = (bf16[512,2304]{1,0:T(8,128)(2,1)}, bf16[512,2304]{1,0:T(8,128)(2,1)}, bf16[512,2304]{1,0:T(8,128)(2,1)}) custom-call(bf16[512,2304]{1,0:T(8,128)(2,1)} %get-tuple-element.279.d_ref.near_ref, bf16[2304,6144]{1,0:T(8,128)(2,1)} %all-gather.5.cloned.1.call-done.gate_w.up_w.down_w, bf16[2304,768]{1,0:T(8,128)(2,1)} %copy-done.2, ...), custom_call_target="tpu_custom_call" | custom-call | flops 16307453952 | bytes 46006272 | tf_op jit(solution)/shard_map/pallas_call | solution.py:323
  384.0 11.3 %shard_map.241 = (bf16[576,2304]{1,0:T(8,128)(2,1)}, bf16[144,2304]{1,0:T(8,128)(2,1)}, bf16[144,2304]{1,0:T(8,128)(2,1)}, bf16[144,2304]{1,0:T(8,128)(2,1)}, bf16[144,2304]{1,0:T(8,128)(2,1)}) custom-call(s32[2]{0:T(128)} %get-tuple-element.506.place_ref, bf16[512,2304]{1,0:T(8,128)(2,1)} %get-tuple-element.279.d_ref.near_ref, ...), custom_call_target="tpu_custom_call" | custom-call | flops 5435817984 | bytes 12386304 | tf_op jit(solution)/shard_map/pallas_call | solution.py:381
  403.5 9.3 %collective-permute-done.38 = bf16[64,2304]{1,0:T(8,128)(2,1)S(1)} collective-permute-done((bf16[64,2304]{1,0:T(8,128)(2,1)S(1)}, bf16[64,2304]{1,0:T(8,128)(2,1)S(1)}, u32[]{:S(2)}, u32[]{:S(2)}) %collective-permute-start.38) | collective-permute-done | bytes 294944 | tf_op jit(solution)/shard_map/ppermute | solution.py:71
  414.4 11.2 %shard_map.242 = (bf16[576,2304]{1,0:T(8,128)(2,1)}, bf16[144,2304]{1,0:T(8,128)(2,1)}, bf16[144,2304]{1,0:T(8,128)(2,1)}, bf16[144,2304]{1,0:T(8,128)(2,1)}, bf16[144,2304]{1,0:T(8,128)(2,1)}) custom-call(s32[2]{0:T(128)} %get-tuple-element.506.place_ref, bf16[512,2304]{1,0:T(8,128)(2,1)} %get-tuple-element.261.x_ref.near_ref, ...), custom_call_target="tpu_custom_call" | custom-call | flops 5435817984 | bytes 12386304 | tf_op jit(solution)/shard_map/pallas_call | solution.py:381
  436.3 11.2 %shard_map.243 = (bf16[576,2304]{1,0:T(8,128)(2,1)}, bf16[144,2304]{1,0:T(8,128)(2,1)}, bf16[144,2304]{1,0:T(8,128)(2,1)}, bf16[144,2304]{1,0:T(8,128)(2,1)}, bf16[144,2304]{1,0:T(8,128)(2,1)}) custom-call(s32[2]{0:T(128)} %get-tuple-element.506.place_ref, bf16[512,2304]{1,0:T(8,128)(2,1)} %get-tuple-element.261.x_ref.near_ref, ...), custom_call_target="tpu_custom_call" | custom-call | flops 5435817984 | bytes 12386304 | tf_op jit(solution)/shard_map/pallas_call | solution.py:381
  449.3 9.7 %collective-permute-done.49 = bf16[64,2304]{1,0:T(8,128)(2,1)S(1)} collective-permute-done((bf16[64,2304]{1,0:T(8,128)(2,1)}, bf16[64,2304]{1,0:T(8,128)(2,1)S(1)}, u32[]{:S(2)}, u32[]{:S(2)}) %collective-permute-start.49) | collective-permute-done | bytes 294944 | tf_op jit(solution)/shard_map/ppermute | solution.py:71
  459.0 6.3 collective-permute-done.50
  483.4 8.4 %collective-permute-done.58 = bf16[64,2304]{1,0:T(8,128)(2,1)S(1)} collective-permute-done((bf16[64,2304]{1,0:T(8,128)(2,1)S(1)}, bf16[64,2304]{1,0:T(8,128)(2,1)S(1)}, u32[]{:S(2)}, u32[]{:S(2)}) %collective-permute-start.58) | collective-permute-done | bytes 294944 | tf_op jit(solution)/shard_map/ppermute | solution.py:71
  496.9 10.5 %shard_map.244 = (f32[512,2304]{1,0:T(8,128)}, bf16[512,2304]{1,0:T(8,128)(2,1)}, f32[8,2304]{1,0:T(8,128)}, f32[8,2304]{1,0:T(8,128)}) custom-call(bf16[512,2304]{1,0:T(8,128)(2,1)} %copy-done.4, f32[512,2304]{1,0:T(8,128)} %get-tuple-element.276.refs_1_, bf16[512,2304]{1,0:T(8,128)(2,1)} %copy-done.3, ...), custom_call_target="tpu_custom_call" | custom-call | flops 23592960 | bytes 28311552 | tf_op jit(solution)/shard_map/pallas_call | solution.py:187
  524.4 15.6 %shard_map.245 = (bf16[512,512]{1,0:T(8,128)(2,1)}, bf16[4,512,512]{2,1,0:T(8,128)(2,1)}) custom-call(s32[2]{0:T(128)} %get-tuple-element.505.scalars_ref, bf16[512,512]{1,0:T(8,128)(2,1)} %copy-done.43, bf16[512,512]{1,0:T(8,128)(2,1)} %fusion.22.d_ref, bf16[512,512]{1,0:T(8,128)(2,1)} %copy-done.22, bf16[2048,512]{1,0:T(8,128)(2,1)} %bitcast.92, ...), custom_call_target="tpu_custom_call" | custom-call | flops 5368709120 | bytes 8388608 | tf_op jit(solution)/shard_map/pallas_call | solution.py:459
  557.4 8.4 %collective-permute-done.69 = bf16[512,512]{1,0:T(8,128)(2,1)S(1)} collective-permute-done((bf16[512,512]{1,0:T(8,128)(2,1)S(1)}, bf16[512,512]{1,0:T(8,128)(2,1)S(1)}, u32[]{:S(2)}, u32[]{:S(2)}) %collective-permute-start.69) | collective-permute-done | bytes 524320 | tf_op jit(solution)/shard_map/ppermute | solution.py:66
  578.2 7.4 %shard_map.247 = (bf16[576,1024]{1,0:T(8,128)(2,1)}, bf16[288,1024]{1,0:T(8,128)(2,1)}, bf16[288,1024]{1,0:T(8,128)(2,1)}) custom-call(s32[2]{0:T(128)} %get-tuple-element.506.place_ref, bf16[512,2304]{1,0:T(8,128)(2,1)} %fusion.2.near_ref, bf16[512,1152]{1,0:T(8,128)(2,1)} %copy-done.61, bf16[512,1024]{1,0:T(8,128)(2,1)} %copy-done.29, ...), custom_call_target="tpu_custom_call" | custom-call | flops 2415919104 | bytes 6815744 | tf_op jit(solution)/shard_map/pallas_call | solution.py:381
  585.7 8.0 %collective-permute-done.71 = bf16[128,2304]{1,0:T(8,128)(2,1)} collective-permute-done((bf16[128,2304]{1,0:T(8,128)(2,1)}, bf16[128,2304]{1,0:T(8,128)(2,1)}, u32[]{:S(2)}, u32[]{:S(2)}) %collective-permute-start.71) | collective-permute-done | bytes 589856 | tf_op jit(solution)/shard_map/ppermute | solution.py:71
  601.8 8.1 %collective-permute-done.77 = bf16[288,1024]{1,0:T(8,128)(2,1)S(1)} collective-permute-done((bf16[288,1024]{1,0:T(8,128)(2,1)}, bf16[288,1024]{1,0:T(8,128)(2,1)S(1)}, u32[]{:S(2)}, u32[]{:S(2)}) %collective-permute-start.77) | collective-permute-done | bytes 589856 | tf_op jit(solution)/shard_map/ppermute | solution.py:66
  650.8 10.3 %collective-permute-done.86 = bf16[128,2304]{1,0:T(8,128)(2,1)S(1)} collective-permute-done((bf16[128,2304]{1,0:T(8,128)(2,1)}, bf16[128,2304]{1,0:T(8,128)(2,1)S(1)}, u32[]{:S(2)}, u32[]{:S(2)}) %collective-permute-start.86) | collective-permute-done | bytes 589856 | tf_op jit(solution)/shard_map/ppermute | solution.py:71
  662.0 12.3 %collective-permute-done.87 = bf16[128,2304]{1,0:T(8,128)(2,1)S(1)} collective-permute-done((bf16[128,2304]{1,0:T(8,128)(2,1)S(1)}, bf16[128,2304]{1,0:T(8,128)(2,1)S(1)}, u32[]{:S(2)}, u32[]{:S(2)}) %collective-permute-start.87) | collective-permute-done | bytes 589856 | tf_op jit(solution)/shard_map/ppermute | solution.py:71
  675.8 7.0 %shard_map.248 = bf16[512,2304]{1,0:T(8,128)(2,1)} custom-call(bf16[512,2304]{1,0:T(8,128)(2,1)} %copy-done.9, bf16[512,2304]{1,0:T(8,128)(2,1)} %bitcast.90, f32[512,2304]{1,0:T(8,128)} %get-tuple-element.432.refs_2_, f32[1,2304]{1,0:T(1,128)} %add.721.refs_3_), custom_call_target="tpu_custom_call" | custom-call | flops 23592960 | bytes 18874368 | tf_op jit(solution)/shard_map/pallas_call | solution.py:187
  (445 shorter events, 314.7 us)
Async XLA Ops:
  7.2 57.6 %all-gather.3.cloned.1.call-start = ((), (), s32[]{:S(2)}) async-start(), calls=%async_computation.2 | async-start | bytes 7962624 | tf_op jit(solution)/shard_map/all_gather | solution.py:552
  11.4 21.7 %collective-permute-start = (bf16[288,768]{1,0:T(8,128)(2,1)}, bf16[288,768]{1,0:T(8,128)(2,1)S(1)}, u32[]{:S(2)}, u32[]{:S(2)}) collective-permute-start(bf16[288,768]{1,0:T(8,128)(2,1)} %slice_bitcast_fusion.6), channel_id=1, source_target_pairs={{0,4},{4,0},{8,12},{12,8},{1,5},{5,1},{9,13},{13,9},{2,6},{6,2},{1... | collective-permute-start | bytes 1327112 | tf_op jit(solution)/shard_map/ppermute | solution.py:66
  14.4 18.7 %collective-permute-start.1 = (bf16[288,768]{1,0:T(8,128)(2,1)}, bf16[288,768]{1,0:T(8,128)(2,1)S(1)}, u32[]{:S(2)}, u32[]{:S(2)}) collective-permute-start(bf16[288,768]{1,0:T(8,128)(2,1)} %slice_bitcast_fusion.6), channel_id=1, source_target_pairs={{0,8},{8,0},{4,12},{12,4},{1,9},{9,1},{5,13},{13,5},{2,10},{10,2},... | collective-permute-start | bytes 1327112 | tf_op jit(solution)/shard_map/ppermute | solution.py:66
  19.9 206.4 %all-gather.5.cloned.1.call-start = ((), (), s32[]{:S(2)}) async-start(), calls=%async_computation.3 | async-start | bytes 31850496 | tf_op jit(solution)/shard_map/all_gather | solution.py:552
  70.6 20.1 %collective-permute-start.2 = (bf16[1,512,512]{2,1,0:T(8,128)(2,1)S(1)}, bf16[1,512,512]{2,1,0:T(8,128)(2,1)S(1)}, u32[]{:S(2)}, u32[]{:S(2)}) collective-permute-start(bf16[1,512,512]{2,1,0:T(8,128)(2,1)S(1)} %get-tuple-element.490), channel_id=1, source_target_pairs={{0,4},{4,0},{8,12},{12,8},{1,5},{5,1},{9,13},{13,9},{2,6},{6,2},{1... | collective-permute-start | bytes 1572872 | tf_op jit(solution)/shard_map/ppermute | solution.py:66
  72.1 22.6 %collective-permute-start.3 = (bf16[1,512,512]{2,1,0:T(8,128)(2,1)S(1)}, bf16[1,512,512]{2,1,0:T(8,128)(2,1)S(1)}, u32[]{:S(2)}, u32[]{:S(2)}) collective-permute-start(bf16[1,512,512]{2,1,0:T(8,128)(2,1)S(1)} %get-tuple-element.490), channel_id=1, source_target_pairs={{0,8},{8,0},{4,12},{12,4},{1,9},{9,1},{5,13},{13,5},{2,10},{10,2},... | collective-permute-start | bytes 1572872 | tf_op jit(solution)/shard_map/ppermute | solution.py:66
  72.7 40.0 %collective-permute-start.4 = (bf16[1,512,512]{2,1,0:T(8,128)(2,1)S(1)}, bf16[1,512,512]{2,1,0:T(8,128)(2,1)S(1)}, u32[]{:S(2)}, u32[]{:S(2)}) collective-permute-start(bf16[1,512,512]{2,1,0:T(8,128)(2,1)S(1)} %get-tuple-element.490), channel_id=1, source_target_pairs={{0,12},{12,0},{4,8},{8,4},{1,13},{13,1},{5,9},{9,5},{2,14},{14,2},... | collective-permute-start | bytes 1572872 | tf_op jit(solution)/shard_map/ppermute | solution.py:66
  173.0 30.6 %collective-permute-start.17 = (bf16[1152,768]{1,0:T(8,128)(2,1)}, bf16[1152,768]{1,0:T(8,128)(2,1)S(1)}, u32[]{:S(2)}, u32[]{:S(2)}) collective-permute-start(bf16[1152,768]{1,0:T(8,128)(2,1)} %constant_dynamic-update-slice_fusion.30), channel_id=1, source_target_pairs={{0,16},{16,0},{1,17},{17,1},{2,18},{18,2},{3,19},{19,3},{4,20},{20... | collective-permute-start | bytes 5308424 | tf_op jit(solution)/shard_map/ppermute | solution.py:66
  257.5 26.0 %collective-permute-start.24 = (bf16[512,1152]{1,0:T(8,128)(2,1)S(1)}, bf16[512,1152]{1,0:T(8,128)(2,1)S(1)}, u32[]{:S(2)}, u32[]{:S(2)}) collective-permute-start(bf16[512,1152]{1,0:T(8,128)(2,1)S(1)} %constant_dynamic-slice_fusion.6), channel_id=1, source_target_pairs={{0,16},{16,0},{1,17},{17,1},{2,18},{18,2},{3,19},{19,3},{4,20},{20... | collective-permute-start | bytes 3538952 | tf_op jit(solution)/shard_map/ppermute | solution.py:66
  257.6 25.9 %collective-permute-start.22 = (bf16[512,2304]{1,0:T(8,128)(2,1)}, bf16[512,2304]{1,0:T(8,128)(2,1)S(1)}, u32[]{:S(2)}, u32[]{:S(2)}) collective-permute-start(bf16[512,2304]{1,0:T(8,128)(2,1)} %get-tuple-element.259.cols_ref), channel_id=1, source_target_pairs={{0,16},{16,0},{1,17},{17,1},{2,18},{18,2},{3,19},{19,3},{4,20},{20... | collective-permute-start | bytes 7077896 | tf_op jit(solution)/shard_map/ppermute | solution.py:66
  258.2 25.3 %collective-permute-start.25 = (bf16[512,1152]{1,0:T(8,128)(2,1)S(1)}, bf16[512,1152]{1,0:T(8,128)(2,1)S(1)}, u32[]{:S(2)}, u32[]{:S(2)}) collective-permute-start(bf16[512,1152]{1,0:T(8,128)(2,1)S(1)} %constant_dynamic-slice_fusion.5), channel_id=1, source_target_pairs={{0,16},{16,0},{1,17},{17,1},{2,18},{18,2},{3,19},{19,3},{4,20},{20... | collective-permute-start | bytes 3538952 | tf_op jit(solution)/shard_map/ppermute | solution.py:66
  349.9 28.9 %collective-permute-start.36 = (bf16[512,1152]{1,0:T(8,128)(2,1)S(1)}, bf16[512,1152]{1,0:T(8,128)(2,1)S(1)}, u32[]{:S(2)}, u32[]{:S(2)}) collective-permute-start(bf16[512,1152]{1,0:T(8,128)(2,1)S(1)} %constant_dynamic-slice_fusion.4), channel_id=1, source_target_pairs={{0,16},{16,0},{1,17},{17,1},{2,18},{18,2},{3,19},{19,3},{4,20},{20... | collective-permute-start | bytes 3538952 | tf_op jit(solution)/shard_map/ppermute | solution.py:66
  379.9 21.2 %collective-permute-start.40 = (bf16[512,2304]{1,0:T(8,128)(2,1)}, bf16[512,2304]{1,0:T(8,128)(2,1)S(1)}, u32[]{:S(2)}, u32[]{:S(2)}) collective-permute-start(bf16[512,2304]{1,0:T(8,128)(2,1)} %get-tuple-element.294.cols_ref), channel_id=1, source_target_pairs={{0,16},{16,0},{1,17},{17,1},{2,18},{18,2},{3,19},{19,3},{4,20},{20... | collective-permute-start | bytes 7077896 | tf_op jit(solution)/shard_map/ppermute | solution.py:66
  383.9 41.6 %collective-permute-start.43 = (bf16[512,2304]{1,0:T(8,128)(2,1)}, bf16[512,2304]{1,0:T(8,128)(2,1)}, u32[]{:S(2)}, u32[]{:S(2)}) collective-permute-start(bf16[512,2304]{1,0:T(8,128)(2,1)} %get-tuple-element.305.cols_ref), channel_id=1, source_target_pairs={{0,16},{16,0},{1,17},{17,1},{2,18},{18,2},{3,19},{19,3},{4,20},{20... | collective-permute-start | bytes 7077896 | tf_op jit(solution)/shard_map/ppermute | solution.py:66
  401.1 25.1 %collective-permute-start.44 = (bf16[144,2304]{1,0:T(8,128)(2,1)}, bf16[144,2304]{1,0:T(8,128)(2,1)S(1)}, u32[]{:S(2)}, u32[]{:S(2)}) collective-permute-start(bf16[144,2304]{1,0:T(8,128)(2,1)} %get-tuple-element.306), channel_id=1, source_target_pairs={{0,4},{4,0},{8,12},{12,8},{1,5},{5,1},{9,13},{13,9},{2,6},{6,2},{1... | collective-permute-start | bytes 1990664 | tf_op jit(solution)/shard_map/ppermute | solution.py:66
  402.6 23.6 %collective-permute-start.45 = (bf16[144,2304]{1,0:T(8,128)(2,1)}, bf16[144,2304]{1,0:T(8,128)(2,1)S(1)}, u32[]{:S(2)}, u32[]{:S(2)}) collective-permute-start(bf16[144,2304]{1,0:T(8,128)(2,1)} %get-tuple-element.307), channel_id=1, source_target_pairs={{0,8},{8,0},{4,12},{12,4},{1,9},{9,1},{5,13},{13,5},{2,10},{10,2},... | collective-permute-start | bytes 1990664 | tf_op jit(solution)/shard_map/ppermute | solution.py:66
  403.2 22.9 %collective-permute-start.42 = (bf16[64,2304]{1,0:T(8,128)(2,1)S(1)}, bf16[64,2304]{1,0:T(8,128)(2,1)S(1)}, u32[]{:S(2)}, u32[]{:S(2)}) collective-permute-start(bf16[64,2304]{1,0:T(8,128)(2,1)S(1)} %add_convert_fusion.16), channel_id=1, source_target_pairs={{0,1},{1,2},{2,3},{3,0},{4,5},{5,6},{6,7},{7,4},{8,9},{9,10},{10,1... | collective-permute-start | bytes 884744 | tf_op jit(solution)/shard_map/ppermute | solution.py:71
  412.9 34.6 %collective-permute-start.47 = (bf16[144,2304]{1,0:T(8,128)(2,1)}, bf16[144,2304]{1,0:T(8,128)(2,1)S(1)}, u32[]{:S(2)}, u32[]{:S(2)}) collective-permute-start(bf16[144,2304]{1,0:T(8,128)(2,1)} %get-tuple-element.317), channel_id=1, source_target_pairs={{0,4},{4,0},{8,12},{12,8},{1,5},{5,1},{9,13},{13,9},{2,6},{6,2},{1... | collective-permute-start | bytes 1990664 | tf_op jit(solution)/shard_map/ppermute | solution.py:66
  425.5 22.0 %collective-permute-start.48 = (bf16[144,2304]{1,0:T(8,128)(2,1)}, bf16[144,2304]{1,0:T(8,128)(2,1)}, u32[]{:S(2)}, u32[]{:S(2)}) collective-permute-start(bf16[144,2304]{1,0:T(8,128)(2,1)} %get-tuple-element.318), channel_id=1, source_target_pairs={{0,8},{8,0},{4,12},{12,4},{1,9},{9,1},{5,13},{13,5},{2,10},{10,2},... | collective-permute-start | bytes 1990664 | tf_op jit(solution)/shard_map/ppermute | solution.py:66
  427.6 37.7 %collective-permute-start.51 = (bf16[144,2304]{1,0:T(8,128)(2,1)}, bf16[144,2304]{1,0:T(8,128)(2,1)}, u32[]{:S(2)}, u32[]{:S(2)}) collective-permute-start(bf16[144,2304]{1,0:T(8,128)(2,1)} %get-tuple-element.472), channel_id=1, source_target_pairs={{0,4},{4,0},{8,12},{12,8},{1,5},{5,1},{9,13},{13,9},{2,6},{6,2},{1... | collective-permute-start | bytes 1990664 | tf_op jit(solution)/shard_map/ppermute | solution.py:66
  428.1 37.2 %collective-permute-start.52 = (bf16[144,2304]{1,0:T(8,128)(2,1)}, bf16[144,2304]{1,0:T(8,128)(2,1)}, u32[]{:S(2)}, u32[]{:S(2)}) collective-permute-start(bf16[144,2304]{1,0:T(8,128)(2,1)} %get-tuple-element.471), channel_id=1, source_target_pairs={{0,8},{8,0},{4,12},{12,4},{1,9},{9,1},{5,13},{13,5},{2,10},{10,2},... | collective-permute-start | bytes 1990664 | tf_op jit(solution)/shard_map/ppermute | solution.py:66
  471.6 20.2 %collective-permute-start.59 = (bf16[144,2304]{1,0:T(8,128)(2,1)}, bf16[144,2304]{1,0:T(8,128)(2,1)}, u32[]{:S(2)}, u32[]{:S(2)}) collective-permute-start(bf16[144,2304]{1,0:T(8,128)(2,1)} %get-tuple-element.350), channel_id=1, source_target_pairs={{0,4},{4,0},{8,12},{12,8},{1,5},{5,1},{9,13},{13,9},{2,6},{6,2},{1... | collective-permute-start | bytes 1990664 | tf_op jit(solution)/shard_map/ppermute | solution.py:66
  495.1 20.9 %collective-permute-start.61 = (bf16[144,2304]{1,0:T(8,128)(2,1)S(1)}, bf16[144,2304]{1,0:T(8,128)(2,1)S(1)}, u32[]{:S(2)}, u32[]{:S(2)}) collective-permute-start(bf16[144,2304]{1,0:T(8,128)(2,1)S(1)} %get-tuple-element.468), channel_id=1, source_target_pairs={{0,4},{4,0},{8,12},{12,8},{1,5},{5,1},{9,13},{13,9},{2,6},{6,2},{1... | collective-permute-start | bytes 1990664 | tf_op jit(solution)/shard_map/ppermute | solution.py:66
  495.2 20.9 %collective-permute-start.62 = (bf16[144,2304]{1,0:T(8,128)(2,1)S(1)}, bf16[144,2304]{1,0:T(8,128)(2,1)S(1)}, u32[]{:S(2)}, u32[]{:S(2)}) collective-permute-start(bf16[144,2304]{1,0:T(8,128)(2,1)S(1)} %get-tuple-element.467), channel_id=1, source_target_pairs={{0,8},{8,0},{4,12},{12,4},{1,9},{9,1},{5,13},{13,5},{2,10},{10,2},... | collective-permute-start | bytes 1990664 | tf_op jit(solution)/shard_map/ppermute | solution.py:66
  512.2 27.7 %collective-permute-start.65 = (bf16[512,1152]{1,0:T(8,128)(2,1)}, bf16[512,1152]{1,0:T(8,128)(2,1)S(1)}, u32[]{:S(2)}, u32[]{:S(2)}) collective-permute-start(bf16[512,1152]{1,0:T(8,128)(2,1)} %constant_dynamic-slice_fusion.1), channel_id=1, source_target_pairs={{0,16},{16,0},{1,17},{17,1},{2,18},{18,2},{3,19},{19,3},{4,20},{20... | collective-permute-start | bytes 3538952 | tf_op jit(solution)/shard_map/ppermute | solution.py:66
  520.3 19.6 %collective-permute-start.66 = (bf16[144,2304]{1,0:T(8,128)(2,1)}, bf16[144,2304]{1,0:T(8,128)(2,1)S(1)}, u32[]{:S(2)}, u32[]{:S(2)}) collective-permute-start(bf16[144,2304]{1,0:T(8,128)(2,1)} %get-tuple-element.364), channel_id=1, source_target_pairs={{0,4},{4,0},{8,12},{12,8},{1,5},{5,1},{9,13},{13,9},{2,6},{6,2},{1... | collective-permute-start | bytes 1990664 | tf_op jit(solution)/shard_map/ppermute | solution.py:66
  521.2 18.7 %collective-permute-start.67 = (bf16[144,2304]{1,0:T(8,128)(2,1)}, bf16[144,2304]{1,0:T(8,128)(2,1)}, u32[]{:S(2)}, u32[]{:S(2)}) collective-permute-start(bf16[144,2304]{1,0:T(8,128)(2,1)} %get-tuple-element.365), channel_id=1, source_target_pairs={{0,8},{8,0},{4,12},{12,4},{1,9},{9,1},{5,13},{13,5},{2,10},{10,2},... | collective-permute-start | bytes 1990664 | tf_op jit(solution)/shard_map/ppermute | solution.py:66
  543.4 22.4 %collective-permute-start.69 = (bf16[512,512]{1,0:T(8,128)(2,1)S(1)}, bf16[512,512]{1,0:T(8,128)(2,1)S(1)}, u32[]{:S(2)}, u32[]{:S(2)}) collective-permute-start(bf16[512,512]{1,0:T(8,128)(2,1)S(1)} %get-tuple-element.480), channel_id=1, source_target_pairs={{0,8},{8,0},{4,12},{12,4},{1,9},{9,1},{5,13},{13,5},{2,10},{10,2},... | collective-permute-start | bytes 1572872 | tf_op jit(solution)/shard_map/ppermute | solution.py:66
  544.8 21.0 %collective-permute-start.70 = (bf16[512,512]{1,0:T(8,128)(2,1)S(1)}, bf16[512,512]{1,0:T(8,128)(2,1)S(1)}, u32[]{:S(2)}, u32[]{:S(2)}) collective-permute-start(bf16[512,512]{1,0:T(8,128)(2,1)S(1)} %get-tuple-element.479), channel_id=1, source_target_pairs={{0,12},{12,0},{4,8},{8,4},{1,13},{13,1},{5,9},{9,5},{2,14},{14,2},... | collective-permute-start | bytes 1572872 | tf_op jit(solution)/shard_map/ppermute | solution.py:66
  573.5 20.1 %collective-permute-start.73 = (bf16[144,2304]{1,0:T(8,128)(2,1)}, bf16[144,2304]{1,0:T(8,128)(2,1)}, u32[]{:S(2)}, u32[]{:S(2)}) collective-permute-start(bf16[144,2304]{1,0:T(8,128)(2,1)} %get-tuple-element.464), channel_id=1, source_target_pairs={{0,4},{4,0},{8,12},{12,8},{1,5},{5,1},{9,13},{13,9},{2,6},{6,2},{1... | collective-permute-start | bytes 1990664 | tf_op jit(solution)/shard_map/ppermute | solution.py:66
  574.6 19.0 %collective-permute-start.74 = (bf16[144,2304]{1,0:T(8,128)(2,1)}, bf16[144,2304]{1,0:T(8,128)(2,1)}, u32[]{:S(2)}, u32[]{:S(2)}) collective-permute-start(bf16[144,2304]{1,0:T(8,128)(2,1)} %get-tuple-element.463), channel_id=1, source_target_pairs={{0,8},{8,0},{4,12},{12,4},{1,9},{9,1},{5,13},{13,5},{2,10},{10,2},... | collective-permute-start | bytes 1990664 | tf_op jit(solution)/shard_map/ppermute | solution.py:66
  633.6 40.7 %all-to-all-start.1 = ((f32[32,4,288]{2,1,0:T(4,128)}), f32[32,4,288]{2,1,0:T(4,128)S(1)}, u32[]{:S(2)}, u32[]{:S(2)}) async-start(f32[32,4,288]{2,1,0:T(4,128)} %bitcast.30), calls=%async_computation.1 | async-start | bytes 393216 | tf_op jit(solution)/shard_map/all_to_all | solution.py:739
  (127 other events, 1453.0 us)
Sparse Core Ops, SparseCore 0:
  10.5 54.2 all-gather.2
  66.7 159.6 all-gather.4
